TPU v7x, 32 devices: a whole 2x2x4 slice. The times are simulated.
32 devices in a mesh: row: 8 (over y, x, core), col: 4 (over z).
Axes of the slice: x: 2, y: 2, z: 4, core: 2. Of those that a mesh axis runs over, the one named last changes fastest.
Arguments:
- features: bfloat16 [16384, 256], P(('col', 'row')), may hold values from -6 to 6
- degree: int32 [16384], P(('col', 'row')), may hold values from 1 to 8
- cotangent: bfloat16 [16384, 256], P(('col', 'row')), may hold values from -6 to 6
- tile_values: bfloat16 [12288, 128, 128], P(('col', 'row')), may hold values from -0.078125 to 0.078125
- tile_row: int32 [12288], P(('col', 'row')), may hold values from 0 to 32, as said below
- tile_col: int32 [12288], P(('col', 'row')), may hold values from 0 to 15, as said below
- w_self: bfloat16 [256, 256], replicated, may hold values from -0.375 to 0.375
- w_neigh: bfloat16 [256, 256], replicated, may hold values from -0.375 to 0.375
- bias: float32 [256], replicated, may hold values from -3 to 3
Outputs:
- hidden: bfloat16 [16384, 256], P(('col', 'row'))
- grad_x: bfloat16 [16384, 256], P(('col', 'row'))
- grad_self: float32 [256, 256], replicated
- grad_neigh: float32 [256, 256], replicated
- grad_bias: float32 [256], replicated
Inputs may be any that keep to these rules, and one draw needn't show every extreme that they name: `tile_row`: on each device the live slots come first and the rest hold 32; no two live slots of one device share a tile row and tile column; every device has between 96 and 384 live slots, and some device has all 384 live. `tile_col`: empty slots hold 0.
All inputs are finite; a program needn't handle non-finite values.
Results may differ from a plain program's by a relative error of at most 0.0054.
Values may be sent and summed in bfloat16 or wider, within the bound.
No kernel may reach another device: no remote copies, remote signals or barrier semaphores. Data moves between devices by JAX's collectives and lax.ppermute only.
A program may use at most 256 MiB of HBM per device.

v0:
```python
import jax
import jax.numpy as jnp
from jax import lax
from jax.sharding import PartitionSpec as P


def weight_totals(features, neigh_mean, d_pre):
    local_self = lax.dot_general(
        features, d_pre, (((0,), (0,)), ((), ())), preferred_element_type=jnp.float32
    )
    local_neigh = lax.dot_general(
        neigh_mean, d_pre, (((0,), (0,)), ((), ())), preferred_element_type=jnp.float32
    )
    local_bias = jnp.sum(d_pre.astype(jnp.float32), axis=0)
    return lax.psum((local_self, local_neigh, local_bias), ("row", "col"))


def body(features, degree, cotangent, tile_values, tile_row, tile_col, w_self, w_neigh, bias):
    nodes = features.shape[0]
    width = features.shape[1]
    slots = tile_values.shape[0]
    tile = tile_values.shape[1]
    n_row = lax.axis_size("row")
    n_col = lax.axis_size("col")
    dest_tiles = n_row * nodes // tile
    src_tiles = n_col * nodes // tile
    row_match = tile_row[:, None] == jnp.arange(dest_tiles, dtype=jnp.int32)[None, :]
    col_match = tile_col[:, None] == jnp.arange(src_tiles, dtype=jnp.int32)[None, :]
    highest = lax.Precision.HIGHEST
    gathered = lax.all_gather(features, "col", axis=0, tiled=True)
    pick_cols = col_match.astype(jnp.bfloat16)
    picked = jnp.dot(
        pick_cols, gathered.reshape(src_tiles, tile * width), preferred_element_type=jnp.float32
    )
    picked = picked.astype(jnp.bfloat16).reshape(slots, tile, width)
    prods = jnp.einsum("tuv,tvd->tud", tile_values, picked, preferred_element_type=jnp.float32)
    place_rows = row_match.astype(jnp.float32)
    partial_value = lax.dot_general(
        place_rows,
        prods.reshape(slots, tile * width),
        (((0,), (0,)), ((), ())),
        precision=highest,
        preferred_element_type=jnp.float32,
    )
    partial_value = partial_value.reshape(dest_tiles, tile, width)
    agg = lax.psum_scatter(
        partial_value.reshape(dest_tiles * tile, width), "row", scatter_dimension=0, tiled=True
    )
    scale = degree.astype(jnp.float32)[:, None]
    neigh_mean = (agg / scale).astype(jnp.bfloat16)
    pre = jnp.dot(features, w_self, preferred_element_type=jnp.float32)
    pre = pre + jnp.dot(neigh_mean, w_neigh, preferred_element_type=jnp.float32) + bias[None, :]
    sig = jax.nn.sigmoid(pre)
    hidden = (pre * sig).astype(jnp.bfloat16)
    d_pre = (cotangent.astype(jnp.float32) * sig * (1.0 + pre * (1.0 - sig))).astype(jnp.bfloat16)
    d_agg = (jnp.dot(d_pre, w_neigh.T, preferred_element_type=jnp.float32) / scale).astype(
        jnp.bfloat16
    )
    dest_rows = lax.all_gather(d_agg, "row", axis=0, tiled=True)
    pick_rows = row_match.astype(jnp.bfloat16)
    chosen = jnp.dot(
        pick_rows, dest_rows.reshape(dest_tiles, tile * width), preferred_element_type=jnp.float32
    )
    chosen = chosen.astype(jnp.bfloat16).reshape(slots, tile, width)
    back = jnp.einsum("tuv,tud->tvd", tile_values, chosen, preferred_element_type=jnp.float32)
    place_cols = col_match.astype(jnp.float32)
    back_sum = lax.dot_general(
        place_cols,
        back.reshape(slots, tile * width),
        (((0,), (0,)), ((), ())),
        precision=highest,
        preferred_element_type=jnp.float32,
    )
    back_sum = back_sum.reshape(src_tiles * tile, width)
    own_back = lax.psum_scatter(back_sum, "col", scatter_dimension=0, tiled=True)
    grad_x = (jnp.dot(d_pre, w_self.T, preferred_element_type=jnp.float32) + own_back).astype(
        jnp.bfloat16
    )
    grad_self, grad_neigh, grad_bias = weight_totals(features, neigh_mean, d_pre)
    return (hidden, grad_x, grad_self, grad_neigh, grad_bias)


def solution(mesh):
    placed = (
        P(("col", "row"), None),
        P(("col", "row")),
        P(("col", "row"), None),
        P(("col", "row"), None, None),
        P(("col", "row")),
        P(("col", "row")),
        P(),
        P(),
        P(),
    )
    return jax.shard_map(
        body,
        mesh=mesh,
        in_specs=placed,
        out_specs=(P(("col", "row"), None), P(("col", "row"), None), P(), P(), P()),
        check_vma=False,
    )
```

profile of v0, /device:TPU:0, one launch (start us, length us, event | category | flops | bytes accessed | tf_op | source)
XLA Modules:
  0.0 477.6 jit_solution(16082496316202153690)
XLA Ops:
  7.2 0.0 copy-start
  7.2 0.0 all-gather.3.cloned.1.call-start
  7.2 0.7 all-gather.3.cloned.1.call-update
  7.9 0.0 reduce-scatter.3.cloned.1.call-start
  8.0 32.3 %all-gather.3.cloned.1.call-done = bf16[2048,256]{1,0:T(8,128)(2,1)} async-done(((bf16[512,256]{1,0:T(8,128)(2,1)}), bf16[2048,256]{1,0:T(8,128)(2,1)}) %all-gather.3.cloned.1.call-update) | async-done | bytes 1048592 | tf_op jit(solution)/shard_map/all_gather | solution.py:30
  40.2 1.6 reshape.35
  41.8 12.4 %convolution_convert_fusion.1 = bf16[384,32768]{1,0:T(8,128)(2,1)} fusion(bf16[16,32768]{1,0:T(8,128)(2,1)S(1)} %reshape.35, s32[384]{0:T(512)} %param.14), kind=kOutput, calls=%fused_computation.1 | convolution fusion | flops 415242240 | bytes 26215936 | tf_op jit(solution)/shard_map/dot_general | solution.py:32
  54.2 23.1 %copy.24 = bf16[48,8,128,256]{3,2,1,0:T(8,128)(2,1)} copy(bf16[48,8,128,256]{3,1,2,0:T(8,128)(2,1)} %bitcast.36) | data formatting | bytes 50331648
  77.3 31.6 %convolution_bitcast_fusion.1 = f32[384,128,256]{1,2,0:T(8,128)} fusion(bf16[384,128,256]{2,1,0:T(8,128)(2,1)} %bitcast.34, bf16[384,128,128]{2,1,0:T(8,128)(2,1)} %param.12), kind=kOutput, calls=%fused_computation.3 | convolution fusion | flops 3221225472 | bytes 88080384 | tf_op jit(solution)/shard_map/tuv,tvd->tud/dot_general | solution.py:36
  108.9 0.0 copy-start.3
  108.9 49.2 %copy.18 = f32[384,128,256]{0,2,1:T(8,128)} copy(f32[384,128,256]{1,2,0:T(8,128)} %convolution_bitcast_fusion.1) | data formatting | bytes 100663296 | tf_op jit(solution)/shard_map/tuv,tvd->tud/dot_general | solution.py:36
  158.1 0.0 copy-done.3
  158.1 0.0 copy-start.5
  158.1 0.0 copy-start.1
  158.1 0.0 copy-start.2
  158.1 0.0 copy-start.6
  158.1 0.0 copy-start.7
  158.1 29.0 %fusion.5 = f32[32,32768]{1,0:T(8,128)} fusion(f32[384,32768]{0,1:T(8,128)} %bitcast.32, s32[384]{0:T(512)S(1)} %copy-done.3), kind=kOutput, calls=%fused_computation.20 | convolution fusion | flops 4831862784 | bytes 54527488 | tf_op jit(solution)/shard_map/dot_general | solution.py:38
  187.1 4.9 %reshape_reshape.3 = f32[4096,256]{1,0:T(8,128)} reshape(f32[32,32768]{1,0:T(8,128)} %fusion.5) | data formatting | bytes 8388608 | tf_op jit(solution)/shard_map/reshape;reshape | solution.py:47
  192.0 0.0 reduce-scatter.3.cloned.1.call-update
  192.0 0.0 all-gather.5.cloned.1.call-start
  192.0 0.0 copy-done.5
  192.1 0.0 copy-done.1
  192.1 0.0 copy-done.2
  192.1 0.2 fusion.13
  192.3 50.7 %reduce-scatter.3.cloned.1.call-done = f32[512,256]{1,0:T(8,128)} async-done(((f32[4096,256]{1,0:T(8,128)}), f32[512,256]{1,0:T(8,128)}) %reduce-scatter.3.cloned.1.call-update) | async-done | bytes 524304 | tf_op jit(solution)/shard_map/reduce_scatter | solution.py:46
  243.0 1.2 divide_convert_fusion
  244.1 0.0 copy-done
  244.2 0.0 copy-done.6
  244.2 0.0 copy-done.7
  244.2 1.1 convert_reduce_fusion
  245.3 1.0 fusion.2
  246.3 0.0 all-gather.5.cloned.1.call-update
  246.3 0.2 all-reduce.3.cloned.1.call-start
  246.5 1.0 convolution_bitcast_fusion.2
  247.5 1.0 fusion.14
  248.5 0.0 all-reduce.3.cloned.1.call-update
  248.5 0.0 reduce-scatter.5.cloned.1.call-start
  248.6 25.8 %all-gather.5.cloned.1.call-done = bf16[4096,256]{1,0:T(8,128)(2,1)} async-done(((bf16[512,256]{1,0:T(8,128)(2,1)}), bf16[4096,256]{1,0:T(8,128)(2,1)}) %all-gather.5.cloned.1.call-update) | async-done | bytes 2097168 | tf_op jit(solution)/shard_map/all_gather | solution.py:59
  274.4 2.9 reshape.38
  277.2 11.8 %convolution_convert_fusion = bf16[384,32768]{1,0:T(8,128)(2,1)} fusion(bf16[32,32768]{1,0:T(8,128)(2,1)S(1)} %reshape.38, s32[384]{0:T(512)S(1)} %copy-done.3), kind=kOutput, calls=%fused_computation | convolution fusion | flops 817901568 | bytes 27264512 | tf_op jit(solution)/shard_map/dot_general | solution.py:61
  289.0 23.1 %copy.25 = bf16[48,8,128,256]{3,2,1,0:T(8,128)(2,1)} copy(bf16[48,8,128,256]{3,1,2,0:T(8,128)(2,1)} %bitcast.37) | data formatting | bytes 50331648
  312.1 31.6 %convolution_bitcast_fusion = f32[384,128,256]{1,2,0:T(8,128)} fusion(bf16[384,128,256]{2,1,0:T(8,128)(2,1)} %bitcast.35, bf16[384,128,128]{2,1,0:T(8,128)(2,1)} %param.12), kind=kOutput, calls=%fused_computation.2 | convolution fusion | flops 3221225472 | bytes 88080384 | tf_op jit(solution)/shard_map/tuv,tud->tvd/dot_general | solution.py:65
  343.7 0.0 copy-start.4
  343.7 49.2 %copy.20 = f32[384,128,256]{0,2,1:T(8,128)} copy(f32[384,128,256]{1,2,0:T(8,128)} %convolution_bitcast_fusion) | data formatting | bytes 100663296 | tf_op jit(solution)/shard_map/tuv,tud->tvd/dot_general | solution.py:65
  393.0 0.0 copy-done.4
  393.0 27.8 %fusion.7 = f32[16,32768]{1,0:T(8,128)S(1)} fusion(f32[384,32768]{0,1:T(8,128)} %bitcast.33, s32[384]{0:T(512)S(1)} %copy-done.4), kind=kOutput, calls=%fused_computation.21 | convolution fusion | flops 2415931392 | bytes 52430336 | tf_op jit(solution)/shard_map/dot_general | solution.py:67
  420.8 1.5 reshape.41
  422.3 0.0 reduce-scatter.5.cloned.1.call-update
  422.3 42.7 %psum.23 = f32[256]{0:T(256)} all-reduce(f32[256]{0:T(256)S(1)} %get-tuple-element.17), channel_id=1, replica_groups=mesh['row'=8,'col'=4] {'row','col'}, use_global_device_ids=true, to_apply=%region_5.0 | all-reduce | flops 256 | bytes 2048 | tf_op jit(solution)/shard_map/psum | solution.py:15
  465.0 0.0 all-reduce.3.cloned.1.call-done
  465.0 1.8 copy.21
  466.8 0.6 reduce-scatter.5.cloned.1.call-done
  467.4 2.0 fusion.1
  469.4 1.7 copy.28
  (1 shorter events, 0.0 us)
Async XLA Ops:
  7.2 237.0 %copy-start = (bf16[256,256]{1,0:T(8,128)(2,1)S(1)}, bf16[256,256]{1,0:T(8,128)(2,1)}, u32[]{:S(2)}) copy-start(bf16[256,256]{1,0:T(8,128)(2,1)} %param.16) | copy-start | bytes 393220
  7.2 33.1 %all-gather.3.cloned.1.call-start = ((), (), s32[]{:S(2)}) async-start(), calls=%async_computation.2 | async-start | bytes 1310720 | tf_op jit(solution)/shard_map/all_gather | solution.py:30
  7.9 235.0 %reduce-scatter.3.cloned.1.call-start = ((), (), s32[]{:S(2)}) async-start(), calls=%async_computation.3 | async-start | bytes 4718592 | tf_op jit(solution)/shard_map/reduce_scatter | solution.py:46
  108.9 49.2 %copy-start.3 = (s32[384]{0:T(512)S(1)}, s32[384]{0:T(512)}, u32[]{:S(2)}) copy-start(s32[384]{0:T(512)} %param.13) | copy-start | bytes 4612
  158.1 34.0 %copy-start.5 = (s32[512]{0:T(512)S(1)}, s32[512]{0:T(512)}, u32[]{:S(2)}) copy-start(s32[512]{0:T(512)} %param.10) | copy-start | bytes 6148
  158.1 34.0 %copy-start.1 = (bf16[512,256]{1,0:T(8,128)(2,1)S(1)}, bf16[512,256]{1,0:T(8,128)(2,1)}, u32[]{:S(2)}) copy-start(bf16[512,256]{1,0:T(8,128)(2,1)} %param.9) | copy-start | bytes 786436
  158.1 34.0 %copy-start.2 = (bf16[256,256]{1,0:T(8,128)(2,1)S(1)}, bf16[256,256]{1,0:T(8,128)(2,1)}, u32[]{:S(2)}) copy-start(bf16[256,256]{1,0:T(8,128)(2,1)} %param.15) | copy-start | bytes 393220
  158.1 86.1 %copy-start.6 = (bf16[512,256]{1,0:T(8,128)(2,1)S(1)}, bf16[512,256]{1,0:T(8,128)(2,1)}, u32[]{:S(2)}) copy-start(bf16[512,256]{1,0:T(8,128)(2,1)} %param.11) | copy-start | bytes 786436
  158.1 86.1 %copy-start.7 = (f32[256]{0:T(256)S(1)}, f32[256]{0:T(256)}, u32[]{:S(2)}) copy-start(f32[256]{0:T(256)} %param.17) | copy-start | bytes 3076
  192.0 82.4 %all-gather.5.cloned.1.call-start = ((), (), s32[]{:S(2)}) async-start(), calls=%async_computation.4 | async-start | bytes 2359296 | tf_op jit(solution)/shard_map/all_gather | solution.py:59
  246.3 218.7 %all-reduce.3.cloned.1.call-start = ((), (), s32[]{:S(2)}) async-start(), calls=%async_computation.6 | async-start | bytes 1048576 | tf_op jit(solution)/shard_map/psum | solution.py:15
  248.5 218.8 %reduce-scatter.5.cloned.1.call-start = ((), (), s32[]{:S(2)}) async-start(), calls=%async_computation.5 | async-start | bytes 2621440 | tf_op jit(solution)/shard_map/reduce_scatter | solution.py:75
  343.7 49.3 %copy-start.4 = (s32[384]{0:T(512)S(1)}, s32[384]{0:T(512)}, u32[]{:S(2)}) copy-start(s32[384]{0:T(512)} %param.14) | copy-start | bytes 4612
Sparse Core Ops, SparseCore 0:
  9.6 30.6 all-gather.2
  192.1 50.8 reduce-scatter.2
  246.4 27.8 all-gather.4
  281.2 128.1 all-reduce.2
  422.4 44.8 reduce-scatter.4
where the time goes:
time: 480 us; the launch traced here: 478 us
  local copies, waits for them, and re-layouts  159 us (33%)
  matrix products  150 us (31%)
  waiting for transfers between devices  110 us (23%)
  blocking collectives  42.7 us (9%)
  between operations  13.9 us (3%)
    reduce_scatter x1, waiting for transfers between devices, body(): lax.psum_scatter(partial_value.reshape(dest_tiles * tile, width), 'row',...  50.7 us
    unnamed x20, local copies, waits for them, and re-layouts  49.7 us
    dot_general x1, local copies, waits for them, and re-layouts, body(): jnp.einsum('tuv,tud->tvd', tile_values, chosen, preferred_element_type=jn...  49.2 us
    dot_general x1, local copies, waits for them, and re-layouts, body(): jnp.einsum('tuv,tvd->tud', tile_values, picked, preferred_element_type=jn...  49.2 us
    psum x1, blocking collectives, weight_totals(): return lax.psum((local_self, local_neigh, local_bias), ('row', 'col'))  42.7 us
    all_gather x1, waiting for transfers between devices, body(): gathered = lax.all_gather(features, 'col', axis=0, tiled=True)  32.3 us
    dot_general x1, matrix products, body(): jnp.einsum('tuv,tud->tvd', tile_values, chosen, preferred_element_type=jn...  31.6 us
    dot_general x1, matrix products, body(): jnp.einsum('tuv,tvd->tud', tile_values, picked, preferred_element_type=jn...  31.6 us
  transfers between devices with their start and end apart: 5, of which 4 were waited for; matrix products, arithmetic and copies ran while one was open for 32% of the time, Pallas kernels for 0%

commit v1 on v0

v1 whole, which is shorter than its diff:
```python
import jax
import jax.numpy as jnp
from jax import lax
from jax.experimental import pallas as pl
from jax.experimental.pallas import tpu as pltpu
from jax.sharding import PartitionSpec as P

F32 = jnp.float32
BF16 = jnp.bfloat16
MIB = 1 << 20
RESIDENT_BYTES = 20 * MIB
PARTS = 2
BIAS_ROWS = 16


def vmem():
    return pl.BlockSpec(memory_space=pltpu.VMEM)


def params(limit_mib):
    return pltpu.CompilerParams(vmem_limit_bytes=limit_mib * MIB)


def sds(shape, dtype):
    return jax.ShapeDtypeStruct(shape, dtype)


def densify(tile_values, tile_row, tile_col, place, n_row, n_col, per_dev, resident):
    slots, tile, _ = tile_values.shape
    chips = n_row // 2
    rows = n_row * per_dev
    cols = n_col * per_dev
    cells = rows * cols

    def kernel(row_ref, col_ref, place_ref, values_ref, dense_ref, table, blank, sem):
        blank[...] = jnp.zeros_like(blank)
        chip = place_ref[0] // 2
        core = place_ref[0] % 2
        col_at = place_ref[1]

        def clear(i, carry):
            for k in range(8):
                table[i * 8 + k] = slots
            return carry

        lax.fori_loop(0, cells // 8, clear, 0)

        def note(i, carry):
            for k in range(4):
                at = i * 4 + k
                table[row_ref[at] * cols + col_ref[at]] = at
            return carry

        lax.fori_loop(0, slots // 4, note, 0)

        def fill(i, carry):
            slot = table[i]
            t = i // cols
            s = i % cols
            owner = t // per_dev
            block = ((owner % 2) ^ core) * chips + ((owner // 2) ^ chip)
            u = (block * per_dev + t % per_dev) * tile
            v = (((s // per_dev) ^ col_at) * per_dev + s % per_dev) * tile
            where = dense_ref.at[
                pl.ds(pl.multiple_of(u, tile), tile), pl.ds(pl.multiple_of(v, tile), tile)
            ]

            @pl.when(slot < slots)
            def _():
                pltpu.make_async_copy(values_ref.at[slot], where, sem).start()

            @pl.when(slot >= slots)
            def _():
                pltpu.make_async_copy(blank, where, sem).start()

            return carry

        lax.fori_loop(0, cells, fill, 0)
        pltpu.make_async_copy(dense_ref, dense_ref, sem).wait()

    shape = (rows * tile, cols * tile)
    out_shape = pltpu.VMEM(shape, BF16) if resident else sds(shape, BF16)
    return pl.pallas_call(
        kernel,
        out_shape=out_shape,
        grid_spec=pltpu.PrefetchScalarGridSpec(
            num_scalar_prefetch=3,
            grid=(),
            in_specs=[pl.BlockSpec(memory_space=pl.ANY)],
            out_specs=vmem() if resident else pl.BlockSpec(memory_space=pl.ANY),
            scratch_shapes=[
                pltpu.SMEM((cells + cols,), jnp.int32),
                pltpu.VMEM((tile, tile), BF16),
                pltpu.SemaphoreType.DMA,
            ],
        ),
        compiler_params=params(8),
        name="densify",
    )(tile_row, tile_col, place, tile_values)


def pinned(dense, resident):
    return pltpu.with_memory_space_constraint(dense, pltpu.VMEM) if resident else dense


def forward(dense, pieces, first, count, dtype, resident):
    n_col = len(pieces)
    nodes, wide = pieces[0].shape
    cols = n_col * nodes

    def kernel(*refs):
        dense_ref, piece_refs, out_ref, source = refs[0], refs[1 : 1 + n_col], refs[-2], refs[-1]
        step = pl.program_id(0)

        @pl.when(step == 0)
        def _():
            for m in range(n_col):
                source[m * nodes : (m + 1) * nodes, :] = piece_refs[m][...]

        if resident:
            at = pl.multiple_of((first + step) * nodes, nodes)
            block = dense_ref[pl.ds(at, nodes), :]
        else:
            block = dense_ref[...]
        out_ref[0] = jnp.dot(block, source[...], preferred_element_type=F32).astype(dtype)

    spec = vmem() if resident else pl.BlockSpec((nodes, cols), lambda i: (i + first, 0))
    return pl.pallas_call(
        kernel,
        out_shape=sds((count, nodes, wide), dtype),
        grid=(count,),
        in_specs=[spec] + [pl.BlockSpec((nodes, wide), lambda i: (0, 0))] * n_col,
        out_specs=pl.BlockSpec((1, nodes, wide), lambda i: (i, 0, 0)),
        scratch_shapes=[pltpu.VMEM((cols, wide), BF16)],
        compiler_params=params(32),
        name="forward",
    )(pinned(dense, resident), *pieces)


def add_parts(keep, got):
    chips, nodes, wide = keep.shape

    def kernel(keep_ref, got_ref, *out_refs):
        for j in range(1, chips):
            out_refs[j - 1][...] = (keep_ref[j] + got_ref[j].astype(F32)).astype(BF16)

    return pl.pallas_call(
        kernel,
        out_shape=[sds((nodes, wide), BF16)] * (chips - 1),
        in_specs=[vmem()] * 2,
        out_specs=[vmem()] * (chips - 1),
        compiler_params=params(16),
        name="add_parts",
    )(keep, got)


def middle(features, scale, cotangent, w_self, w_neigh, bias, parts, n_row):
    nodes, width = features.shape
    chips = n_row // 2
    count = len(parts)
    wide = width // count
    share = width // n_row
    flat = []
    for keep, got, arrivals in parts:
        flat += [keep, got, *arrivals]
    each = len(flat) // count
    extra = 2 * share + BIAS_ROWS

    def kernel(*refs):
        feat_ref, scale_ref, cot_ref, ws_ref, wn_ref, bias_ref = refs[:6]
        part_refs = refs[6 : 6 + len(flat)]
        hidden_ref, d_pre_ref = refs[6 + len(flat) : 8 + len(flat)]
        send_refs = refs[8 + len(flat) : 8 + len(flat) + chips]
        rest_refs = refs[8 + len(flat) + chips :]
        inv = scale_ref[...]
        sums = []
        for h in range(count):
            mine = part_refs[h * each : (h + 1) * each]
            total = mine[0][0] + mine[1][0].astype(F32)
            for ref in mine[2:]:
                total = total + ref[...].astype(F32)
            sums.append(total)
        agg = jnp.concatenate(sums, axis=1) if count > 1 else sums[0]
        neigh_mean = (agg / inv).astype(BF16)
        features_now = feat_ref[...]
        pre = jnp.dot(features_now, ws_ref[...], preferred_element_type=F32)
        pre = pre + jnp.dot(neigh_mean, wn_ref[...], preferred_element_type=F32) + bias_ref[...]
        sig = jax.nn.sigmoid(pre)
        hidden_ref[...] = (pre * sig).astype(BF16)
        d_pre = (cot_ref[...].astype(F32) * sig * (1.0 + pre * (1.0 - sig))).astype(BF16)
        d_pre_ref[...] = d_pre
        d_agg = lax.dot_general(
            d_pre, wn_ref[...], (((1,), (1,)), ((), ())), preferred_element_type=F32
        )
        d_agg = jnp.transpose(d_agg / inv).astype(BF16)
        over = (((0,), (0,)), ((), ()))
        grad_self = lax.dot_general(features_now, d_pre, over, preferred_element_type=F32)
        grad_neigh = lax.dot_general(neigh_mean, d_pre, over, preferred_element_type=F32)
        grads = jnp.concatenate([grad_self, grad_neigh], axis=1).astype(BF16)
        bias_sum = jnp.sum(d_pre.astype(F32), axis=0, keepdims=True)
        bias_row = jnp.concatenate([bias_sum, bias_sum], axis=1).astype(BF16)
        bias_rows = jnp.broadcast_to(bias_row, (BIAS_ROWS, 2 * width))
        place_chip = lax.axis_index("row") // 2
        place_core = lax.axis_index("row") % 2
        grads_ref = rest_refs[-1]
        grads_ref[...] = grads.astype(F32)
        for j in range(chips):
            send_refs[j][0:wide, :] = d_agg[0:wide]
            for k in range(2):
                owner = (place_chip ^ j) * 2 + (place_core ^ k)
                at = pl.multiple_of(owner * share, share)
                low = wide + k * share
                send_refs[j][low : low + share, :] = grads_ref[pl.ds(at, share), :].astype(BF16)
            send_refs[j][wide + 2 * share :, :] = bias_rows
        for h in range(1, count):
            rest_refs[h - 1][...] = d_agg[h * wide : (h + 1) * wide]

    first_two = [pl.BlockSpec((1, nodes, wide), lambda i: (0, 0, 0))] * 2
    whole = lambda shape: pl.BlockSpec(shape, lambda i: (0,) * len(shape))
    part_specs = (first_two + [whole((nodes, wide))] * (each - 2)) * count
    outs = (
        [sds((nodes, width), BF16)] * 2
        + [sds((wide + extra, nodes), BF16)] * chips
        + [sds((wide, nodes), BF16)] * (count - 1)
    )
    args = [features, scale, cotangent, w_self, w_neigh, bias]
    res = pl.pallas_call(
        kernel,
        out_shape=outs,
        grid=(1,),
        in_specs=[whole(a.shape) for a in args] + part_specs,
        out_specs=[whole(o.shape) for o in outs],
        scratch_shapes=[pltpu.VMEM((width, 2 * width), F32)],
        compiler_params=params(32),
        name="middle",
    )(*args, *flat)
    return res[0], res[1], res[2 : 2 + chips], res[2 + chips :]


def backward(dense, pieces, n_col, wide, share, resident):
    n_row = len(pieces)
    nodes = pieces[0].shape[1]
    rows = n_row * nodes
    height = pieces[0].shape[0]
    extra = share + BIAS_ROWS if share else 0

    def kernel(*refs):
        dense_ref, piece_refs = refs[0], refs[1 : 1 + n_row]
        out_refs = refs[1 + n_row : 1 + n_row + n_col]
        total_ref = refs[1 + n_row + n_col] if share else None
        stacked = refs[-1]
        step = pl.program_id(0)

        @pl.when(step == 0)
        def _():
            for b in range(n_row):
                stacked[:, b * nodes : (b + 1) * nodes] = piece_refs[b][0:wide, :]
            if share:
                chips = n_row // 2
                total = jnp.zeros((share, nodes), F32)
                bias_total = jnp.zeros((BIAS_ROWS, nodes), F32)
                for b in range(n_row):
                    low = wide + (b // chips) * share
                    total = total + piece_refs[b][low : low + share, :].astype(F32)
                    bias_total = bias_total + piece_refs[b][wide + 2 * share :, :].astype(F32)
                total_ref[0:share, :] = total
                total_ref[share:, :] = bias_total
                for m in range(1, n_col):
                    out_refs[m][wide : wide + share, :] = total.astype(BF16)
                    out_refs[m][wide + share :, :] = bias_total.astype(BF16)

        for m in range(n_col):

            @pl.when(step == m)
            def _():
                if resident:
                    block = dense_ref[:, m * nodes : (m + 1) * nodes]
                else:
                    block = dense_ref[...]
                out = jnp.dot(stacked[...], block, preferred_element_type=F32)
                out_refs[m][0:wide, :] = out.astype(out_refs[m].dtype)

    spec = vmem() if resident else pl.BlockSpec((rows, nodes), lambda i: (0, i))
    whole = lambda shape: pl.BlockSpec(shape, lambda i: (0,) * len(shape))
    outs = [sds((wide, nodes), F32)] + [sds((wide + extra, nodes), BF16)] * (n_col - 1)
    if share:
        outs.append(sds((extra, nodes), F32))
    res = pl.pallas_call(
        kernel,
        out_shape=outs,
        grid=(n_col,),
        in_specs=[spec] + [whole((height, nodes))] * n_row,
        out_specs=[whole(o.shape) for o in outs],
        scratch_shapes=[pltpu.VMEM((wide, rows), BF16)],
        compiler_params=params(36),
        name="backward",
    )(pinned(dense, resident), *pieces)
    return res[0], res[1:n_col], (res[n_col] if share else None)


def share_total(total, arrivals, wide):
    height, nodes = total.shape

    def kernel(total_ref, *refs):
        out_ref = refs[-1]
        acc = total_ref[...]
        for ref in refs[:-1]:
            acc = acc + ref[wide : wide + height, :].astype(F32)
        out_ref[...] = acc

    return pl.pallas_call(
        kernel,
        out_shape=sds((height, nodes), F32),
        in_specs=[vmem()] * (1 + len(arrivals)),
        out_specs=vmem(),
        compiler_params=params(8),
        name="share_total",
    )(total, *arrivals)


def weight_grads(shares, n_row):
    share = shares[0].shape[0]
    width = shares[0].shape[1] // 2
    chips = n_row // 2

    def kernel(*refs):
        self_ref, neigh_ref = refs[-2:]
        chip = lax.axis_index("row") // 2
        core = lax.axis_index("row") % 2
        for b in range(n_row):
            owner = (chip ^ (b % chips)) * 2 + (core ^ (b // chips))
            at = pl.multiple_of(owner * share, share)
            self_ref[pl.ds(at, share), :] = refs[b][:, 0:width]
            neigh_ref[pl.ds(at, share), :] = refs[b][:, width:]

    return pl.pallas_call(
        kernel,
        out_shape=[sds((width, width), F32)] * 2,
        in_specs=[vmem()] * n_row,
        out_specs=[vmem()] * 2,
        compiler_params=params(8),
        name="weight_grads",
    )(*shares)


def finish(d_pre, w_self, owns, arrivals):
    nodes, width = d_pre.shape
    count = len(owns)
    wide = width // count
    others = len(arrivals[0])
    flat = list(owns) + [a for part in arrivals for a in part]

    def kernel(d_pre_ref, ws_ref, *refs):
        out_ref = refs[-1]
        direct = lax.dot_general(
            d_pre_ref[...], ws_ref[...], (((1,), (1,)), ((), ())), preferred_element_type=F32
        )
        for h in range(count):
            acc = refs[h][...]
            for ref in refs[count + h * others : count + (h + 1) * others]:
                acc = acc + ref[0:wide, :].astype(F32)
            low = h * wide
            out = direct[:, low : low + wide] + jnp.transpose(acc)
            out_ref[:, low : low + wide] = out.astype(BF16)

    return pl.pallas_call(
        kernel,
        out_shape=sds((nodes, width), BF16),
        in_specs=[vmem()] * (2 + len(flat)),
        out_specs=vmem(),
        compiler_params=params(16),
        name="finish",
    )(d_pre, w_self, *flat)


def swap(x, axis, mask):
    size = lax.axis_size(axis)
    return lax.ppermute(x, axis, [(i, i ^ mask) for i in range(size)])


def far_first(n):
    return sorted(range(1, n), key=lambda m: -bin(m).count("1") * n - m)


def body(features, degree, cotangent, tile_values, tile_row, tile_col, w_self, w_neigh, bias):
    nodes, width = features.shape
    tile = tile_values.shape[1]
    n_row = lax.axis_size("row")
    n_col = lax.axis_size("col")
    chips = n_row // 2
    per_dev = nodes // tile
    wide = width // PARTS
    share = width // n_row
    resident = n_row * nodes * n_col * nodes * 2 <= RESIDENT_BYTES

    sources = []
    for h in range(PARTS):
        own = features[:, h * wide : (h + 1) * wide]
        pieces = {0: own}
        for m in far_first(n_col):
            pieces[m] = swap(own, "col", m)
        sources.append([pieces[m] for m in range(n_col)])

    place = jnp.stack([lax.axis_index("row"), lax.axis_index("col")]).astype(jnp.int32)
    dense = densify(tile_values, tile_row, tile_col, place, n_row, n_col, per_dev, resident)
    scale = degree.astype(F32)[:, None]

    parts = []
    for h in range(PARTS):
        give = forward(dense, sources[h], chips, chips, BF16, resident)
        got = swap(give, "row", 1)
        keep = forward(dense, sources[h], 0, chips, F32, resident)
        sends = add_parts(keep, got)
        arrivals = [swap(sends[j - 1], "row", 2 * j) for j in range(1, chips)]
        parts.append((keep, got, arrivals))

    hidden, d_pre, first_sends, later = middle(
        features, scale, cotangent, w_self, w_neigh, bias[None, :], parts, n_row
    )

    owns, backs = [], []
    for h in range(PARTS):
        if h == 0:
            mine = [first_sends[0]] + [
                swap(first_sends[j], "row", 2 * j) for j in range(1, chips)
            ]
        else:
            mine = [later[h - 1]] + [swap(later[h - 1], "row", 2 * j) for j in range(1, chips)]
        siblings = [swap(piece, "row", 1) for piece in mine]
        own, sends, total = backward(
            dense, mine + siblings, n_col, wide, share if h == 0 else 0, resident
        )
        arrived = {m: swap(sends[m - 1], "col", m) for m in far_first(n_col)}
        arrived = [arrived[m] for m in range(1, n_col)]
        owns.append(own)
        backs.append(arrived)
        if h == 0:
            summed = share_total(total, arrived, wide)
            grad_bias = summed[share, 0:width]
            piece = summed[0:share]
            shares = [piece] + [swap(piece, "row", 2 * j) for j in range(1, chips)]
            shares = shares + [swap(s, "row", 1) for s in shares]
            grad_self, grad_neigh = weight_grads(shares, n_row)

    grad_x = finish(d_pre, w_self, owns, backs)
    return (hidden, grad_x, grad_self, grad_neigh, grad_bias)


def solution(mesh):
    placed = (
        P(("col", "row"), None),
        P(("col", "row")),
        P(("col", "row"), None),
        P(("col", "row"), None, None),
        P(("col", "row")),
        P(("col", "row")),
        P(),
        P(),
        P(),
    )
    return jax.shard_map(
        body,
        mesh=mesh,
        in_specs=placed,
        out_specs=(P(("col", "row"), None), P(("col", "row"), None), P(), P(), P()),
        check_vma=False,
    )
```

time: 480 us -> 154 us (0.32)
  matrix products: 150 us -> 0 us
  local copies, waits for them, and re-layouts: 159 us -> 23.2 us
  waiting for transfers between devices: 110 us -> 33.5 us
  Pallas kernels: 0 us -> 49.3 us
  starting transfers between devices: 0.38 us -> 44.9 us
  blocking collectives: 42.7 us -> 0 us
  between operations: 13.9 us -> 0.86 us
    dot_general x12 -> x0, matrix products: 150 us -> none  [the longest x1 31.6 us: body(): jnp.einsum('tuv,tud->tvd', tile_values, chosen, preferred_element_type=jn...]
    dot_general x2 -> x0, local copies, waits for them, and re-layouts: 98.4 us -> none  [the longest x1 49.2 us: body(): jnp.einsum('tuv,tud->tvd', tile_values, chosen, preferred_element_type=jn...]
    all_gather x2 -> x0, waiting for transfers between devices: 58.1 us -> none  [the longest x1 32.3 us: body(): gathered = lax.all_gather(features, 'col', axis=0, tiled=True)]
    reduce_scatter x2 -> x0, waiting for transfers between devices: 51.2 us -> none  [the longest x1 50.7 us: body(): lax.psum_scatter(partial_value.reshape(dest_tiles * tile, width), 'row',...]
    pallas_call x0 -> x13, Pallas kernels: none -> 49.3 us  [the longest x1 24.1 us: densify(): pl.pallas_call(kernel, out_shape=out_shape, grid_spec=pltpu.PrefetchScala...]
    ppermute x0 -> x41, starting transfers between devices: none -> 44.9 us  [swap(): return lax.ppermute(x, axis, [(i, i ^ mask) for i in range(size)])]
    psum x1 -> x0, blocking collectives: 42.7 us -> none  [weight_totals(): return lax.psum((local_self, local_neigh, local_bias), ('row', 'col'))]
    ppermute x0 -> x41, waiting for transfers between devices: none -> 33.5 us  [swap(): return lax.ppermute(x, axis, [(i, i ^ mask) for i in range(size)])]
  transfers between devices with their start and end apart: 5 -> 41, of which waited for: 4 -> 10; matrix products, arithmetic and copies ran while one was open for 32% -> 1% of each run, Pallas kernels for 0% -> 30%
where the time goes in v1:
time: 154 us; the launch traced here: 152 us
  Pallas kernels  49.3 us (32%)
  starting transfers between devices  44.9 us (29%)
  waiting for transfers between devices  33.5 us (22%)
  local copies, waits for them, and re-layouts  23.2 us (15%)
    ppermute x41, starting transfers between devices, swap(): return lax.ppermute(x, axis, [(i, i ^ mask) for i in range(size)])  44.9 us
    ppermute x41, waiting for transfers between devices, swap(): return lax.ppermute(x, axis, [(i, i ^ mask) for i in range(size)])  33.5 us
    pallas_call x1, Pallas kernels, densify(): pl.pallas_call(kernel, out_shape=out_shape, grid_spec=pltpu.PrefetchScala...  24.1 us
    unnamed x48, local copies, waits for them, and re-layouts  20.8 us
    pallas_call x4, Pallas kernels, forward(): pl.pallas_call(kernel, out_shape=sds((count, nodes, wide), dtype), grid=(...  11.6 us
    pallas_call x2, Pallas kernels, backward(): pl.pallas_call(kernel, out_shape=outs, grid=(n_col,), in_specs=[spec] + [...  7.75 us
  transfers between devices with their start and end apart: 41, of which 10 were waited for; matrix products, arithmetic and copies ran while one was open for 1% of the time, Pallas kernels for 30%

profile of v1, /device:TPU:0, one launch (start us, length us, event | category | flops | bytes accessed | tf_op | source)
XLA Modules:
  0.0 151.8 jit_solution(14468487964677170740)
XLA Ops:
  0.6 1.0 fusion
  1.6 5.1 %collective-permute-start.2 = (bf16[512,128]{1,0:T(8,128)(2,1)S(1)}, bf16[512,128]{1,0:T(8,128)(2,1)S(1)}, u32[]{:S(2)}, u32[]{:S(2)}) collective-permute-start(bf16[512,128]{1,0:T(8,128)(2,1)S(1)} %get-tuple-element.54.refs_1_), channel_id=1, source_target_pairs={{0,3},{1,2},{2,1},{3,0},{4,7},{5,6},{6,5},{7,4},{8,11},{9,10},{10,... | collective-permute-start | bytes 393224 | tf_op jit(solution)/shard_map/ppermute | solution.py:378
  6.7 0.6 collective-permute-start
  7.4 3.7 %collective-permute-start.9 = (bf16[512,128]{1,0:T(8,128)(2,1)S(1)}, bf16[512,128]{1,0:T(8,128)(2,1)S(1)}, u32[]{:S(2)}, u32[]{:S(2)}) collective-permute-start(bf16[512,128]{1,0:T(8,128)(2,1)S(1)} %get-tuple-element.53.refs_1_), channel_id=1, source_target_pairs={{0,3},{1,2},{2,1},{3,0},{4,7},{5,6},{6,5},{7,4},{8,11},{9,10},{10,... | collective-permute-start | bytes 393224 | tf_op jit(solution)/shard_map/ppermute | solution.py:378
  11.2 6.2 %collective-permute-start.7 = (bf16[512,128]{1,0:T(8,128)(2,1)S(1)}, bf16[512,128]{1,0:T(8,128)(2,1)S(1)}, u32[]{:S(2)}, u32[]{:S(2)}) collective-permute-start(bf16[512,128]{1,0:T(8,128)(2,1)S(1)} %get-tuple-element.53.refs_1_), channel_id=1, source_target_pairs={{0,1},{1,0},{2,3},{3,2},{4,5},{5,4},{6,7},{7,6},{8,9},{9,8},{10,11... | collective-permute-start | bytes 393224 | tf_op jit(solution)/shard_map/ppermute | solution.py:378
  17.4 4.6 %copy-done.2 = bf16[384,128,128]{2,1,0:T(8,128)(2,1)S(1)} copy-done((bf16[384,128,128]{2,1,0:T(8,128)(2,1)S(1)}, bf16[384,128,128]{2,1,0:T(8,128)(2,1)}, u32[]{:S(2)}) %copy-start.2) | copy-done | bytes 12582936
  21.9 0.7 copy-done.18
  22.6 0.7 copy-done.19
  23.3 24.1 %densify.1.refs_0_ = bf16[4096,2048]{1,0:T(8,128)(2,1)S(1)} custom-call(s32[384]{0:T(512)S(1)} %copy-done.18, s32[384]{0:T(512)S(1)} %copy-done.19, s32[2]{0:T(128)S(1)} %pad_add_fusion.place_ref, bf16[384,128,128]{2,1,0:T(8,128)(2,1)S(1)} %copy-done.2), custom_call_target="tpu_custom_call" | custom-call | tf_op jit(solution)/shard_map/densify/pallas_call | solution.py:83
  47.5 2.9 %forward.5 = bf16[4,512,128]{2,1,0:T(8,128)(2,1)S(1)} custom-call(bf16[4096,2048]{1,0:T(8,128)(2,1)S(1)} %densify.1.refs_0_, bf16[512,128]{1,0:T(8,128)(2,1)S(1)} %get-tuple-element.54.refs_1_, bf16[512,128]{1,0:T(8,128)(2,1)S(1)} %collective-permute-done.refs_2_, bf16[512,128]{1,0:T(8,128)(2,1)S(1)} %collective-permute-done.1.refs_3_, ...), custom_call_target="tpu_custom_call" | custom-call | tf_op jit(solution)/shard_map/forward/pallas_call | solution.py:128
  50.5 2.9 %forward.7 = bf16[4,512,128]{2,1,0:T(8,128)(2,1)S(1)} custom-call(bf16[4096,2048]{1,0:T(8,128)(2,1)S(1)} %densify.1.refs_0_, bf16[512,128]{1,0:T(8,128)(2,1)S(1)} %get-tuple-element.53.refs_1_, bf16[512,128]{1,0:T(8,128)(2,1)S(1)} %collective-permute-done.7.refs_2_, bf16[512,128]{1,0:T(8,128)(2,1)S(1)} %collective-permute-done.8.refs_3_, ...), custom_call_target="tpu_custom_call" | custom-call | tf_op jit(solution)/shard_map/forward/pallas_call | solution.py:128
  53.4 0.6 copy-done.5
  54.1 0.7 copy-done.7
  54.7 0.5 collective-permute-start.10
  55.2 2.9 %forward.4.keep_ref.refs_6_ = f32[4,512,128]{2,1,0:T(8,128)S(1)} custom-call(bf16[4096,2048]{1,0:T(8,128)(2,1)S(1)} %densify.1.refs_0_, bf16[512,128]{1,0:T(8,128)(2,1)S(1)} %get-tuple-element.54.refs_1_, bf16[512,128]{1,0:T(8,128)(2,1)S(1)} %collective-permute-done.refs_2_, bf16[512,128]{1,0:T(8,128)(2,1)S(1)} %collective-permute-done.1.refs_3_, ...), custom_call_target="tpu_custom_call" | custom-call | tf_op jit(solution)/shard_map/forward/pallas_call | solution.py:128
  58.1 0.7 add_parts.2
  58.9 1.9 %collective-permute-start.4 = (bf16[512,128]{1,0:T(8,128)(2,1)S(1)}, bf16[512,128]{1,0:T(8,128)(2,1)S(1)}, u32[]{:S(2)}, u32[]{:S(2)}) collective-permute-start(bf16[512,128]{1,0:T(8,128)(2,1)S(1)} %get-tuple-element.29), channel_id=1, source_target_pairs={{0,8},{4,12},{8,0},{12,4},{16,24},{20,28},{24,16},{28,20},{1,9},{5... | collective-permute-start | bytes 393224 | tf_op jit(solution)/shard_map/ppermute | solution.py:378
  60.8 2.9 %forward.6.keep_ref.refs_11_ = f32[4,512,128]{2,1,0:T(8,128)S(1)} custom-call(bf16[4096,2048]{1,0:T(8,128)(2,1)S(1)} %densify.1.refs_0_, bf16[512,128]{1,0:T(8,128)(2,1)S(1)} %get-tuple-element.53.refs_1_, bf16[512,128]{1,0:T(8,128)(2,1)S(1)} %collective-permute-done.7.refs_2_, bf16[512,128]{1,0:T(8,128)(2,1)S(1)} %copy-done.8, bf16[512,128]{1,0:T(8,128)(2,1)S(1)} %copy-done.6), custom_call_target="tpu_custom_call" | custom-call | tf_op jit(solution)/shard_map/forward/pallas_call | solution.py:128
  63.8 1.2 collective-permute-start.5
  65.4 0.8 add_parts.3
  66.2 1.9 %collective-permute-start.11 = (bf16[512,128]{1,0:T(8,128)(2,1)}, bf16[512,128]{1,0:T(8,128)(2,1)}, u32[]{:S(2)}, u32[]{:S(2)}) collective-permute-start(bf16[512,128]{1,0:T(8,128)(2,1)} %get-tuple-element.32), channel_id=1, source_target_pairs={{0,8},{4,12},{8,0},{12,4},{16,24},{20,28},{24,16},{28,20},{1,9},{5... | collective-permute-start | bytes 393224 | tf_op jit(solution)/shard_map/ppermute | solution.py:378
  68.1 1.1 collective-permute-start.12
  69.3 0.7 copy-done.14
  70.3 0.9 copy.14.refs_1_
  71.2 2.0 %collective-permute-done.5.refs_9_ = bf16[512,128]{1,0:T(8,128)(2,1)S(1)} collective-permute-done((bf16[512,128]{1,0:T(8,128)(2,1)}, bf16[512,128]{1,0:T(8,128)(2,1)S(1)}, u32[]{:S(2)}, u32[]{:S(2)}) %collective-permute-start.5) | collective-permute-done | bytes 131104 | tf_op jit(solution)/shard_map/ppermute | solution.py:378
  73.2 0.7 copy-done.16
  73.9 0.9 collective-permute-done.11.refs_13_
  74.7 3.0 %collective-permute-done.12.refs_14_ = bf16[512,128]{1,0:T(8,128)(2,1)} collective-permute-done((bf16[512,128]{1,0:T(8,128)(2,1)}, bf16[512,128]{1,0:T(8,128)(2,1)}, u32[]{:S(2)}, u32[]{:S(2)}) %collective-permute-start.12) | collective-permute-done | bytes 131104 | tf_op jit(solution)/shard_map/ppermute | solution.py:378
  77.8 0.9 copy-done.4
  78.7 0.9 copy-done.9
  79.6 0.9 copy-done.12
  80.6 0.9 copy-done.13
  81.5 0.9 copy-done.15
  82.4 0.9 copy-done.17
  83.3 2.4 %middle.1 = (bf16[512,256]{1,0:T(8,128)(2,1)}, bf16[512,256]{1,0:T(8,128)(2,1)S(1)}, bf16[208,512]{1,0:T(8,128)(2,1)S(1)}, bf16[208,512]{1,0:T(8,128)(2,1)S(1)},...) custom-call(bf16[512,256]{1,0:T(8,128)(2,1)S(1)} %copy-done.3, ...), custom_call_target="tpu_custom_call" | custom-call | tf_op jit(solution)/shard_map/middle/pallas_call | solution.py:227
  85.9 1.5 collective-permute-start.15
  87.5 1.7 %collective-permute-start.23 = (bf16[128,512]{1,0:T(8,128)(2,1)S(1)}, bf16[128,512]{1,0:T(8,128)(2,1)S(1)}, u32[]{:S(2)}, u32[]{:S(2)}) collective-permute-start(bf16[128,512]{1,0:T(8,128)(2,1)S(1)} %get-tuple-element.42.refs_1_), channel_id=1, source_target_pairs={{0,24},{4,28},{8,16},{12,20},{16,8},{20,12},{24,0},{28,4},{1,25},{... | collective-permute-start | bytes 393224 | tf_op jit(solution)/shard_map/ppermute | solution.py:378
  89.1 1.3 collective-permute-start.16
  90.4 0.5 collective-permute-start.22
  90.9 6.4 %collective-permute-done.23.refs_4_ = bf16[128,512]{1,0:T(8,128)(2,1)S(1)} collective-permute-done((bf16[128,512]{1,0:T(8,128)(2,1)S(1)}, bf16[128,512]{1,0:T(8,128)(2,1)S(1)}, u32[]{:S(2)}, u32[]{:S(2)}) %collective-permute-start.23) | collective-permute-done | bytes 131104 | tf_op jit(solution)/shard_map/ppermute | solution.py:378
  97.3 0.5 collective-permute-start.18
  97.8 3.1 %collective-permute-done.15.refs_3_ = bf16[208,512]{1,0:T(8,128)(2,1)S(1)} collective-permute-done((bf16[208,512]{1,0:T(8,128)(2,1)S(1)}, bf16[208,512]{1,0:T(8,128)(2,1)S(1)}, u32[]{:S(2)}, u32[]{:S(2)}) %collective-permute-start.15) | collective-permute-done | bytes 213024 | tf_op jit(solution)/shard_map/ppermute | solution.py:378
  100.9 1.4 collective-permute-done.22.refs_3_
  102.3 1.7 %collective-permute-start.21 = (bf16[128,512]{1,0:T(8,128)(2,1)S(1)}, bf16[128,512]{1,0:T(8,128)(2,1)S(1)}, u32[]{:S(2)}, u32[]{:S(2)}) collective-permute-start(bf16[128,512]{1,0:T(8,128)(2,1)S(1)} %get-tuple-element.42.refs_1_), channel_id=1, source_target_pairs={{0,8},{4,12},{8,0},{12,4},{16,24},{20,28},{24,16},{28,20},{1,9},{5... | collective-permute-start | bytes 393224 | tf_op jit(solution)/shard_map/ppermute | solution.py:378
  104.1 3.2 %collective-permute-done.21.refs_2_ = bf16[128,512]{1,0:T(8,128)(2,1)S(1)} collective-permute-done((bf16[128,512]{1,0:T(8,128)(2,1)S(1)}, bf16[128,512]{1,0:T(8,128)(2,1)S(1)}, u32[]{:S(2)}, u32[]{:S(2)}) %collective-permute-start.21) | collective-permute-done | bytes 131104 | tf_op jit(solution)/shard_map/ppermute | solution.py:378
  107.3 0.5 collective-permute-start.27
  107.9 0.4 collective-permute-start.25
  108.6 0.7 copy-done.22
  109.3 5.8 %copy-done.1 = bf16[4096,2048]{1,0:T(8,128)(2,1)S(1)} copy-done((bf16[4096,2048]{1,0:T(8,128)(2,1)S(1)}, bf16[4096,2048]{1,0:T(8,128)(2,1)}, u32[]{:S(2)}) %copy-start.1) | copy-done | bytes 16777240
  115.0 4.8 %backward.2 = (f32[128,512]{1,0:T(8,128)}, bf16[176,512]{1,0:T(8,128)(2,1)S(1)}, bf16[176,512]{1,0:T(8,128)(2,1)S(1)}, bf16[176,512]{1,0:T(8,128)(2,1)S(1)}, f32[48,512]{1,0:T(8,128)S(1)}) custom-call(bf16[4096,2048]{1,0:T(8,128)(2,1)S(1)} %copy-done.1, bf16[208,512]{1,0:T(8,128)(2,1)S(1)} %get-tuple-element.37.refs_1_, ...), custom_call_target="tpu_custom_call" | custom-call | tf_op jit(solution)/shard_map/backward/pallas_call | solution.py:288
  120.0 2.5 %collective-permute-start.29 = (bf16[176,512]{1,0:T(8,128)(2,1)S(1)}, bf16[176,512]{1,0:T(8,128)(2,1)S(1)}, u32[]{:S(2)}, u32[]{:S(2)}) collective-permute-start(bf16[176,512]{1,0:T(8,128)(2,1)S(1)} %get-tuple-element.45), channel_id=1, source_target_pairs={{0,2},{1,3},{2,0},{3,1},{4,6},{5,7},{6,4},{7,5},{8,10},{9,11},{10,... | collective-permute-start | bytes 540680 | tf_op jit(solution)/shard_map/ppermute | solution.py:378
  122.4 1.8 %collective-permute-start.30 = (bf16[176,512]{1,0:T(8,128)(2,1)S(1)}, bf16[176,512]{1,0:T(8,128)(2,1)S(1)}, u32[]{:S(2)}, u32[]{:S(2)}) collective-permute-start(bf16[176,512]{1,0:T(8,128)(2,1)S(1)} %get-tuple-element.46), channel_id=1, source_target_pairs={{0,3},{1,2},{2,1},{3,0},{4,7},{5,6},{6,5},{7,4},{8,11},{9,10},{10,... | collective-permute-start | bytes 540680 | tf_op jit(solution)/shard_map/ppermute | solution.py:378
  124.2 3.0 %backward.3 = (f32[128,512]{1,0:T(8,128)S(1)}, bf16[128,512]{1,0:T(8,128)(2,1)S(1)}, bf16[128,512]{1,0:T(8,128)(2,1)S(1)}, bf16[128,512]{1,0:T(8,128)(2,1)S(1)}) custom-call(bf16[4096,2048]{1,0:T(8,128)(2,1)S(1)} %copy-done.1, bf16[128,512]{1,0:T(8,128)(2,1)S(1)} %get-tuple-element.42.refs_1_, bf16[128,512]{1,0:T(8,128)(2,1)S(1)} %collective-permute-done.21.refs_2_, ...), custom_call_target="tpu_custom_call" | custom-call | tf_op jit(solution)/shard_map/backward/pallas_call | solution.py:288
  127.3 2.6 %collective-permute-start.32 = (bf16[128,512]{1,0:T(8,128)(2,1)S(1)}, bf16[128,512]{1,0:T(8,128)(2,1)S(1)}, u32[]{:S(2)}, u32[]{:S(2)}) collective-permute-start(bf16[128,512]{1,0:T(8,128)(2,1)S(1)} %get-tuple-element.48), channel_id=1, source_target_pairs={{0,2},{1,3},{2,0},{3,1},{4,6},{5,7},{6,4},{7,5},{8,10},{9,11},{10,... | collective-permute-start | bytes 393224 | tf_op jit(solution)/shard_map/ppermute | solution.py:378
  129.9 0.5 collective-permute-done.28.refs_2_.refs_0_
  130.4 1.5 collective-permute-start.33
  131.9 4.2 %collective-permute-done.29.refs_3_.refs_1_ = bf16[176,512]{1,0:T(8,128)(2,1)S(1)} collective-permute-done((bf16[176,512]{1,0:T(8,128)(2,1)S(1)}, bf16[176,512]{1,0:T(8,128)(2,1)S(1)}, u32[]{:S(2)}, u32[]{:S(2)}) %collective-permute-start.29) | collective-permute-done | bytes 180256 | tf_op jit(solution)/shard_map/ppermute | solution.py:378
  136.1 2.1 %collective-permute-start.36 = (f32[32,512]{1,0:T(8,128)S(1)}, f32[32,512]{1,0:T(8,128)S(1)}, u32[]{:S(2)}, u32[]{:S(2)}) collective-permute-start(f32[32,512]{1,0:T(8,128)S(1)} %slice.16.refs_0_), channel_id=1, source_target_pairs={{0,24},{4,28},{8,16},{12,20},{16,8},{20,12},{24,0},{28,4},{1,25},{... | collective-permute-start | bytes 196616 | tf_op jit(solution)/shard_map/ppermute | solution.py:378
  138.2 1.1 collective-permute-start.35
  139.7 8.7 %collective-permute-done.32.refs_6_ = bf16[128,512]{1,0:T(8,128)(2,1)S(1)} collective-permute-done((bf16[128,512]{1,0:T(8,128)(2,1)S(1)}, bf16[128,512]{1,0:T(8,128)(2,1)S(1)}, u32[]{:S(2)}, u32[]{:S(2)}) %collective-permute-start.32) | collective-permute-done | bytes 131104 | tf_op jit(solution)/shard_map/ppermute | solution.py:378
  148.3 0.5 collective-permute-start.40
  149.4 0.6 slice.17
  149.9 1.0 finish.1
  150.9 0.9 weight_grads.1
  (85 shorter events, 2.8 us)
Async XLA Ops:
  1.6 9.6 %collective-permute-start.2 = (bf16[512,128]{1,0:T(8,128)(2,1)S(1)}, bf16[512,128]{1,0:T(8,128)(2,1)S(1)}, u32[]{:S(2)}, u32[]{:S(2)}) collective-permute-start(bf16[512,128]{1,0:T(8,128)(2,1)S(1)} %get-tuple-element.54.refs_1_), channel_id=1, source_target_pairs={{0,3},{1,2},{2,1},{3,0},{4,7},{5,6},{6,5},{7,4},{8,11},{9,10},{10,... | collective-permute-start | bytes 393224 | tf_op jit(solution)/shard_map/ppermute | solution.py:378
  6.7 40.7 %collective-permute-start.1 = (bf16[512,128]{1,0:T(8,128)(2,1)S(1)}, bf16[512,128]{1,0:T(8,128)(2,1)S(1)}, u32[]{:S(2)}, u32[]{:S(2)}) collective-permute-start(bf16[512,128]{1,0:T(8,128)(2,1)S(1)} %get-tuple-element.54.refs_1_), channel_id=1, source_target_pairs={{0,2},{1,3},{2,0},{3,1},{4,6},{5,7},{6,4},{7,5},{8,10},{9,11},{10,... | collective-permute-start | bytes 393224 | tf_op jit(solution)/shard_map/ppermute | solution.py:378
  6.7 40.7 %collective-permute-start = (bf16[512,128]{1,0:T(8,128)(2,1)S(1)}, bf16[512,128]{1,0:T(8,128)(2,1)S(1)}, u32[]{:S(2)}, u32[]{:S(2)}) collective-permute-start(bf16[512,128]{1,0:T(8,128)(2,1)S(1)} %get-tuple-element.54.refs_1_), channel_id=1, source_target_pairs={{0,1},{1,0},{2,3},{3,2},{4,5},{5,4},{6,7},{7,6},{8,9},{9,8},{10,11... | collective-permute-start | bytes 393224 | tf_op jit(solution)/shard_map/ppermute | solution.py:378
  7.4 43.1 %collective-permute-start.9 = (bf16[512,128]{1,0:T(8,128)(2,1)S(1)}, bf16[512,128]{1,0:T(8,128)(2,1)S(1)}, u32[]{:S(2)}, u32[]{:S(2)}) collective-permute-start(bf16[512,128]{1,0:T(8,128)(2,1)S(1)} %get-tuple-element.53.refs_1_), channel_id=1, source_target_pairs={{0,3},{1,2},{2,1},{3,0},{4,7},{5,6},{6,5},{7,4},{8,11},{9,10},{10,... | collective-permute-start | bytes 393224 | tf_op jit(solution)/shard_map/ppermute | solution.py:378
  11.1 39.3 %collective-permute-start.8 = (bf16[512,128]{1,0:T(8,128)(2,1)S(1)}, bf16[512,128]{1,0:T(8,128)(2,1)S(1)}, u32[]{:S(2)}, u32[]{:S(2)}) collective-permute-start(bf16[512,128]{1,0:T(8,128)(2,1)S(1)} %get-tuple-element.53.refs_1_), channel_id=1, source_target_pairs={{0,2},{1,3},{2,0},{3,1},{4,6},{5,7},{6,4},{7,5},{8,10},{9,11},{10,... | collective-permute-start | bytes 393224 | tf_op jit(solution)/shard_map/ppermute | solution.py:378
  11.2 39.3 %collective-permute-start.7 = (bf16[512,128]{1,0:T(8,128)(2,1)S(1)}, bf16[512,128]{1,0:T(8,128)(2,1)S(1)}, u32[]{:S(2)}, u32[]{:S(2)}) collective-permute-start(bf16[512,128]{1,0:T(8,128)(2,1)S(1)} %get-tuple-element.53.refs_1_), channel_id=1, source_target_pairs={{0,1},{1,0},{2,3},{3,2},{4,5},{5,4},{6,7},{7,6},{8,9},{9,8},{10,11... | collective-permute-start | bytes 393224 | tf_op jit(solution)/shard_map/ppermute | solution.py:378
  17.4 4.6 %copy-start.2 = (bf16[384,128,128]{2,1,0:T(8,128)(2,1)S(1)}, bf16[384,128,128]{2,1,0:T(8,128)(2,1)}, u32[]{:S(2)}) copy-start(bf16[384,128,128]{2,1,0:T(8,128)(2,1)} %values_ref.1) | copy-start | bytes 37748740
  21.9 0.7 copy-start.18
  22.6 0.7 copy-start.19
  47.4 13.4 %copy-start = (bf16[4096,2048]{1,0:T(8,128)(2,1)}, bf16[4096,2048]{1,0:T(8,128)(2,1)S(1)}, u32[]{:S(2)}) copy-start(bf16[4096,2048]{1,0:T(8,128)(2,1)S(1)} %densify.1.refs_0_) | copy-start | bytes 50331652
  50.4 7.8 %collective-permute-start.3 = (bf16[4,512,128]{2,1,0:T(8,128)(2,1)S(1)}, bf16[4,512,128]{2,1,0:T(8,128)(2,1)S(1)}, u32[]{:S(2)}, u32[]{:S(2)}) collective-permute-start(bf16[4,512,128]{2,1,0:T(8,128)(2,1)S(1)} %forward.5), channel_id=1, source_target_pairs={{0,4},{4,0},{8,12},{12,8},{16,20},{20,16},{24,28},{28,24},{1,5},{5... | collective-permute-start | bytes 1572872 | tf_op jit(solution)/shard_map/ppermute | solution.py:378
  53.4 0.7 copy-start.5
  54.7 15.6 %copy-start.23 = (s32[512]{0:T(512)S(1)}, s32[512]{0:T(512)}, u32[]{:S(2)}) copy-start(s32[512]{0:T(512)} %param.10) | copy-start | bytes 6148
  54.7 23.0 %copy-start.3 = (bf16[512,256]{1,0:T(8,128)(2,1)S(1)}, bf16[512,256]{1,0:T(8,128)(2,1)}, u32[]{:S(2)}) copy-start(bf16[512,256]{1,0:T(8,128)(2,1)} %refs_0_.1) | copy-start | bytes 786436
  54.7 23.0 %copy-start.20 = (f32[256]{0:T(256)S(1)}, f32[256]{0:T(256)}, u32[]{:S(2)}) copy-start(f32[256]{0:T(256)} %param.17) | copy-start | bytes 3076
  54.7 10.6 %collective-permute-start.10 = (bf16[4,512,128]{2,1,0:T(8,128)(2,1)S(1)}, bf16[4,512,128]{2,1,0:T(8,128)(2,1)S(1)}, u32[]{:S(2)}, u32[]{:S(2)}) collective-permute-start(bf16[4,512,128]{2,1,0:T(8,128)(2,1)S(1)} %forward.7), channel_id=1, source_target_pairs={{0,4},{4,0},{8,12},{12,8},{16,20},{20,16},{24,28},{28,24},{1,5},{5... | collective-permute-start | bytes 1572872 | tf_op jit(solution)/shard_map/ppermute | solution.py:378
  55.2 5.6 %copy-start.6 = (bf16[512,128]{1,0:T(8,128)(2,1)S(1)}, bf16[512,128]{1,0:T(8,128)(2,1)}, u32[]{:S(2)}) copy-start(bf16[512,128]{1,0:T(8,128)(2,1)} %copy-done.5) | copy-start | bytes 393220
  55.2 5.6 %copy-start.8 = (bf16[512,128]{1,0:T(8,128)(2,1)S(1)}, bf16[512,128]{1,0:T(8,128)(2,1)}, u32[]{:S(2)}) copy-start(bf16[512,128]{1,0:T(8,128)(2,1)} %copy-done.7) | copy-start | bytes 393220
  58.9 10.4 %collective-permute-start.4 = (bf16[512,128]{1,0:T(8,128)(2,1)S(1)}, bf16[512,128]{1,0:T(8,128)(2,1)S(1)}, u32[]{:S(2)}, u32[]{:S(2)}) collective-permute-start(bf16[512,128]{1,0:T(8,128)(2,1)S(1)} %get-tuple-element.29), channel_id=1, source_target_pairs={{0,8},{4,12},{8,0},{12,4},{16,24},{20,28},{24,16},{28,20},{1,9},{5... | collective-permute-start | bytes 393224 | tf_op jit(solution)/shard_map/ppermute | solution.py:378
  63.8 9.5 %collective-permute-start.5 = (bf16[512,128]{1,0:T(8,128)(2,1)}, bf16[512,128]{1,0:T(8,128)(2,1)S(1)}, u32[]{:S(2)}, u32[]{:S(2)}) collective-permute-start(bf16[512,128]{1,0:T(8,128)(2,1)} %get-tuple-element.30), channel_id=1, source_target_pairs={{0,16},{4,20},{8,24},{12,28},{16,0},{20,4},{24,8},{28,12},{1,17},{... | collective-permute-start | bytes 393224 | tf_op jit(solution)/shard_map/ppermute | solution.py:378
  65.0 8.9 %collective-permute-start.6 = (bf16[512,128]{1,0:T(8,128)(2,1)}, bf16[512,128]{1,0:T(8,128)(2,1)}, u32[]{:S(2)}, u32[]{:S(2)}) collective-permute-start(bf16[512,128]{1,0:T(8,128)(2,1)} %get-tuple-element.31), channel_id=1, source_target_pairs={{0,24},{4,28},{8,16},{12,20},{16,8},{20,12},{24,0},{28,4},{1,25},{... | collective-permute-start | bytes 393224 | tf_op jit(solution)/shard_map/ppermute | solution.py:378
  66.2 8.6 %collective-permute-start.11 = (bf16[512,128]{1,0:T(8,128)(2,1)}, bf16[512,128]{1,0:T(8,128)(2,1)}, u32[]{:S(2)}, u32[]{:S(2)}) collective-permute-start(bf16[512,128]{1,0:T(8,128)(2,1)} %get-tuple-element.32), channel_id=1, source_target_pairs={{0,8},{4,12},{8,0},{12,4},{16,24},{20,28},{24,16},{28,20},{1,9},{5... | collective-permute-start | bytes 393224 | tf_op jit(solution)/shard_map/ppermute | solution.py:378
  68.1 9.6 %collective-permute-start.12 = (bf16[512,128]{1,0:T(8,128)(2,1)}, bf16[512,128]{1,0:T(8,128)(2,1)}, u32[]{:S(2)}, u32[]{:S(2)}) collective-permute-start(bf16[512,128]{1,0:T(8,128)(2,1)} %get-tuple-element.33), channel_id=1, source_target_pairs={{0,16},{4,20},{8,24},{12,28},{16,0},{20,4},{24,8},{28,12},{1,17},{... | collective-permute-start | bytes 393224 | tf_op jit(solution)/shard_map/ppermute | solution.py:378
  69.3 0.7 copy-start.14
  69.9 7.8 %collective-permute-start.13 = (bf16[512,128]{1,0:T(8,128)(2,1)}, bf16[512,128]{1,0:T(8,128)(2,1)}, u32[]{:S(2)}, u32[]{:S(2)}) collective-permute-start(bf16[512,128]{1,0:T(8,128)(2,1)} %get-tuple-element.34), channel_id=1, source_target_pairs={{0,24},{4,28},{8,16},{12,20},{16,8},{20,12},{24,0},{28,4},{1,25},{... | collective-permute-start | bytes 393224 | tf_op jit(solution)/shard_map/ppermute | solution.py:378
  73.2 0.7 copy-start.16
  77.7 1.0 copy-start.4
  78.7 0.9 copy-start.9
  79.6 0.9 copy-start.12
  80.6 0.9 copy-start.13
  81.5 0.9 copy-start.15
  82.4 0.9 copy-start.17
  83.3 66.7 %copy-start.10 = (bf16[256,256]{1,0:T(8,128)(2,1)S(1)}, bf16[256,256]{1,0:T(8,128)(2,1)}, u32[]{:S(2)}) copy-start(bf16[256,256]{1,0:T(8,128)(2,1)} %ws_ref.1) | copy-start | bytes 393220
  85.6 11.7 %collective-permute-start.14 = (bf16[208,512]{1,0:T(8,128)(2,1)S(1)}, bf16[208,512]{1,0:T(8,128)(2,1)S(1)}, u32[]{:S(2)}, u32[]{:S(2)}) collective-permute-start(bf16[208,512]{1,0:T(8,128)(2,1)S(1)} %get-tuple-element.38), channel_id=1, source_target_pairs={{0,8},{4,12},{8,0},{12,4},{16,24},{20,28},{24,16},{28,20},{1,9},{5... | collective-permute-start | bytes 638984 | tf_op jit(solution)/shard_map/ppermute | solution.py:378
  85.9 15.0 %collective-permute-start.15 = (bf16[208,512]{1,0:T(8,128)(2,1)S(1)}, bf16[208,512]{1,0:T(8,128)(2,1)S(1)}, u32[]{:S(2)}, u32[]{:S(2)}) collective-permute-start(bf16[208,512]{1,0:T(8,128)(2,1)S(1)} %get-tuple-element.39), channel_id=1, source_target_pairs={{0,16},{4,20},{8,24},{12,28},{16,0},{20,4},{24,8},{28,12},{1,17},{... | collective-permute-start | bytes 638984 | tf_op jit(solution)/shard_map/ppermute | solution.py:378
  87.5 9.9 %collective-permute-start.23 = (bf16[128,512]{1,0:T(8,128)(2,1)S(1)}, bf16[128,512]{1,0:T(8,128)(2,1)S(1)}, u32[]{:S(2)}, u32[]{:S(2)}) collective-permute-start(bf16[128,512]{1,0:T(8,128)(2,1)S(1)} %get-tuple-element.42.refs_1_), channel_id=1, source_target_pairs={{0,24},{4,28},{8,16},{12,20},{16,8},{20,12},{24,0},{28,4},{1,25},{... | collective-permute-start | bytes 393224 | tf_op jit(solution)/shard_map/ppermute | solution.py:378
  89.1 15.0 %collective-permute-start.16 = (bf16[208,512]{1,0:T(8,128)(2,1)S(1)}, bf16[208,512]{1,0:T(8,128)(2,1)S(1)}, u32[]{:S(2)}, u32[]{:S(2)}) collective-permute-start(bf16[208,512]{1,0:T(8,128)(2,1)S(1)} %get-tuple-element.40), channel_id=1, source_target_pairs={{0,24},{4,28},{8,16},{12,20},{16,8},{20,12},{24,0},{28,4},{1,25},{... | collective-permute-start | bytes 638984 | tf_op jit(solution)/shard_map/ppermute | solution.py:378
  90.4 12.0 %collective-permute-start.22 = (bf16[128,512]{1,0:T(8,128)(2,1)S(1)}, bf16[128,512]{1,0:T(8,128)(2,1)S(1)}, u32[]{:S(2)}, u32[]{:S(2)}) collective-permute-start(bf16[128,512]{1,0:T(8,128)(2,1)S(1)} %get-tuple-element.42.refs_1_), channel_id=1, source_target_pairs={{0,16},{4,20},{8,24},{12,28},{16,0},{20,4},{24,8},{28,12},{1,17},{... | collective-permute-start | bytes 393224 | tf_op jit(solution)/shard_map/ppermute | solution.py:378
  97.3 10.0 %collective-permute-start.17 = (bf16[208,512]{1,0:T(8,128)(2,1)S(1)}, bf16[208,512]{1,0:T(8,128)(2,1)S(1)}, u32[]{:S(2)}, u32[]{:S(2)}) collective-permute-start(bf16[208,512]{1,0:T(8,128)(2,1)S(1)} %get-tuple-element.37.refs_1_), channel_id=1, source_target_pairs={{0,4},{4,0},{8,12},{12,8},{16,20},{20,16},{24,28},{28,24},{1,5},{5... | collective-permute-start | bytes 638984 | tf_op jit(solution)/shard_map/ppermute | solution.py:378
  97.3 10.5 %collective-permute-start.18 = (bf16[208,512]{1,0:T(8,128)(2,1)S(1)}, bf16[208,512]{1,0:T(8,128)(2,1)S(1)}, u32[]{:S(2)}, u32[]{:S(2)}) collective-permute-start(bf16[208,512]{1,0:T(8,128)(2,1)S(1)} %collective-permute-done.14.refs_2_), channel_id=1, source_target_pairs={{0,4},{4,0},{8,12},{12,8},{16,20},{20,16},{24,28},{28,24},{1,5},{5... | collective-permute-start | bytes 638984 | tf_op jit(solution)/shard_map/ppermute | solution.py:378
  100.9 7.0 %collective-permute-start.19 = (bf16[208,512]{1,0:T(8,128)(2,1)S(1)}, bf16[208,512]{1,0:T(8,128)(2,1)S(1)}, u32[]{:S(2)}, u32[]{:S(2)}) collective-permute-start(bf16[208,512]{1,0:T(8,128)(2,1)S(1)} %collective-permute-done.15.refs_3_), channel_id=1, source_target_pairs={{0,4},{4,0},{8,12},{12,8},{16,20},{20,16},{24,28},{28,24},{1,5},{5... | collective-permute-start | bytes 638984 | tf_op jit(solution)/shard_map/ppermute | solution.py:378
  102.3 5.0 %collective-permute-start.21 = (bf16[128,512]{1,0:T(8,128)(2,1)S(1)}, bf16[128,512]{1,0:T(8,128)(2,1)S(1)}, u32[]{:S(2)}, u32[]{:S(2)}) collective-permute-start(bf16[128,512]{1,0:T(8,128)(2,1)S(1)} %get-tuple-element.42.refs_1_), channel_id=1, source_target_pairs={{0,8},{4,12},{8,0},{12,4},{16,24},{20,28},{24,16},{28,20},{1,9},{5... | collective-permute-start | bytes 393224 | tf_op jit(solution)/shard_map/ppermute | solution.py:378
  104.1 4.3 %collective-permute-start.20 = (bf16[208,512]{1,0:T(8,128)(2,1)S(1)}, bf16[208,512]{1,0:T(8,128)(2,1)S(1)}, u32[]{:S(2)}, u32[]{:S(2)}) collective-permute-start(bf16[208,512]{1,0:T(8,128)(2,1)S(1)} %collective-permute-done.16.refs_4_), channel_id=1, source_target_pairs={{0,4},{4,0},{8,12},{12,8},{16,20},{20,16},{24,28},{28,24},{1,5},{5... | collective-permute-start | bytes 638984 | tf_op jit(solution)/shard_map/ppermute | solution.py:378
  107.3 12.6 %collective-permute-start.24 = (bf16[128,512]{1,0:T(8,128)(2,1)S(1)}, bf16[128,512]{1,0:T(8,128)(2,1)S(1)}, u32[]{:S(2)}, u32[]{:S(2)}) collective-permute-start(bf16[128,512]{1,0:T(8,128)(2,1)S(1)} %get-tuple-element.42.refs_1_), channel_id=1, source_target_pairs={{0,4},{4,0},{8,12},{12,8},{16,20},{20,16},{24,28},{28,24},{1,5},{5... | collective-permute-start | bytes 393224 | tf_op jit(solution)/shard_map/ppermute | solution.py:378
  107.3 15.1 %collective-permute-start.27 = (bf16[128,512]{1,0:T(8,128)(2,1)S(1)}, bf16[128,512]{1,0:T(8,128)(2,1)S(1)}, u32[]{:S(2)}, u32[]{:S(2)}) collective-permute-start(bf16[128,512]{1,0:T(8,128)(2,1)S(1)} %collective-permute-done.23.refs_4_), channel_id=1, source_target_pairs={{0,4},{4,0},{8,12},{12,8},{16,20},{20,16},{24,28},{28,24},{1,5},{5... | collective-permute-start | bytes 393224 | tf_op jit(solution)/shard_map/ppermute | solution.py:378
  107.8 16.4 %collective-permute-start.26 = (bf16[128,512]{1,0:T(8,128)(2,1)S(1)}, bf16[128,512]{1,0:T(8,128)(2,1)S(1)}, u32[]{:S(2)}, u32[]{:S(2)}) collective-permute-start(bf16[128,512]{1,0:T(8,128)(2,1)S(1)} %collective-permute-done.22.refs_3_), channel_id=1, source_target_pairs={{0,4},{4,0},{8,12},{12,8},{16,20},{20,16},{24,28},{28,24},{1,5},{5... | collective-permute-start | bytes 393224 | tf_op jit(solution)/shard_map/ppermute | solution.py:378
  107.9 0.7 copy-start.21
  107.9 16.3 %collective-permute-start.25 = (bf16[128,512]{1,0:T(8,128)(2,1)S(1)}, bf16[128,512]{1,0:T(8,128)(2,1)S(1)}, u32[]{:S(2)}, u32[]{:S(2)}) collective-permute-start(bf16[128,512]{1,0:T(8,128)(2,1)S(1)} %collective-permute-done.21.refs_2_), channel_id=1, source_target_pairs={{0,4},{4,0},{8,12},{12,8},{16,20},{20,16},{24,28},{28,24},{1,5},{5... | collective-permute-start | bytes 393224 | tf_op jit(solution)/shard_map/ppermute | solution.py:378
  108.6 0.7 copy-start.22
  109.3 5.8 %copy-start.1 = (bf16[4096,2048]{1,0:T(8,128)(2,1)S(1)}, bf16[4096,2048]{1,0:T(8,128)(2,1)}, u32[]{:S(2)}) copy-start(bf16[4096,2048]{1,0:T(8,128)(2,1)} %copy-done) | copy-start | bytes 50331652
  119.8 30.1 %copy-start.11 = (f32[128,512]{1,0:T(8,128)S(1)}, f32[128,512]{1,0:T(8,128)}, u32[]{:S(2)}) copy-start(f32[128,512]{1,0:T(8,128)} %get-tuple-element.41.refs_0_) | copy-start | bytes 786436
  119.8 10.6 %collective-permute-start.28 = (bf16[176,512]{1,0:T(8,128)(2,1)S(1)}, bf16[176,512]{1,0:T(8,128)(2,1)S(1)}, u32[]{:S(2)}, u32[]{:S(2)}) collective-permute-start(bf16[176,512]{1,0:T(8,128)(2,1)S(1)} %get-tuple-element.44), channel_id=1, source_target_pairs={{0,1},{1,0},{2,3},{3,2},{4,5},{5,4},{6,7},{7,6},{8,9},{9,8},{10,11... | collective-permute-start | bytes 540680 | tf_op jit(solution)/shard_map/ppermute | solution.py:378
  120.0 16.1 %collective-permute-start.29 = (bf16[176,512]{1,0:T(8,128)(2,1)S(1)}, bf16[176,512]{1,0:T(8,128)(2,1)S(1)}, u32[]{:S(2)}, u32[]{:S(2)}) collective-permute-start(bf16[176,512]{1,0:T(8,128)(2,1)S(1)} %get-tuple-element.45), channel_id=1, source_target_pairs={{0,2},{1,3},{2,0},{3,1},{4,6},{5,7},{6,4},{7,5},{8,10},{9,11},{10,... | collective-permute-start | bytes 540680 | tf_op jit(solution)/shard_map/ppermute | solution.py:378
  122.4 13.6 %collective-permute-start.30 = (bf16[176,512]{1,0:T(8,128)(2,1)S(1)}, bf16[176,512]{1,0:T(8,128)(2,1)S(1)}, u32[]{:S(2)}, u32[]{:S(2)}) collective-permute-start(bf16[176,512]{1,0:T(8,128)(2,1)S(1)} %get-tuple-element.46), channel_id=1, source_target_pairs={{0,3},{1,2},{2,1},{3,0},{4,7},{5,6},{6,5},{7,4},{8,11},{9,10},{10,... | collective-permute-start | bytes 540680 | tf_op jit(solution)/shard_map/ppermute | solution.py:378
  127.2 12.2 %collective-permute-start.31 = (bf16[128,512]{1,0:T(8,128)(2,1)S(1)}, bf16[128,512]{1,0:T(8,128)(2,1)S(1)}, u32[]{:S(2)}, u32[]{:S(2)}) collective-permute-start(bf16[128,512]{1,0:T(8,128)(2,1)S(1)} %get-tuple-element.47), channel_id=1, source_target_pairs={{0,1},{1,0},{2,3},{3,2},{4,5},{5,4},{6,7},{7,6},{8,9},{9,8},{10,11... | collective-permute-start | bytes 393224 | tf_op jit(solution)/shard_map/ppermute | solution.py:378
  127.3 21.1 %collective-permute-start.32 = (bf16[128,512]{1,0:T(8,128)(2,1)S(1)}, bf16[128,512]{1,0:T(8,128)(2,1)S(1)}, u32[]{:S(2)}, u32[]{:S(2)}) collective-permute-start(bf16[128,512]{1,0:T(8,128)(2,1)S(1)} %get-tuple-element.48), channel_id=1, source_target_pairs={{0,2},{1,3},{2,0},{3,1},{4,6},{5,7},{6,4},{7,5},{8,10},{9,11},{10,... | collective-permute-start | bytes 393224 | tf_op jit(solution)/shard_map/ppermute | solution.py:378
  130.4 19.5 %collective-permute-start.33 = (bf16[128,512]{1,0:T(8,128)(2,1)S(1)}, bf16[128,512]{1,0:T(8,128)(2,1)S(1)}, u32[]{:S(2)}, u32[]{:S(2)}) collective-permute-start(bf16[128,512]{1,0:T(8,128)(2,1)S(1)} %get-tuple-element.49), channel_id=1, source_target_pairs={{0,3},{1,2},{2,1},{3,0},{4,7},{5,6},{6,5},{7,4},{8,11},{9,10},{10,... | collective-permute-start | bytes 393224 | tf_op jit(solution)/shard_map/ppermute | solution.py:378
  136.1 12.2 %collective-permute-start.36 = (f32[32,512]{1,0:T(8,128)S(1)}, f32[32,512]{1,0:T(8,128)S(1)}, u32[]{:S(2)}, u32[]{:S(2)}) collective-permute-start(f32[32,512]{1,0:T(8,128)S(1)} %slice.16.refs_0_), channel_id=1, source_target_pairs={{0,24},{4,28},{8,16},{12,20},{16,8},{20,12},{24,0},{28,4},{1,25},{... | collective-permute-start | bytes 196616 | tf_op jit(solution)/shard_map/ppermute | solution.py:378
  138.2 10.6 %collective-permute-start.35 = (f32[32,512]{1,0:T(8,128)S(1)}, f32[32,512]{1,0:T(8,128)S(1)}, u32[]{:S(2)}, u32[]{:S(2)}) collective-permute-start(f32[32,512]{1,0:T(8,128)S(1)} %slice.16.refs_0_), channel_id=1, source_target_pairs={{0,16},{4,20},{8,24},{12,28},{16,0},{20,4},{24,8},{28,12},{1,17},{... | collective-permute-start | bytes 196616 | tf_op jit(solution)/shard_map/ppermute | solution.py:378
  139.4 9.6 %collective-permute-start.34 = (f32[32,512]{1,0:T(8,128)S(1)}, f32[32,512]{1,0:T(8,128)S(1)}, u32[]{:S(2)}, u32[]{:S(2)}) collective-permute-start(f32[32,512]{1,0:T(8,128)S(1)} %slice.16.refs_0_), channel_id=1, source_target_pairs={{0,8},{4,12},{8,0},{12,4},{16,24},{20,28},{24,16},{28,20},{1,9},{5... | collective-permute-start | bytes 196616 | tf_op jit(solution)/shard_map/ppermute | solution.py:378
  148.3 2.6 %collective-permute-start.37 = (f32[32,512]{1,0:T(8,128)S(1)}, f32[32,512]{1,0:T(8,128)S(1)}, u32[]{:S(2)}, u32[]{:S(2)}) collective-permute-start(f32[32,512]{1,0:T(8,128)S(1)} %slice.16.refs_0_), channel_id=1, source_target_pairs={{0,4},{4,0},{8,12},{12,8},{16,20},{20,16},{24,28},{28,24},{1,5},{5... | collective-permute-start | bytes 196616 | tf_op jit(solution)/shard_map/ppermute | solution.py:378
  148.3 2.6 %collective-permute-start.40 = (f32[32,512]{1,0:T(8,128)S(1)}, f32[32,512]{1,0:T(8,128)S(1)}, u32[]{:S(2)}, u32[]{:S(2)}) collective-permute-start(f32[32,512]{1,0:T(8,128)S(1)} %collective-permute-done.36.refs_3_), channel_id=1, source_target_pairs={{0,4},{4,0},{8,12},{12,8},{16,20},{20,16},{24,28},{28,24},{1,5},{5... | collective-permute-start | bytes 196616 | tf_op jit(solution)/shard_map/ppermute | solution.py:378
  148.9 2.1 %collective-permute-start.39 = (f32[32,512]{1,0:T(8,128)S(1)}, f32[32,512]{1,0:T(8,128)S(1)}, u32[]{:S(2)}, u32[]{:S(2)}) collective-permute-start(f32[32,512]{1,0:T(8,128)S(1)} %collective-permute-done.35.refs_2_), channel_id=1, source_target_pairs={{0,4},{4,0},{8,12},{12,8},{16,20},{20,16},{24,28},{28,24},{1,5},{5... | collective-permute-start | bytes 196616 | tf_op jit(solution)/shard_map/ppermute | solution.py:378
  148.9 2.0 %collective-permute-start.38 = (f32[32,512]{1,0:T(8,128)S(1)}, f32[32,512]{1,0:T(8,128)S(1)}, u32[]{:S(2)}, u32[]{:S(2)}) collective-permute-start(f32[32,512]{1,0:T(8,128)S(1)} %collective-permute-done.34.refs_1_), channel_id=1, source_target_pairs={{0,4},{4,0},{8,12},{12,8},{16,20},{20,16},{24,28},{28,24},{1,5},{5... | collective-permute-start | bytes 196616 | tf_op jit(solution)/shard_map/ppermute | solution.py:378
  (1 other events, 0.7 us)

commit v2 on v1

v2 whole, which is shorter than its diff:
```python
import jax
import jax.numpy as jnp
from jax import lax
from jax.experimental import pallas as pl
from jax.experimental.pallas import tpu as pltpu
from jax.sharding import PartitionSpec as P

F32 = jnp.float32
BF16 = jnp.bfloat16
MIB = 1 << 20
RESIDENT_BYTES = 20 * MIB
PARTS = 2
BIAS_ROWS = 16


def vmem():
    return pl.BlockSpec(memory_space=pltpu.VMEM)


def params(limit_mib):
    return pltpu.CompilerParams(vmem_limit_bytes=limit_mib * MIB)


def sds(shape, dtype):
    return jax.ShapeDtypeStruct(shape, dtype)


def densify_far(tile_values, tile_row, tile_col, n_row, n_col, per_dev):
    slots, tile, _ = tile_values.shape
    chips = n_row // 2
    rows = n_row * per_dev
    cols = n_col * per_dev
    cells = rows * cols

    def kernel(row_ref, col_ref, values_ref, dense_ref, table, blank, sem):
        blank[...] = jnp.zeros_like(blank)
        chip = lax.axis_index("row") // 2
        core = lax.axis_index("row") % 2
        col_at = lax.axis_index("col")

        def clear(i, carry):
            for k in range(8):
                table[i * 8 + k] = slots
            return carry

        lax.fori_loop(0, cells // 8, clear, 0)

        def note(i, carry):
            for k in range(4):
                at = i * 4 + k
                table[row_ref[at] * cols + col_ref[at]] = at
            return carry

        lax.fori_loop(0, slots // 4, note, 0)

        def fill(i, carry):
            slot = table[i]
            t = i // cols
            s = i % cols
            owner = t // per_dev
            block = ((owner % 2) ^ core) * chips + ((owner // 2) ^ chip)
            u = (block * per_dev + t % per_dev) * tile
            v = (((s // per_dev) ^ col_at) * per_dev + s % per_dev) * tile
            where = dense_ref.at[
                pl.ds(pl.multiple_of(u, tile), tile), pl.ds(pl.multiple_of(v, tile), tile)
            ]

            @pl.when(slot < slots)
            def _():
                pltpu.make_async_copy(values_ref.at[slot], where, sem).start()

            @pl.when(slot >= slots)
            def _():
                pltpu.make_async_copy(blank, where, sem).start()

            return carry

        lax.fori_loop(0, cells, fill, 0)
        pltpu.make_async_copy(dense_ref, dense_ref, sem).wait()

    shape = (rows * tile, cols * tile)
    return pl.pallas_call(
        kernel,
        out_shape=sds(shape, BF16),
        grid_spec=pltpu.PrefetchScalarGridSpec(
            num_scalar_prefetch=2,
            grid=(),
            in_specs=[pl.BlockSpec(memory_space=pl.ANY)],
            out_specs=pl.BlockSpec(memory_space=pl.ANY),
            scratch_shapes=[
                pltpu.SMEM((cells + cols,), jnp.int32),
                pltpu.VMEM((tile, tile), BF16),
                pltpu.SemaphoreType.DMA,
            ],
        ),
        compiler_params=params(8),
        name="densify_far",
    )(tile_row, tile_col, tile_values)


def densify(tile_values, tile_row, tile_col, features, n_row, n_col, per_dev, wide):
    slots, tile, _ = tile_values.shape
    nodes, width = features.shape
    later = width // wide - 1
    chips = n_row // 2
    rows = n_row * per_dev
    cols = n_col * per_dev
    chip = lax.axis_index("row") // 2
    core = lax.axis_index("row") % 2
    owner = tile_row // per_dev
    block = ((owner % 2) ^ core) * chips + ((owner // 2) ^ chip)
    down = (block * per_dev + tile_row % per_dev) * tile
    down = jnp.where(tile_row < rows, down, rows * tile)
    right = ((tile_col // per_dev) ^ lax.axis_index("col")) * per_dev + tile_col % per_dev
    right = right * tile
    step_slots = 32
    while slots % step_slots:
        step_slots //= 2

    def kernel(down_ref, right_ref, values_ref, feat_ref, dense_ref, *cut_refs):
        step = pl.program_id(0)

        @pl.when(step == 0)
        def _():
            for h in range(later):
                cut_refs[h][...] = feat_ref[:, (h + 1) * wide : (h + 2) * wide]

            def clear(i, carry):
                at = pl.multiple_of(i * tile, tile)
                dense_ref[pl.ds(at, tile), :] = jnp.zeros((tile, cols * tile), BF16)
                return carry

            lax.fori_loop(0, rows, clear, 0)

        for k in range(step_slots):
            u = pl.multiple_of(down_ref[step * step_slots + k], tile)
            v = pl.multiple_of(right_ref[step * step_slots + k], tile)
            dense_ref[pl.ds(u, tile), pl.ds(v, tile)] = values_ref[k]

    res = pl.pallas_call(
        kernel,
        out_shape=[pltpu.VMEM(((rows + 1) * tile, cols * tile), BF16)]
        + [sds((nodes, wide), BF16)] * later,
        grid_spec=pltpu.PrefetchScalarGridSpec(
            num_scalar_prefetch=2,
            grid=(slots // step_slots,),
            in_specs=[
                pl.BlockSpec((step_slots, tile, tile), lambda i, *_: (i, 0, 0)),
                pl.BlockSpec((nodes, width), lambda i, *_: (0, 0)),
            ],
            out_specs=[vmem()] + [pl.BlockSpec((nodes, wide), lambda i, *_: (0, 0))] * later,
        ),
        compiler_params=params(8),
        name="densify",
    )(down, right, pltpu.with_memory_space_constraint(tile_values, pltpu.HBM), features)
    return res[0], res[1:]


def pinned(dense, resident):
    return pltpu.with_memory_space_constraint(dense, pltpu.VMEM) if resident else dense


def forward(dense, pieces, first, count, dtype, resident):
    n_col = len(pieces)
    nodes, wide = pieces[0].shape
    cols = n_col * nodes

    def kernel(*refs):
        dense_ref, piece_refs, out_ref, source = refs[0], refs[1 : 1 + n_col], refs[-2], refs[-1]
        step = pl.program_id(0)

        @pl.when(step == 0)
        def _():
            for m in range(n_col):
                source[m * nodes : (m + 1) * nodes, :] = piece_refs[m][...]

        if resident:
            at = pl.multiple_of((first + step) * nodes, nodes)
            block = dense_ref[pl.ds(at, nodes), :]
        else:
            block = dense_ref[...]
        out_ref[0] = jnp.dot(block, source[...], preferred_element_type=F32).astype(dtype)

    spec = vmem() if resident else pl.BlockSpec((nodes, cols), lambda i: (i + first, 0))
    return pl.pallas_call(
        kernel,
        out_shape=sds((count, nodes, wide), dtype),
        grid=(count,),
        in_specs=[spec] + [pl.BlockSpec((nodes, wide), lambda i: (0, 0))] * n_col,
        out_specs=pl.BlockSpec((1, nodes, wide), lambda i: (i, 0, 0)),
        scratch_shapes=[pltpu.VMEM((cols, wide), BF16)],
        compiler_params=params(8 if resident else 24),
        name="forward",
    )(pinned(dense, resident), *pieces)


def add_parts(keep, got):
    chips, nodes, wide = keep.shape

    def kernel(keep_ref, got_ref, *out_refs):
        for j in range(1, chips):
            out_refs[j - 1][...] = (keep_ref[j] + got_ref[j].astype(F32)).astype(BF16)

    return pl.pallas_call(
        kernel,
        out_shape=[sds((nodes, wide), BF16)] * (chips - 1),
        in_specs=[vmem()] * 2,
        out_specs=[vmem()] * (chips - 1),
        compiler_params=params(8),
        name="add_parts",
    )(keep, got)


def middle(features, degree, cotangent, w_self, w_neigh, bias, parts):
    nodes, width = features.shape
    count = len(parts)
    wide = width // count
    flat = []
    for keep, got, arrivals in parts:
        flat += [keep, got, *arrivals]
    each = len(flat) // count

    def kernel(*refs):
        feat_ref, degree_ref, cot_ref, ws_ref, wn_ref, bias_ref = refs[:6]
        part_refs = refs[6 : 6 + len(flat)]
        hidden_ref, mean_ref, d_pre_ref = refs[6 + len(flat) : 9 + len(flat)]
        d_agg_refs = refs[9 + len(flat) :]
        scale = degree_ref[...].astype(F32)
        scale_down = jnp.transpose(jnp.broadcast_to(scale, (wide, nodes)))
        means = []
        for h in range(count):
            mine = part_refs[h * each : (h + 1) * each]
            total = mine[0][0] + mine[1][0].astype(F32)
            for ref in mine[2:]:
                total = total + ref[...].astype(F32)
            means.append((total / scale_down).astype(BF16))
        neigh_mean = jnp.concatenate(means, axis=1) if count > 1 else means[0]
        mean_ref[...] = neigh_mean
        pre = jnp.dot(feat_ref[...], ws_ref[...], preferred_element_type=F32)
        pre = pre + jnp.dot(neigh_mean, wn_ref[...], preferred_element_type=F32) + bias_ref[...]
        sig = jax.nn.sigmoid(pre)
        hidden_ref[...] = (pre * sig).astype(BF16)
        d_pre = (cot_ref[...].astype(F32) * sig * (1.0 + pre * (1.0 - sig))).astype(BF16)
        d_pre_ref[...] = d_pre
        d_agg = lax.dot_general(
            d_pre, wn_ref[...], (((1,), (1,)), ((), ())), preferred_element_type=F32
        )
        d_agg = (jnp.transpose(d_agg) / scale).astype(BF16)
        for h in range(count):
            d_agg_refs[h][...] = d_agg[h * wide : (h + 1) * wide]

    first_two = [pl.BlockSpec((1, nodes, wide), lambda i: (0, 0, 0))] * 2
    whole = lambda shape: pl.BlockSpec(shape, lambda i: (0,) * len(shape))
    part_specs = (first_two + [whole((nodes, wide))] * (each - 2)) * count
    outs = [sds((nodes, width), BF16)] * 3 + [sds((wide, nodes), BF16)] * count
    args = [features, degree, cotangent, w_self, w_neigh, bias]
    res = pl.pallas_call(
        kernel,
        out_shape=outs,
        grid=(1,),
        in_specs=[whole(a.shape) for a in args] + part_specs,
        out_specs=[whole(o.shape) for o in outs],
        compiler_params=params(12),
        name="middle",
    )(*args, *flat)
    return res[0], res[1], res[2], res[3:]


def local_grads(features, neigh_mean, d_pre, d_agg, n_row):
    nodes, width = features.shape
    wide = d_agg.shape[0]
    chips = n_row // 2
    share = width // n_row

    def kernel(feat_ref, mean_ref, d_pre_ref, d_agg_ref, *refs):
        send_refs, grads_ref = refs[:-1], refs[-1]
        d_pre_now = d_pre_ref[...]
        over = (((0,), (0,)), ((), ()))
        grads_ref[:, 0:width] = lax.dot_general(
            feat_ref[...], d_pre_now, over, preferred_element_type=F32
        )
        grads_ref[:, width:] = lax.dot_general(
            mean_ref[...], d_pre_now, over, preferred_element_type=F32
        )
        bias_sum = jnp.sum(d_pre_now.astype(F32), axis=0, keepdims=True)
        bias_row = jnp.concatenate([bias_sum, bias_sum], axis=1).astype(BF16)
        bias_rows = jnp.broadcast_to(bias_row, (BIAS_ROWS, 2 * width))
        chip = lax.axis_index("row") // 2
        core = lax.axis_index("row") % 2
        for j in range(chips):
            send_refs[j][0:wide, :] = d_agg_ref[...]
            for k in range(2):
                owner = (chip ^ j) * 2 + (core ^ k)
                at = pl.multiple_of(owner * share, share)
                low = wide + k * share
                send_refs[j][low : low + share, :] = grads_ref[pl.ds(at, share), :].astype(BF16)
            send_refs[j][wide + 2 * share :, :] = bias_rows

    return pl.pallas_call(
        kernel,
        out_shape=[sds((wide + 2 * share + BIAS_ROWS, nodes), BF16)] * chips,
        in_specs=[vmem()] * 4,
        out_specs=[vmem()] * chips,
        scratch_shapes=[pltpu.VMEM((width, 2 * width), F32)],
        compiler_params=params(8),
        name="local_grads",
    )(features, neigh_mean, d_pre, d_agg)


def share_partial(pieces, wide, share):
    n_row = len(pieces)
    nodes = pieces[0].shape[1]
    chips = n_row // 2

    def kernel(*refs):
        total_ref, send_ref = refs[-2:]
        total = jnp.zeros((share, nodes), F32)
        bias_total = jnp.zeros((BIAS_ROWS, nodes), F32)
        for b in range(n_row):
            low = wide + (b // chips) * share
            total = total + refs[b][low : low + share, :].astype(F32)
            bias_total = bias_total + refs[b][wide + 2 * share :, :].astype(F32)
        total_ref[0:share, :] = total
        total_ref[share:, :] = bias_total
        send_ref[0:share, :] = total.astype(BF16)
        send_ref[share:, :] = bias_total.astype(BF16)

    return pl.pallas_call(
        kernel,
        out_shape=[sds((share + BIAS_ROWS, nodes), d) for d in (F32, BF16)],
        in_specs=[vmem()] * n_row,
        out_specs=[vmem()] * 2,
        compiler_params=params(8),
        name="share_partial",
    )(*pieces)


def backward(dense, pieces, n_col, wide, resident):
    n_row = len(pieces)
    height, nodes = pieces[0].shape
    rows = n_row * nodes

    def kernel(*refs):
        dense_ref, piece_refs = refs[0], refs[1 : 1 + n_row]
        out_refs = refs[1 + n_row : 1 + n_row + n_col]
        stacked = refs[-1]
        step = pl.program_id(0)

        @pl.when(step == 0)
        def _():
            for b in range(n_row):
                stacked[:, b * nodes : (b + 1) * nodes] = piece_refs[b][0:wide, :]

        for m in range(n_col):

            @pl.when(step == m)
            def _():
                if resident:
                    block = dense_ref[0:rows, m * nodes : (m + 1) * nodes]
                else:
                    block = dense_ref[...]
                out = jnp.dot(stacked[...], block, preferred_element_type=F32)
                out_refs[m][...] = out.astype(out_refs[m].dtype)

    spec = vmem() if resident else pl.BlockSpec((rows, nodes), lambda i: (0, i))
    whole = lambda shape: pl.BlockSpec(shape, lambda i: (0,) * len(shape))
    outs = [sds((wide, nodes), F32)] + [sds((wide, nodes), BF16)] * (n_col - 1)
    res = pl.pallas_call(
        kernel,
        out_shape=outs,
        grid=(n_col,),
        in_specs=[spec] + [whole((height, nodes))] * n_row,
        out_specs=[whole(o.shape) for o in outs],
        scratch_shapes=[pltpu.VMEM((wide, rows), BF16)],
        compiler_params=params(12 if resident else 40),
        name="backward",
    )(pinned(dense, resident), *pieces)
    return res[0], res[1:]


def share_total(total, arrivals):
    height, nodes = total.shape

    def kernel(total_ref, *refs):
        out_ref = refs[-1]
        acc = total_ref[...]
        for ref in refs[:-1]:
            acc = acc + ref[...].astype(F32)
        out_ref[...] = acc

    return pl.pallas_call(
        kernel,
        out_shape=sds((height, nodes), F32),
        in_specs=[vmem()] * (1 + len(arrivals)),
        out_specs=vmem(),
        compiler_params=params(8),
        name="share_total",
    )(total, *arrivals)


def weight_grads(shares, n_row):
    share = shares[0].shape[0]
    width = shares[0].shape[1] // 2
    chips = n_row // 2

    def kernel(*refs):
        self_ref, neigh_ref = refs[-2:]
        chip = lax.axis_index("row") // 2
        core = lax.axis_index("row") % 2
        for b in range(n_row):
            owner = (chip ^ (b % chips)) * 2 + (core ^ (b // chips))
            at = pl.multiple_of(owner * share, share)
            self_ref[pl.ds(at, share), :] = refs[b][:, 0:width]
            neigh_ref[pl.ds(at, share), :] = refs[b][:, width:]

    return pl.pallas_call(
        kernel,
        out_shape=[sds((width, width), F32)] * 2,
        in_specs=[vmem()] * n_row,
        out_specs=[vmem()] * 2,
        compiler_params=params(8),
        name="weight_grads",
    )(*shares)


def finish(d_pre, w_self, owns, arrivals):
    nodes, width = d_pre.shape
    count = len(owns)
    wide = width // count
    others = len(arrivals[0])
    flat = list(owns) + [a for part in arrivals for a in part]

    def kernel(d_pre_ref, ws_ref, *refs):
        out_ref = refs[-1]
        direct = lax.dot_general(
            d_pre_ref[...], ws_ref[...], (((1,), (1,)), ((), ())), preferred_element_type=F32
        )
        for h in range(count):
            acc = refs[h][...]
            for ref in refs[count + h * others : count + (h + 1) * others]:
                acc = acc + ref[...].astype(F32)
            low = h * wide
            out = direct[:, low : low + wide] + jnp.transpose(acc)
            out_ref[:, low : low + wide] = out.astype(BF16)

    return pl.pallas_call(
        kernel,
        out_shape=sds((nodes, width), BF16),
        in_specs=[vmem()] * (2 + len(flat)),
        out_specs=vmem(),
        compiler_params=params(8),
        name="finish",
    )(d_pre, w_self, *flat)


def swap(x, axis, mask):
    size = lax.axis_size(axis)
    return lax.ppermute(x, axis, [(i, i ^ mask) for i in range(size)])


def far_first(n):
    return sorted(range(1, n), key=lambda m: -bin(m).count("1") * n - m)


def body(features, degree, cotangent, tile_values, tile_row, tile_col, w_self, w_neigh, bias):
    nodes, width = features.shape
    tile = tile_values.shape[1]
    n_row = lax.axis_size("row")
    n_col = lax.axis_size("col")
    chips = n_row // 2
    per_dev = nodes // tile
    wide = width // PARTS
    share = width // n_row
    resident = n_row * nodes * n_col * nodes * 2 <= RESIDENT_BYTES

    if resident:
        dense, cuts = densify(
            tile_values, tile_row, tile_col, features, n_row, n_col, per_dev, wide
        )
    else:
        dense = densify_far(tile_values, tile_row, tile_col, n_row, n_col, per_dev)
        cuts = [features[:, h * wide : (h + 1) * wide] for h in range(1, PARTS)]

    parts = []
    for h in range(PARTS):
        own = features[:, 0:wide] if h == 0 else cuts[h - 1]
        pieces = {m: swap(own, "col", m) for m in far_first(n_col)}
        source = [own] + [pieces[m] for m in range(1, n_col)]
        give = forward(dense, source, chips, chips, BF16, resident)
        got = swap(give, "row", 1)
        keep = forward(dense, source, 0, chips, F32, resident)
        sends = add_parts(keep, got)
        arrivals = [swap(sends[j - 1], "row", 2 * j) for j in range(1, chips)]
        parts.append((keep, got, arrivals))

    hidden, neigh_mean, d_pre, d_aggs = middle(
        features, degree[None, :], cotangent, w_self, w_neigh, bias[None, :], parts
    )

    owns, backs = [], []
    for h in range(PARTS):
        last = h == PARTS - 1
        sends = [d_aggs[h]] * chips
        if last:
            sends = local_grads(features, neigh_mean, d_pre, d_aggs[h], n_row)
        if h > 0:
            tied = lax.optimization_barrier((tuple(sends), tuple(mine)))
            sends = tied[0]
        mine = [sends[0]] + [swap(sends[j], "row", 2 * j) for j in range(1, chips)]
        siblings = [swap(piece, "row", 1) for piece in mine]
        pieces = mine + siblings
        own, outs = backward(dense, pieces, n_col, wide, resident)
        arrived = {m: swap(outs[m - 1], "col", m) for m in far_first(n_col)}
        owns.append(own)
        backs.append([arrived[m] for m in range(1, n_col)])
        if last:
            total, send = share_partial(pieces, wide, share)
            summed = share_total(total, [swap(send, "col", m) for m in range(1, n_col)])
            grad_bias = summed[share, 0:width]
            piece = summed[0:share]
            shares = [piece] + [swap(piece, "row", 2 * j) for j in range(1, chips)]
            shares = shares + [swap(part, "row", 1) for part in shares]
            grad_self, grad_neigh = weight_grads(shares, n_row)

    grad_x = finish(d_pre, w_self, owns, backs)
    return (hidden, grad_x, grad_self, grad_neigh, grad_bias)


def solution(mesh):
    placed = (
        P(("col", "row"), None),
        P(("col", "row")),
        P(("col", "row"), None),
        P(("col", "row"), None, None),
        P(("col", "row")),
        P(("col", "row")),
        P(),
        P(),
        P(),
    )
    return jax.shard_map(
        body,
        mesh=mesh,
        in_specs=placed,
        out_specs=(P(("col", "row"), None), P(("col", "row"), None), P(), P(), P()),
        check_vma=False,
    )
```

time: 154 us -> 123 us (0.80); the launches traced: 152 us -> 123 us
  local copies, waits for them, and re-layouts: 23.2 us -> 2.47 us
  Pallas kernels: 49.3 us -> 32.7 us
  waiting for transfers between devices: 33.5 us -> 40.2 us
    unnamed x48 -> x14, local copies, waits for them, and re-layouts: 20.8 us -> 0.98 us
    pallas_call x1 -> x3, Pallas kernels: 24.1 us -> 11.9 us  [the longest x1 11.5 us: densify(): pl.pallas_call(kernel, out_shape=[pltpu.VMEM(((rows + 1) * tile, cols * t...]
    ppermute x41 -> x44, waiting for transfers between devices: 33.5 us -> 40.2 us  [swap(): return lax.ppermute(x, axis, [(i, i ^ mask) for i in range(size)])]
    pallas_call x2, Pallas kernels: 7.75 us -> 5.94 us  [backward(): pl.pallas_call(kernel, out_shape=outs, grid=(n_col,), in_specs=[spec] + [...]
    ppermute x41 -> x44, starting transfers between devices: 44.9 us -> 46 us  [swap(): return lax.ppermute(x, axis, [(i, i ^ mask) for i in range(size)])]
  transfers between devices with their start and end apart: 41 -> 44, of which waited for: 10 -> 16; matrix products, arithmetic and copies ran while one was open for 1% -> 1% of each run, Pallas kernels for 30% -> 25%
where the time goes in v2:
time: 123 us
  starting transfers between devices  46 us (37%)
  waiting for transfers between devices  40.2 us (33%)
  Pallas kernels  32.7 us (27%)
  local copies, waits for them, and re-layouts  2.47 us (2%)
    ppermute x44, starting transfers between devices, swap(): return lax.ppermute(x, axis, [(i, i ^ mask) for i in range(size)])  46 us
    ppermute x44, waiting for transfers between devices, swap(): return lax.ppermute(x, axis, [(i, i ^ mask) for i in range(size)])  40.2 us
    pallas_call x4, Pallas kernels, forward(): pl.pallas_call(kernel, out_shape=sds((count, nodes, wide), dtype), grid=(...  11.6 us
    pallas_call x1, Pallas kernels, densify(): pl.pallas_call(kernel, out_shape=[pltpu.VMEM(((rows + 1) * tile, cols * t...  11.5 us
    pallas_call x2, Pallas kernels, backward(): pl.pallas_call(kernel, out_shape=outs, grid=(n_col,), in_specs=[spec] + [...  5.94 us
  transfers between devices with their start and end apart: 44, of which 16 were waited for; matrix products, arithmetic and copies ran while one was open for 1% of the time, Pallas kernels for 25%

profile of v2, /device:TPU:0, one launch (start us, length us, event | category | flops | bytes accessed | tf_op | source)
XLA Modules:
  0.0 123.0 jit_solution(10298187635846782803)
XLA Ops:
  0.6 0.9 slice.9.refs_1_
  1.5 5.1 %collective-permute-start.2 = (bf16[512,128]{1,0:T(8,128)(2,1)S(1)}, bf16[512,128]{1,0:T(8,128)(2,1)S(1)}, u32[]{:S(2)}, u32[]{:S(2)}) collective-permute-start(bf16[512,128]{1,0:T(8,128)(2,1)S(1)} %slice.9.refs_1_), channel_id=1, source_target_pairs={{0,3},{1,2},{2,1},{3,0},{4,7},{5,6},{6,5},{7,4},{8,11},{9,10},{10,... | collective-permute-start | bytes 393224 | tf_op jit(solution)/shard_map/ppermute | solution.py:458
  6.7 0.6 collective-permute-start
  7.3 0.7 fusion.6
  8.0 0.9 copy-done
  9.0 11.5 %densify.1 = (bf16[4224,2048]{1,0:T(8,128)(2,1)S(1)}, bf16[512,128]{1,0:T(8,128)(2,1)S(1)}) custom-call(s32[384]{0:T(512)S(1)} %get-tuple-element.71.down_ref, s32[384]{0:T(512)S(1)} %get-tuple-element.72.right_ref, bf16[384,128,128]{2,1,0:T(8,128)(2,1)} %values_ref.1, bf16[512,256]{1,0:T(8,128)(2,1)S(1)} %copy-done), custom_call_target="tpu_custom_call" | custom-call | tf_op jit(solution)/shard_map/densify/pallas_call | solution.py:140
  20.5 3.8 %collective-permute-start.9 = (bf16[512,128]{1,0:T(8,128)(2,1)S(1)}, bf16[512,128]{1,0:T(8,128)(2,1)S(1)}, u32[]{:S(2)}, u32[]{:S(2)}) collective-permute-start(bf16[512,128]{1,0:T(8,128)(2,1)S(1)} %get-tuple-element.42.refs_1_), channel_id=1, source_target_pairs={{0,3},{1,2},{2,1},{3,0},{4,7},{5,6},{6,5},{7,4},{8,11},{9,10},{10,... | collective-permute-start | bytes 393224 | tf_op jit(solution)/shard_map/ppermute | solution.py:458
  24.3 0.6 collective-permute-start.7
  24.9 2.9 %forward.5 = bf16[4,512,128]{2,1,0:T(8,128)(2,1)S(1)} custom-call(bf16[4224,2048]{1,0:T(8,128)(2,1)S(1)} %get-tuple-element.38.refs_0_, bf16[512,128]{1,0:T(8,128)(2,1)S(1)} %slice.9.refs_1_, bf16[512,128]{1,0:T(8,128)(2,1)S(1)} %collective-permute-done.refs_2_, bf16[512,128]{1,0:T(8,128)(2,1)S(1)} %collective-permute-done.1.refs_3_, ...), custom_call_target="tpu_custom_call" | custom-call | tf_op jit(solution)/shard_map/forward/pallas_call | solution.py:185
  27.8 0.1 collective-permute-start.3
  27.9 0.8 collective-permute-done.9.refs_4_
  28.8 5.8 %collective-permute-done.8.refs_3_ = bf16[512,128]{1,0:T(8,128)(2,1)S(1)} collective-permute-done((bf16[512,128]{1,0:T(8,128)(2,1)S(1)}, bf16[512,128]{1,0:T(8,128)(2,1)S(1)}, u32[]{:S(2)}, u32[]{:S(2)}) %collective-permute-start.8) | collective-permute-done | bytes 131104 | tf_op jit(solution)/shard_map/ppermute | solution.py:458
  34.5 2.9 %forward.7 = bf16[4,512,128]{2,1,0:T(8,128)(2,1)S(1)} custom-call(bf16[4224,2048]{1,0:T(8,128)(2,1)S(1)} %get-tuple-element.38.refs_0_, bf16[512,128]{1,0:T(8,128)(2,1)S(1)} %get-tuple-element.42.refs_1_, bf16[512,128]{1,0:T(8,128)(2,1)S(1)} %collective-permute-done.7.refs_2_, bf16[512,128]{1,0:T(8,128)(2,1)S(1)} %collective-permute-done.8.refs_3_, ...), custom_call_target="tpu_custom_call" | custom-call | tf_op jit(solution)/shard_map/forward/pallas_call | solution.py:185
  37.5 0.1 collective-permute-start.10
  37.6 2.9 %forward.4.keep_ref.refs_6_ = f32[4,512,128]{2,1,0:T(8,128)S(1)} custom-call(bf16[4224,2048]{1,0:T(8,128)(2,1)S(1)} %get-tuple-element.38.refs_0_, bf16[512,128]{1,0:T(8,128)(2,1)S(1)} %slice.9.refs_1_, bf16[512,128]{1,0:T(8,128)(2,1)S(1)} %collective-permute-done.refs_2_, bf16[512,128]{1,0:T(8,128)(2,1)S(1)} %collective-permute-done.1.refs_3_, ...), custom_call_target="tpu_custom_call" | custom-call | tf_op jit(solution)/shard_map/forward/pallas_call | solution.py:185
  40.6 1.5 %collective-permute-start.4 = (bf16[512,128]{1,0:T(8,128)(2,1)S(1)}, bf16[512,128]{1,0:T(8,128)(2,1)S(1)}, u32[]{:S(2)}, u32[]{:S(2)}) collective-permute-start(bf16[512,128]{1,0:T(8,128)(2,1)S(1)} %get-tuple-element.39), channel_id=1, source_target_pairs={{0,8},{4,12},{8,0},{12,4},{16,24},{20,28},{24,16},{28,20},{1,9},{5... | collective-permute-start | bytes 393224 | tf_op jit(solution)/shard_map/ppermute | solution.py:458
  42.1 2.9 %forward.6.keep_ref.refs_11_ = f32[4,512,128]{2,1,0:T(8,128)S(1)} custom-call(bf16[4224,2048]{1,0:T(8,128)(2,1)S(1)} %get-tuple-element.38.refs_0_, bf16[512,128]{1,0:T(8,128)(2,1)S(1)} %get-tuple-element.42.refs_1_, bf16[512,128]{1,0:T(8,128)(2,1)S(1)} %collective-permute-done.7.refs_2_, bf16[512,128]{1,0:T(8,128)(2,1)S(1)} %collective-permute-done.8.refs_3_, ...), custom_call_target="tpu_custom_call" | custom-call | tf_op jit(solution)/shard_map/forward/pallas_call | solution.py:185
  45.0 1.6 %collective-permute-start.5 = (bf16[512,128]{1,0:T(8,128)(2,1)S(1)}, bf16[512,128]{1,0:T(8,128)(2,1)S(1)}, u32[]{:S(2)}, u32[]{:S(2)}) collective-permute-start(bf16[512,128]{1,0:T(8,128)(2,1)S(1)} %get-tuple-element.40), channel_id=1, source_target_pairs={{0,16},{4,20},{8,24},{12,28},{16,0},{20,4},{24,8},{28,12},{1,17},{... | collective-permute-start | bytes 393224 | tf_op jit(solution)/shard_map/ppermute | solution.py:458
  46.6 0.5 collective-permute-start.6
  47.2 1.5 %collective-permute-start.11 = (bf16[512,128]{1,0:T(8,128)(2,1)S(1)}, bf16[512,128]{1,0:T(8,128)(2,1)S(1)}, u32[]{:S(2)}, u32[]{:S(2)}) collective-permute-start(bf16[512,128]{1,0:T(8,128)(2,1)S(1)} %get-tuple-element.43), channel_id=1, source_target_pairs={{0,8},{4,12},{8,0},{12,4},{16,24},{20,28},{24,16},{28,20},{1,9},{5... | collective-permute-start | bytes 393224 | tf_op jit(solution)/shard_map/ppermute | solution.py:458
  48.7 1.5 %collective-permute-start.12 = (bf16[512,128]{1,0:T(8,128)(2,1)S(1)}, bf16[512,128]{1,0:T(8,128)(2,1)S(1)}, u32[]{:S(2)}, u32[]{:S(2)}) collective-permute-start(bf16[512,128]{1,0:T(8,128)(2,1)S(1)} %get-tuple-element.44), channel_id=1, source_target_pairs={{0,16},{4,20},{8,24},{12,28},{16,0},{20,4},{24,8},{28,12},{1,17},{... | collective-permute-start | bytes 393224 | tf_op jit(solution)/shard_map/ppermute | solution.py:458
  50.2 0.5 collective-permute-start.13
  50.7 3.3 %collective-permute-done.5.refs_9_ = bf16[512,128]{1,0:T(8,128)(2,1)S(1)} collective-permute-done((bf16[512,128]{1,0:T(8,128)(2,1)S(1)}, bf16[512,128]{1,0:T(8,128)(2,1)S(1)}, u32[]{:S(2)}, u32[]{:S(2)}) %collective-permute-start.5) | collective-permute-done | bytes 131104 | tf_op jit(solution)/shard_map/ppermute | solution.py:458
  54.0 1.8 %collective-permute-done.11.refs_13_ = bf16[512,128]{1,0:T(8,128)(2,1)S(1)} collective-permute-done((bf16[512,128]{1,0:T(8,128)(2,1)S(1)}, bf16[512,128]{1,0:T(8,128)(2,1)S(1)}, u32[]{:S(2)}, u32[]{:S(2)}) %collective-permute-start.11) | collective-permute-done | bytes 131104 | tf_op jit(solution)/shard_map/ppermute | solution.py:458
  55.7 3.4 %collective-permute-done.12.refs_14_ = bf16[512,128]{1,0:T(8,128)(2,1)S(1)} collective-permute-done((bf16[512,128]{1,0:T(8,128)(2,1)S(1)}, bf16[512,128]{1,0:T(8,128)(2,1)S(1)}, u32[]{:S(2)}, u32[]{:S(2)}) %collective-permute-start.12) | collective-permute-done | bytes 131104 | tf_op jit(solution)/shard_map/ppermute | solution.py:458
  59.2 1.2 middle.1
  60.4 1.5 %collective-permute-start.16 = (bf16[128,512]{1,0:T(8,128)(2,1)S(1)}, bf16[128,512]{1,0:T(8,128)(2,1)S(1)}, u32[]{:S(2)}, u32[]{:S(2)}) collective-permute-start(bf16[128,512]{1,0:T(8,128)(2,1)S(1)} %get-tuple-element.48.refs_1_), channel_id=1, source_target_pairs={{0,24},{4,28},{8,16},{12,20},{16,8},{20,12},{24,0},{28,4},{1,25},{... | collective-permute-start | bytes 393224 | tf_op jit(solution)/shard_map/ppermute | solution.py:458
  61.9 0.5 collective-permute-start.15
  62.4 1.5 %collective-permute-start.14 = (bf16[128,512]{1,0:T(8,128)(2,1)S(1)}, bf16[128,512]{1,0:T(8,128)(2,1)S(1)}, u32[]{:S(2)}, u32[]{:S(2)}) collective-permute-start(bf16[128,512]{1,0:T(8,128)(2,1)S(1)} %get-tuple-element.48.refs_1_), channel_id=1, source_target_pairs={{0,8},{4,12},{8,0},{12,4},{16,24},{20,28},{24,16},{28,20},{1,9},{5... | collective-permute-start | bytes 393224 | tf_op jit(solution)/shard_map/ppermute | solution.py:458
  63.9 0.4 local_grads.1
  64.3 3.4 %collective-permute-done.16.refs_4_ = bf16[128,512]{1,0:T(8,128)(2,1)S(1)} collective-permute-done((bf16[128,512]{1,0:T(8,128)(2,1)S(1)}, bf16[128,512]{1,0:T(8,128)(2,1)S(1)}, u32[]{:S(2)}, u32[]{:S(2)}) %collective-permute-start.16) | collective-permute-done | bytes 131104 | tf_op jit(solution)/shard_map/ppermute | solution.py:458
  67.7 1.4 %collective-permute-done.15.refs_3_ = bf16[128,512]{1,0:T(8,128)(2,1)S(1)} collective-permute-done((bf16[128,512]{1,0:T(8,128)(2,1)S(1)}, bf16[128,512]{1,0:T(8,128)(2,1)S(1)}, u32[]{:S(2)}, u32[]{:S(2)}) %collective-permute-start.15) | collective-permute-done | bytes 131104 | tf_op jit(solution)/shard_map/ppermute | solution.py:458
  69.1 0.5 collective-permute-start.21
  69.6 1.3 %collective-permute-start.22 = (bf16[208,512]{1,0:T(8,128)(2,1)S(1)}, bf16[208,512]{1,0:T(8,128)(2,1)S(1)}, u32[]{:S(2)}, u32[]{:S(2)}) collective-permute-start(bf16[208,512]{1,0:T(8,128)(2,1)S(1)} %get-tuple-element.58), channel_id=1, source_target_pairs={{0,16},{4,20},{8,24},{12,28},{16,0},{20,4},{24,8},{28,12},{1,17},{... | collective-permute-start | bytes 638984 | tf_op jit(solution)/shard_map/ppermute | solution.py:458
  70.9 1.7 %collective-permute-start.23 = (bf16[208,512]{1,0:T(8,128)(2,1)S(1)}, bf16[208,512]{1,0:T(8,128)(2,1)S(1)}, u32[]{:S(2)}, u32[]{:S(2)}) collective-permute-start(bf16[208,512]{1,0:T(8,128)(2,1)S(1)} %get-tuple-element.59), channel_id=1, source_target_pairs={{0,24},{4,28},{8,16},{12,20},{16,8},{20,12},{24,0},{28,4},{1,25},{... | collective-permute-start | bytes 638984 | tf_op jit(solution)/shard_map/ppermute | solution.py:458
  72.6 0.5 collective-permute-start.20
  73.1 0.8 collective-permute-done.17.refs_5_
  74.0 0.1 collective-permute-start.19
  74.1 0.3 collective-permute-start.24
  74.5 2.8 %collective-permute-done.21.refs_2_.refs_1_ = bf16[208,512]{1,0:T(8,128)(2,1)S(1)} collective-permute-done((bf16[208,512]{1,0:T(8,128)(2,1)S(1)}, bf16[208,512]{1,0:T(8,128)(2,1)S(1)}, u32[]{:S(2)}, u32[]{:S(2)}) %collective-permute-start.21) | collective-permute-done | bytes 213024 | tf_op jit(solution)/shard_map/ppermute | solution.py:458
  77.3 3.5 %collective-permute-done.22.refs_3_.refs_2_ = bf16[208,512]{1,0:T(8,128)(2,1)S(1)} collective-permute-done((bf16[208,512]{1,0:T(8,128)(2,1)S(1)}, bf16[208,512]{1,0:T(8,128)(2,1)S(1)}, u32[]{:S(2)}, u32[]{:S(2)}) %collective-permute-start.22) | collective-permute-done | bytes 213024 | tf_op jit(solution)/shard_map/ppermute | solution.py:458
  80.8 0.5 collective-permute-start.27
  81.4 1.4 %collective-permute-done.18.refs_6_ = bf16[128,512]{1,0:T(8,128)(2,1)S(1)} collective-permute-done((bf16[128,512]{1,0:T(8,128)(2,1)S(1)}, bf16[128,512]{1,0:T(8,128)(2,1)S(1)}, u32[]{:S(2)}, u32[]{:S(2)}) %collective-permute-start.18) | collective-permute-done | bytes 131104 | tf_op jit(solution)/shard_map/ppermute | solution.py:458
  82.7 3.0 %backward.2 = (f32[128,512]{1,0:T(8,128)S(1)}, bf16[128,512]{1,0:T(8,128)(2,1)S(1)}, bf16[128,512]{1,0:T(8,128)(2,1)S(1)}, bf16[128,512]{1,0:T(8,128)(2,1)S(1)}) custom-call(bf16[4224,2048]{1,0:T(8,128)(2,1)S(1)} %get-tuple-element.38.refs_0_, bf16[128,512]{1,0:T(8,128)(2,1)S(1)} %get-tuple-element.48.refs_1_, ...), custom_call_target="tpu_custom_call" | custom-call | tf_op jit(solution)/shard_map/backward/pallas_call | solution.py:368
  85.7 0.1 collective-permute-start.28
  85.9 2.5 %collective-permute-start.36 = (bf16[48,512]{1,0:T(8,128)(2,1)S(1)}, bf16[48,512]{1,0:T(8,128)(2,1)S(1)}, u32[]{:S(2)}, u32[]{:S(2)}) collective-permute-start(bf16[48,512]{1,0:T(8,128)(2,1)S(1)} %get-tuple-element.68), channel_id=1, source_target_pairs={{0,3},{1,2},{2,1},{3,0},{4,7},{5,6},{6,5},{7,4},{8,11},{9,10},{10,... | collective-permute-start | bytes 147464 | tf_op jit(solution)/shard_map/ppermute | solution.py:458
  88.4 1.0 collective-permute-start.29
  89.4 2.4 %collective-permute-start.30 = (bf16[128,512]{1,0:T(8,128)(2,1)S(1)}, bf16[128,512]{1,0:T(8,128)(2,1)S(1)}, u32[]{:S(2)}, u32[]{:S(2)}) collective-permute-start(bf16[128,512]{1,0:T(8,128)(2,1)S(1)} %get-tuple-element.63), channel_id=1, source_target_pairs={{0,3},{1,2},{2,1},{3,0},{4,7},{5,6},{6,5},{7,4},{8,11},{9,10},{10,... | collective-permute-start | bytes 393224 | tf_op jit(solution)/shard_map/ppermute | solution.py:458
  91.8 1.8 %collective-permute-done.36.refs_2_ = bf16[48,512]{1,0:T(8,128)(2,1)S(1)} collective-permute-done((bf16[48,512]{1,0:T(8,128)(2,1)S(1)}, bf16[48,512]{1,0:T(8,128)(2,1)S(1)}, u32[]{:S(2)}, u32[]{:S(2)}) %collective-permute-start.36) | collective-permute-done | bytes 49184 | tf_op jit(solution)/shard_map/ppermute | solution.py:458
  93.6 5.4 %collective-permute-start.34 = (bf16[48,512]{1,0:T(8,128)(2,1)S(1)}, bf16[48,512]{1,0:T(8,128)(2,1)S(1)}, u32[]{:S(2)}, u32[]{:S(2)}) collective-permute-start(bf16[48,512]{1,0:T(8,128)(2,1)S(1)} %get-tuple-element.68), channel_id=1, source_target_pairs={{0,1},{1,0},{2,3},{3,2},{4,5},{5,4},{6,7},{7,6},{8,9},{9,8},{10,11... | collective-permute-start | bytes 147464 | tf_op jit(solution)/shard_map/ppermute | solution.py:458
  99.0 3.0 %backward.3 = (f32[128,512]{1,0:T(8,128)S(1)}, bf16[128,512]{1,0:T(8,128)(2,1)S(1)}, bf16[128,512]{1,0:T(8,128)(2,1)S(1)}, bf16[128,512]{1,0:T(8,128)(2,1)S(1)}) custom-call(bf16[4224,2048]{1,0:T(8,128)(2,1)S(1)} %get-tuple-element.38.refs_0_, bf16[208,512]{1,0:T(8,128)(2,1)S(1)} %get-tuple-element.56.refs_1_.refs_0_, ...), custom_call_target="tpu_custom_call" | custom-call | tf_op jit(solution)/shard_map/backward/pallas_call | solution.py:368
  102.0 4.1 %collective-permute-done.35.refs_1_ = bf16[48,512]{1,0:T(8,128)(2,1)S(1)} collective-permute-done((bf16[48,512]{1,0:T(8,128)(2,1)S(1)}, bf16[48,512]{1,0:T(8,128)(2,1)S(1)}, u32[]{:S(2)}, u32[]{:S(2)}) %collective-permute-start.35) | collective-permute-done | bytes 49184 | tf_op jit(solution)/shard_map/ppermute | solution.py:458
  106.2 1.7 %collective-permute-start.39 = (f32[32,512]{1,0:T(8,128)S(1)}, f32[32,512]{1,0:T(8,128)S(1)}, u32[]{:S(2)}, u32[]{:S(2)}) collective-permute-start(f32[32,512]{1,0:T(8,128)S(1)} %slice.12.refs_0_), channel_id=1, source_target_pairs={{0,24},{4,28},{8,16},{12,20},{16,8},{20,12},{24,0},{28,4},{1,25},{... | collective-permute-start | bytes 196616 | tf_op jit(solution)/shard_map/ppermute | solution.py:458
  107.9 2.4 %collective-permute-start.32 = (bf16[128,512]{1,0:T(8,128)(2,1)S(1)}, bf16[128,512]{1,0:T(8,128)(2,1)S(1)}, u32[]{:S(2)}, u32[]{:S(2)}) collective-permute-start(bf16[128,512]{1,0:T(8,128)(2,1)S(1)} %get-tuple-element.65), channel_id=1, source_target_pairs={{0,2},{1,3},{2,0},{3,1},{4,6},{5,7},{6,4},{7,5},{8,10},{9,11},{10,... | collective-permute-start | bytes 393224 | tf_op jit(solution)/shard_map/ppermute | solution.py:458
  110.3 2.0 %collective-permute-start.33 = (bf16[128,512]{1,0:T(8,128)(2,1)S(1)}, bf16[128,512]{1,0:T(8,128)(2,1)S(1)}, u32[]{:S(2)}, u32[]{:S(2)}) collective-permute-start(bf16[128,512]{1,0:T(8,128)(2,1)S(1)} %get-tuple-element.66), channel_id=1, source_target_pairs={{0,3},{1,2},{2,1},{3,0},{4,7},{5,6},{6,5},{7,4},{8,11},{9,10},{10,... | collective-permute-start | bytes 393224 | tf_op jit(solution)/shard_map/ppermute | solution.py:458
  112.3 1.3 %collective-permute-start.38 = (f32[32,512]{1,0:T(8,128)S(1)}, f32[32,512]{1,0:T(8,128)S(1)}, u32[]{:S(2)}, u32[]{:S(2)}) collective-permute-start(f32[32,512]{1,0:T(8,128)S(1)} %slice.12.refs_0_), channel_id=1, source_target_pairs={{0,16},{4,20},{8,24},{12,28},{16,0},{20,4},{24,8},{28,12},{1,17},{... | collective-permute-start | bytes 196616 | tf_op jit(solution)/shard_map/ppermute | solution.py:458
  113.5 0.6 collective-permute-start.37
  114.1 2.4 %collective-permute-done.38.refs_2_ = f32[32,512]{1,0:T(8,128)S(1)} collective-permute-done((f32[32,512]{1,0:T(8,128)S(1)}, f32[32,512]{1,0:T(8,128)S(1)}, u32[]{:S(2)}, u32[]{:S(2)}) %collective-permute-start.38) | collective-permute-done | bytes 65568 | tf_op jit(solution)/shard_map/ppermute | solution.py:458
  116.5 1.3 %collective-permute-done.37.refs_1_ = f32[32,512]{1,0:T(8,128)S(1)} collective-permute-done((f32[32,512]{1,0:T(8,128)S(1)}, f32[32,512]{1,0:T(8,128)S(1)}, u32[]{:S(2)}, u32[]{:S(2)}) %collective-permute-start.37) | collective-permute-done | bytes 65568 | tf_op jit(solution)/shard_map/ppermute | solution.py:458
  117.8 0.5 collective-permute-start.42
  118.3 2.3 %collective-permute-done.32.refs_6_ = bf16[128,512]{1,0:T(8,128)(2,1)S(1)} collective-permute-done((bf16[128,512]{1,0:T(8,128)(2,1)S(1)}, bf16[128,512]{1,0:T(8,128)(2,1)S(1)}, u32[]{:S(2)}, u32[]{:S(2)}) %collective-permute-start.32) | collective-permute-done | bytes 131104 | tf_op jit(solution)/shard_map/ppermute | solution.py:458
  120.6 0.6 slice.13
  121.2 1.0 finish.1
  122.2 0.9 weight_grads.1
  (57 shorter events, 0.5 us)
Async XLA Ops:
  1.5 22.7 %collective-permute-start.2 = (bf16[512,128]{1,0:T(8,128)(2,1)S(1)}, bf16[512,128]{1,0:T(8,128)(2,1)S(1)}, u32[]{:S(2)}, u32[]{:S(2)}) collective-permute-start(bf16[512,128]{1,0:T(8,128)(2,1)S(1)} %slice.9.refs_1_), channel_id=1, source_target_pairs={{0,3},{1,2},{2,1},{3,0},{4,7},{5,6},{6,5},{7,4},{8,11},{9,10},{10,... | collective-permute-start | bytes 393224 | tf_op jit(solution)/shard_map/ppermute | solution.py:458
  6.7 18.3 %collective-permute-start.1 = (bf16[512,128]{1,0:T(8,128)(2,1)S(1)}, bf16[512,128]{1,0:T(8,128)(2,1)S(1)}, u32[]{:S(2)}, u32[]{:S(2)}) collective-permute-start(bf16[512,128]{1,0:T(8,128)(2,1)S(1)} %slice.9.refs_1_), channel_id=1, source_target_pairs={{0,2},{1,3},{2,0},{3,1},{4,6},{5,7},{6,4},{7,5},{8,10},{9,11},{10,... | collective-permute-start | bytes 393224 | tf_op jit(solution)/shard_map/ppermute | solution.py:458
  6.7 18.3 %collective-permute-start = (bf16[512,128]{1,0:T(8,128)(2,1)S(1)}, bf16[512,128]{1,0:T(8,128)(2,1)S(1)}, u32[]{:S(2)}, u32[]{:S(2)}) collective-permute-start(bf16[512,128]{1,0:T(8,128)(2,1)S(1)} %slice.9.refs_1_), channel_id=1, source_target_pairs={{0,1},{1,0},{2,3},{3,2},{4,5},{5,4},{6,7},{7,6},{8,9},{9,8},{10,11... | collective-permute-start | bytes 393224 | tf_op jit(solution)/shard_map/ppermute | solution.py:458
  8.0 1.0 copy-start
  20.5 8.3 %collective-permute-start.9 = (bf16[512,128]{1,0:T(8,128)(2,1)S(1)}, bf16[512,128]{1,0:T(8,128)(2,1)S(1)}, u32[]{:S(2)}, u32[]{:S(2)}) collective-permute-start(bf16[512,128]{1,0:T(8,128)(2,1)S(1)} %get-tuple-element.42.refs_1_), channel_id=1, source_target_pairs={{0,3},{1,2},{2,1},{3,0},{4,7},{5,6},{6,5},{7,4},{8,11},{9,10},{10,... | collective-permute-start | bytes 393224 | tf_op jit(solution)/shard_map/ppermute | solution.py:458
  24.3 10.2 %collective-permute-start.8 = (bf16[512,128]{1,0:T(8,128)(2,1)S(1)}, bf16[512,128]{1,0:T(8,128)(2,1)S(1)}, u32[]{:S(2)}, u32[]{:S(2)}) collective-permute-start(bf16[512,128]{1,0:T(8,128)(2,1)S(1)} %get-tuple-element.42.refs_1_), channel_id=1, source_target_pairs={{0,2},{1,3},{2,0},{3,1},{4,6},{5,7},{6,4},{7,5},{8,10},{9,11},{10,... | collective-permute-start | bytes 393224 | tf_op jit(solution)/shard_map/ppermute | solution.py:458
  24.3 10.2 %collective-permute-start.7 = (bf16[512,128]{1,0:T(8,128)(2,1)S(1)}, bf16[512,128]{1,0:T(8,128)(2,1)S(1)}, u32[]{:S(2)}, u32[]{:S(2)}) collective-permute-start(bf16[512,128]{1,0:T(8,128)(2,1)S(1)} %get-tuple-element.42.refs_1_), channel_id=1, source_target_pairs={{0,1},{1,0},{2,3},{3,2},{4,5},{5,4},{6,7},{7,6},{8,9},{9,8},{10,11... | collective-permute-start | bytes 393224 | tf_op jit(solution)/shard_map/ppermute | solution.py:458
  27.8 12.7 %collective-permute-start.3 = (bf16[4,512,128]{2,1,0:T(8,128)(2,1)S(1)}, bf16[4,512,128]{2,1,0:T(8,128)(2,1)S(1)}, u32[]{:S(2)}, u32[]{:S(2)}) collective-permute-start(bf16[4,512,128]{2,1,0:T(8,128)(2,1)S(1)} %forward.5), channel_id=1, source_target_pairs={{0,4},{4,0},{8,12},{12,8},{16,20},{20,16},{24,28},{28,24},{1,5},{5... | collective-permute-start | bytes 1572872 | tf_op jit(solution)/shard_map/ppermute | solution.py:458
  37.4 21.7 %copy-start.1 = (bf16[512,256]{1,0:T(8,128)(2,1)S(1)}, bf16[512,256]{1,0:T(8,128)(2,1)}, u32[]{:S(2)}) copy-start(bf16[512,256]{1,0:T(8,128)(2,1)} %feat_ref.3) | copy-start | bytes 786436
  37.4 21.7 %copy-start.2 = (bf16[256,256]{1,0:T(8,128)(2,1)S(1)}, bf16[256,256]{1,0:T(8,128)(2,1)}, u32[]{:S(2)}) copy-start(bf16[256,256]{1,0:T(8,128)(2,1)} %ws_ref.1) | copy-start | bytes 393220
  37.4 21.7 %copy-start.3 = (bf16[512,256]{1,0:T(8,128)(2,1)S(1)}, bf16[512,256]{1,0:T(8,128)(2,1)}, u32[]{:S(2)}) copy-start(bf16[512,256]{1,0:T(8,128)(2,1)} %refs_2_.1) | copy-start | bytes 786436
  37.5 21.7 %copy-start.4 = (bf16[256,256]{1,0:T(8,128)(2,1)S(1)}, bf16[256,256]{1,0:T(8,128)(2,1)}, u32[]{:S(2)}) copy-start(bf16[256,256]{1,0:T(8,128)(2,1)} %refs_4_.1) | copy-start | bytes 393220
  37.5 21.7 %copy-start.5 = (s32[512]{0:T(512)S(1)}, s32[512]{0:T(512)}, u32[]{:S(2)}) copy-start(s32[512]{0:T(512)} %param.10) | copy-start | bytes 6148
  37.5 21.7 %copy-start.6 = (f32[256]{0:T(256)S(1)}, f32[256]{0:T(256)}, u32[]{:S(2)}) copy-start(f32[256]{0:T(256)} %param.17) | copy-start | bytes 3076
  37.5 9.6 %collective-permute-start.10 = (bf16[4,512,128]{2,1,0:T(8,128)(2,1)S(1)}, bf16[4,512,128]{2,1,0:T(8,128)(2,1)S(1)}, u32[]{:S(2)}, u32[]{:S(2)}) collective-permute-start(bf16[4,512,128]{2,1,0:T(8,128)(2,1)S(1)} %forward.7), channel_id=1, source_target_pairs={{0,4},{4,0},{8,12},{12,8},{16,20},{20,16},{24,28},{28,24},{1,5},{5... | collective-permute-start | bytes 1572872 | tf_op jit(solution)/shard_map/ppermute | solution.py:458
  40.6 9.7 %collective-permute-start.4 = (bf16[512,128]{1,0:T(8,128)(2,1)S(1)}, bf16[512,128]{1,0:T(8,128)(2,1)S(1)}, u32[]{:S(2)}, u32[]{:S(2)}) collective-permute-start(bf16[512,128]{1,0:T(8,128)(2,1)S(1)} %get-tuple-element.39), channel_id=1, source_target_pairs={{0,8},{4,12},{8,0},{12,4},{16,24},{20,28},{24,16},{28,20},{1,9},{5... | collective-permute-start | bytes 393224 | tf_op jit(solution)/shard_map/ppermute | solution.py:458
  45.0 9.0 %collective-permute-start.5 = (bf16[512,128]{1,0:T(8,128)(2,1)S(1)}, bf16[512,128]{1,0:T(8,128)(2,1)S(1)}, u32[]{:S(2)}, u32[]{:S(2)}) collective-permute-start(bf16[512,128]{1,0:T(8,128)(2,1)S(1)} %get-tuple-element.40), channel_id=1, source_target_pairs={{0,16},{4,20},{8,24},{12,28},{16,0},{20,4},{24,8},{28,12},{1,17},{... | collective-permute-start | bytes 393224 | tf_op jit(solution)/shard_map/ppermute | solution.py:458
  46.6 7.4 %collective-permute-start.6 = (bf16[512,128]{1,0:T(8,128)(2,1)S(1)}, bf16[512,128]{1,0:T(8,128)(2,1)S(1)}, u32[]{:S(2)}, u32[]{:S(2)}) collective-permute-start(bf16[512,128]{1,0:T(8,128)(2,1)S(1)} %get-tuple-element.41), channel_id=1, source_target_pairs={{0,24},{4,28},{8,16},{12,20},{16,8},{20,12},{24,0},{28,4},{1,25},{... | collective-permute-start | bytes 393224 | tf_op jit(solution)/shard_map/ppermute | solution.py:458
  47.2 8.6 %collective-permute-start.11 = (bf16[512,128]{1,0:T(8,128)(2,1)S(1)}, bf16[512,128]{1,0:T(8,128)(2,1)S(1)}, u32[]{:S(2)}, u32[]{:S(2)}) collective-permute-start(bf16[512,128]{1,0:T(8,128)(2,1)S(1)} %get-tuple-element.43), channel_id=1, source_target_pairs={{0,8},{4,12},{8,0},{12,4},{16,24},{20,28},{24,16},{28,20},{1,9},{5... | collective-permute-start | bytes 393224 | tf_op jit(solution)/shard_map/ppermute | solution.py:458
  48.7 10.4 %collective-permute-start.12 = (bf16[512,128]{1,0:T(8,128)(2,1)S(1)}, bf16[512,128]{1,0:T(8,128)(2,1)S(1)}, u32[]{:S(2)}, u32[]{:S(2)}) collective-permute-start(bf16[512,128]{1,0:T(8,128)(2,1)S(1)} %get-tuple-element.44), channel_id=1, source_target_pairs={{0,16},{4,20},{8,24},{12,28},{16,0},{20,4},{24,8},{28,12},{1,17},{... | collective-permute-start | bytes 393224 | tf_op jit(solution)/shard_map/ppermute | solution.py:458
  50.2 8.9 %collective-permute-start.13 = (bf16[512,128]{1,0:T(8,128)(2,1)S(1)}, bf16[512,128]{1,0:T(8,128)(2,1)S(1)}, u32[]{:S(2)}, u32[]{:S(2)}) collective-permute-start(bf16[512,128]{1,0:T(8,128)(2,1)S(1)} %get-tuple-element.45), channel_id=1, source_target_pairs={{0,24},{4,28},{8,16},{12,20},{16,8},{20,12},{24,0},{28,4},{1,25},{... | collective-permute-start | bytes 393224 | tf_op jit(solution)/shard_map/ppermute | solution.py:458
  60.4 7.3 %collective-permute-start.16 = (bf16[128,512]{1,0:T(8,128)(2,1)S(1)}, bf16[128,512]{1,0:T(8,128)(2,1)S(1)}, u32[]{:S(2)}, u32[]{:S(2)}) collective-permute-start(bf16[128,512]{1,0:T(8,128)(2,1)S(1)} %get-tuple-element.48.refs_1_), channel_id=1, source_target_pairs={{0,24},{4,28},{8,16},{12,20},{16,8},{20,12},{24,0},{28,4},{1,25},{... | collective-permute-start | bytes 393224 | tf_op jit(solution)/shard_map/ppermute | solution.py:458
  61.9 7.2 %collective-permute-start.15 = (bf16[128,512]{1,0:T(8,128)(2,1)S(1)}, bf16[128,512]{1,0:T(8,128)(2,1)S(1)}, u32[]{:S(2)}, u32[]{:S(2)}) collective-permute-start(bf16[128,512]{1,0:T(8,128)(2,1)S(1)} %get-tuple-element.48.refs_1_), channel_id=1, source_target_pairs={{0,16},{4,20},{8,24},{12,28},{16,0},{20,4},{24,8},{28,12},{1,17},{... | collective-permute-start | bytes 393224 | tf_op jit(solution)/shard_map/ppermute | solution.py:458
  62.4 6.7 %collective-permute-start.14 = (bf16[128,512]{1,0:T(8,128)(2,1)S(1)}, bf16[128,512]{1,0:T(8,128)(2,1)S(1)}, u32[]{:S(2)}, u32[]{:S(2)}) collective-permute-start(bf16[128,512]{1,0:T(8,128)(2,1)S(1)} %get-tuple-element.48.refs_1_), channel_id=1, source_target_pairs={{0,8},{4,12},{8,0},{12,4},{16,24},{20,28},{24,16},{28,20},{1,9},{5... | collective-permute-start | bytes 393224 | tf_op jit(solution)/shard_map/ppermute | solution.py:458
  69.1 8.1 %collective-permute-start.21 = (bf16[208,512]{1,0:T(8,128)(2,1)S(1)}, bf16[208,512]{1,0:T(8,128)(2,1)S(1)}, u32[]{:S(2)}, u32[]{:S(2)}) collective-permute-start(bf16[208,512]{1,0:T(8,128)(2,1)S(1)} %get-tuple-element.57), channel_id=1, source_target_pairs={{0,8},{4,12},{8,0},{12,4},{16,24},{20,28},{24,16},{28,20},{1,9},{5... | collective-permute-start | bytes 638984 | tf_op jit(solution)/shard_map/ppermute | solution.py:458
  69.6 11.1 %collective-permute-start.22 = (bf16[208,512]{1,0:T(8,128)(2,1)S(1)}, bf16[208,512]{1,0:T(8,128)(2,1)S(1)}, u32[]{:S(2)}, u32[]{:S(2)}) collective-permute-start(bf16[208,512]{1,0:T(8,128)(2,1)S(1)} %get-tuple-element.58), channel_id=1, source_target_pairs={{0,16},{4,20},{8,24},{12,28},{16,0},{20,4},{24,8},{28,12},{1,17},{... | collective-permute-start | bytes 638984 | tf_op jit(solution)/shard_map/ppermute | solution.py:458
  70.9 9.8 %collective-permute-start.23 = (bf16[208,512]{1,0:T(8,128)(2,1)S(1)}, bf16[208,512]{1,0:T(8,128)(2,1)S(1)}, u32[]{:S(2)}, u32[]{:S(2)}) collective-permute-start(bf16[208,512]{1,0:T(8,128)(2,1)S(1)} %get-tuple-element.59), channel_id=1, source_target_pairs={{0,24},{4,28},{8,16},{12,20},{16,8},{20,12},{24,0},{28,4},{1,25},{... | collective-permute-start | bytes 638984 | tf_op jit(solution)/shard_map/ppermute | solution.py:458
  72.6 1.3 %collective-permute-start.17 = (bf16[128,512]{1,0:T(8,128)(2,1)S(1)}, bf16[128,512]{1,0:T(8,128)(2,1)S(1)}, u32[]{:S(2)}, u32[]{:S(2)}) collective-permute-start(bf16[128,512]{1,0:T(8,128)(2,1)S(1)} %get-tuple-element.48.refs_1_), channel_id=1, source_target_pairs={{0,4},{4,0},{8,12},{12,8},{16,20},{20,16},{24,28},{28,24},{1,5},{5... | collective-permute-start | bytes 393224 | tf_op jit(solution)/shard_map/ppermute | solution.py:458
  72.6 1.5 %collective-permute-start.20 = (bf16[128,512]{1,0:T(8,128)(2,1)S(1)}, bf16[128,512]{1,0:T(8,128)(2,1)S(1)}, u32[]{:S(2)}, u32[]{:S(2)}) collective-permute-start(bf16[128,512]{1,0:T(8,128)(2,1)S(1)} %collective-permute-done.16.refs_4_), channel_id=1, source_target_pairs={{0,4},{4,0},{8,12},{12,8},{16,20},{20,16},{24,28},{28,24},{1,5},{5... | collective-permute-start | bytes 393224 | tf_op jit(solution)/shard_map/ppermute | solution.py:458
  74.0 7.3 %collective-permute-start.19 = (bf16[128,512]{1,0:T(8,128)(2,1)S(1)}, bf16[128,512]{1,0:T(8,128)(2,1)S(1)}, u32[]{:S(2)}, u32[]{:S(2)}) collective-permute-start(bf16[128,512]{1,0:T(8,128)(2,1)S(1)} %collective-permute-done.15.refs_3_), channel_id=1, source_target_pairs={{0,4},{4,0},{8,12},{12,8},{16,20},{20,16},{24,28},{28,24},{1,5},{5... | collective-permute-start | bytes 393224 | tf_op jit(solution)/shard_map/ppermute | solution.py:458
  74.1 11.6 %collective-permute-start.24 = (bf16[208,512]{1,0:T(8,128)(2,1)S(1)}, bf16[208,512]{1,0:T(8,128)(2,1)S(1)}, u32[]{:S(2)}, u32[]{:S(2)}) collective-permute-start(bf16[208,512]{1,0:T(8,128)(2,1)S(1)} %get-tuple-element.56.refs_1_.refs_0_), channel_id=1, source_target_pairs={{0,4},{4,0},{8,12},{12,8},{16,20},{20,16},{24,28},{28,24},{1,5},{5... | collective-permute-start | bytes 638984 | tf_op jit(solution)/shard_map/ppermute | solution.py:458
  77.3 8.5 %collective-permute-start.25 = (bf16[208,512]{1,0:T(8,128)(2,1)S(1)}, bf16[208,512]{1,0:T(8,128)(2,1)S(1)}, u32[]{:S(2)}, u32[]{:S(2)}) collective-permute-start(bf16[208,512]{1,0:T(8,128)(2,1)S(1)} %collective-permute-done.21.refs_2_.refs_1_), channel_id=1, source_target_pairs={{0,4},{4,0},{8,12},{12,8},{16,20},{20,16},{24,28},{28,24},{1,5},{5... | collective-permute-start | bytes 638984 | tf_op jit(solution)/shard_map/ppermute | solution.py:458
  80.8 5.0 %collective-permute-start.26 = (bf16[208,512]{1,0:T(8,128)(2,1)S(1)}, bf16[208,512]{1,0:T(8,128)(2,1)S(1)}, u32[]{:S(2)}, u32[]{:S(2)}) collective-permute-start(bf16[208,512]{1,0:T(8,128)(2,1)S(1)} %collective-permute-done.22.refs_3_.refs_2_), channel_id=1, source_target_pairs={{0,4},{4,0},{8,12},{12,8},{16,20},{20,16},{24,28},{28,24},{1,5},{5... | collective-permute-start | bytes 638984 | tf_op jit(solution)/shard_map/ppermute | solution.py:458
  80.8 5.0 %collective-permute-start.27 = (bf16[208,512]{1,0:T(8,128)(2,1)S(1)}, bf16[208,512]{1,0:T(8,128)(2,1)S(1)}, u32[]{:S(2)}, u32[]{:S(2)}) collective-permute-start(bf16[208,512]{1,0:T(8,128)(2,1)S(1)} %collective-permute-done.23.refs_4_.refs_3_), channel_id=1, source_target_pairs={{0,4},{4,0},{8,12},{12,8},{16,20},{20,16},{24,28},{28,24},{1,5},{5... | collective-permute-start | bytes 638984 | tf_op jit(solution)/shard_map/ppermute | solution.py:458
  81.3 1.4 %collective-permute-start.18 = (bf16[128,512]{1,0:T(8,128)(2,1)S(1)}, bf16[128,512]{1,0:T(8,128)(2,1)S(1)}, u32[]{:S(2)}, u32[]{:S(2)}) collective-permute-start(bf16[128,512]{1,0:T(8,128)(2,1)S(1)} %collective-permute-done.14.refs_2_), channel_id=1, source_target_pairs={{0,4},{4,0},{8,12},{12,8},{16,20},{20,16},{24,28},{28,24},{1,5},{5... | collective-permute-start | bytes 393224 | tf_op jit(solution)/shard_map/ppermute | solution.py:458
  85.7 22.2 %collective-permute-start.28 = (bf16[128,512]{1,0:T(8,128)(2,1)S(1)}, bf16[128,512]{1,0:T(8,128)(2,1)S(1)}, u32[]{:S(2)}, u32[]{:S(2)}) collective-permute-start(bf16[128,512]{1,0:T(8,128)(2,1)S(1)} %get-tuple-element.61), channel_id=1, source_target_pairs={{0,1},{1,0},{2,3},{3,2},{4,5},{5,4},{6,7},{7,6},{8,9},{9,8},{10,11... | collective-permute-start | bytes 393224 | tf_op jit(solution)/shard_map/ppermute | solution.py:458
  85.9 7.7 %collective-permute-start.36 = (bf16[48,512]{1,0:T(8,128)(2,1)S(1)}, bf16[48,512]{1,0:T(8,128)(2,1)S(1)}, u32[]{:S(2)}, u32[]{:S(2)}) collective-permute-start(bf16[48,512]{1,0:T(8,128)(2,1)S(1)} %get-tuple-element.68), channel_id=1, source_target_pairs={{0,3},{1,2},{2,1},{3,0},{4,7},{5,6},{6,5},{7,4},{8,11},{9,10},{10,... | collective-permute-start | bytes 147464 | tf_op jit(solution)/shard_map/ppermute | solution.py:458
  88.4 21.9 %collective-permute-start.29 = (bf16[128,512]{1,0:T(8,128)(2,1)S(1)}, bf16[128,512]{1,0:T(8,128)(2,1)S(1)}, u32[]{:S(2)}, u32[]{:S(2)}) collective-permute-start(bf16[128,512]{1,0:T(8,128)(2,1)S(1)} %get-tuple-element.62), channel_id=1, source_target_pairs={{0,2},{1,3},{2,0},{3,1},{4,6},{5,7},{6,4},{7,5},{8,10},{9,11},{10,... | collective-permute-start | bytes 393224 | tf_op jit(solution)/shard_map/ppermute | solution.py:458
  89.4 22.8 %collective-permute-start.30 = (bf16[128,512]{1,0:T(8,128)(2,1)S(1)}, bf16[128,512]{1,0:T(8,128)(2,1)S(1)}, u32[]{:S(2)}, u32[]{:S(2)}) collective-permute-start(bf16[128,512]{1,0:T(8,128)(2,1)S(1)} %get-tuple-element.63), channel_id=1, source_target_pairs={{0,3},{1,2},{2,1},{3,0},{4,7},{5,6},{6,5},{7,4},{8,11},{9,10},{10,... | collective-permute-start | bytes 393224 | tf_op jit(solution)/shard_map/ppermute | solution.py:458
  91.8 14.3 %collective-permute-start.35 = (bf16[48,512]{1,0:T(8,128)(2,1)S(1)}, bf16[48,512]{1,0:T(8,128)(2,1)S(1)}, u32[]{:S(2)}, u32[]{:S(2)}) collective-permute-start(bf16[48,512]{1,0:T(8,128)(2,1)S(1)} %get-tuple-element.68), channel_id=1, source_target_pairs={{0,2},{1,3},{2,0},{3,1},{4,6},{5,7},{6,4},{7,5},{8,10},{9,11},{10,... | collective-permute-start | bytes 147464 | tf_op jit(solution)/shard_map/ppermute | solution.py:458
  93.6 12.5 %collective-permute-start.34 = (bf16[48,512]{1,0:T(8,128)(2,1)S(1)}, bf16[48,512]{1,0:T(8,128)(2,1)S(1)}, u32[]{:S(2)}, u32[]{:S(2)}) collective-permute-start(bf16[48,512]{1,0:T(8,128)(2,1)S(1)} %get-tuple-element.68), channel_id=1, source_target_pairs={{0,1},{1,0},{2,3},{3,2},{4,5},{5,4},{6,7},{7,6},{8,9},{9,8},{10,11... | collective-permute-start | bytes 147464 | tf_op jit(solution)/shard_map/ppermute | solution.py:458
  106.2 7.4 %collective-permute-start.39 = (f32[32,512]{1,0:T(8,128)S(1)}, f32[32,512]{1,0:T(8,128)S(1)}, u32[]{:S(2)}, u32[]{:S(2)}) collective-permute-start(f32[32,512]{1,0:T(8,128)S(1)} %slice.12.refs_0_), channel_id=1, source_target_pairs={{0,24},{4,28},{8,16},{12,20},{16,8},{20,12},{24,0},{28,4},{1,25},{... | collective-permute-start | bytes 196616 | tf_op jit(solution)/shard_map/ppermute | solution.py:458
  107.9 9.9 %collective-permute-start.31 = (bf16[128,512]{1,0:T(8,128)(2,1)S(1)}, bf16[128,512]{1,0:T(8,128)(2,1)S(1)}, u32[]{:S(2)}, u32[]{:S(2)}) collective-permute-start(bf16[128,512]{1,0:T(8,128)(2,1)S(1)} %get-tuple-element.64), channel_id=1, source_target_pairs={{0,1},{1,0},{2,3},{3,2},{4,5},{5,4},{6,7},{7,6},{8,9},{9,8},{10,11... | collective-permute-start | bytes 393224 | tf_op jit(solution)/shard_map/ppermute | solution.py:458
  107.9 12.7 %collective-permute-start.32 = (bf16[128,512]{1,0:T(8,128)(2,1)S(1)}, bf16[128,512]{1,0:T(8,128)(2,1)S(1)}, u32[]{:S(2)}, u32[]{:S(2)}) collective-permute-start(bf16[128,512]{1,0:T(8,128)(2,1)S(1)} %get-tuple-element.65), channel_id=1, source_target_pairs={{0,2},{1,3},{2,0},{3,1},{4,6},{5,7},{6,4},{7,5},{8,10},{9,11},{10,... | collective-permute-start | bytes 393224 | tf_op jit(solution)/shard_map/ppermute | solution.py:458
  110.3 10.9 %collective-permute-start.33 = (bf16[128,512]{1,0:T(8,128)(2,1)S(1)}, bf16[128,512]{1,0:T(8,128)(2,1)S(1)}, u32[]{:S(2)}, u32[]{:S(2)}) collective-permute-start(bf16[128,512]{1,0:T(8,128)(2,1)S(1)} %get-tuple-element.66), channel_id=1, source_target_pairs={{0,3},{1,2},{2,1},{3,0},{4,7},{5,6},{6,5},{7,4},{8,11},{9,10},{10,... | collective-permute-start | bytes 393224 | tf_op jit(solution)/shard_map/ppermute | solution.py:458
  112.3 4.3 %collective-permute-start.38 = (f32[32,512]{1,0:T(8,128)S(1)}, f32[32,512]{1,0:T(8,128)S(1)}, u32[]{:S(2)}, u32[]{:S(2)}) collective-permute-start(f32[32,512]{1,0:T(8,128)S(1)} %slice.12.refs_0_), channel_id=1, source_target_pairs={{0,16},{4,20},{8,24},{12,28},{16,0},{20,4},{24,8},{28,12},{1,17},{... | collective-permute-start | bytes 196616 | tf_op jit(solution)/shard_map/ppermute | solution.py:458
  113.5 4.3 %collective-permute-start.37 = (f32[32,512]{1,0:T(8,128)S(1)}, f32[32,512]{1,0:T(8,128)S(1)}, u32[]{:S(2)}, u32[]{:S(2)}) collective-permute-start(f32[32,512]{1,0:T(8,128)S(1)} %slice.12.refs_0_), channel_id=1, source_target_pairs={{0,8},{4,12},{8,0},{12,4},{16,24},{20,28},{24,16},{28,20},{1,9},{5... | collective-permute-start | bytes 196616 | tf_op jit(solution)/shard_map/ppermute | solution.py:458
  116.5 5.6 %collective-permute-start.40 = (f32[32,512]{1,0:T(8,128)S(1)}, f32[32,512]{1,0:T(8,128)S(1)}, u32[]{:S(2)}, u32[]{:S(2)}) collective-permute-start(f32[32,512]{1,0:T(8,128)S(1)} %slice.12.refs_0_), channel_id=1, source_target_pairs={{0,4},{4,0},{8,12},{12,8},{16,20},{20,16},{24,28},{28,24},{1,5},{5... | collective-permute-start | bytes 196616 | tf_op jit(solution)/shard_map/ppermute | solution.py:458
  117.8 4.4 %collective-permute-start.43 = (f32[32,512]{1,0:T(8,128)S(1)}, f32[32,512]{1,0:T(8,128)S(1)}, u32[]{:S(2)}, u32[]{:S(2)}) collective-permute-start(f32[32,512]{1,0:T(8,128)S(1)} %collective-permute-done.39.refs_3_), channel_id=1, source_target_pairs={{0,4},{4,0},{8,12},{12,8},{16,20},{20,16},{24,28},{28,24},{1,5},{5... | collective-permute-start | bytes 196616 | tf_op jit(solution)/shard_map/ppermute | solution.py:458
  117.8 4.4 %collective-permute-start.42 = (f32[32,512]{1,0:T(8,128)S(1)}, f32[32,512]{1,0:T(8,128)S(1)}, u32[]{:S(2)}, u32[]{:S(2)}) collective-permute-start(f32[32,512]{1,0:T(8,128)S(1)} %collective-permute-done.38.refs_2_), channel_id=1, source_target_pairs={{0,4},{4,0},{8,12},{12,8},{16,20},{20,16},{24,28},{28,24},{1,5},{5... | collective-permute-start | bytes 196616 | tf_op jit(solution)/shard_map/ppermute | solution.py:458
  120.6 1.6 %collective-permute-start.41 = (f32[32,512]{1,0:T(8,128)S(1)}, f32[32,512]{1,0:T(8,128)S(1)}, u32[]{:S(2)}, u32[]{:S(2)}) collective-permute-start(f32[32,512]{1,0:T(8,128)S(1)} %collective-permute-done.37.refs_1_), channel_id=1, source_target_pairs={{0,4},{4,0},{8,12},{12,8},{16,20},{20,16},{24,28},{28,24},{1,5},{5... | collective-permute-start | bytes 196616 | tf_op jit(solution)/shard_map/ppermute | solution.py:458

commit v3 on v2

v3 whole, which is shorter than its diff:
```python
import jax
import jax.numpy as jnp
from jax import lax
from jax.experimental import pallas as pl
from jax.experimental.pallas import tpu as pltpu
from jax.sharding import PartitionSpec as P

F32 = jnp.float32
BF16 = jnp.bfloat16
MIB = 1 << 20
RESIDENT_BYTES = 20 * MIB
BIAS_ROWS = 16


def vmem():
    return pl.BlockSpec(memory_space=pltpu.VMEM)


def params(limit_mib):
    return pltpu.CompilerParams(vmem_limit_bytes=limit_mib * MIB)


def cost(us):
    return pl.CostEstimate(flops=0, bytes_accessed=int(us * 3.7e6), transcendentals=0)


def sds(shape, dtype):
    return jax.ShapeDtypeStruct(shape, dtype)


def densify_far(tile_values, tile_row, tile_col, n_row, n_col, per_dev):
    slots, tile, _ = tile_values.shape
    chips = n_row // 2
    rows = n_row * per_dev
    cols = n_col * per_dev
    cells = rows * cols

    def kernel(row_ref, col_ref, values_ref, dense_ref, table, blank, sem):
        blank[...] = jnp.zeros_like(blank)
        chip = lax.axis_index("row") // 2
        core = lax.axis_index("row") % 2
        col_at = lax.axis_index("col")

        def clear(i, carry):
            for k in range(8):
                table[i * 8 + k] = slots
            return carry

        lax.fori_loop(0, cells // 8, clear, 0)

        def note(i, carry):
            for k in range(4):
                at = i * 4 + k
                table[row_ref[at] * cols + col_ref[at]] = at
            return carry

        lax.fori_loop(0, slots // 4, note, 0)

        def fill(i, carry):
            slot = table[i]
            t = i // cols
            s = i % cols
            owner = t // per_dev
            block = ((owner % 2) ^ core) * chips + ((owner // 2) ^ chip)
            u = (block * per_dev + t % per_dev) * tile
            v = (((s // per_dev) ^ col_at) * per_dev + s % per_dev) * tile
            where = dense_ref.at[
                pl.ds(pl.multiple_of(u, tile), tile), pl.ds(pl.multiple_of(v, tile), tile)
            ]

            @pl.when(slot < slots)
            def _():
                pltpu.make_async_copy(values_ref.at[slot], where, sem).start()

            @pl.when(slot >= slots)
            def _():
                pltpu.make_async_copy(blank, where, sem).start()

            return carry

        lax.fori_loop(0, cells, fill, 0)
        pltpu.make_async_copy(dense_ref, dense_ref, sem).wait()

    shape = (rows * tile, cols * tile)
    return pl.pallas_call(
        kernel,
        out_shape=sds(shape, BF16),
        grid_spec=pltpu.PrefetchScalarGridSpec(
            num_scalar_prefetch=2,
            grid=(),
            in_specs=[pl.BlockSpec(memory_space=pl.ANY)],
            out_specs=pl.BlockSpec(memory_space=pl.ANY),
            scratch_shapes=[
                pltpu.SMEM((cells + cols,), jnp.int32),
                pltpu.VMEM((tile, tile), BF16),
                pltpu.SemaphoreType.DMA,
            ],
        ),
        compiler_params=params(8),
        cost_estimate=cost(40),
        name="densify_far",
    )(tile_row, tile_col, tile_values)


def densify(tile_values, tile_row, tile_col, n_row, n_col, per_dev):
    slots, tile, _ = tile_values.shape
    chips = n_row // 2
    rows = n_row * per_dev
    cols = n_col * per_dev
    chip = lax.axis_index("row") // 2
    core = lax.axis_index("row") % 2
    owner = tile_row // per_dev
    block = ((owner % 2) ^ core) * chips + ((owner // 2) ^ chip)
    down = (block * per_dev + tile_row % per_dev) * tile
    down = jnp.where(tile_row < rows, down, rows * tile)
    right = ((tile_col // per_dev) ^ lax.axis_index("col")) * per_dev + tile_col % per_dev
    right = right * tile
    step_slots = 32
    while slots % step_slots:
        step_slots //= 2

    def kernel(down_ref, right_ref, values_ref, dense_ref):
        step = pl.program_id(0)

        @pl.when(step == 0)
        def _():
            def clear(i, carry):
                at = pl.multiple_of(i * tile, tile)
                dense_ref[pl.ds(at, tile), :] = jnp.zeros((tile, cols * tile), BF16)
                return carry

            lax.fori_loop(0, rows, clear, 0)

        for k in range(step_slots):
            u = pl.multiple_of(down_ref[step * step_slots + k], tile)
            v = pl.multiple_of(right_ref[step * step_slots + k], tile)
            dense_ref[pl.ds(u, tile), pl.ds(v, tile)] = values_ref[k]

    return pl.pallas_call(
        kernel,
        out_shape=pltpu.VMEM(((rows + 1) * tile, cols * tile), BF16),
        grid_spec=pltpu.PrefetchScalarGridSpec(
            num_scalar_prefetch=2,
            grid=(slots // step_slots,),
            in_specs=[pl.BlockSpec((step_slots, tile, tile), lambda i, *_: (i, 0, 0))],
            out_specs=vmem(),
        ),
        compiler_params=params(8),
        cost_estimate=cost(10),
        name="densify",
    )(down, right, pltpu.with_memory_space_constraint(tile_values, pltpu.HBM))


def pinned(dense, resident):
    return pltpu.with_memory_space_constraint(dense, pltpu.VMEM) if resident else dense


def forward(dense, pieces, first, count, dtype, resident):
    n_col = len(pieces)
    nodes, wide = pieces[0].shape
    cols = n_col * nodes

    def kernel(*refs):
        dense_ref, piece_refs, out_ref, source = refs[0], refs[1 : 1 + n_col], refs[-2], refs[-1]
        step = pl.program_id(0)

        @pl.when(step == 0)
        def _():
            for m in range(n_col):
                source[m * nodes : (m + 1) * nodes, :] = piece_refs[m][...]

        if resident:
            at = pl.multiple_of((first + step) * nodes, nodes)
            block = dense_ref[pl.ds(at, nodes), :]
        else:
            block = dense_ref[...]
        out_ref[0] = jnp.dot(block, source[...], preferred_element_type=F32).astype(dtype)

    spec = vmem() if resident else pl.BlockSpec((nodes, cols), lambda i: (i + first, 0))
    return pl.pallas_call(
        kernel,
        out_shape=sds((count, nodes, wide), dtype),
        grid=(count,),
        in_specs=[spec] + [pl.BlockSpec((nodes, wide), lambda i: (0, 0))] * n_col,
        out_specs=pl.BlockSpec((1, nodes, wide), lambda i: (i, 0, 0)),
        scratch_shapes=[pltpu.VMEM((cols, wide), BF16)],
        compiler_params=params(8 if resident else 24),
        cost_estimate=cost(0.01),
        name="forward",
    )(pinned(dense, resident), *pieces)


def add_parts(keep, got):
    count, nodes, wide = keep.shape

    def kernel(keep_ref, got_ref, *out_refs):
        for j in range(count):
            out_refs[j][...] = (keep_ref[j] + got_ref[j].astype(F32)).astype(BF16)

    return pl.pallas_call(
        kernel,
        out_shape=[sds((nodes, wide), BF16)] * count,
        in_specs=[vmem()] * 2,
        out_specs=[vmem()] * count,
        compiler_params=params(8),
        cost_estimate=cost(0.1),
        name="add_parts",
    )(keep, got)


def middle(features, degree, cotangent, w_self, w_neigh, bias, keep, got, arrivals):
    nodes, width = features.shape

    def kernel(*refs):
        feat_ref, degree_ref, cot_ref, ws_ref, wn_ref, bias_ref = refs[:6]
        keep_ref, got_ref, *part_refs = refs[6:-4]
        hidden_ref, mean_ref, d_pre_ref, d_agg_ref = refs[-4:]
        scale = degree_ref[...].astype(F32)
        scale_down = jnp.transpose(jnp.broadcast_to(scale, (width, nodes)))
        total = keep_ref[0] + got_ref[0].astype(F32)
        for ref in part_refs:
            total = total + ref[...].astype(F32)
        neigh_mean = (total / scale_down).astype(BF16)
        mean_ref[...] = neigh_mean
        pre = jnp.dot(feat_ref[...], ws_ref[...], preferred_element_type=F32)
        pre = pre + jnp.dot(neigh_mean, wn_ref[...], preferred_element_type=F32) + bias_ref[...]
        sig = jax.nn.sigmoid(pre)
        hidden_ref[...] = (pre * sig).astype(BF16)
        d_pre = (cot_ref[...].astype(F32) * sig * (1.0 + pre * (1.0 - sig))).astype(BF16)
        d_pre_ref[...] = d_pre
        d_agg = lax.dot_general(
            d_pre, wn_ref[...], (((1,), (1,)), ((), ())), preferred_element_type=F32
        )
        d_agg_ref[...] = (jnp.transpose(d_agg) / scale).astype(BF16)

    args = [features, degree, cotangent, w_self, w_neigh, bias, keep, got, *arrivals]
    return pl.pallas_call(
        kernel,
        out_shape=[sds((nodes, width), BF16)] * 3 + [sds((width, nodes), BF16)],
        in_specs=[vmem()] * len(args),
        out_specs=[vmem()] * 4,
        compiler_params=params(12),
        cost_estimate=cost(1.5),
        name="middle",
    )(*args)


def local_grads(features, neigh_mean, d_pre, n_row):
    nodes, width = features.shape
    share = width // n_row
    half = width // 2

    def kernel(feat_ref, mean_ref, d_pre_ref, keep_ref, give_ref, grads_ref):
        d_pre_now = d_pre_ref[...]
        over = (((0,), (0,)), ((), ()))
        grads_ref[:, 0:width] = lax.dot_general(
            feat_ref[...], d_pre_now, over, preferred_element_type=F32
        )
        grads_ref[:, width:] = lax.dot_general(
            mean_ref[...], d_pre_now, over, preferred_element_type=F32
        )
        bias_sum = jnp.sum(d_pre_now.astype(F32), axis=0, keepdims=True)
        bias_row = jnp.concatenate([bias_sum, bias_sum], axis=1)
        bias_rows = jnp.broadcast_to(bias_row, (BIAS_ROWS, 2 * width))
        core = lax.axis_index("row") % 2
        for k, ref in enumerate((keep_ref, give_ref)):
            for j in range(n_row // 2):
                at = pl.multiple_of((j * 2 + (core ^ k)) * share, share)
                ref[j * share : (j + 1) * share, :] = grads_ref[pl.ds(at, share), :].astype(ref.dtype)
            ref[half:, :] = bias_rows.astype(ref.dtype)

    return pl.pallas_call(
        kernel,
        out_shape=[sds((half + BIAS_ROWS, 2 * width), d) for d in (F32, BF16)],
        in_specs=[vmem()] * 3,
        out_specs=[vmem()] * 2,
        scratch_shapes=[pltpu.VMEM((width, 2 * width), F32)],
        compiler_params=params(8),
        cost_estimate=cost(0.5),
        name="local_grads",
    )(features, neigh_mean, d_pre)


def column_parts(keep, got, n_col):
    height, columns = keep.shape
    part = (height - BIAS_ROWS) // n_col

    def kernel(keep_ref, got_ref, *refs):
        out_refs, sum_ref = refs[:-1], refs[-1]
        sum_ref[...] = keep_ref[...] + got_ref[...].astype(F32)
        col = lax.axis_index("col")
        for m, ref in enumerate(out_refs):
            at = pl.multiple_of((col ^ m) * part, part)
            ref[0:part, :] = sum_ref[pl.ds(at, part), :].astype(ref.dtype)
            ref[part:, :] = sum_ref[height - BIAS_ROWS :, :].astype(ref.dtype)

    return pl.pallas_call(
        kernel,
        out_shape=[sds((part + BIAS_ROWS, columns), F32 if m == 0 else BF16) for m in range(n_col)],
        in_specs=[vmem()] * 2,
        out_specs=[vmem()] * n_col,
        scratch_shapes=[pltpu.VMEM(keep.shape, F32)],
        compiler_params=params(8),
        cost_estimate=cost(0.1),
        name="column_parts",
    )(keep, got)


def column_sum(own, arrivals):
    height, columns = own.shape
    part = height - BIAS_ROWS

    def kernel(own_ref, *refs):
        send_ref, bias_ref = refs[-2:]
        acc = own_ref[...]
        for ref in refs[:-2]:
            acc = acc + ref[...].astype(F32)
        send_ref[...] = acc[0:part].astype(BF16)
        bias_ref[...] = acc[part:]

    return pl.pallas_call(
        kernel,
        out_shape=[sds((part, columns), BF16), sds((BIAS_ROWS, columns), F32)],
        in_specs=[vmem()] * (1 + len(arrivals)),
        out_specs=[vmem()] * 2,
        compiler_params=params(8),
        cost_estimate=cost(0.1),
        name="column_sum",
    )(own, *arrivals)


def chip_parts(parts, bias_rows, n_row):
    part, columns = parts[0].shape
    n_col = len(parts)
    chips = n_row // 2
    share = part * n_col // chips

    def kernel(*refs):
        part_refs, bias_ref = refs[:n_col], refs[n_col]
        out_refs, whole_ref = refs[n_col + 1 : -1], refs[-1]
        col = lax.axis_index("col")
        for m, ref in enumerate(part_refs):
            at = pl.multiple_of((col ^ m) * part, part)
            whole_ref[pl.ds(at, part), :] = ref[...].astype(F32)
        chip = lax.axis_index("row") // 2
        for j, ref in enumerate(out_refs):
            at = pl.multiple_of((chip ^ j) * share, share)
            ref[0:share, :] = whole_ref[pl.ds(at, share), :]
            ref[share:, :] = bias_ref[...]

    return pl.pallas_call(
        kernel,
        out_shape=[sds((share + BIAS_ROWS, columns), F32)] * chips,
        in_specs=[vmem()] * (n_col + 1),
        out_specs=[vmem()] * chips,
        scratch_shapes=[pltpu.VMEM((part * n_col, columns), F32)],
        compiler_params=params(8),
        cost_estimate=cost(0.1),
        name="chip_parts",
    )(*parts, bias_rows)


def side_by_side(pieces):
    wide, nodes = pieces[0].shape

    def kernel(*refs):
        for j, ref in enumerate(refs[:-1]):
            refs[-1][:, j * nodes : (j + 1) * nodes] = ref[...]

    return pl.pallas_call(
        kernel,
        out_shape=sds((wide, len(pieces) * nodes), BF16),
        in_specs=[vmem()] * len(pieces),
        out_specs=vmem(),
        compiler_params=params(8),
        cost_estimate=cost(0.3),
        name="side_by_side",
    )(*pieces)


def backward(dense, mine, siblings, columns, nodes, resident):
    wide, half = mine.shape
    count = len(columns)
    first = columns[0]

    def kernel(dense_ref, mine_ref, siblings_ref, *out_refs):
        step = pl.program_id(0)
        for i, m in enumerate(columns):

            @pl.when(step == i)
            def _():
                if resident:
                    upper = dense_ref[0:half, m * nodes : (m + 1) * nodes]
                    lower = dense_ref[half : 2 * half, m * nodes : (m + 1) * nodes]
                else:
                    upper = dense_ref[0:half, :]
                    lower = dense_ref[half:, :]
                out = jnp.dot(mine_ref[...], upper, preferred_element_type=F32)
                out = out + jnp.dot(siblings_ref[...], lower, preferred_element_type=F32)
                out_refs[i][...] = out.astype(out_refs[i].dtype)

    spec = vmem() if resident else pl.BlockSpec((2 * half, nodes), lambda i: (0, i + first))
    whole = lambda shape: pl.BlockSpec(shape, lambda i: (0,) * len(shape))
    outs = [sds((wide, nodes), F32 if m == 0 else BF16) for m in columns]
    return pl.pallas_call(
        kernel,
        out_shape=outs,
        grid=(count,),
        in_specs=[spec] + [whole((wide, half))] * 2,
        out_specs=[whole(o.shape) for o in outs],
        compiler_params=params(16 if resident else 48),
        cost_estimate=cost(2.5),
        name="backward",
    )(pinned(dense, resident), mine, siblings)


def share_total(total, arrivals):
    height, columns = total.shape
    share = height - BIAS_ROWS
    width = columns // 2

    def kernel(total_ref, *refs):
        share_ref, bias_ref = refs[-2:]
        acc = total_ref[...]
        for ref in refs[:-2]:
            acc = acc + ref[...].astype(F32)
        share_ref[...] = acc[0:share]
        bias_ref[...] = acc[share : share + 1, 0:width]

    return pl.pallas_call(
        kernel,
        out_shape=[sds((share, columns), F32), sds((1, width), F32)],
        in_specs=[vmem()] * (1 + len(arrivals)),
        out_specs=[vmem()] * 2,
        compiler_params=params(8),
        cost_estimate=cost(0.1),
        name="share_total",
    )(total, *arrivals)


def join(pieces):
    height, columns = pieces[0].shape

    def kernel(*refs):
        for j, ref in enumerate(refs[:-1]):
            refs[-1][j * height : (j + 1) * height, :] = ref[...]

    return pl.pallas_call(
        kernel,
        out_shape=sds((len(pieces) * height, columns), F32),
        in_specs=[vmem()] * len(pieces),
        out_specs=vmem(),
        compiler_params=params(4),
        cost_estimate=cost(0.1),
        name="join",
    )(*pieces)


def weight_grads(mine, siblings, n_row):
    chips = n_row // 2
    share = mine.shape[0] // chips
    width = mine.shape[1] // 2

    def kernel(mine_ref, siblings_ref, self_ref, neigh_ref):
        chip = lax.axis_index("row") // 2
        core = lax.axis_index("row") % 2
        for k, ref in enumerate((mine_ref, siblings_ref)):
            for j in range(chips):
                at = pl.multiple_of(((chip ^ j) * 2 + (core ^ k)) * share, share)
                low = j * share
                self_ref[pl.ds(at, share), :] = ref[low : low + share, 0:width]
                neigh_ref[pl.ds(at, share), :] = ref[low : low + share, width:]

    return pl.pallas_call(
        kernel,
        out_shape=[sds((width, width), F32)] * 2,
        in_specs=[vmem()] * 2,
        out_specs=[vmem()] * 2,
        compiler_params=params(8),
        cost_estimate=cost(1),
        name="weight_grads",
    )(mine, siblings)


def finish(d_pre, w_self, own, arrived):
    nodes, width = d_pre.shape

    def kernel(d_pre_ref, ws_ref, own_ref, *refs):
        out_ref = refs[-1]
        direct = lax.dot_general(
            d_pre_ref[...], ws_ref[...], (((1,), (1,)), ((), ())), preferred_element_type=F32
        )
        acc = own_ref[...]
        for ref in refs[:-1]:
            acc = acc + ref[...].astype(F32)
        out_ref[...] = (direct + jnp.transpose(acc)).astype(BF16)

    return pl.pallas_call(
        kernel,
        out_shape=sds((nodes, width), BF16),
        in_specs=[vmem()] * (3 + len(arrived)),
        out_specs=vmem(),
        compiler_params=params(8),
        cost_estimate=cost(1),
        name="finish",
    )(d_pre, w_self, own, *arrived)


def swap(x, axis, mask):
    size = lax.axis_size(axis)
    return lax.ppermute(x, axis, [(i, i ^ mask) for i in range(size)])


def far_first(n):
    return sorted(range(1, n), key=lambda m: -bin(m).count("1") * n - m)


def body(features, degree, cotangent, tile_values, tile_row, tile_col, w_self, w_neigh, bias):
    nodes, width = features.shape
    tile = tile_values.shape[1]
    n_row = lax.axis_size("row")
    n_col = lax.axis_size("col")
    chips = n_row // 2
    per_dev = nodes // tile
    resident = n_row * nodes * n_col * nodes * 2 <= RESIDENT_BYTES

    arrived = {m: swap(features, "col", m) for m in far_first(n_col)}
    source = [features] + [arrived[m] for m in range(1, n_col)]
    build = densify if resident else densify_far
    dense = build(tile_values, tile_row, tile_col, n_row, n_col, per_dev)

    give = forward(dense, source, chips + 1, chips - 1, BF16, resident)
    got = swap(give, "row", 1)
    keep = forward(dense, source, 1, chips - 1, F32, resident)
    sends = add_parts(keep, got)
    arrivals = [swap(sends[j - 1], "row", 2 * j) for j in range(1, chips)]
    give_own = forward(dense, source, chips, 1, BF16, resident)
    got_own = swap(give_own, "row", 1)
    keep_own = forward(dense, source, 0, 1, F32, resident)
    hidden, neigh_mean, d_pre, d_agg = middle(
        features,
        degree[None, :],
        cotangent,
        w_self,
        w_neigh,
        bias[None, :],
        keep_own,
        got_own,
        arrivals,
    )

    pieces = [d_agg] + [swap(d_agg, "row", 2 * j) for j in range(1, chips)]

    grads_keep, grads_give = local_grads(features, neigh_mean, d_pre, n_row)
    cuts = column_parts(grads_keep, swap(grads_give, "row", 1), n_col)
    part, bias_rows = column_sum(cuts[0], [swap(cuts[m], "col", m) for m in range(1, n_col)])
    pieces, part = lax.optimization_barrier((pieces, part))
    mine = side_by_side(pieces)
    siblings = swap(mine, "row", 1)
    cut = [part] + [swap(part, "col", m) for m in range(1, n_col)]

    near = n_col // 2
    far_outs = backward(dense, mine, siblings, list(range(near, n_col)), nodes, resident)
    mine, siblings, cut, far_outs = lax.optimization_barrier((mine, siblings, cut, far_outs))
    own, *near_outs = backward(dense, mine, siblings, list(range(near)), nodes, resident)
    outs = near_outs + list(far_outs)
    back = {m: swap(outs[m - 1], "col", m) for m in far_first(n_col)}
    back = tuple(back[m] for m in range(1, n_col))

    cuts = chip_parts(cut, bias_rows, n_row)
    arrivals = [swap(cuts[j], "row", 2 * j) for j in range(1, chips)]
    piece, grad_bias = share_total(cuts[0], arrivals)
    shares = join([piece] + [swap(piece, "row", 2 * j) for j in range(1, chips)])
    shares, back = lax.optimization_barrier((shares, back))
    grad_self, grad_neigh = weight_grads(shares, swap(shares, "row", 1), n_row)
    grad_x = finish(d_pre, w_self, own, back)
    return (hidden, grad_x, grad_self, grad_neigh, grad_bias.reshape(width))


def solution(mesh):
    placed = (
        P(("col", "row"), None),
        P(("col", "row")),
        P(("col", "row"), None),
        P(("col", "row"), None, None),
        P(("col", "row")),
        P(("col", "row")),
        P(),
        P(),
        P(),
    )
    return jax.shard_map(
        body,
        mesh=mesh,
        in_specs=placed,
        out_specs=(P(("col", "row"), None), P(("col", "row"), None), P(), P(), P()),
        check_vma=False,
    )
```

time: 123 us -> 105 us (0.85); the launches traced: 123 us -> 103 us
  starting transfers between devices: 46 us -> 35.5 us
  Pallas kernels: 32.7 us -> 26.8 us
  local copies, waits for them, and re-layouts: 2.47 us -> 0.04 us
    ppermute x44 -> x29, starting transfers between devices: 46 us -> 35.5 us  [swap(): return lax.ppermute(x, axis, [(i, i ^ mask) for i in range(size)])]
    pallas_call x4, Pallas kernels: 11.6 us -> 5.89 us  [forward(): pl.pallas_call(kernel, out_shape=sds((count, nodes, wide), dtype), grid=(...]
    slice x3 -> x0, local copies, waits for them, and re-layouts: 1.49 us -> none  [the longest x1 0.92 us: body(): own = features[:, 0:wide] if h == 0 else cuts[h - 1]]
    ppermute x44 -> x29, waiting for transfers between devices: 40.2 us -> 39.3 us  [swap(): return lax.ppermute(x, axis, [(i, i ^ mask) for i in range(size)])]
    pallas_call x9 -> x12, Pallas kernels: 19.3 us -> 19.1 us  [the longest x1 11.5 us: densify(): pl.pallas_call(kernel, out_shape=pltpu.VMEM(((rows + 1) * tile, cols * ti...]
  transfers between devices with their start and end apart: 44 -> 29, of which waited for: 16 -> 13; matrix products, arithmetic and copies ran while one was open for 1% -> 1% of each run, Pallas kernels for 25% -> 22%
where the time goes in v3:
time: 105 us; the launch traced here: 103 us
  waiting for transfers between devices  39.3 us (37%)
  starting transfers between devices  35.5 us (34%)
  Pallas kernels  26.8 us (26%)
    ppermute x29, waiting for transfers between devices, swap(): return lax.ppermute(x, axis, [(i, i ^ mask) for i in range(size)])  39.3 us
    ppermute x29, starting transfers between devices, swap(): return lax.ppermute(x, axis, [(i, i ^ mask) for i in range(size)])  35.5 us
    pallas_call x1, Pallas kernels, densify(): pl.pallas_call(kernel, out_shape=pltpu.VMEM(((rows + 1) * tile, cols * ti...  11.5 us
    pallas_call x4, Pallas kernels, forward(): pl.pallas_call(kernel, out_shape=sds((count, nodes, wide), dtype), grid=(...  5.89 us
    pallas_call x2, Pallas kernels, backward(): pl.pallas_call(kernel, out_shape=outs, grid=(count,), in_specs=[spec] + [...  5.03 us
  transfers between devices with their start and end apart: 29, of which 13 were waited for; matrix products, arithmetic and copies ran while one was open for 1% of the time, Pallas kernels for 22%

profile of v3, /device:TPU:0, one launch (start us, length us, event | category | flops | bytes accessed | tf_op | source)
XLA Modules:
  0.0 103.3 jit_solution(15527757959284287735)
XLA Ops:
  0.6 5.1 %collective-permute-start.2 = (bf16[512,256]{1,0:T(8,128)(2,1)}, bf16[512,256]{1,0:T(8,128)(2,1)S(1)}, u32[]{:S(2)}, u32[]{:S(2)}) collective-permute-start(bf16[512,256]{1,0:T(8,128)(2,1)} %feat_ref.1), channel_id=1, source_target_pairs={{0,3},{1,2},{2,1},{3,0},{4,7},{5,6},{6,5},{7,4},{8,11},{9,10},{10,... | collective-permute-start | bytes 786440 | tf_op jit(solution)/shard_map/ppermute | solution.py:511
  5.7 0.0 collective-permute-start.1
  5.7 0.6 collective-permute-start
  6.4 0.7 fusion.6
  7.1 0.0 copy-start
  7.1 11.5 %densify.1.refs_0_.dense_ref = bf16[4224,2048]{1,0:T(8,128)(2,1)S(1)} custom-call(s32[384]{0:T(512)S(1)} %get-tuple-element.93.down_ref, s32[384]{0:T(512)S(1)} %get-tuple-element.94.right_ref, bf16[384,128,128]{2,1,0:T(8,128)(2,1)} %values_ref.1), custom_call_target="tpu_custom_call" | custom-call | bytes 37000000 | tf_op jit(solution)/shard_map/densify/pallas_call | solution.py:139
  18.7 0.0 collective-permute-done.2.refs_4_
  18.7 9.6 %collective-permute-done.1.refs_3_ = bf16[512,256]{1,0:T(8,128)(2,1)S(1)} collective-permute-done((bf16[512,256]{1,0:T(8,128)(2,1)}, bf16[512,256]{1,0:T(8,128)(2,1)S(1)}, u32[]{:S(2)}, u32[]{:S(2)}) %collective-permute-start.1) | collective-permute-done | bytes 262176 | tf_op jit(solution)/shard_map/ppermute | solution.py:511
  28.3 2.2 %forward.7 = bf16[3,512,256]{2,1,0:T(8,128)(2,1)S(1)} custom-call(bf16[4224,2048]{1,0:T(8,128)(2,1)S(1)} %densify.1.refs_0_.dense_ref, bf16[512,256]{1,0:T(8,128)(2,1)S(1)} %copy-done, bf16[512,256]{1,0:T(8,128)(2,1)S(1)} %collective-permute-done.refs_2_, bf16[512,256]{1,0:T(8,128)(2,1)S(1)} %collective-permute-done.1.refs_3_, ...), custom_call_target="tpu_custom_call" | custom-call | bytes 37000 | tf_op jit(solution)/shard_map/forward/pallas_call | solution.py:180
  30.5 0.1 collective-permute-start.4
  30.6 0.7 forward.5
  31.3 0.6 collective-permute-start.3
  31.9 2.2 %forward.6.keep_ref = f32[3,512,256]{2,1,0:T(8,128)S(1)} custom-call(bf16[4224,2048]{1,0:T(8,128)(2,1)S(1)} %densify.1.refs_0_.dense_ref, bf16[512,256]{1,0:T(8,128)(2,1)S(1)} %copy-done, bf16[512,256]{1,0:T(8,128)(2,1)S(1)} %collective-permute-done.refs_2_, bf16[512,256]{1,0:T(8,128)(2,1)S(1)} %collective-permute-done.1.refs_3_, ...), custom_call_target="tpu_custom_call" | custom-call | bytes 37000 | tf_op jit(solution)/shard_map/forward/pallas_call | solution.py:180
  34.1 0.0 copy-start.1
  34.1 0.0 copy-start.2
  34.1 0.0 copy-start.3
  34.2 0.0 copy-start.4
  34.2 0.0 copy-start.5
  34.2 0.0 collective-permute-done.4.got_ref
  34.2 0.1 add_parts.1
  34.3 1.6 %collective-permute-start.5 = (bf16[512,256]{1,0:T(8,128)(2,1)S(1)}, bf16[512,256]{1,0:T(8,128)(2,1)S(1)}, u32[]{:S(2)}, u32[]{:S(2)}) collective-permute-start(bf16[512,256]{1,0:T(8,128)(2,1)S(1)} %get-tuple-element.49), channel_id=1, source_target_pairs={{0,8},{4,12},{8,0},{12,4},{16,24},{20,28},{24,16},{28,20},{1,9},{5... | collective-permute-start | bytes 786440 | tf_op jit(solution)/shard_map/ppermute | solution.py:511
  35.9 1.5 %collective-permute-start.6 = (bf16[512,256]{1,0:T(8,128)(2,1)S(1)}, bf16[512,256]{1,0:T(8,128)(2,1)S(1)}, u32[]{:S(2)}, u32[]{:S(2)}) collective-permute-start(bf16[512,256]{1,0:T(8,128)(2,1)S(1)} %get-tuple-element.50), channel_id=1, source_target_pairs={{0,16},{4,20},{8,24},{12,28},{16,0},{20,4},{24,8},{28,12},{1,17},{... | collective-permute-start | bytes 786440 | tf_op jit(solution)/shard_map/ppermute | solution.py:511
  37.4 0.5 collective-permute-start.7
  37.9 0.7 forward.4.refs_6_
  38.6 5.0 %collective-permute-done.5.refs_8_ = bf16[512,256]{1,0:T(8,128)(2,1)S(1)} collective-permute-done((bf16[512,256]{1,0:T(8,128)(2,1)S(1)}, bf16[512,256]{1,0:T(8,128)(2,1)S(1)}, u32[]{:S(2)}, u32[]{:S(2)}) %collective-permute-start.5) | collective-permute-done | bytes 262176 | tf_op jit(solution)/shard_map/ppermute | solution.py:511
  43.6 5.9 %collective-permute-done.6.refs_9_ = bf16[512,256]{1,0:T(8,128)(2,1)S(1)} collective-permute-done((bf16[512,256]{1,0:T(8,128)(2,1)S(1)}, bf16[512,256]{1,0:T(8,128)(2,1)S(1)}, u32[]{:S(2)}, u32[]{:S(2)}) %collective-permute-start.6) | collective-permute-done | bytes 262176 | tf_op jit(solution)/shard_map/ppermute | solution.py:511
  49.5 1.2 %middle.1 = (bf16[512,256]{1,0:T(8,128)(2,1)}, bf16[512,256]{1,0:T(8,128)(2,1)S(1)}, bf16[512,256]{1,0:T(8,128)(2,1)S(1)}, bf16[256,512]{1,0:T(8,128)(2,1)S(1)}) custom-call(bf16[512,256]{1,0:T(8,128)(2,1)S(1)} %copy-done, s32[1,512]{1,0:T(1,128)S(1)} %bitcast.3, bf16[512,256]{1,0:T(8,128)(2,1)S(1)} %copy-done.2, bf16[256,256]{1,0:T(8,128)(2,1)S(1)} %copy-done.1, ...), custom_call_target="tpu_custom_call" | custom-call | bytes 5550000 | tf_op jit(solution)/shard_map/middle/pallas_call | solution.py:237
  50.7 1.5 %collective-permute-start.10 = (bf16[256,512]{1,0:T(8,128)(2,1)S(1)}, bf16[256,512]{1,0:T(8,128)(2,1)S(1)}, u32[]{:S(2)}, u32[]{:S(2)}) collective-permute-start(bf16[256,512]{1,0:T(8,128)(2,1)S(1)} %get-tuple-element.63.refs_0_), channel_id=1, source_target_pairs={{0,24},{4,28},{8,16},{12,20},{16,8},{20,12},{24,0},{28,4},{1,25},{... | collective-permute-start | bytes 786440 | tf_op jit(solution)/shard_map/ppermute | solution.py:511
  52.2 1.2 %collective-permute-start.9 = (bf16[256,512]{1,0:T(8,128)(2,1)S(1)}, bf16[256,512]{1,0:T(8,128)(2,1)S(1)}, u32[]{:S(2)}, u32[]{:S(2)}) collective-permute-start(bf16[256,512]{1,0:T(8,128)(2,1)S(1)} %get-tuple-element.63.refs_0_), channel_id=1, source_target_pairs={{0,16},{4,20},{8,24},{12,28},{16,0},{20,4},{24,8},{28,12},{1,17},{... | collective-permute-start | bytes 786440 | tf_op jit(solution)/shard_map/ppermute | solution.py:511
  53.4 0.8 collective-permute-start.8
  54.2 0.4 local_grads.1
  54.6 0.1 collective-permute-start.11
  54.7 1.4 %collective-permute-done.11.got_ref = bf16[144,512]{1,0:T(8,128)(2,1)S(1)} collective-permute-done((bf16[144,512]{1,0:T(8,128)(2,1)S(1)}, bf16[144,512]{1,0:T(8,128)(2,1)S(1)}, u32[]{:S(2)}, u32[]{:S(2)}) %collective-permute-start.11) | collective-permute-done | bytes 147488 | tf_op jit(solution)/shard_map/ppermute | solution.py:511
  56.0 0.1 column_parts.1
  56.1 0.1 collective-permute-start.12
  56.2 3.0 %collective-permute-start.13 = (bf16[48,512]{1,0:T(8,128)(2,1)S(1)}, bf16[48,512]{1,0:T(8,128)(2,1)S(1)}, u32[]{:S(2)}, u32[]{:S(2)}) collective-permute-start(bf16[48,512]{1,0:T(8,128)(2,1)S(1)} %get-tuple-element.60), channel_id=1, source_target_pairs={{0,2},{1,3},{2,0},{3,1},{4,6},{5,7},{6,4},{7,5},{8,10},{9,11},{10,... | collective-permute-start | bytes 147464 | tf_op jit(solution)/shard_map/ppermute | solution.py:511
  59.2 1.9 %collective-permute-done.12.refs_0_ = bf16[48,512]{1,0:T(8,128)(2,1)S(1)} collective-permute-done((bf16[48,512]{1,0:T(8,128)(2,1)S(1)}, bf16[48,512]{1,0:T(8,128)(2,1)S(1)}, u32[]{:S(2)}, u32[]{:S(2)}) %collective-permute-start.12) | collective-permute-done | bytes 49184 | tf_op jit(solution)/shard_map/ppermute | solution.py:511
  61.1 2.6 %collective-permute-start.14 = (bf16[48,512]{1,0:T(8,128)(2,1)S(1)}, bf16[48,512]{1,0:T(8,128)(2,1)S(1)}, u32[]{:S(2)}, u32[]{:S(2)}) collective-permute-start(bf16[48,512]{1,0:T(8,128)(2,1)S(1)} %get-tuple-element.61), channel_id=1, source_target_pairs={{0,3},{1,2},{2,1},{3,0},{4,7},{5,6},{6,5},{7,4},{8,11},{9,10},{10,... | collective-permute-start | bytes 147464 | tf_op jit(solution)/shard_map/ppermute | solution.py:511
  63.6 3.3 %collective-permute-done.14.refs_2_ = bf16[48,512]{1,0:T(8,128)(2,1)S(1)} collective-permute-done((bf16[48,512]{1,0:T(8,128)(2,1)S(1)}, bf16[48,512]{1,0:T(8,128)(2,1)S(1)}, u32[]{:S(2)}, u32[]{:S(2)}) %collective-permute-start.14) | collective-permute-done | bytes 49184 | tf_op jit(solution)/shard_map/ppermute | solution.py:511
  67.0 0.1 side_by_side.1.mine_ref
  67.1 0.1 collective-permute-start.15
  67.2 2.6 %collective-permute-start.18 = (bf16[32,512]{1,0:T(8,128)(2,1)S(1)}, bf16[32,512]{1,0:T(8,128)(2,1)S(1)}, u32[]{:S(2)}, u32[]{:S(2)}) collective-permute-start(bf16[32,512]{1,0:T(8,128)(2,1)S(1)} %get-tuple-element.73.refs_0_), channel_id=1, source_target_pairs={{0,3},{1,2},{2,1},{3,0},{4,7},{5,6},{6,5},{7,4},{8,11},{9,10},{10,... | collective-permute-start | bytes 98312 | tf_op jit(solution)/shard_map/ppermute | solution.py:511
  69.8 1.8 %collective-permute-start.16 = (bf16[32,512]{1,0:T(8,128)(2,1)S(1)}, bf16[32,512]{1,0:T(8,128)(2,1)S(1)}, u32[]{:S(2)}, u32[]{:S(2)}) collective-permute-start(bf16[32,512]{1,0:T(8,128)(2,1)S(1)} %get-tuple-element.73.refs_0_), channel_id=1, source_target_pairs={{0,1},{1,0},{2,3},{3,2},{4,5},{5,4},{6,7},{7,6},{8,9},{9,8},{10,11... | collective-permute-start | bytes 98312 | tf_op jit(solution)/shard_map/ppermute | solution.py:511
  71.6 2.5 %backward.2 = (bf16[256,512]{1,0:T(8,128)(2,1)S(1)}, bf16[256,512]{1,0:T(8,128)(2,1)S(1)}) custom-call(bf16[4224,2048]{1,0:T(8,128)(2,1)S(1)} %densify.1.refs_0_.dense_ref, bf16[256,2048]{1,0:T(8,128)(2,1)S(1)} %side_by_side.1.mine_ref, bf16[256,2048]{1,0:T(8,128)(2,1)S(1)} %collective-permute-done.15.siblings_ref), custom_call_target="tpu_custom_call" | custom-call | bytes 9250000 | tf_op jit(solution)/shard_map/backward/pallas_call | solution.py:405
  74.2 0.5 collective-permute-done.17.refs_2_
  74.7 1.3 %collective-permute-start.19 = (f32[48,512]{1,0:T(8,128)S(1)}, f32[48,512]{1,0:T(8,128)S(1)}, u32[]{:S(2)}, u32[]{:S(2)}) collective-permute-start(f32[48,512]{1,0:T(8,128)S(1)} %get-tuple-element.79), channel_id=1, source_target_pairs={{0,8},{4,12},{8,0},{12,4},{16,24},{20,28},{24,16},{28,20},{1,9},{5... | collective-permute-start | bytes 294920 | tf_op jit(solution)/shard_map/ppermute | solution.py:511
  76.0 2.5 %backward.3 = (f32[256,512]{1,0:T(8,128)S(1)}, bf16[256,512]{1,0:T(8,128)(2,1)S(1)}) custom-call(bf16[4224,2048]{1,0:T(8,128)(2,1)S(1)} %densify.1.refs_0_.dense_ref, bf16[256,2048]{1,0:T(8,128)(2,1)S(1)} %side_by_side.1.mine_ref, bf16[256,2048]{1,0:T(8,128)(2,1)S(1)} %collective-permute-done.15.siblings_ref), custom_call_target="tpu_custom_call" | custom-call | bytes 9250000 | tf_op jit(solution)/shard_map/backward/pallas_call | solution.py:405
  78.5 1.0 %collective-permute-start.25 = (bf16[256,512]{1,0:T(8,128)(2,1)S(1)}, bf16[256,512]{1,0:T(8,128)(2,1)S(1)}, u32[]{:S(2)}, u32[]{:S(2)}) collective-permute-start(bf16[256,512]{1,0:T(8,128)(2,1)S(1)} %get-tuple-element.83), channel_id=1, source_target_pairs={{0,1},{1,0},{2,3},{3,2},{4,5},{5,4},{6,7},{7,6},{8,9},{9,8},{10,11... | collective-permute-start | bytes 786440 | tf_op jit(solution)/shard_map/ppermute | solution.py:511
  79.5 1.7 %collective-permute-start.26 = (bf16[256,512]{1,0:T(8,128)(2,1)S(1)}, bf16[256,512]{1,0:T(8,128)(2,1)S(1)}, u32[]{:S(2)}, u32[]{:S(2)}) collective-permute-start(bf16[256,512]{1,0:T(8,128)(2,1)S(1)} %get-tuple-element.84), channel_id=1, source_target_pairs={{0,2},{1,3},{2,0},{3,1},{4,6},{5,7},{6,4},{7,5},{8,10},{9,11},{10,... | collective-permute-start | bytes 786440 | tf_op jit(solution)/shard_map/ppermute | solution.py:511
  81.3 1.7 %collective-permute-start.27 = (bf16[256,512]{1,0:T(8,128)(2,1)S(1)}, bf16[256,512]{1,0:T(8,128)(2,1)S(1)}, u32[]{:S(2)}, u32[]{:S(2)}) collective-permute-start(bf16[256,512]{1,0:T(8,128)(2,1)S(1)} %get-tuple-element.85), channel_id=1, source_target_pairs={{0,3},{1,2},{2,1},{3,0},{4,7},{5,6},{6,5},{7,4},{8,11},{9,10},{10,... | collective-permute-start | bytes 786440 | tf_op jit(solution)/shard_map/ppermute | solution.py:511
  83.0 0.8 collective-permute-start.20
  83.8 1.4 %collective-permute-start.21 = (f32[48,512]{1,0:T(8,128)S(1)}, f32[48,512]{1,0:T(8,128)S(1)}, u32[]{:S(2)}, u32[]{:S(2)}) collective-permute-start(f32[48,512]{1,0:T(8,128)S(1)} %get-tuple-element.81), channel_id=1, source_target_pairs={{0,24},{4,28},{8,16},{12,20},{16,8},{20,12},{24,0},{28,4},{1,25},{... | collective-permute-start | bytes 294920 | tf_op jit(solution)/shard_map/ppermute | solution.py:511
  85.2 2.3 %collective-permute-done.20.refs_1_ = f32[48,512]{1,0:T(8,128)S(1)} collective-permute-done((f32[48,512]{1,0:T(8,128)S(1)}, f32[48,512]{1,0:T(8,128)S(1)}, u32[]{:S(2)}, u32[]{:S(2)}) %collective-permute-start.20) | collective-permute-done | bytes 98336 | tf_op jit(solution)/shard_map/ppermute | solution.py:511
  87.6 1.7 %collective-permute-done.21.refs_2_ = f32[48,512]{1,0:T(8,128)S(1)} collective-permute-done((f32[48,512]{1,0:T(8,128)S(1)}, f32[48,512]{1,0:T(8,128)S(1)}, u32[]{:S(2)}, u32[]{:S(2)}) %collective-permute-start.21) | collective-permute-done | bytes 98336 | tf_op jit(solution)/shard_map/ppermute | solution.py:511
  89.3 0.6 share_total.1
  89.9 1.4 %collective-permute-start.24 = (f32[32,512]{1,0:T(8,128)S(1)}, f32[32,512]{1,0:T(8,128)S(1)}, u32[]{:S(2)}, u32[]{:S(2)}) collective-permute-start(f32[32,512]{1,0:T(8,128)S(1)} %get-tuple-element.82.refs_0_), channel_id=1, source_target_pairs={{0,24},{4,28},{8,16},{12,20},{16,8},{20,12},{24,0},{28,4},{1,25},{... | collective-permute-start | bytes 196616 | tf_op jit(solution)/shard_map/ppermute | solution.py:511
  91.3 1.5 %collective-permute-start.23 = (f32[32,512]{1,0:T(8,128)S(1)}, f32[32,512]{1,0:T(8,128)S(1)}, u32[]{:S(2)}, u32[]{:S(2)}) collective-permute-start(f32[32,512]{1,0:T(8,128)S(1)} %get-tuple-element.82.refs_0_), channel_id=1, source_target_pairs={{0,16},{4,20},{8,24},{12,28},{16,0},{20,4},{24,8},{28,12},{1,17},{... | collective-permute-start | bytes 196616 | tf_op jit(solution)/shard_map/ppermute | solution.py:511
  92.8 2.9 %collective-permute-done.24.refs_3_ = f32[32,512]{1,0:T(8,128)S(1)} collective-permute-done((f32[32,512]{1,0:T(8,128)S(1)}, f32[32,512]{1,0:T(8,128)S(1)}, u32[]{:S(2)}, u32[]{:S(2)}) %collective-permute-start.24) | collective-permute-done | bytes 65568 | tf_op jit(solution)/shard_map/ppermute | solution.py:511
  95.7 0.9 collective-permute-start.22
  96.6 3.4 %collective-permute-done.22.refs_1_ = f32[32,512]{1,0:T(8,128)S(1)} collective-permute-done((f32[32,512]{1,0:T(8,128)S(1)}, f32[32,512]{1,0:T(8,128)S(1)}, u32[]{:S(2)}, u32[]{:S(2)}) %collective-permute-start.22) | collective-permute-done | bytes 65568 | tf_op jit(solution)/shard_map/ppermute | solution.py:511
  100.0 0.9 collective-permute-done.26.refs_1_
  100.9 1.0 finish.1
  101.9 0.6 collective-permute-done.28.siblings_ref
  102.5 0.8 weight_grads.1
  (25 shorter events, 0.1 us)
Async XLA Ops:
  0.6 18.0 %collective-permute-start.2 = (bf16[512,256]{1,0:T(8,128)(2,1)}, bf16[512,256]{1,0:T(8,128)(2,1)S(1)}, u32[]{:S(2)}, u32[]{:S(2)}) collective-permute-start(bf16[512,256]{1,0:T(8,128)(2,1)} %feat_ref.1), channel_id=1, source_target_pairs={{0,3},{1,2},{2,1},{3,0},{4,7},{5,6},{6,5},{7,4},{8,11},{9,10},{10,... | collective-permute-start | bytes 786440 | tf_op jit(solution)/shard_map/ppermute | solution.py:511
  5.7 22.5 %collective-permute-start.1 = (bf16[512,256]{1,0:T(8,128)(2,1)}, bf16[512,256]{1,0:T(8,128)(2,1)S(1)}, u32[]{:S(2)}, u32[]{:S(2)}) collective-permute-start(bf16[512,256]{1,0:T(8,128)(2,1)} %feat_ref.1), channel_id=1, source_target_pairs={{0,2},{1,3},{2,0},{3,1},{4,6},{5,7},{6,4},{7,5},{8,10},{9,11},{10,... | collective-permute-start | bytes 786440 | tf_op jit(solution)/shard_map/ppermute | solution.py:511
  5.7 22.5 %collective-permute-start = (bf16[512,256]{1,0:T(8,128)(2,1)}, bf16[512,256]{1,0:T(8,128)(2,1)S(1)}, u32[]{:S(2)}, u32[]{:S(2)}) collective-permute-start(bf16[512,256]{1,0:T(8,128)(2,1)} %feat_ref.1), channel_id=1, source_target_pairs={{0,1},{1,0},{2,3},{3,2},{4,5},{5,4},{6,7},{7,6},{8,9},{9,8},{10,11... | collective-permute-start | bytes 786440 | tf_op jit(solution)/shard_map/ppermute | solution.py:511
  7.1 21.2 %copy-start = (bf16[512,256]{1,0:T(8,128)(2,1)S(1)}, bf16[512,256]{1,0:T(8,128)(2,1)}, u32[]{:S(2)}) copy-start(bf16[512,256]{1,0:T(8,128)(2,1)} %feat_ref.1) | copy-start | bytes 786436
  30.5 3.7 %collective-permute-start.4 = (bf16[3,512,256]{2,1,0:T(8,128)(2,1)S(1)}, bf16[3,512,256]{2,1,0:T(8,128)(2,1)S(1)}, u32[]{:S(2)}, u32[]{:S(2)}) collective-permute-start(bf16[3,512,256]{2,1,0:T(8,128)(2,1)S(1)} %forward.7), channel_id=1, source_target_pairs={{0,4},{4,0},{8,12},{12,8},{16,20},{20,16},{24,28},{28,24},{1,5},{5... | collective-permute-start | bytes 2359304 | tf_op jit(solution)/shard_map/ppermute | solution.py:511
  31.3 7.3 %collective-permute-start.3 = (bf16[1,512,256]{2,1,0:T(8,128)(2,1)S(1)}, bf16[1,512,256]{2,1,0:T(8,128)(2,1)S(1)}, u32[]{:S(2)}, u32[]{:S(2)}) collective-permute-start(bf16[1,512,256]{2,1,0:T(8,128)(2,1)S(1)} %forward.5), channel_id=1, source_target_pairs={{0,4},{4,0},{8,12},{12,8},{16,20},{20,16},{24,28},{28,24},{1,5},{5... | collective-permute-start | bytes 786440 | tf_op jit(solution)/shard_map/ppermute | solution.py:511
  34.1 15.4 %copy-start.1 = (bf16[256,256]{1,0:T(8,128)(2,1)S(1)}, bf16[256,256]{1,0:T(8,128)(2,1)}, u32[]{:S(2)}) copy-start(bf16[256,256]{1,0:T(8,128)(2,1)} %ws_ref.1) | copy-start | bytes 393220
  34.1 15.3 %copy-start.2 = (bf16[512,256]{1,0:T(8,128)(2,1)S(1)}, bf16[512,256]{1,0:T(8,128)(2,1)}, u32[]{:S(2)}) copy-start(bf16[512,256]{1,0:T(8,128)(2,1)} %refs_2_.1) | copy-start | bytes 786436
  34.1 15.3 %copy-start.3 = (bf16[256,256]{1,0:T(8,128)(2,1)S(1)}, bf16[256,256]{1,0:T(8,128)(2,1)}, u32[]{:S(2)}) copy-start(bf16[256,256]{1,0:T(8,128)(2,1)} %refs_4_.1) | copy-start | bytes 393220
  34.2 15.3 %copy-start.4 = (s32[512]{0:T(512)S(1)}, s32[512]{0:T(512)}, u32[]{:S(2)}) copy-start(s32[512]{0:T(512)} %param.10) | copy-start | bytes 6148
  34.2 15.3 %copy-start.5 = (f32[256]{0:T(256)S(1)}, f32[256]{0:T(256)}, u32[]{:S(2)}) copy-start(f32[256]{0:T(256)} %param.17) | copy-start | bytes 3076
  34.3 9.2 %collective-permute-start.5 = (bf16[512,256]{1,0:T(8,128)(2,1)S(1)}, bf16[512,256]{1,0:T(8,128)(2,1)S(1)}, u32[]{:S(2)}, u32[]{:S(2)}) collective-permute-start(bf16[512,256]{1,0:T(8,128)(2,1)S(1)} %get-tuple-element.49), channel_id=1, source_target_pairs={{0,8},{4,12},{8,0},{12,4},{16,24},{20,28},{24,16},{28,20},{1,9},{5... | collective-permute-start | bytes 786440 | tf_op jit(solution)/shard_map/ppermute | solution.py:511
  35.9 13.6 %collective-permute-start.6 = (bf16[512,256]{1,0:T(8,128)(2,1)S(1)}, bf16[512,256]{1,0:T(8,128)(2,1)S(1)}, u32[]{:S(2)}, u32[]{:S(2)}) collective-permute-start(bf16[512,256]{1,0:T(8,128)(2,1)S(1)} %get-tuple-element.50), channel_id=1, source_target_pairs={{0,16},{4,20},{8,24},{12,28},{16,0},{20,4},{24,8},{28,12},{1,17},{... | collective-permute-start | bytes 786440 | tf_op jit(solution)/shard_map/ppermute | solution.py:511
  37.4 12.1 %collective-permute-start.7 = (bf16[512,256]{1,0:T(8,128)(2,1)S(1)}, bf16[512,256]{1,0:T(8,128)(2,1)S(1)}, u32[]{:S(2)}, u32[]{:S(2)}) collective-permute-start(bf16[512,256]{1,0:T(8,128)(2,1)S(1)} %get-tuple-element.51), channel_id=1, source_target_pairs={{0,24},{4,28},{8,16},{12,20},{16,8},{20,12},{24,0},{28,4},{1,25},{... | collective-permute-start | bytes 786440 | tf_op jit(solution)/shard_map/ppermute | solution.py:511
  50.7 16.3 %collective-permute-start.10 = (bf16[256,512]{1,0:T(8,128)(2,1)S(1)}, bf16[256,512]{1,0:T(8,128)(2,1)S(1)}, u32[]{:S(2)}, u32[]{:S(2)}) collective-permute-start(bf16[256,512]{1,0:T(8,128)(2,1)S(1)} %get-tuple-element.63.refs_0_), channel_id=1, source_target_pairs={{0,24},{4,28},{8,16},{12,20},{16,8},{20,12},{24,0},{28,4},{1,25},{... | collective-permute-start | bytes 786440 | tf_op jit(solution)/shard_map/ppermute | solution.py:511
  52.2 14.8 %collective-permute-start.9 = (bf16[256,512]{1,0:T(8,128)(2,1)S(1)}, bf16[256,512]{1,0:T(8,128)(2,1)S(1)}, u32[]{:S(2)}, u32[]{:S(2)}) collective-permute-start(bf16[256,512]{1,0:T(8,128)(2,1)S(1)} %get-tuple-element.63.refs_0_), channel_id=1, source_target_pairs={{0,16},{4,20},{8,24},{12,28},{16,0},{20,4},{24,8},{28,12},{1,17},{... | collective-permute-start | bytes 786440 | tf_op jit(solution)/shard_map/ppermute | solution.py:511
  53.4 13.6 %collective-permute-start.8 = (bf16[256,512]{1,0:T(8,128)(2,1)S(1)}, bf16[256,512]{1,0:T(8,128)(2,1)S(1)}, u32[]{:S(2)}, u32[]{:S(2)}) collective-permute-start(bf16[256,512]{1,0:T(8,128)(2,1)S(1)} %get-tuple-element.63.refs_0_), channel_id=1, source_target_pairs={{0,8},{4,12},{8,0},{12,4},{16,24},{20,28},{24,16},{28,20},{1,9},{5... | collective-permute-start | bytes 786440 | tf_op jit(solution)/shard_map/ppermute | solution.py:511
  54.6 1.4 %collective-permute-start.11 = (bf16[144,512]{1,0:T(8,128)(2,1)S(1)}, bf16[144,512]{1,0:T(8,128)(2,1)S(1)}, u32[]{:S(2)}, u32[]{:S(2)}) collective-permute-start(bf16[144,512]{1,0:T(8,128)(2,1)S(1)} %get-tuple-element.57), channel_id=1, source_target_pairs={{0,4},{4,0},{8,12},{12,8},{16,20},{20,16},{24,28},{28,24},{1,5},{5... | collective-permute-start | bytes 442376 | tf_op jit(solution)/shard_map/ppermute | solution.py:511
  56.1 5.0 %collective-permute-start.12 = (bf16[48,512]{1,0:T(8,128)(2,1)S(1)}, bf16[48,512]{1,0:T(8,128)(2,1)S(1)}, u32[]{:S(2)}, u32[]{:S(2)}) collective-permute-start(bf16[48,512]{1,0:T(8,128)(2,1)S(1)} %get-tuple-element.59), channel_id=1, source_target_pairs={{0,1},{1,0},{2,3},{3,2},{4,5},{5,4},{6,7},{7,6},{8,9},{9,8},{10,11... | collective-permute-start | bytes 147464 | tf_op jit(solution)/shard_map/ppermute | solution.py:511
  56.2 7.5 %collective-permute-start.13 = (bf16[48,512]{1,0:T(8,128)(2,1)S(1)}, bf16[48,512]{1,0:T(8,128)(2,1)S(1)}, u32[]{:S(2)}, u32[]{:S(2)}) collective-permute-start(bf16[48,512]{1,0:T(8,128)(2,1)S(1)} %get-tuple-element.60), channel_id=1, source_target_pairs={{0,2},{1,3},{2,0},{3,1},{4,6},{5,7},{6,4},{7,5},{8,10},{9,11},{10,... | collective-permute-start | bytes 147464 | tf_op jit(solution)/shard_map/ppermute | solution.py:511
  61.1 5.9 %collective-permute-start.14 = (bf16[48,512]{1,0:T(8,128)(2,1)S(1)}, bf16[48,512]{1,0:T(8,128)(2,1)S(1)}, u32[]{:S(2)}, u32[]{:S(2)}) collective-permute-start(bf16[48,512]{1,0:T(8,128)(2,1)S(1)} %get-tuple-element.61), channel_id=1, source_target_pairs={{0,3},{1,2},{2,1},{3,0},{4,7},{5,6},{6,5},{7,4},{8,11},{9,10},{10,... | collective-permute-start | bytes 147464 | tf_op jit(solution)/shard_map/ppermute | solution.py:511
  67.1 4.5 %collective-permute-start.15 = (bf16[256,2048]{1,0:T(8,128)(2,1)S(1)}, bf16[256,2048]{1,0:T(8,128)(2,1)S(1)}, u32[]{:S(2)}, u32[]{:S(2)}) collective-permute-start(bf16[256,2048]{1,0:T(8,128)(2,1)S(1)} %side_by_side.1.mine_ref), channel_id=1, source_target_pairs={{0,4},{4,0},{8,12},{12,8},{16,20},{20,16},{24,28},{28,24},{1,5},{5... | collective-permute-start | bytes 3145736 | tf_op jit(solution)/shard_map/ppermute | solution.py:511
  67.2 7.0 %collective-permute-start.18 = (bf16[32,512]{1,0:T(8,128)(2,1)S(1)}, bf16[32,512]{1,0:T(8,128)(2,1)S(1)}, u32[]{:S(2)}, u32[]{:S(2)}) collective-permute-start(bf16[32,512]{1,0:T(8,128)(2,1)S(1)} %get-tuple-element.73.refs_0_), channel_id=1, source_target_pairs={{0,3},{1,2},{2,1},{3,0},{4,7},{5,6},{6,5},{7,4},{8,11},{9,10},{10,... | collective-permute-start | bytes 98312 | tf_op jit(solution)/shard_map/ppermute | solution.py:511
  69.8 4.8 %collective-permute-start.17 = (bf16[32,512]{1,0:T(8,128)(2,1)S(1)}, bf16[32,512]{1,0:T(8,128)(2,1)S(1)}, u32[]{:S(2)}, u32[]{:S(2)}) collective-permute-start(bf16[32,512]{1,0:T(8,128)(2,1)S(1)} %get-tuple-element.73.refs_0_), channel_id=1, source_target_pairs={{0,2},{1,3},{2,0},{3,1},{4,6},{5,7},{6,4},{7,5},{8,10},{9,11},{10,... | collective-permute-start | bytes 98312 | tf_op jit(solution)/shard_map/ppermute | solution.py:511
  69.8 4.8 %collective-permute-start.16 = (bf16[32,512]{1,0:T(8,128)(2,1)S(1)}, bf16[32,512]{1,0:T(8,128)(2,1)S(1)}, u32[]{:S(2)}, u32[]{:S(2)}) collective-permute-start(bf16[32,512]{1,0:T(8,128)(2,1)S(1)} %get-tuple-element.73.refs_0_), channel_id=1, source_target_pairs={{0,1},{1,0},{2,3},{3,2},{4,5},{5,4},{6,7},{7,6},{8,9},{9,8},{10,11... | collective-permute-start | bytes 98312 | tf_op jit(solution)/shard_map/ppermute | solution.py:511
  74.7 9.1 %collective-permute-start.19 = (f32[48,512]{1,0:T(8,128)S(1)}, f32[48,512]{1,0:T(8,128)S(1)}, u32[]{:S(2)}, u32[]{:S(2)}) collective-permute-start(f32[48,512]{1,0:T(8,128)S(1)} %get-tuple-element.79), channel_id=1, source_target_pairs={{0,8},{4,12},{8,0},{12,4},{16,24},{20,28},{24,16},{28,20},{1,9},{5... | collective-permute-start | bytes 294920 | tf_op jit(solution)/shard_map/ppermute | solution.py:511
  78.5 21.5 %collective-permute-start.25 = (bf16[256,512]{1,0:T(8,128)(2,1)S(1)}, bf16[256,512]{1,0:T(8,128)(2,1)S(1)}, u32[]{:S(2)}, u32[]{:S(2)}) collective-permute-start(bf16[256,512]{1,0:T(8,128)(2,1)S(1)} %get-tuple-element.83), channel_id=1, source_target_pairs={{0,1},{1,0},{2,3},{3,2},{4,5},{5,4},{6,7},{7,6},{8,9},{9,8},{10,11... | collective-permute-start | bytes 786440 | tf_op jit(solution)/shard_map/ppermute | solution.py:511
  79.5 21.4 %collective-permute-start.26 = (bf16[256,512]{1,0:T(8,128)(2,1)S(1)}, bf16[256,512]{1,0:T(8,128)(2,1)S(1)}, u32[]{:S(2)}, u32[]{:S(2)}) collective-permute-start(bf16[256,512]{1,0:T(8,128)(2,1)S(1)} %get-tuple-element.84), channel_id=1, source_target_pairs={{0,2},{1,3},{2,0},{3,1},{4,6},{5,7},{6,4},{7,5},{8,10},{9,11},{10,... | collective-permute-start | bytes 786440 | tf_op jit(solution)/shard_map/ppermute | solution.py:511
  81.3 19.7 %collective-permute-start.27 = (bf16[256,512]{1,0:T(8,128)(2,1)S(1)}, bf16[256,512]{1,0:T(8,128)(2,1)S(1)}, u32[]{:S(2)}, u32[]{:S(2)}) collective-permute-start(bf16[256,512]{1,0:T(8,128)(2,1)S(1)} %get-tuple-element.85), channel_id=1, source_target_pairs={{0,3},{1,2},{2,1},{3,0},{4,7},{5,6},{6,5},{7,4},{8,11},{9,10},{10,... | collective-permute-start | bytes 786440 | tf_op jit(solution)/shard_map/ppermute | solution.py:511
  83.0 4.6 %collective-permute-start.20 = (f32[48,512]{1,0:T(8,128)S(1)}, f32[48,512]{1,0:T(8,128)S(1)}, u32[]{:S(2)}, u32[]{:S(2)}) collective-permute-start(f32[48,512]{1,0:T(8,128)S(1)} %get-tuple-element.80), channel_id=1, source_target_pairs={{0,16},{4,20},{8,24},{12,28},{16,0},{20,4},{24,8},{28,12},{1,17},{... | collective-permute-start | bytes 294920 | tf_op jit(solution)/shard_map/ppermute | solution.py:511
  83.8 5.5 %collective-permute-start.21 = (f32[48,512]{1,0:T(8,128)S(1)}, f32[48,512]{1,0:T(8,128)S(1)}, u32[]{:S(2)}, u32[]{:S(2)}) collective-permute-start(f32[48,512]{1,0:T(8,128)S(1)} %get-tuple-element.81), channel_id=1, source_target_pairs={{0,24},{4,28},{8,16},{12,20},{16,8},{20,12},{24,0},{28,4},{1,25},{... | collective-permute-start | bytes 294920 | tf_op jit(solution)/shard_map/ppermute | solution.py:511
  89.9 5.8 %collective-permute-start.24 = (f32[32,512]{1,0:T(8,128)S(1)}, f32[32,512]{1,0:T(8,128)S(1)}, u32[]{:S(2)}, u32[]{:S(2)}) collective-permute-start(f32[32,512]{1,0:T(8,128)S(1)} %get-tuple-element.82.refs_0_), channel_id=1, source_target_pairs={{0,24},{4,28},{8,16},{12,20},{16,8},{20,12},{24,0},{28,4},{1,25},{... | collective-permute-start | bytes 196616 | tf_op jit(solution)/shard_map/ppermute | solution.py:511
  91.3 5.3 %collective-permute-start.23 = (f32[32,512]{1,0:T(8,128)S(1)}, f32[32,512]{1,0:T(8,128)S(1)}, u32[]{:S(2)}, u32[]{:S(2)}) collective-permute-start(f32[32,512]{1,0:T(8,128)S(1)} %get-tuple-element.82.refs_0_), channel_id=1, source_target_pairs={{0,16},{4,20},{8,24},{12,28},{16,0},{20,4},{24,8},{28,12},{1,17},{... | collective-permute-start | bytes 196616 | tf_op jit(solution)/shard_map/ppermute | solution.py:511
  95.7 4.3 %collective-permute-start.22 = (f32[32,512]{1,0:T(8,128)S(1)}, f32[32,512]{1,0:T(8,128)S(1)}, u32[]{:S(2)}, u32[]{:S(2)}) collective-permute-start(f32[32,512]{1,0:T(8,128)S(1)} %get-tuple-element.82.refs_0_), channel_id=1, source_target_pairs={{0,8},{4,12},{8,0},{12,4},{16,24},{20,28},{24,16},{28,20},{1,9},{5... | collective-permute-start | bytes 196616 | tf_op jit(solution)/shard_map/ppermute | solution.py:511
  100.9 1.5 %collective-permute-start.28 = (f32[128,512]{1,0:T(8,128)S(1)}, f32[128,512]{1,0:T(8,128)S(1)}, u32[]{:S(2)}, u32[]{:S(2)}) collective-permute-start(f32[128,512]{1,0:T(8,128)S(1)} %join.1.mine_ref), channel_id=1, source_target_pairs={{0,4},{4,0},{8,12},{12,8},{16,20},{20,16},{24,28},{28,24},{1,5},{5... | collective-permute-start | bytes 786440 | tf_op jit(solution)/shard_map/ppermute | solution.py:511

commit v4 on v3

--- a/solution.py
+++ b/solution.py
@@ -155,39 +155,61 @@
     return pltpu.with_memory_space_constraint(dense, pltpu.VMEM) if resident else dense
 
 
-def forward(dense, pieces, first, count, dtype, resident):
-    n_col = len(pieces)
-    nodes, wide = pieces[0].shape
-    cols = n_col * nodes
-
-    def kernel(*refs):
-        dense_ref, piece_refs, out_ref, source = refs[0], refs[1 : 1 + n_col], refs[-2], refs[-1]
-        step = pl.program_id(0)
-
-        @pl.when(step == 0)
-        def _():
-            for m in range(n_col):
-                source[m * nodes : (m + 1) * nodes, :] = piece_refs[m][...]
-
+def forward_early(dense, sources, n_row, resident):
+    places = sorted(sources)
+    nodes, width = sources[places[0]].shape
+    cols = dense.shape[1]
+
+    def kernel(dense_ref, *refs):
+        out_ref = refs[-1]
+        rows = pl.ds(pl.multiple_of(pl.program_id(0) * nodes, nodes), nodes) if resident else slice(None)
+        total = None
+        for m, ref in zip(places, refs[:-1]):
+            block = dense_ref[rows, m * nodes : (m + 1) * nodes]
+            out = jnp.dot(block, ref[...], preferred_element_type=F32)
+            total = out if total is None else total + out
+        out_ref[0] = total
+
+    spec = vmem() if resident else pl.BlockSpec((nodes, cols), lambda i: (i, 0))
+    return pl.pallas_call(
+        kernel,
+        out_shape=sds((n_row, nodes, width), F32),
+        grid=(n_row,),
+        in_specs=[spec] + [pl.BlockSpec((nodes, width), lambda i: (0, 0))] * len(places),
+        out_specs=pl.BlockSpec((1, nodes, width), lambda i: (i, 0, 0)),
+        compiler_params=params(8 if resident else 32),
+        cost_estimate=cost(5),
+        name="forward_early",
+    )(pinned(dense, resident), *[sources[m] for m in places])
+
+
+def forward_late(dense, early, place, piece, first, count, dtype, resident):
+    nodes, width = piece.shape
+
+    def kernel(dense_ref, early_ref, piece_ref, out_ref):
         if resident:
-            at = pl.multiple_of((first + step) * nodes, nodes)
-            block = dense_ref[pl.ds(at, nodes), :]
+            at = pl.multiple_of((first + pl.program_id(0)) * nodes, nodes)
+            block = dense_ref[pl.ds(at, nodes), place * nodes : (place + 1) * nodes]
         else:
             block = dense_ref[...]
-        out_ref[0] = jnp.dot(block, source[...], preferred_element_type=F32).astype(dtype)
-
-    spec = vmem() if resident else pl.BlockSpec((nodes, cols), lambda i: (i + first, 0))
-    return pl.pallas_call(
-        kernel,
-        out_shape=sds((count, nodes, wide), dtype),
+        out = jnp.dot(block, piece_ref[...], preferred_element_type=F32)
+        out_ref[0] = (early_ref[0] + out).astype(dtype)
+
+    spec = vmem() if resident else pl.BlockSpec((nodes, nodes), lambda i: (i + first, place))
+    return pl.pallas_call(
+        kernel,
+        out_shape=sds((count, nodes, width), dtype),
         grid=(count,),
-        in_specs=[spec] + [pl.BlockSpec((nodes, wide), lambda i: (0, 0))] * n_col,
-        out_specs=pl.BlockSpec((1, nodes, wide), lambda i: (i, 0, 0)),
-        scratch_shapes=[pltpu.VMEM((cols, wide), BF16)],
-        compiler_params=params(8 if resident else 24),
-        cost_estimate=cost(0.01),
-        name="forward",
-    )(pinned(dense, resident), *pieces)
+        in_specs=[
+            spec,
+            pl.BlockSpec((1, nodes, width), lambda i: (i + first, 0, 0)),
+            pl.BlockSpec((nodes, width), lambda i: (0, 0)),
+        ],
+        out_specs=pl.BlockSpec((1, nodes, width), lambda i: (i, 0, 0)),
+        compiler_params=params(8),
+        cost_estimate=cost(1),
+        name="forward_late",
+    )(pinned(dense, resident), early, piece)
 
 
 def add_parts(keep, got):
@@ -267,7 +289,7 @@
             for j in range(n_row // 2):
                 at = pl.multiple_of((j * 2 + (core ^ k)) * share, share)
                 ref[j * share : (j + 1) * share, :] = grads_ref[pl.ds(at, share), :].astype(ref.dtype)
-            ref[half:, :] = bias_rows.astype(ref.dtype)
+            ref[half:, :] = bias_rows.astype(BF16).astype(ref.dtype)
 
     return pl.pallas_call(
         kernel,
@@ -281,83 +303,43 @@
     )(features, neigh_mean, d_pre)
 
 
-def column_parts(keep, got, n_col):
-    height, columns = keep.shape
-    part = (height - BIAS_ROWS) // n_col
-
-    def kernel(keep_ref, got_ref, *refs):
-        out_refs, sum_ref = refs[:-1], refs[-1]
-        sum_ref[...] = keep_ref[...] + got_ref[...].astype(F32)
-        col = lax.axis_index("col")
-        for m, ref in enumerate(out_refs):
-            at = pl.multiple_of((col ^ m) * part, part)
-            ref[0:part, :] = sum_ref[pl.ds(at, part), :].astype(ref.dtype)
-            ref[part:, :] = sum_ref[height - BIAS_ROWS :, :].astype(ref.dtype)
-
-    return pl.pallas_call(
-        kernel,
-        out_shape=[sds((part + BIAS_ROWS, columns), F32 if m == 0 else BF16) for m in range(n_col)],
+def add_sent(keep, got, kind):
+    def kernel(keep_ref, got_ref, out_ref):
+        out_ref[...] = (keep_ref[...].astype(F32) + got_ref[...].astype(F32)).astype(kind)
+
+    return pl.pallas_call(
+        kernel,
+        out_shape=sds(keep.shape, kind),
         in_specs=[vmem()] * 2,
-        out_specs=[vmem()] * n_col,
-        scratch_shapes=[pltpu.VMEM(keep.shape, F32)],
+        out_specs=vmem(),
         compiler_params=params(8),
         cost_estimate=cost(0.1),
-        name="column_parts",
+        name="add_sent",
     )(keep, got)
 
 
-def column_sum(own, arrivals):
-    height, columns = own.shape
-    part = height - BIAS_ROWS
-
-    def kernel(own_ref, *refs):
-        send_ref, bias_ref = refs[-2:]
-        acc = own_ref[...]
-        for ref in refs[:-2]:
-            acc = acc + ref[...].astype(F32)
-        send_ref[...] = acc[0:part].astype(BF16)
-        bias_ref[...] = acc[part:]
-
-    return pl.pallas_call(
-        kernel,
-        out_shape=[sds((part, columns), BF16), sds((BIAS_ROWS, columns), F32)],
-        in_specs=[vmem()] * (1 + len(arrivals)),
-        out_specs=[vmem()] * 2,
-        compiler_params=params(8),
-        cost_estimate=cost(0.1),
-        name="column_sum",
-    )(own, *arrivals)
-
-
-def chip_parts(parts, bias_rows, n_row):
-    part, columns = parts[0].shape
-    n_col = len(parts)
+def chip_parts(half, n_row):
+    height, columns = half.shape
+    rows = height - BIAS_ROWS
     chips = n_row // 2
-    share = part * n_col // chips
-
-    def kernel(*refs):
-        part_refs, bias_ref = refs[:n_col], refs[n_col]
-        out_refs, whole_ref = refs[n_col + 1 : -1], refs[-1]
-        col = lax.axis_index("col")
-        for m, ref in enumerate(part_refs):
-            at = pl.multiple_of((col ^ m) * part, part)
-            whole_ref[pl.ds(at, part), :] = ref[...].astype(F32)
+    share = rows // chips
+
+    def kernel(half_ref, *out_refs):
         chip = lax.axis_index("row") // 2
         for j, ref in enumerate(out_refs):
             at = pl.multiple_of((chip ^ j) * share, share)
-            ref[0:share, :] = whole_ref[pl.ds(at, share), :]
-            ref[share:, :] = bias_ref[...]
+            ref[0:share, :] = half_ref[pl.ds(at, share), :]
+            ref[share:, :] = half_ref[rows:, :]
 
     return pl.pallas_call(
         kernel,
         out_shape=[sds((share + BIAS_ROWS, columns), F32)] * chips,
-        in_specs=[vmem()] * (n_col + 1),
+        in_specs=[vmem()],
         out_specs=[vmem()] * chips,
-        scratch_shapes=[pltpu.VMEM((part * n_col, columns), F32)],
         compiler_params=params(8),
         cost_estimate=cost(0.1),
         name="chip_parts",
-    )(*parts, bias_rows)
+    )(half)
 
 
 def side_by_side(pieces):
@@ -378,64 +360,83 @@
     )(*pieces)
 
 
-def backward(dense, mine, siblings, columns, nodes, resident):
+def backward_early(dense, mine, n_col, nodes, resident):
     wide, half = mine.shape
-    count = len(columns)
-    first = columns[0]
-
-    def kernel(dense_ref, mine_ref, siblings_ref, *out_refs):
+
+    def kernel(dense_ref, mine_ref, out_ref):
+        if resident:
+            at = pl.multiple_of(pl.program_id(0) * nodes, nodes)
+            block = dense_ref[0:half, pl.ds(at, nodes)]
+        else:
+            block = dense_ref[...]
+        out_ref[0] = jnp.dot(mine_ref[...], block, preferred_element_type=F32)
+
+    spec = vmem() if resident else pl.BlockSpec((half, nodes), lambda i: (0, i))
+    return pl.pallas_call(
+        kernel,
+        out_shape=sds((n_col, wide, nodes), F32),
+        grid=(n_col,),
+        in_specs=[spec, pl.BlockSpec((wide, half), lambda i: (0, 0))],
+        out_specs=pl.BlockSpec((1, wide, nodes), lambda i: (i, 0, 0)),
+        compiler_params=params(8 if resident else 24),
+        cost_estimate=cost(2.5),
+        name="backward_early",
+    )(pinned(dense, resident), mine)
+
+
+def backward_late(dense, early, siblings, n_col, nodes, resident):
+    wide, half = siblings.shape
+
+    def kernel(dense_ref, early_ref, siblings_ref, *out_refs):
         step = pl.program_id(0)
-        for i, m in enumerate(columns):
-
-            @pl.when(step == i)
+        for m in range(n_col):
+
+            @pl.when(step == m)
             def _():
                 if resident:
-                    upper = dense_ref[0:half, m * nodes : (m + 1) * nodes]
-                    lower = dense_ref[half : 2 * half, m * nodes : (m + 1) * nodes]
+                    block = dense_ref[half : 2 * half, m * nodes : (m + 1) * nodes]
                 else:
-                    upper = dense_ref[0:half, :]
-                    lower = dense_ref[half:, :]
-                out = jnp.dot(mine_ref[...], upper, preferred_element_type=F32)
-                out = out + jnp.dot(siblings_ref[...], lower, preferred_element_type=F32)
-                out_refs[i][...] = out.astype(out_refs[i].dtype)
-
-    spec = vmem() if resident else pl.BlockSpec((2 * half, nodes), lambda i: (0, i + first))
+                    block = dense_ref[...]
+                out = jnp.dot(siblings_ref[...], block, preferred_element_type=F32)
+                out_refs[m][...] = (early_ref[0] + out).astype(out_refs[m].dtype)
+
+    spec = vmem() if resident else pl.BlockSpec((half, nodes), lambda i: (1, i))
     whole = lambda shape: pl.BlockSpec(shape, lambda i: (0,) * len(shape))
-    outs = [sds((wide, nodes), F32 if m == 0 else BF16) for m in columns]
+    outs = [sds((wide, nodes), F32 if m == 0 else BF16) for m in range(n_col)]
     return pl.pallas_call(
         kernel,
         out_shape=outs,
-        grid=(count,),
-        in_specs=[spec] + [whole((wide, half))] * 2,
+        grid=(n_col,),
+        in_specs=[spec, pl.BlockSpec((1, wide, nodes), lambda i: (i, 0, 0)), whole((wide, half))],
         out_specs=[whole(o.shape) for o in outs],
-        compiler_params=params(16 if resident else 48),
+        compiler_params=params(10 if resident else 32),
         cost_estimate=cost(2.5),
-        name="backward",
-    )(pinned(dense, resident), mine, siblings)
-
-
-def share_total(total, arrivals):
-    height, columns = total.shape
+        name="backward_late",
+    )(pinned(dense, resident), early, siblings)
+
+
+def share_total(pieces):
+    height, columns = pieces[0].shape
     share = height - BIAS_ROWS
     width = columns // 2
 
-    def kernel(total_ref, *refs):
+    def kernel(*refs):
         share_ref, bias_ref = refs[-2:]
-        acc = total_ref[...]
-        for ref in refs[:-2]:
-            acc = acc + ref[...].astype(F32)
-        share_ref[...] = acc[0:share]
-        bias_ref[...] = acc[share : share + 1, 0:width]
+        terms = [ref[...] for ref in refs[:-2]]
+        while len(terms) > 1:
+            terms = [terms[i] + terms[i + 1] for i in range(0, len(terms), 2)]
+        share_ref[...] = terms[0][0:share]
+        bias_ref[...] = terms[0][share : share + 1, 0:width]
 
     return pl.pallas_call(
         kernel,
         out_shape=[sds((share, columns), F32), sds((1, width), F32)],
-        in_specs=[vmem()] * (1 + len(arrivals)),
+        in_specs=[vmem()] * len(pieces),
         out_specs=[vmem()] * 2,
         compiler_params=params(8),
         cost_estimate=cost(0.1),
         name="share_total",
-    )(total, *arrivals)
+    )(*pieces)
 
 
 def join(pieces):
@@ -524,19 +525,26 @@
     per_dev = nodes // tile
     resident = n_row * nodes * n_col * nodes * 2 <= RESIDENT_BYTES
 
-    arrived = {m: swap(features, "col", m) for m in far_first(n_col)}
-    source = [features] + [arrived[m] for m in range(1, n_col)]
+    source = {m: swap(features, "col", m) for m in far_first(n_col)}
+    source[0] = features
     build = densify if resident else densify_far
     dense = build(tile_values, tile_row, tile_col, n_row, n_col, per_dev)
 
-    give = forward(dense, source, chips + 1, chips - 1, BF16, resident)
+    last = n_col // 2
+    last_piece = source.pop(last)
+    early = forward_early(dense, source, n_row, resident)
+
+    def late(first, count, dtype):
+        return forward_late(dense, early, last, last_piece, first, count, dtype, resident)
+
+    give = late(chips + 1, chips - 1, BF16)
     got = swap(give, "row", 1)
-    keep = forward(dense, source, 1, chips - 1, F32, resident)
+    keep = late(1, chips - 1, F32)
     sends = add_parts(keep, got)
     arrivals = [swap(sends[j - 1], "row", 2 * j) for j in range(1, chips)]
-    give_own = forward(dense, source, chips, 1, BF16, resident)
+    give_own = late(chips, 1, BF16)
     got_own = swap(give_own, "row", 1)
-    keep_own = forward(dense, source, 0, 1, F32, resident)
+    keep_own = late(0, 1, F32)
     hidden, neigh_mean, d_pre, d_agg = middle(
         features,
         degree[None, :],
@@ -551,25 +559,26 @@
 
     pieces = [d_agg] + [swap(d_agg, "row", 2 * j) for j in range(1, chips)]
 
-    grads_keep, grads_give = local_grads(features, neigh_mean, d_pre, n_row)
-    cuts = column_parts(grads_keep, swap(grads_give, "row", 1), n_col)
-    part, bias_rows = column_sum(cuts[0], [swap(cuts[m], "col", m) for m in range(1, n_col)])
-    pieces, part = lax.optimization_barrier((pieces, part))
+    kept, sent = local_grads(features, neigh_mean, d_pre, n_row)
+    total = add_sent(kept, swap(sent, "row", 1), BF16)
+    mask = n_col // 2
+    while mask > 1:
+        total = add_sent(total, swap(total, "col", mask), BF16)
+        mask //= 2
+    pieces, total = lax.optimization_barrier((pieces, total))
     mine = side_by_side(pieces)
     siblings = swap(mine, "row", 1)
-    cut = [part] + [swap(part, "col", m) for m in range(1, n_col)]
-
-    near = n_col // 2
-    far_outs = backward(dense, mine, siblings, list(range(near, n_col)), nodes, resident)
-    mine, siblings, cut, far_outs = lax.optimization_barrier((mine, siblings, cut, far_outs))
-    own, *near_outs = backward(dense, mine, siblings, list(range(near)), nodes, resident)
-    outs = near_outs + list(far_outs)
+    got_last = swap(total, "col", 1)
+
+    early = backward_early(dense, mine, n_col, nodes, resident)
+    own, *outs = backward_late(dense, early, siblings, n_col, nodes, resident)
     back = {m: swap(outs[m - 1], "col", m) for m in far_first(n_col)}
     back = tuple(back[m] for m in range(1, n_col))
 
-    cuts = chip_parts(cut, bias_rows, n_row)
+    got_last, _ = lax.optimization_barrier((got_last, outs))
+    cuts = chip_parts(add_sent(total, got_last, F32), n_row)
     arrivals = [swap(cuts[j], "row", 2 * j) for j in range(1, chips)]
-    piece, grad_bias = share_total(cuts[0], arrivals)
+    piece, grad_bias = share_total([cuts[0]] + arrivals)
     shares = join([piece] + [swap(piece, "row", 2 * j) for j in range(1, chips)])
     shares, back = lax.optimization_barrier((shares, back))
     grad_self, grad_neigh = weight_grads(shares, swap(shares, "row", 1), n_row)

time: 105 us -> 99.5 us (0.948)
  the two profiles are of different devices: /device:TPU:0 before, /device:TPU:17 now
where the time goes in v4:
time: 99.5 us; the launch traced here: 99.2 us
  waiting for transfers between devices  39.3 us (39%)
  starting transfers between devices  29.5 us (30%)
  Pallas kernels  28.7 us (29%)
    ppermute x25, waiting for transfers between devices, swap(): return lax.ppermute(x, axis, [(i, i ^ mask) for i in range(size)])  39.3 us
    ppermute x25, starting transfers between devices, swap(): return lax.ppermute(x, axis, [(i, i ^ mask) for i in range(size)])  29.5 us
    pallas_call x1, Pallas kernels, densify(): pl.pallas_call(kernel, out_shape=pltpu.VMEM(((rows + 1) * tile, cols * ti...  11.5 us
    pallas_call x1, Pallas kernels, forward_early(): pl.pallas_call(kernel, out_shape=sds((n_row, nodes, width), F32), grid=(n...  4.62 us
    pallas_call x1, Pallas kernels, backward_late(): pl.pallas_call(kernel, out_shape=outs, grid=(n_col,), in_specs=[spec, pl....  2.93 us
    pallas_call x1, Pallas kernels, backward_early(): pl.pallas_call(kernel, out_shape=sds((n_col, wide, nodes), F32), grid=(n_...  2.87 us
    pallas_call x4, Pallas kernels, forward_late(): pl.pallas_call(kernel, out_shape=sds((count, nodes, width), dtype), grid=...  2.44 us
  transfers between devices with their start and end apart: 25, of which 13 were waited for; matrix products, arithmetic and copies ran while one was open for 1% of the time, Pallas kernels for 25%

profile of v4, /device:TPU:17, one launch (start us, length us, event | category | flops | bytes accessed | tf_op | source)
XLA Modules:
  0.0 99.2 jit_solution(17254688104996027012)
XLA Ops:
  0.6 0.2 collective-permute-start.1
  0.9 1.2 %collective-permute-start = (bf16[512,256]{1,0:T(8,128)(2,1)}, bf16[512,256]{1,0:T(8,128)(2,1)S(1)}, u32[]{:S(2)}, u32[]{:S(2)}) collective-permute-start(bf16[512,256]{1,0:T(8,128)(2,1)} %feat_ref.1), channel_id=1, source_target_pairs={{0,1},{1,0},{2,3},{3,2},{4,5},{5,4},{6,7},{7,6},{8,9},{9,8},{10,11... | collective-permute-start | bytes 786440 | tf_op jit(solution)/shard_map/ppermute | solution.py:512
  2.1 2.0 %collective-permute-start.2 = (bf16[512,256]{1,0:T(8,128)(2,1)}, bf16[512,256]{1,0:T(8,128)(2,1)S(1)}, u32[]{:S(2)}, u32[]{:S(2)}) collective-permute-start(bf16[512,256]{1,0:T(8,128)(2,1)} %feat_ref.1), channel_id=1, source_target_pairs={{0,2},{1,3},{2,0},{3,1},{4,6},{5,7},{6,4},{7,5},{8,10},{9,11},{10,... | collective-permute-start | bytes 786440 | tf_op jit(solution)/shard_map/ppermute | solution.py:512
  4.1 0.7 fusion.6
  4.8 0.0 copy-start
  4.8 11.5 %densify.1.dense_ref = bf16[4224,2048]{1,0:T(8,128)(2,1)S(1)} custom-call(s32[384]{0:T(512)S(1)} %get-tuple-element.67.down_ref, s32[384]{0:T(512)S(1)} %get-tuple-element.68.right_ref, bf16[384,128,128]{2,1,0:T(8,128)(2,1)} %values_ref.1), custom_call_target="tpu_custom_call" | custom-call | bytes 37000000 | tf_op jit(solution)/shard_map/densify/pallas_call | solution.py:139
  16.3 0.0 collective-permute-done.1.refs_2_
  16.3 0.0 collective-permute-done.refs_1_
  16.3 4.6 %forward_early.1.early_ref = f32[8,512,256]{2,1,0:T(8,128)S(1)} custom-call(bf16[4224,2048]{1,0:T(8,128)(2,1)S(1)} %densify.1.dense_ref, bf16[512,256]{1,0:T(8,128)(2,1)S(1)} %copy-done, bf16[512,256]{1,0:T(8,128)(2,1)S(1)} %collective-permute-done.refs_1_, bf16[512,256]{1,0:T(8,128)(2,1)S(1)} %collective-permute-done.1.refs_2_), custom_call_target="tpu_custom_call" | custom-call | bytes 18500000 | tf_op jit(solution)/shard_map/forward_early/pallas_call | solution.py:174
  21.0 2.2 %collective-permute-done.2.piece_ref = bf16[512,256]{1,0:T(8,128)(2,1)S(1)} collective-permute-done((bf16[512,256]{1,0:T(8,128)(2,1)}, bf16[512,256]{1,0:T(8,128)(2,1)S(1)}, u32[]{:S(2)}, u32[]{:S(2)}) %collective-permute-start.2) | collective-permute-done | bytes 262176 | tf_op jit(solution)/shard_map/ppermute | solution.py:512
  23.2 0.9 forward_late.7
  24.1 1.4 %collective-permute-start.4 = (bf16[3,512,256]{2,1,0:T(8,128)(2,1)S(1)}, bf16[3,512,256]{2,1,0:T(8,128)(2,1)S(1)}, u32[]{:S(2)}, u32[]{:S(2)}) collective-permute-start(bf16[3,512,256]{2,1,0:T(8,128)(2,1)S(1)} %forward_late.7), channel_id=1, source_target_pairs={{0,4},{4,0},{8,12},{12,8},{16,20},{20,16},{24,28},{28,24},{1,5},{5... | collective-permute-start | bytes 2359304 | tf_op jit(solution)/shard_map/ppermute | solution.py:512
  25.5 0.3 forward_late.5
  25.8 0.1 collective-permute-start.3
  25.9 0.9 forward_late.6.keep_ref
  26.9 0.6 collective-permute-done.4.got_ref
  27.5 0.1 add_parts.1
  27.6 1.3 %collective-permute-start.5 = (bf16[512,256]{1,0:T(8,128)(2,1)S(1)}, bf16[512,256]{1,0:T(8,128)(2,1)S(1)}, u32[]{:S(2)}, u32[]{:S(2)}) collective-permute-start(bf16[512,256]{1,0:T(8,128)(2,1)S(1)} %get-tuple-element.36), channel_id=1, source_target_pairs={{0,8},{4,12},{8,0},{12,4},{16,24},{20,28},{24,16},{28,20},{1,9},{5... | collective-permute-start | bytes 786440 | tf_op jit(solution)/shard_map/ppermute | solution.py:512
  28.9 1.2 %collective-permute-start.6 = (bf16[512,256]{1,0:T(8,128)(2,1)S(1)}, bf16[512,256]{1,0:T(8,128)(2,1)S(1)}, u32[]{:S(2)}, u32[]{:S(2)}) collective-permute-start(bf16[512,256]{1,0:T(8,128)(2,1)S(1)} %get-tuple-element.37), channel_id=1, source_target_pairs={{0,16},{4,20},{8,24},{12,28},{16,0},{20,4},{24,8},{28,12},{1,17},{... | collective-permute-start | bytes 786440 | tf_op jit(solution)/shard_map/ppermute | solution.py:512
  30.1 0.0 copy-start.5
  30.1 0.3 collective-permute-start.7
  30.4 0.3 forward_late.4.refs_6_
  30.7 0.0 collective-permute-done.3.refs_7_
  30.7 4.5 %collective-permute-done.5.refs_8_ = bf16[512,256]{1,0:T(8,128)(2,1)S(1)} collective-permute-done((bf16[512,256]{1,0:T(8,128)(2,1)S(1)}, bf16[512,256]{1,0:T(8,128)(2,1)S(1)}, u32[]{:S(2)}, u32[]{:S(2)}) %collective-permute-start.5) | collective-permute-done | bytes 262176 | tf_op jit(solution)/shard_map/ppermute | solution.py:512
  35.2 0.9 collective-permute-done.6.refs_9_
  36.1 5.7 %collective-permute-done.7.refs_10_ = bf16[512,256]{1,0:T(8,128)(2,1)S(1)} collective-permute-done((bf16[512,256]{1,0:T(8,128)(2,1)S(1)}, bf16[512,256]{1,0:T(8,128)(2,1)S(1)}, u32[]{:S(2)}, u32[]{:S(2)}) %collective-permute-start.7) | collective-permute-done | bytes 262176 | tf_op jit(solution)/shard_map/ppermute | solution.py:512
  41.8 1.2 %middle.1 = (bf16[512,256]{1,0:T(8,128)(2,1)}, bf16[512,256]{1,0:T(8,128)(2,1)S(1)}, bf16[512,256]{1,0:T(8,128)(2,1)S(1)}, bf16[256,512]{1,0:T(8,128)(2,1)S(1)}) custom-call(bf16[512,256]{1,0:T(8,128)(2,1)S(1)} %copy-done, s32[1,512]{1,0:T(1,128)S(1)} %bitcast.3, bf16[512,256]{1,0:T(8,128)(2,1)S(1)} %copy-done.2, bf16[256,256]{1,0:T(8,128)(2,1)S(1)} %copy-done.1, ...), custom_call_target="tpu_custom_call" | custom-call | bytes 5550000 | tf_op jit(solution)/shard_map/middle/pallas_call | solution.py:259
  43.0 0.4 local_grads.1
  43.4 1.5 %collective-permute-start.11 = (bf16[144,512]{1,0:T(8,128)(2,1)S(1)}, bf16[144,512]{1,0:T(8,128)(2,1)S(1)}, u32[]{:S(2)}, u32[]{:S(2)}) collective-permute-start(bf16[144,512]{1,0:T(8,128)(2,1)S(1)} %get-tuple-element.44), channel_id=1, source_target_pairs={{0,4},{4,0},{8,12},{12,8},{16,20},{20,16},{24,28},{28,24},{1,5},{5... | collective-permute-start | bytes 442376 | tf_op jit(solution)/shard_map/ppermute | solution.py:512
  44.9 1.2 %collective-permute-start.10 = (bf16[256,512]{1,0:T(8,128)(2,1)S(1)}, bf16[256,512]{1,0:T(8,128)(2,1)S(1)}, u32[]{:S(2)}, u32[]{:S(2)}) collective-permute-start(bf16[256,512]{1,0:T(8,128)(2,1)S(1)} %get-tuple-element.45.refs_0_), channel_id=1, source_target_pairs={{0,24},{4,28},{8,16},{12,20},{16,8},{20,12},{24,0},{28,4},{1,25},{... | collective-permute-start | bytes 786440 | tf_op jit(solution)/shard_map/ppermute | solution.py:512
  46.1 0.9 collective-permute-start.9
  47.1 0.5 collective-permute-start.8
  47.6 0.0 collective-permute-done.11.got_ref
  47.6 3.1 %collective-permute-start.12 = (bf16[144,512]{1,0:T(8,128)(2,1)S(1)}, bf16[144,512]{1,0:T(8,128)(2,1)S(1)}, u32[]{:S(2)}, u32[]{:S(2)}) collective-permute-start(bf16[144,512]{1,0:T(8,128)(2,1)S(1)} %add_sent.3.keep_ref), channel_id=1, source_target_pairs={{0,2},{1,3},{2,0},{3,1},{4,6},{5,7},{6,4},{7,5},{8,10},{9,11},{10,... | collective-permute-start | bytes 442376 | tf_op jit(solution)/shard_map/ppermute | solution.py:512
  50.7 6.6 %collective-permute-done.12.got_ref = bf16[144,512]{1,0:T(8,128)(2,1)S(1)} collective-permute-done((bf16[144,512]{1,0:T(8,128)(2,1)S(1)}, bf16[144,512]{1,0:T(8,128)(2,1)S(1)}, u32[]{:S(2)}, u32[]{:S(2)}) %collective-permute-start.12) | collective-permute-done | bytes 147488 | tf_op jit(solution)/shard_map/ppermute | solution.py:512
  57.3 0.0 collective-permute-done.10.refs_3_
  57.3 2.4 %collective-permute-done.9.refs_2_ = bf16[256,512]{1,0:T(8,128)(2,1)S(1)} collective-permute-done((bf16[256,512]{1,0:T(8,128)(2,1)S(1)}, bf16[256,512]{1,0:T(8,128)(2,1)S(1)}, u32[]{:S(2)}, u32[]{:S(2)}) %collective-permute-start.9) | collective-permute-done | bytes 262176 | tf_op jit(solution)/shard_map/ppermute | solution.py:512
  59.7 0.0 collective-permute-done.8.refs_1_
  59.7 0.1 side_by_side.1.mine_ref
  59.8 0.6 collective-permute-start.13
  60.4 3.1 %collective-permute-start.14 = (bf16[144,512]{1,0:T(8,128)(2,1)S(1)}, bf16[144,512]{1,0:T(8,128)(2,1)S(1)}, u32[]{:S(2)}, u32[]{:S(2)}) collective-permute-start(bf16[144,512]{1,0:T(8,128)(2,1)S(1)} %add_sent.4.keep_ref), channel_id=1, source_target_pairs={{0,1},{1,0},{2,3},{3,2},{4,5},{5,4},{6,7},{7,6},{8,9},{9,8},{10,11... | collective-permute-start | bytes 442376 | tf_op jit(solution)/shard_map/ppermute | solution.py:512
  63.5 2.9 %backward_early.1.early_ref = f32[4,256,512]{2,1,0:T(8,128)S(1)} custom-call(bf16[4224,2048]{1,0:T(8,128)(2,1)S(1)} %densify.1.dense_ref, bf16[256,2048]{1,0:T(8,128)(2,1)S(1)} %side_by_side.1.mine_ref), custom_call_target="tpu_custom_call" | custom-call | bytes 9250000 | tf_op jit(solution)/shard_map/backward_early/pallas_call | solution.py:375
  66.4 0.0 collective-permute-done.13.siblings_ref
  66.4 2.9 %backward_late.1 = (f32[256,512]{1,0:T(8,128)S(1)}, bf16[256,512]{1,0:T(8,128)(2,1)S(1)}, bf16[256,512]{1,0:T(8,128)(2,1)S(1)}, bf16[256,512]{1,0:T(8,128)(2,1)S(1)}) custom-call(bf16[4224,2048]{1,0:T(8,128)(2,1)S(1)} %densify.1.dense_ref, f32[4,256,512]{2,1,0:T(8,128)S(1)} %backward_early.1.early_ref, bf16[256,2048]{1,0:T(8,128)(2,1)S(1)} %collective-permute-done.13.siblings_ref), custom_call_target="tpu_custom_call" | custom-call | bytes 9250000 | tf_op jit(solution)/shard_map/backward_late/pallas_call | solution.py:406
  69.5 0.9 collective-permute-start.15
  70.4 1.3 %collective-permute-start.22 = (bf16[256,512]{1,0:T(8,128)(2,1)S(1)}, bf16[256,512]{1,0:T(8,128)(2,1)S(1)}, u32[]{:S(2)}, u32[]{:S(2)}) collective-permute-start(bf16[256,512]{1,0:T(8,128)(2,1)S(1)} %get-tuple-element.52), channel_id=1, source_target_pairs={{0,2},{1,3},{2,0},{3,1},{4,6},{5,7},{6,4},{7,5},{8,10},{9,11},{10,... | collective-permute-start | bytes 786440 | tf_op jit(solution)/shard_map/ppermute | solution.py:512
  71.7 1.3 %collective-permute-start.23 = (bf16[256,512]{1,0:T(8,128)(2,1)S(1)}, bf16[256,512]{1,0:T(8,128)(2,1)S(1)}, u32[]{:S(2)}, u32[]{:S(2)}) collective-permute-start(bf16[256,512]{1,0:T(8,128)(2,1)S(1)} %get-tuple-element.53), channel_id=1, source_target_pairs={{0,3},{1,2},{2,1},{3,0},{4,7},{5,6},{6,5},{7,4},{8,11},{9,10},{10,... | collective-permute-start | bytes 786440 | tf_op jit(solution)/shard_map/ppermute | solution.py:512
  73.0 0.5 collective-permute-start.16
  73.5 0.0 collective-permute-done.15.refs_1_
  73.6 1.3 %collective-permute-start.17 = (f32[48,512]{1,0:T(8,128)S(1)}, f32[48,512]{1,0:T(8,128)S(1)}, u32[]{:S(2)}, u32[]{:S(2)}) collective-permute-start(f32[48,512]{1,0:T(8,128)S(1)} %get-tuple-element.58), channel_id=1, source_target_pairs={{0,24},{4,28},{8,16},{12,20},{16,8},{20,12},{24,0},{28,4},{1,25},{... | collective-permute-start | bytes 294920 | tf_op jit(solution)/shard_map/ppermute | solution.py:512
  74.8 2.0 %collective-permute-done.16.refs_2_ = f32[48,512]{1,0:T(8,128)S(1)} collective-permute-done((f32[48,512]{1,0:T(8,128)S(1)}, f32[48,512]{1,0:T(8,128)S(1)}, u32[]{:S(2)}, u32[]{:S(2)}) %collective-permute-start.16) | collective-permute-done | bytes 98336 | tf_op jit(solution)/shard_map/ppermute | solution.py:512
  76.8 1.2 %collective-permute-done.17.refs_3_ = f32[48,512]{1,0:T(8,128)S(1)} collective-permute-done((f32[48,512]{1,0:T(8,128)S(1)}, f32[48,512]{1,0:T(8,128)S(1)}, u32[]{:S(2)}, u32[]{:S(2)}) %collective-permute-start.17) | collective-permute-done | bytes 98336 | tf_op jit(solution)/shard_map/ppermute | solution.py:512
  78.0 0.6 share_total.1
  78.6 1.2 %collective-permute-start.20 = (f32[32,512]{1,0:T(8,128)S(1)}, f32[32,512]{1,0:T(8,128)S(1)}, u32[]{:S(2)}, u32[]{:S(2)}) collective-permute-start(f32[32,512]{1,0:T(8,128)S(1)} %get-tuple-element.59.refs_0_), channel_id=1, source_target_pairs={{0,24},{4,28},{8,16},{12,20},{16,8},{20,12},{24,0},{28,4},{1,25},{... | collective-permute-start | bytes 196616 | tf_op jit(solution)/shard_map/ppermute | solution.py:512
  79.8 1.2 %collective-permute-start.19 = (f32[32,512]{1,0:T(8,128)S(1)}, f32[32,512]{1,0:T(8,128)S(1)}, u32[]{:S(2)}, u32[]{:S(2)}) collective-permute-start(f32[32,512]{1,0:T(8,128)S(1)} %get-tuple-element.59.refs_0_), channel_id=1, source_target_pairs={{0,16},{4,20},{8,24},{12,28},{16,0},{20,4},{24,8},{28,12},{1,17},{... | collective-permute-start | bytes 196616 | tf_op jit(solution)/shard_map/ppermute | solution.py:512
  81.0 1.9 %collective-permute-done.20.refs_3_ = f32[32,512]{1,0:T(8,128)S(1)} collective-permute-done((f32[32,512]{1,0:T(8,128)S(1)}, f32[32,512]{1,0:T(8,128)S(1)}, u32[]{:S(2)}, u32[]{:S(2)}) %collective-permute-start.20) | collective-permute-done | bytes 65568 | tf_op jit(solution)/shard_map/ppermute | solution.py:512
  82.9 1.3 %collective-permute-start.18 = (f32[32,512]{1,0:T(8,128)S(1)}, f32[32,512]{1,0:T(8,128)S(1)}, u32[]{:S(2)}, u32[]{:S(2)}) collective-permute-start(f32[32,512]{1,0:T(8,128)S(1)} %get-tuple-element.59.refs_0_), channel_id=1, source_target_pairs={{0,8},{4,12},{8,0},{12,4},{16,24},{20,28},{24,16},{28,20},{1,9},{5... | collective-permute-start | bytes 196616 | tf_op jit(solution)/shard_map/ppermute | solution.py:512
  84.1 0.0 collective-permute-done.19.refs_2_
  84.1 2.5 %collective-permute-done.18.refs_1_ = f32[32,512]{1,0:T(8,128)S(1)} collective-permute-done((f32[32,512]{1,0:T(8,128)S(1)}, f32[32,512]{1,0:T(8,128)S(1)}, u32[]{:S(2)}, u32[]{:S(2)}) %collective-permute-start.18) | collective-permute-done | bytes 65568 | tf_op jit(solution)/shard_map/ppermute | solution.py:512
  86.7 8.7 %collective-permute-done.23.refs_2_ = bf16[256,512]{1,0:T(8,128)(2,1)S(1)} collective-permute-done((bf16[256,512]{1,0:T(8,128)(2,1)S(1)}, bf16[256,512]{1,0:T(8,128)(2,1)S(1)}, u32[]{:S(2)}, u32[]{:S(2)}) %collective-permute-start.23) | collective-permute-done | bytes 262176 | tf_op jit(solution)/shard_map/ppermute | solution.py:512
  95.4 1.8 %collective-permute-start.24 = (f32[128,512]{1,0:T(8,128)S(1)}, f32[128,512]{1,0:T(8,128)S(1)}, u32[]{:S(2)}, u32[]{:S(2)}) collective-permute-start(f32[128,512]{1,0:T(8,128)S(1)} %join.1.mine_ref), channel_id=1, source_target_pairs={{0,4},{4,0},{8,12},{12,8},{16,20},{20,16},{24,28},{28,24},{1,5},{5... | collective-permute-start | bytes 786440 | tf_op jit(solution)/shard_map/ppermute | solution.py:512
  97.2 1.0 finish.1
  98.2 0.2 collective-permute-done.24.siblings_ref
  98.3 0.8 weight_grads.1
  (19 shorter events, 0.2 us)
Async XLA Ops:
  0.6 15.7 %collective-permute-start.1 = (bf16[512,256]{1,0:T(8,128)(2,1)}, bf16[512,256]{1,0:T(8,128)(2,1)S(1)}, u32[]{:S(2)}, u32[]{:S(2)}) collective-permute-start(bf16[512,256]{1,0:T(8,128)(2,1)} %feat_ref.1), channel_id=1, source_target_pairs={{0,3},{1,2},{2,1},{3,0},{4,7},{5,6},{6,5},{7,4},{8,11},{9,10},{10,... | collective-permute-start | bytes 786440 | tf_op jit(solution)/shard_map/ppermute | solution.py:512
  0.9 15.5 %collective-permute-start = (bf16[512,256]{1,0:T(8,128)(2,1)}, bf16[512,256]{1,0:T(8,128)(2,1)S(1)}, u32[]{:S(2)}, u32[]{:S(2)}) collective-permute-start(bf16[512,256]{1,0:T(8,128)(2,1)} %feat_ref.1), channel_id=1, source_target_pairs={{0,1},{1,0},{2,3},{3,2},{4,5},{5,4},{6,7},{7,6},{8,9},{9,8},{10,11... | collective-permute-start | bytes 786440 | tf_op jit(solution)/shard_map/ppermute | solution.py:512
  2.1 21.1 %collective-permute-start.2 = (bf16[512,256]{1,0:T(8,128)(2,1)}, bf16[512,256]{1,0:T(8,128)(2,1)S(1)}, u32[]{:S(2)}, u32[]{:S(2)}) collective-permute-start(bf16[512,256]{1,0:T(8,128)(2,1)} %feat_ref.1), channel_id=1, source_target_pairs={{0,2},{1,3},{2,0},{3,1},{4,6},{5,7},{6,4},{7,5},{8,10},{9,11},{10,... | collective-permute-start | bytes 786440 | tf_op jit(solution)/shard_map/ppermute | solution.py:512
  4.8 11.5 %copy-start = (bf16[512,256]{1,0:T(8,128)(2,1)S(1)}, bf16[512,256]{1,0:T(8,128)(2,1)}, u32[]{:S(2)}) copy-start(bf16[512,256]{1,0:T(8,128)(2,1)} %feat_ref.1) | copy-start | bytes 786436
  24.1 3.3 %collective-permute-start.4 = (bf16[3,512,256]{2,1,0:T(8,128)(2,1)S(1)}, bf16[3,512,256]{2,1,0:T(8,128)(2,1)S(1)}, u32[]{:S(2)}, u32[]{:S(2)}) collective-permute-start(bf16[3,512,256]{2,1,0:T(8,128)(2,1)S(1)} %forward_late.7), channel_id=1, source_target_pairs={{0,4},{4,0},{8,12},{12,8},{16,20},{20,16},{24,28},{28,24},{1,5},{5... | collective-permute-start | bytes 2359304 | tf_op jit(solution)/shard_map/ppermute | solution.py:512
  25.8 4.8 %collective-permute-start.3 = (bf16[1,512,256]{2,1,0:T(8,128)(2,1)S(1)}, bf16[1,512,256]{2,1,0:T(8,128)(2,1)S(1)}, u32[]{:S(2)}, u32[]{:S(2)}) collective-permute-start(bf16[1,512,256]{2,1,0:T(8,128)(2,1)S(1)} %forward_late.5), channel_id=1, source_target_pairs={{0,4},{4,0},{8,12},{12,8},{16,20},{20,16},{24,28},{28,24},{1,5},{5... | collective-permute-start | bytes 786440 | tf_op jit(solution)/shard_map/ppermute | solution.py:512
  27.6 7.6 %collective-permute-start.5 = (bf16[512,256]{1,0:T(8,128)(2,1)S(1)}, bf16[512,256]{1,0:T(8,128)(2,1)S(1)}, u32[]{:S(2)}, u32[]{:S(2)}) collective-permute-start(bf16[512,256]{1,0:T(8,128)(2,1)S(1)} %get-tuple-element.36), channel_id=1, source_target_pairs={{0,8},{4,12},{8,0},{12,4},{16,24},{20,28},{24,16},{28,20},{1,9},{5... | collective-permute-start | bytes 786440 | tf_op jit(solution)/shard_map/ppermute | solution.py:512
  28.9 7.2 %collective-permute-start.6 = (bf16[512,256]{1,0:T(8,128)(2,1)S(1)}, bf16[512,256]{1,0:T(8,128)(2,1)S(1)}, u32[]{:S(2)}, u32[]{:S(2)}) collective-permute-start(bf16[512,256]{1,0:T(8,128)(2,1)S(1)} %get-tuple-element.37), channel_id=1, source_target_pairs={{0,16},{4,20},{8,24},{12,28},{16,0},{20,4},{24,8},{28,12},{1,17},{... | collective-permute-start | bytes 786440 | tf_op jit(solution)/shard_map/ppermute | solution.py:512
  30.1 11.7 %copy-start.1 = (bf16[256,256]{1,0:T(8,128)(2,1)S(1)}, bf16[256,256]{1,0:T(8,128)(2,1)}, u32[]{:S(2)}) copy-start(bf16[256,256]{1,0:T(8,128)(2,1)} %ws_ref.1) | copy-start | bytes 393220
  30.1 11.7 %copy-start.2 = (bf16[512,256]{1,0:T(8,128)(2,1)S(1)}, bf16[512,256]{1,0:T(8,128)(2,1)}, u32[]{:S(2)}) copy-start(bf16[512,256]{1,0:T(8,128)(2,1)} %refs_2_.1) | copy-start | bytes 786436
  30.1 11.7 %copy-start.3 = (bf16[256,256]{1,0:T(8,128)(2,1)S(1)}, bf16[256,256]{1,0:T(8,128)(2,1)}, u32[]{:S(2)}) copy-start(bf16[256,256]{1,0:T(8,128)(2,1)} %refs_4_.1) | copy-start | bytes 393220
  30.1 11.7 %copy-start.4 = (s32[512]{0:T(512)S(1)}, s32[512]{0:T(512)}, u32[]{:S(2)}) copy-start(s32[512]{0:T(512)} %param.10) | copy-start | bytes 6148
  30.1 11.7 %copy-start.5 = (f32[256]{0:T(256)S(1)}, f32[256]{0:T(256)}, u32[]{:S(2)}) copy-start(f32[256]{0:T(256)} %param.17) | copy-start | bytes 3076
  30.1 11.7 %collective-permute-start.7 = (bf16[512,256]{1,0:T(8,128)(2,1)S(1)}, bf16[512,256]{1,0:T(8,128)(2,1)S(1)}, u32[]{:S(2)}, u32[]{:S(2)}) collective-permute-start(bf16[512,256]{1,0:T(8,128)(2,1)S(1)} %get-tuple-element.38), channel_id=1, source_target_pairs={{0,24},{4,28},{8,16},{12,20},{16,8},{20,12},{24,0},{28,4},{1,25},{... | collective-permute-start | bytes 786440 | tf_op jit(solution)/shard_map/ppermute | solution.py:512
  43.4 4.1 %collective-permute-start.11 = (bf16[144,512]{1,0:T(8,128)(2,1)S(1)}, bf16[144,512]{1,0:T(8,128)(2,1)S(1)}, u32[]{:S(2)}, u32[]{:S(2)}) collective-permute-start(bf16[144,512]{1,0:T(8,128)(2,1)S(1)} %get-tuple-element.44), channel_id=1, source_target_pairs={{0,4},{4,0},{8,12},{12,8},{16,20},{20,16},{24,28},{28,24},{1,5},{5... | collective-permute-start | bytes 442376 | tf_op jit(solution)/shard_map/ppermute | solution.py:512
  44.9 12.4 %collective-permute-start.10 = (bf16[256,512]{1,0:T(8,128)(2,1)S(1)}, bf16[256,512]{1,0:T(8,128)(2,1)S(1)}, u32[]{:S(2)}, u32[]{:S(2)}) collective-permute-start(bf16[256,512]{1,0:T(8,128)(2,1)S(1)} %get-tuple-element.45.refs_0_), channel_id=1, source_target_pairs={{0,24},{4,28},{8,16},{12,20},{16,8},{20,12},{24,0},{28,4},{1,25},{... | collective-permute-start | bytes 786440 | tf_op jit(solution)/shard_map/ppermute | solution.py:512
  46.1 13.6 %collective-permute-start.9 = (bf16[256,512]{1,0:T(8,128)(2,1)S(1)}, bf16[256,512]{1,0:T(8,128)(2,1)S(1)}, u32[]{:S(2)}, u32[]{:S(2)}) collective-permute-start(bf16[256,512]{1,0:T(8,128)(2,1)S(1)} %get-tuple-element.45.refs_0_), channel_id=1, source_target_pairs={{0,16},{4,20},{8,24},{12,28},{16,0},{20,4},{24,8},{28,12},{1,17},{... | collective-permute-start | bytes 786440 | tf_op jit(solution)/shard_map/ppermute | solution.py:512
  47.1 12.6 %collective-permute-start.8 = (bf16[256,512]{1,0:T(8,128)(2,1)S(1)}, bf16[256,512]{1,0:T(8,128)(2,1)S(1)}, u32[]{:S(2)}, u32[]{:S(2)}) collective-permute-start(bf16[256,512]{1,0:T(8,128)(2,1)S(1)} %get-tuple-element.45.refs_0_), channel_id=1, source_target_pairs={{0,8},{4,12},{8,0},{12,4},{16,24},{20,28},{24,16},{28,20},{1,9},{5... | collective-permute-start | bytes 786440 | tf_op jit(solution)/shard_map/ppermute | solution.py:512
  47.6 9.6 %collective-permute-start.12 = (bf16[144,512]{1,0:T(8,128)(2,1)S(1)}, bf16[144,512]{1,0:T(8,128)(2,1)S(1)}, u32[]{:S(2)}, u32[]{:S(2)}) collective-permute-start(bf16[144,512]{1,0:T(8,128)(2,1)S(1)} %add_sent.3.keep_ref), channel_id=1, source_target_pairs={{0,2},{1,3},{2,0},{3,1},{4,6},{5,7},{6,4},{7,5},{8,10},{9,11},{10,... | collective-permute-start | bytes 442376 | tf_op jit(solution)/shard_map/ppermute | solution.py:512
  59.8 6.7 %collective-permute-start.13 = (bf16[256,2048]{1,0:T(8,128)(2,1)S(1)}, bf16[256,2048]{1,0:T(8,128)(2,1)S(1)}, u32[]{:S(2)}, u32[]{:S(2)}) collective-permute-start(bf16[256,2048]{1,0:T(8,128)(2,1)S(1)} %side_by_side.1.mine_ref), channel_id=1, source_target_pairs={{0,4},{4,0},{8,12},{12,8},{16,20},{20,16},{24,28},{28,24},{1,5},{5... | collective-permute-start | bytes 3145736 | tf_op jit(solution)/shard_map/ppermute | solution.py:512
  60.4 9.0 %collective-permute-start.14 = (bf16[144,512]{1,0:T(8,128)(2,1)S(1)}, bf16[144,512]{1,0:T(8,128)(2,1)S(1)}, u32[]{:S(2)}, u32[]{:S(2)}) collective-permute-start(bf16[144,512]{1,0:T(8,128)(2,1)S(1)} %add_sent.4.keep_ref), channel_id=1, source_target_pairs={{0,1},{1,0},{2,3},{3,2},{4,5},{5,4},{6,7},{7,6},{8,9},{9,8},{10,11... | collective-permute-start | bytes 442376 | tf_op jit(solution)/shard_map/ppermute | solution.py:512
  69.5 4.1 %collective-permute-start.15 = (f32[48,512]{1,0:T(8,128)S(1)}, f32[48,512]{1,0:T(8,128)S(1)}, u32[]{:S(2)}, u32[]{:S(2)}) collective-permute-start(f32[48,512]{1,0:T(8,128)S(1)} %get-tuple-element.56), channel_id=1, source_target_pairs={{0,8},{4,12},{8,0},{12,4},{16,24},{20,28},{24,16},{28,20},{1,9},{5... | collective-permute-start | bytes 294920 | tf_op jit(solution)/shard_map/ppermute | solution.py:512
  70.4 16.3 %collective-permute-start.21 = (bf16[256,512]{1,0:T(8,128)(2,1)S(1)}, bf16[256,512]{1,0:T(8,128)(2,1)S(1)}, u32[]{:S(2)}, u32[]{:S(2)}) collective-permute-start(bf16[256,512]{1,0:T(8,128)(2,1)S(1)} %get-tuple-element.51), channel_id=1, source_target_pairs={{0,1},{1,0},{2,3},{3,2},{4,5},{5,4},{6,7},{7,6},{8,9},{9,8},{10,11... | collective-permute-start | bytes 786440 | tf_op jit(solution)/shard_map/ppermute | solution.py:512
  70.4 16.3 %collective-permute-start.22 = (bf16[256,512]{1,0:T(8,128)(2,1)S(1)}, bf16[256,512]{1,0:T(8,128)(2,1)S(1)}, u32[]{:S(2)}, u32[]{:S(2)}) collective-permute-start(bf16[256,512]{1,0:T(8,128)(2,1)S(1)} %get-tuple-element.52), channel_id=1, source_target_pairs={{0,2},{1,3},{2,0},{3,1},{4,6},{5,7},{6,4},{7,5},{8,10},{9,11},{10,... | collective-permute-start | bytes 786440 | tf_op jit(solution)/shard_map/ppermute | solution.py:512
  71.7 23.7 %collective-permute-start.23 = (bf16[256,512]{1,0:T(8,128)(2,1)S(1)}, bf16[256,512]{1,0:T(8,128)(2,1)S(1)}, u32[]{:S(2)}, u32[]{:S(2)}) collective-permute-start(bf16[256,512]{1,0:T(8,128)(2,1)S(1)} %get-tuple-element.53), channel_id=1, source_target_pairs={{0,3},{1,2},{2,1},{3,0},{4,7},{5,6},{6,5},{7,4},{8,11},{9,10},{10,... | collective-permute-start | bytes 786440 | tf_op jit(solution)/shard_map/ppermute | solution.py:512
  73.0 3.8 %collective-permute-start.16 = (f32[48,512]{1,0:T(8,128)S(1)}, f32[48,512]{1,0:T(8,128)S(1)}, u32[]{:S(2)}, u32[]{:S(2)}) collective-permute-start(f32[48,512]{1,0:T(8,128)S(1)} %get-tuple-element.57), channel_id=1, source_target_pairs={{0,16},{4,20},{8,24},{12,28},{16,0},{20,4},{24,8},{28,12},{1,17},{... | collective-permute-start | bytes 294920 | tf_op jit(solution)/shard_map/ppermute | solution.py:512
  73.6 4.4 %collective-permute-start.17 = (f32[48,512]{1,0:T(8,128)S(1)}, f32[48,512]{1,0:T(8,128)S(1)}, u32[]{:S(2)}, u32[]{:S(2)}) collective-permute-start(f32[48,512]{1,0:T(8,128)S(1)} %get-tuple-element.58), channel_id=1, source_target_pairs={{0,24},{4,28},{8,16},{12,20},{16,8},{20,12},{24,0},{28,4},{1,25},{... | collective-permute-start | bytes 294920 | tf_op jit(solution)/shard_map/ppermute | solution.py:512
  78.6 4.3 %collective-permute-start.20 = (f32[32,512]{1,0:T(8,128)S(1)}, f32[32,512]{1,0:T(8,128)S(1)}, u32[]{:S(2)}, u32[]{:S(2)}) collective-permute-start(f32[32,512]{1,0:T(8,128)S(1)} %get-tuple-element.59.refs_0_), channel_id=1, source_target_pairs={{0,24},{4,28},{8,16},{12,20},{16,8},{20,12},{24,0},{28,4},{1,25},{... | collective-permute-start | bytes 196616 | tf_op jit(solution)/shard_map/ppermute | solution.py:512
  79.8 4.3 %collective-permute-start.19 = (f32[32,512]{1,0:T(8,128)S(1)}, f32[32,512]{1,0:T(8,128)S(1)}, u32[]{:S(2)}, u32[]{:S(2)}) collective-permute-start(f32[32,512]{1,0:T(8,128)S(1)} %get-tuple-element.59.refs_0_), channel_id=1, source_target_pairs={{0,16},{4,20},{8,24},{12,28},{16,0},{20,4},{24,8},{28,12},{1,17},{... | collective-permute-start | bytes 196616 | tf_op jit(solution)/shard_map/ppermute | solution.py:512
  82.9 3.7 %collective-permute-start.18 = (f32[32,512]{1,0:T(8,128)S(1)}, f32[32,512]{1,0:T(8,128)S(1)}, u32[]{:S(2)}, u32[]{:S(2)}) collective-permute-start(f32[32,512]{1,0:T(8,128)S(1)} %get-tuple-element.59.refs_0_), channel_id=1, source_target_pairs={{0,8},{4,12},{8,0},{12,4},{16,24},{20,28},{24,16},{28,20},{1,9},{5... | collective-permute-start | bytes 196616 | tf_op jit(solution)/shard_map/ppermute | solution.py:512
  95.4 2.9 %collective-permute-start.24 = (f32[128,512]{1,0:T(8,128)S(1)}, f32[128,512]{1,0:T(8,128)S(1)}, u32[]{:S(2)}, u32[]{:S(2)}) collective-permute-start(f32[128,512]{1,0:T(8,128)S(1)} %join.1.mine_ref), channel_id=1, source_target_pairs={{0,4},{4,0},{8,12},{12,8},{16,20},{20,16},{24,28},{28,24},{1,5},{5... | collective-permute-start | bytes 786440 | tf_op jit(solution)/shard_map/ppermute | solution.py:512

commit v5 on v4

--- a/solution.py
+++ b/solution.py
@@ -384,33 +384,38 @@
     )(pinned(dense, resident), mine)
 
 
-def backward_late(dense, early, siblings, n_col, nodes, resident):
+def backward_late(dense, early, siblings, columns, nodes, resident):
     wide, half = siblings.shape
+    first = columns[0]
 
     def kernel(dense_ref, early_ref, siblings_ref, *out_refs):
         step = pl.program_id(0)
-        for m in range(n_col):
-
-            @pl.when(step == m)
+        for i, m in enumerate(columns):
+
+            @pl.when(step == i)
             def _():
                 if resident:
                     block = dense_ref[half : 2 * half, m * nodes : (m + 1) * nodes]
                 else:
                     block = dense_ref[...]
                 out = jnp.dot(siblings_ref[...], block, preferred_element_type=F32)
-                out_refs[m][...] = (early_ref[0] + out).astype(out_refs[m].dtype)
-
-    spec = vmem() if resident else pl.BlockSpec((half, nodes), lambda i: (1, i))
+                out_refs[i][...] = (early_ref[0] + out).astype(out_refs[i].dtype)
+
+    spec = vmem() if resident else pl.BlockSpec((half, nodes), lambda i: (1, i + first))
     whole = lambda shape: pl.BlockSpec(shape, lambda i: (0,) * len(shape))
-    outs = [sds((wide, nodes), F32 if m == 0 else BF16) for m in range(n_col)]
+    outs = [sds((wide, nodes), F32 if m == 0 else BF16) for m in columns]
     return pl.pallas_call(
         kernel,
         out_shape=outs,
-        grid=(n_col,),
-        in_specs=[spec, pl.BlockSpec((1, wide, nodes), lambda i: (i, 0, 0)), whole((wide, half))],
+        grid=(len(columns),),
+        in_specs=[
+            spec,
+            pl.BlockSpec((1, wide, nodes), lambda i: (i + first, 0, 0)),
+            whole((wide, half)),
+        ],
         out_specs=[whole(o.shape) for o in outs],
         compiler_params=params(10 if resident else 32),
-        cost_estimate=cost(2.5),
+        cost_estimate=cost(1.5),
         name="backward_late",
     )(pinned(dense, resident), early, siblings)
 
@@ -571,18 +576,20 @@
     got_last = swap(total, "col", 1)
 
     early = backward_early(dense, mine, n_col, nodes, resident)
-    own, *outs = backward_late(dense, early, siblings, n_col, nodes, resident)
-    back = {m: swap(outs[m - 1], "col", m) for m in far_first(n_col)}
-    back = tuple(back[m] for m in range(1, n_col))
-
-    got_last, _ = lax.optimization_barrier((got_last, outs))
+    far_columns, near_columns = list(range(n_col // 2, n_col)), list(range(n_col // 2))
+    far = backward_late(dense, early, siblings, far_columns, nodes, resident)
+    own, *near = backward_late(dense, early, siblings, near_columns, nodes, resident)
+    far_back = tuple(swap(x, "col", m) for m, x in zip(far_columns, far))
+    near_back = [swap(x, "col", m) for m, x in zip(near_columns[1:], near)]
+
+    got_last, _ = lax.optimization_barrier((got_last, far))
     cuts = chip_parts(add_sent(total, got_last, F32), n_row)
     arrivals = [swap(cuts[j], "row", 2 * j) for j in range(1, chips)]
     piece, grad_bias = share_total([cuts[0]] + arrivals)
     shares = join([piece] + [swap(piece, "row", 2 * j) for j in range(1, chips)])
-    shares, back = lax.optimization_barrier((shares, back))
+    shares, far_back = lax.optimization_barrier((shares, far_back))
     grad_self, grad_neigh = weight_grads(shares, swap(shares, "row", 1), n_row)
-    grad_x = finish(d_pre, w_self, own, back)
+    grad_x = finish(d_pre, w_self, own, [*near_back, *far_back])
     return (hidden, grad_x, grad_self, grad_neigh, grad_bias.reshape(width))
 
 

time: 99.5 us -> 97.3 us (0.978)
  the two profiles are of different devices: /device:TPU:17 before, /device:TPU:0 now
where the time goes in v5:
time: 97.3 us; the launch traced here: 97 us
  waiting for transfers between devices  41.4 us (43%)
  Pallas kernels  28.6 us (29%)
  starting transfers between devices  25.3 us (26%)
    ppermute x25, waiting for transfers between devices, swap(): return lax.ppermute(x, axis, [(i, i ^ mask) for i in range(size)])  41.4 us
    ppermute x25, starting transfers between devices, swap(): return lax.ppermute(x, axis, [(i, i ^ mask) for i in range(size)])  25.3 us
    pallas_call x1, Pallas kernels, densify(): pl.pallas_call(kernel, out_shape=pltpu.VMEM(((rows + 1) * tile, cols * ti...  11.5 us
    pallas_call x1, Pallas kernels, forward_early(): pl.pallas_call(kernel, out_shape=sds((n_row, nodes, width), F32), grid=(n...  4.61 us
    pallas_call x2, Pallas kernels, backward_late(): pl.pallas_call(kernel, out_shape=outs, grid=(len(columns),), in_specs=[sp...  2.9 us
    pallas_call x1, Pallas kernels, backward_early(): pl.pallas_call(kernel, out_shape=sds((n_col, wide, nodes), F32), grid=(n_...  2.88 us
    pallas_call x4, Pallas kernels, forward_late(): pl.pallas_call(kernel, out_shape=sds((count, nodes, width), dtype), grid=...  2.4 us
  transfers between devices with their start and end apart: 25, of which 15 were waited for; matrix products, arithmetic and copies ran while one was open for 1% of the time, Pallas kernels for 26%

profile of v5, /device:TPU:0, one launch (start us, length us, event | category | flops | bytes accessed | tf_op | source)
XLA Modules:
  0.0 97.0 jit_solution(15654515854881835904)
XLA Ops:
  0.6 5.1 %collective-permute-start.1 = (bf16[512,256]{1,0:T(8,128)(2,1)}, bf16[512,256]{1,0:T(8,128)(2,1)S(1)}, u32[]{:S(2)}, u32[]{:S(2)}) collective-permute-start(bf16[512,256]{1,0:T(8,128)(2,1)} %feat_ref.1), channel_id=1, source_target_pairs={{0,3},{1,2},{2,1},{3,0},{4,7},{5,6},{6,5},{7,4},{8,11},{9,10},{10,... | collective-permute-start | bytes 786440 | tf_op jit(solution)/shard_map/ppermute | solution.py:517
  5.7 0.0 collective-permute-start
  5.7 0.6 collective-permute-start.2
  6.4 0.7 fusion.6
  7.1 0.0 copy-start
  7.1 11.5 %densify.1.dense_ref = bf16[4224,2048]{1,0:T(8,128)(2,1)S(1)} custom-call(s32[384]{0:T(512)S(1)} %get-tuple-element.65.down_ref, s32[384]{0:T(512)S(1)} %get-tuple-element.66.right_ref, bf16[384,128,128]{2,1,0:T(8,128)(2,1)} %values_ref.1), custom_call_target="tpu_custom_call" | custom-call | bytes 37000000 | tf_op jit(solution)/shard_map/densify/pallas_call | solution.py:139
  18.6 0.0 collective-permute-done.1.refs_2_
  18.6 0.4 collective-permute-done.refs_1_
  19.0 4.6 %forward_early.1.early_ref = f32[8,512,256]{2,1,0:T(8,128)S(1)} custom-call(bf16[4224,2048]{1,0:T(8,128)(2,1)S(1)} %densify.1.dense_ref, bf16[512,256]{1,0:T(8,128)(2,1)S(1)} %copy-done, bf16[512,256]{1,0:T(8,128)(2,1)S(1)} %collective-permute-done.refs_1_, bf16[512,256]{1,0:T(8,128)(2,1)S(1)} %collective-permute-done.1.refs_2_), custom_call_target="tpu_custom_call" | custom-call | bytes 18500000 | tf_op jit(solution)/shard_map/forward_early/pallas_call | solution.py:174
  23.6 4.6 %collective-permute-done.2.piece_ref = bf16[512,256]{1,0:T(8,128)(2,1)S(1)} collective-permute-done((bf16[512,256]{1,0:T(8,128)(2,1)}, bf16[512,256]{1,0:T(8,128)(2,1)S(1)}, u32[]{:S(2)}, u32[]{:S(2)}) %collective-permute-start.2) | collective-permute-done | bytes 262176 | tf_op jit(solution)/shard_map/ppermute | solution.py:517
  28.3 0.9 forward_late.7
  29.2 0.1 collective-permute-start.4
  29.3 0.3 forward_late.5
  29.6 0.6 collective-permute-start.3
  30.1 0.9 forward_late.6.keep_ref
  31.0 0.5 collective-permute-done.4.got_ref
  31.5 0.1 add_parts.1
  31.7 1.6 %collective-permute-start.5 = (bf16[512,256]{1,0:T(8,128)(2,1)S(1)}, bf16[512,256]{1,0:T(8,128)(2,1)S(1)}, u32[]{:S(2)}, u32[]{:S(2)}) collective-permute-start(bf16[512,256]{1,0:T(8,128)(2,1)S(1)} %get-tuple-element.35), channel_id=1, source_target_pairs={{0,8},{4,12},{8,0},{12,4},{16,24},{20,28},{24,16},{28,20},{1,9},{5... | collective-permute-start | bytes 786440 | tf_op jit(solution)/shard_map/ppermute | solution.py:517
  33.2 1.5 %collective-permute-start.6 = (bf16[512,256]{1,0:T(8,128)(2,1)S(1)}, bf16[512,256]{1,0:T(8,128)(2,1)S(1)}, u32[]{:S(2)}, u32[]{:S(2)}) collective-permute-start(bf16[512,256]{1,0:T(8,128)(2,1)S(1)} %get-tuple-element.36), channel_id=1, source_target_pairs={{0,16},{4,20},{8,24},{12,28},{16,0},{20,4},{24,8},{28,12},{1,17},{... | collective-permute-start | bytes 786440 | tf_op jit(solution)/shard_map/ppermute | solution.py:517
  34.8 0.0 copy-start.5
  34.8 0.5 collective-permute-start.7
  35.3 0.3 forward_late.4.refs_6_
  35.6 0.0 collective-permute-done.3.refs_7_
  35.6 5.3 %collective-permute-done.5.refs_8_ = bf16[512,256]{1,0:T(8,128)(2,1)S(1)} collective-permute-done((bf16[512,256]{1,0:T(8,128)(2,1)S(1)}, bf16[512,256]{1,0:T(8,128)(2,1)S(1)}, u32[]{:S(2)}, u32[]{:S(2)}) %collective-permute-start.5) | collective-permute-done | bytes 262176 | tf_op jit(solution)/shard_map/ppermute | solution.py:517
  40.9 6.0 %collective-permute-done.6.refs_9_ = bf16[512,256]{1,0:T(8,128)(2,1)S(1)} collective-permute-done((bf16[512,256]{1,0:T(8,128)(2,1)S(1)}, bf16[512,256]{1,0:T(8,128)(2,1)S(1)}, u32[]{:S(2)}, u32[]{:S(2)}) %collective-permute-start.6) | collective-permute-done | bytes 262176 | tf_op jit(solution)/shard_map/ppermute | solution.py:517
  47.0 1.2 %middle.1 = (bf16[512,256]{1,0:T(8,128)(2,1)}, bf16[512,256]{1,0:T(8,128)(2,1)S(1)}, bf16[512,256]{1,0:T(8,128)(2,1)S(1)}, bf16[256,512]{1,0:T(8,128)(2,1)S(1)}) custom-call(bf16[512,256]{1,0:T(8,128)(2,1)S(1)} %copy-done, s32[1,512]{1,0:T(1,128)S(1)} %bitcast.3, bf16[512,256]{1,0:T(8,128)(2,1)S(1)} %copy-done.2, bf16[256,256]{1,0:T(8,128)(2,1)S(1)} %copy-done.1, ...), custom_call_target="tpu_custom_call" | custom-call | bytes 5550000 | tf_op jit(solution)/shard_map/middle/pallas_call | solution.py:259
  48.2 0.4 local_grads.1
  48.6 0.1 collective-permute-start.11
  48.6 1.5 %collective-permute-start.10 = (bf16[256,512]{1,0:T(8,128)(2,1)S(1)}, bf16[256,512]{1,0:T(8,128)(2,1)S(1)}, u32[]{:S(2)}, u32[]{:S(2)}) collective-permute-start(bf16[256,512]{1,0:T(8,128)(2,1)S(1)} %get-tuple-element.44.refs_0_), channel_id=1, source_target_pairs={{0,24},{4,28},{8,16},{12,20},{16,8},{20,12},{24,0},{28,4},{1,25},{... | collective-permute-start | bytes 786440 | tf_op jit(solution)/shard_map/ppermute | solution.py:517
  50.2 1.2 %collective-permute-start.9 = (bf16[256,512]{1,0:T(8,128)(2,1)S(1)}, bf16[256,512]{1,0:T(8,128)(2,1)S(1)}, u32[]{:S(2)}, u32[]{:S(2)}) collective-permute-start(bf16[256,512]{1,0:T(8,128)(2,1)S(1)} %get-tuple-element.44.refs_0_), channel_id=1, source_target_pairs={{0,16},{4,20},{8,24},{12,28},{16,0},{20,4},{24,8},{28,12},{1,17},{... | collective-permute-start | bytes 786440 | tf_op jit(solution)/shard_map/ppermute | solution.py:517
  51.4 0.8 collective-permute-start.8
  52.2 0.0 collective-permute-done.11.got_ref
  52.2 0.1 collective-permute-start.12
  52.3 9.2 %collective-permute-done.12.got_ref = bf16[144,512]{1,0:T(8,128)(2,1)S(1)} collective-permute-done((bf16[144,512]{1,0:T(8,128)(2,1)S(1)}, bf16[144,512]{1,0:T(8,128)(2,1)S(1)}, u32[]{:S(2)}, u32[]{:S(2)}) %collective-permute-start.12) | collective-permute-done | bytes 147488 | tf_op jit(solution)/shard_map/ppermute | solution.py:517
  61.6 0.0 collective-permute-done.10.refs_3_
  61.6 2.3 %collective-permute-done.9.refs_2_ = bf16[256,512]{1,0:T(8,128)(2,1)S(1)} collective-permute-done((bf16[256,512]{1,0:T(8,128)(2,1)S(1)}, bf16[256,512]{1,0:T(8,128)(2,1)S(1)}, u32[]{:S(2)}, u32[]{:S(2)}) %collective-permute-start.9) | collective-permute-done | bytes 262176 | tf_op jit(solution)/shard_map/ppermute | solution.py:517
  63.9 0.1 collective-permute-done.8.refs_1_
  64.0 0.1 side_by_side.1.mine_ref
  64.1 0.1 collective-permute-start.13
  64.1 0.1 collective-permute-start.15
  64.2 2.9 %backward_early.1.early_ref = f32[4,256,512]{2,1,0:T(8,128)S(1)} custom-call(bf16[4224,2048]{1,0:T(8,128)(2,1)S(1)} %densify.1.dense_ref, bf16[256,2048]{1,0:T(8,128)(2,1)S(1)} %side_by_side.1.mine_ref), custom_call_target="tpu_custom_call" | custom-call | bytes 9250000 | tf_op jit(solution)/shard_map/backward_early/pallas_call | solution.py:375
  67.1 1.5 %backward_late.3 = (bf16[256,512]{1,0:T(8,128)(2,1)S(1)}, bf16[256,512]{1,0:T(8,128)(2,1)S(1)}) custom-call(bf16[4224,2048]{1,0:T(8,128)(2,1)S(1)} %densify.1.dense_ref, f32[4,256,512]{2,1,0:T(8,128)S(1)} %backward_early.1.early_ref, bf16[256,2048]{1,0:T(8,128)(2,1)S(1)} %collective-permute-done.13.siblings_ref), custom_call_target="tpu_custom_call" | custom-call | bytes 5550000 | tf_op jit(solution)/shard_map/backward_late/pallas_call | solution.py:407
  68.6 3.1 %collective-permute-start.22 = (bf16[256,512]{1,0:T(8,128)(2,1)S(1)}, bf16[256,512]{1,0:T(8,128)(2,1)S(1)}, u32[]{:S(2)}, u32[]{:S(2)}) collective-permute-start(bf16[256,512]{1,0:T(8,128)(2,1)S(1)} %get-tuple-element.51), channel_id=1, source_target_pairs={{0,2},{1,3},{2,0},{3,1},{4,6},{5,7},{6,4},{7,5},{8,10},{9,11},{10,... | collective-permute-start | bytes 786440 | tf_op jit(solution)/shard_map/ppermute | solution.py:517
  71.7 1.3 %collective-permute-start.23 = (bf16[256,512]{1,0:T(8,128)(2,1)S(1)}, bf16[256,512]{1,0:T(8,128)(2,1)S(1)}, u32[]{:S(2)}, u32[]{:S(2)}) collective-permute-start(bf16[256,512]{1,0:T(8,128)(2,1)S(1)} %get-tuple-element.52), channel_id=1, source_target_pairs={{0,3},{1,2},{2,1},{3,0},{4,7},{5,6},{6,5},{7,4},{8,11},{9,10},{10,... | collective-permute-start | bytes 786440 | tf_op jit(solution)/shard_map/ppermute | solution.py:517
  73.0 0.0 collective-permute-done.15.got_ref
  73.1 1.2 %collective-permute-start.16 = (f32[48,512]{1,0:T(8,128)S(1)}, f32[48,512]{1,0:T(8,128)S(1)}, u32[]{:S(2)}, u32[]{:S(2)}) collective-permute-start(f32[48,512]{1,0:T(8,128)S(1)} %get-tuple-element.55), channel_id=1, source_target_pairs={{0,8},{4,12},{8,0},{12,4},{16,24},{20,28},{24,16},{28,20},{1,9},{5... | collective-permute-start | bytes 294920 | tf_op jit(solution)/shard_map/ppermute | solution.py:517
  74.3 0.8 collective-permute-start.17
  75.1 1.5 %collective-permute-start.18 = (f32[48,512]{1,0:T(8,128)S(1)}, f32[48,512]{1,0:T(8,128)S(1)}, u32[]{:S(2)}, u32[]{:S(2)}) collective-permute-start(f32[48,512]{1,0:T(8,128)S(1)} %get-tuple-element.57), channel_id=1, source_target_pairs={{0,24},{4,28},{8,16},{12,20},{16,8},{20,12},{24,0},{28,4},{1,25},{... | collective-permute-start | bytes 294920 | tf_op jit(solution)/shard_map/ppermute | solution.py:517
  76.6 1.6 %collective-permute-done.16.refs_1_ = f32[48,512]{1,0:T(8,128)S(1)} collective-permute-done((f32[48,512]{1,0:T(8,128)S(1)}, f32[48,512]{1,0:T(8,128)S(1)}, u32[]{:S(2)}, u32[]{:S(2)}) %collective-permute-start.16) | collective-permute-done | bytes 98336 | tf_op jit(solution)/shard_map/ppermute | solution.py:517
  78.2 2.7 %collective-permute-done.17.refs_2_ = f32[48,512]{1,0:T(8,128)S(1)} collective-permute-done((f32[48,512]{1,0:T(8,128)S(1)}, f32[48,512]{1,0:T(8,128)S(1)}, u32[]{:S(2)}, u32[]{:S(2)}) %collective-permute-start.17) | collective-permute-done | bytes 98336 | tf_op jit(solution)/shard_map/ppermute | solution.py:517
  80.9 0.0 collective-permute-done.18.refs_3_
  80.9 0.6 share_total.1
  81.5 1.6 %collective-permute-start.21 = (f32[32,512]{1,0:T(8,128)S(1)}, f32[32,512]{1,0:T(8,128)S(1)}, u32[]{:S(2)}, u32[]{:S(2)}) collective-permute-start(f32[32,512]{1,0:T(8,128)S(1)} %get-tuple-element.58.refs_0_), channel_id=1, source_target_pairs={{0,24},{4,28},{8,16},{12,20},{16,8},{20,12},{24,0},{28,4},{1,25},{... | collective-permute-start | bytes 196616 | tf_op jit(solution)/shard_map/ppermute | solution.py:517
  83.1 1.1 %collective-permute-start.20 = (f32[32,512]{1,0:T(8,128)S(1)}, f32[32,512]{1,0:T(8,128)S(1)}, u32[]{:S(2)}, u32[]{:S(2)}) collective-permute-start(f32[32,512]{1,0:T(8,128)S(1)} %get-tuple-element.58.refs_0_), channel_id=1, source_target_pairs={{0,16},{4,20},{8,24},{12,28},{16,0},{20,4},{24,8},{28,12},{1,17},{... | collective-permute-start | bytes 196616 | tf_op jit(solution)/shard_map/ppermute | solution.py:517
  84.1 0.8 collective-permute-start.19
  85.0 1.4 %backward_late.2 = (f32[256,512]{1,0:T(8,128)S(1)}, bf16[256,512]{1,0:T(8,128)(2,1)S(1)}) custom-call(bf16[4224,2048]{1,0:T(8,128)(2,1)S(1)} %densify.1.dense_ref, f32[4,256,512]{2,1,0:T(8,128)S(1)} %backward_early.1.early_ref, bf16[256,2048]{1,0:T(8,128)(2,1)S(1)} %collective-permute-done.13.siblings_ref), custom_call_target="tpu_custom_call" | custom-call | bytes 5550000 | tf_op jit(solution)/shard_map/backward_late/pallas_call | solution.py:407
  86.4 0.2 collective-permute-done.21.refs_3_
  86.6 0.7 collective-permute-done.20.refs_2_
  87.4 1.1 %collective-permute-done.19.refs_1_ = f32[32,512]{1,0:T(8,128)S(1)} collective-permute-done((f32[32,512]{1,0:T(8,128)S(1)}, f32[32,512]{1,0:T(8,128)S(1)}, u32[]{:S(2)}, u32[]{:S(2)}) %collective-permute-start.19) | collective-permute-done | bytes 65568 | tf_op jit(solution)/shard_map/ppermute | solution.py:517
  88.4 1.6 %collective-permute-done.22.refs_1_ = bf16[256,512]{1,0:T(8,128)(2,1)S(1)} collective-permute-done((bf16[256,512]{1,0:T(8,128)(2,1)S(1)}, bf16[256,512]{1,0:T(8,128)(2,1)S(1)}, u32[]{:S(2)}, u32[]{:S(2)}) %collective-permute-start.22) | collective-permute-done | bytes 262176 | tf_op jit(solution)/shard_map/ppermute | solution.py:517
  90.0 5.1 %collective-permute-done.14.refs_0_ = bf16[256,512]{1,0:T(8,128)(2,1)S(1)} collective-permute-done((bf16[256,512]{1,0:T(8,128)(2,1)S(1)}, bf16[256,512]{1,0:T(8,128)(2,1)S(1)}, u32[]{:S(2)}, u32[]{:S(2)}) %collective-permute-start.14) | collective-permute-done | bytes 262176 | tf_op jit(solution)/shard_map/ppermute | solution.py:517
  95.2 1.0 %finish.1 = bf16[512,256]{1,0:T(8,128)(2,1)} custom-call(bf16[512,256]{1,0:T(8,128)(2,1)S(1)} %get-tuple-element.39.d_pre_ref, bf16[256,256]{1,0:T(8,128)(2,1)S(1)} %copy-done.1, f32[256,512]{1,0:T(8,128)S(1)} %get-tuple-element.48.own_ref, bf16[256,512]{1,0:T(8,128)(2,1)S(1)} %collective-permute-done.14.refs_0_, ...), custom_call_target="tpu_custom_call" | custom-call | bytes 3700000 | tf_op jit(solution)/shard_map/finish/pallas_call | solution.py:504
  96.1 0.0 collective-permute-done.24.siblings_ref
  96.1 0.8 weight_grads.1
  (20 shorter events, 0.2 us)
Async XLA Ops:
  0.6 18.0 %collective-permute-start.1 = (bf16[512,256]{1,0:T(8,128)(2,1)}, bf16[512,256]{1,0:T(8,128)(2,1)S(1)}, u32[]{:S(2)}, u32[]{:S(2)}) collective-permute-start(bf16[512,256]{1,0:T(8,128)(2,1)} %feat_ref.1), channel_id=1, source_target_pairs={{0,3},{1,2},{2,1},{3,0},{4,7},{5,6},{6,5},{7,4},{8,11},{9,10},{10,... | collective-permute-start | bytes 786440 | tf_op jit(solution)/shard_map/ppermute | solution.py:517
  5.7 13.3 %collective-permute-start = (bf16[512,256]{1,0:T(8,128)(2,1)}, bf16[512,256]{1,0:T(8,128)(2,1)S(1)}, u32[]{:S(2)}, u32[]{:S(2)}) collective-permute-start(bf16[512,256]{1,0:T(8,128)(2,1)} %feat_ref.1), channel_id=1, source_target_pairs={{0,1},{1,0},{2,3},{3,2},{4,5},{5,4},{6,7},{7,6},{8,9},{9,8},{10,11... | collective-permute-start | bytes 786440 | tf_op jit(solution)/shard_map/ppermute | solution.py:517
  5.7 22.5 %collective-permute-start.2 = (bf16[512,256]{1,0:T(8,128)(2,1)}, bf16[512,256]{1,0:T(8,128)(2,1)S(1)}, u32[]{:S(2)}, u32[]{:S(2)}) collective-permute-start(bf16[512,256]{1,0:T(8,128)(2,1)} %feat_ref.1), channel_id=1, source_target_pairs={{0,2},{1,3},{2,0},{3,1},{4,6},{5,7},{6,4},{7,5},{8,10},{9,11},{10,... | collective-permute-start | bytes 786440 | tf_op jit(solution)/shard_map/ppermute | solution.py:517
  7.1 11.9 %copy-start = (bf16[512,256]{1,0:T(8,128)(2,1)S(1)}, bf16[512,256]{1,0:T(8,128)(2,1)}, u32[]{:S(2)}) copy-start(bf16[512,256]{1,0:T(8,128)(2,1)} %feat_ref.1) | copy-start | bytes 786436
  29.2 2.4 %collective-permute-start.4 = (bf16[3,512,256]{2,1,0:T(8,128)(2,1)S(1)}, bf16[3,512,256]{2,1,0:T(8,128)(2,1)S(1)}, u32[]{:S(2)}, u32[]{:S(2)}) collective-permute-start(bf16[3,512,256]{2,1,0:T(8,128)(2,1)S(1)} %forward_late.7), channel_id=1, source_target_pairs={{0,4},{4,0},{8,12},{12,8},{16,20},{20,16},{24,28},{28,24},{1,5},{5... | collective-permute-start | bytes 2359304 | tf_op jit(solution)/shard_map/ppermute | solution.py:517
  29.6 6.0 %collective-permute-start.3 = (bf16[1,512,256]{2,1,0:T(8,128)(2,1)S(1)}, bf16[1,512,256]{2,1,0:T(8,128)(2,1)S(1)}, u32[]{:S(2)}, u32[]{:S(2)}) collective-permute-start(bf16[1,512,256]{2,1,0:T(8,128)(2,1)S(1)} %forward_late.5), channel_id=1, source_target_pairs={{0,4},{4,0},{8,12},{12,8},{16,20},{20,16},{24,28},{28,24},{1,5},{5... | collective-permute-start | bytes 786440 | tf_op jit(solution)/shard_map/ppermute | solution.py:517
  31.7 9.2 %collective-permute-start.5 = (bf16[512,256]{1,0:T(8,128)(2,1)S(1)}, bf16[512,256]{1,0:T(8,128)(2,1)S(1)}, u32[]{:S(2)}, u32[]{:S(2)}) collective-permute-start(bf16[512,256]{1,0:T(8,128)(2,1)S(1)} %get-tuple-element.35), channel_id=1, source_target_pairs={{0,8},{4,12},{8,0},{12,4},{16,24},{20,28},{24,16},{28,20},{1,9},{5... | collective-permute-start | bytes 786440 | tf_op jit(solution)/shard_map/ppermute | solution.py:517
  33.2 13.7 %collective-permute-start.6 = (bf16[512,256]{1,0:T(8,128)(2,1)S(1)}, bf16[512,256]{1,0:T(8,128)(2,1)S(1)}, u32[]{:S(2)}, u32[]{:S(2)}) collective-permute-start(bf16[512,256]{1,0:T(8,128)(2,1)S(1)} %get-tuple-element.36), channel_id=1, source_target_pairs={{0,16},{4,20},{8,24},{12,28},{16,0},{20,4},{24,8},{28,12},{1,17},{... | collective-permute-start | bytes 786440 | tf_op jit(solution)/shard_map/ppermute | solution.py:517
  34.8 12.2 %copy-start.1 = (bf16[256,256]{1,0:T(8,128)(2,1)S(1)}, bf16[256,256]{1,0:T(8,128)(2,1)}, u32[]{:S(2)}) copy-start(bf16[256,256]{1,0:T(8,128)(2,1)} %ws_ref.1) | copy-start | bytes 393220
  34.8 12.2 %copy-start.2 = (bf16[512,256]{1,0:T(8,128)(2,1)S(1)}, bf16[512,256]{1,0:T(8,128)(2,1)}, u32[]{:S(2)}) copy-start(bf16[512,256]{1,0:T(8,128)(2,1)} %refs_2_.1) | copy-start | bytes 786436
  34.8 12.2 %copy-start.3 = (bf16[256,256]{1,0:T(8,128)(2,1)S(1)}, bf16[256,256]{1,0:T(8,128)(2,1)}, u32[]{:S(2)}) copy-start(bf16[256,256]{1,0:T(8,128)(2,1)} %refs_4_.1) | copy-start | bytes 393220
  34.8 12.2 %copy-start.4 = (s32[512]{0:T(512)S(1)}, s32[512]{0:T(512)}, u32[]{:S(2)}) copy-start(s32[512]{0:T(512)} %param.10) | copy-start | bytes 6148
  34.8 12.2 %copy-start.5 = (f32[256]{0:T(256)S(1)}, f32[256]{0:T(256)}, u32[]{:S(2)}) copy-start(f32[256]{0:T(256)} %param.17) | copy-start | bytes 3076
  34.8 12.1 %collective-permute-start.7 = (bf16[512,256]{1,0:T(8,128)(2,1)S(1)}, bf16[512,256]{1,0:T(8,128)(2,1)S(1)}, u32[]{:S(2)}, u32[]{:S(2)}) collective-permute-start(bf16[512,256]{1,0:T(8,128)(2,1)S(1)} %get-tuple-element.37), channel_id=1, source_target_pairs={{0,24},{4,28},{8,16},{12,20},{16,8},{20,12},{24,0},{28,4},{1,25},{... | collective-permute-start | bytes 786440 | tf_op jit(solution)/shard_map/ppermute | solution.py:517
  48.6 3.6 %collective-permute-start.11 = (bf16[144,512]{1,0:T(8,128)(2,1)S(1)}, bf16[144,512]{1,0:T(8,128)(2,1)S(1)}, u32[]{:S(2)}, u32[]{:S(2)}) collective-permute-start(bf16[144,512]{1,0:T(8,128)(2,1)S(1)} %get-tuple-element.43), channel_id=1, source_target_pairs={{0,4},{4,0},{8,12},{12,8},{16,20},{20,16},{24,28},{28,24},{1,5},{5... | collective-permute-start | bytes 442376 | tf_op jit(solution)/shard_map/ppermute | solution.py:517
  48.6 12.9 %collective-permute-start.10 = (bf16[256,512]{1,0:T(8,128)(2,1)S(1)}, bf16[256,512]{1,0:T(8,128)(2,1)S(1)}, u32[]{:S(2)}, u32[]{:S(2)}) collective-permute-start(bf16[256,512]{1,0:T(8,128)(2,1)S(1)} %get-tuple-element.44.refs_0_), channel_id=1, source_target_pairs={{0,24},{4,28},{8,16},{12,20},{16,8},{20,12},{24,0},{28,4},{1,25},{... | collective-permute-start | bytes 786440 | tf_op jit(solution)/shard_map/ppermute | solution.py:517
  50.2 13.7 %collective-permute-start.9 = (bf16[256,512]{1,0:T(8,128)(2,1)S(1)}, bf16[256,512]{1,0:T(8,128)(2,1)S(1)}, u32[]{:S(2)}, u32[]{:S(2)}) collective-permute-start(bf16[256,512]{1,0:T(8,128)(2,1)S(1)} %get-tuple-element.44.refs_0_), channel_id=1, source_target_pairs={{0,16},{4,20},{8,24},{12,28},{16,0},{20,4},{24,8},{28,12},{1,17},{... | collective-permute-start | bytes 786440 | tf_op jit(solution)/shard_map/ppermute | solution.py:517
  51.4 12.6 %collective-permute-start.8 = (bf16[256,512]{1,0:T(8,128)(2,1)S(1)}, bf16[256,512]{1,0:T(8,128)(2,1)S(1)}, u32[]{:S(2)}, u32[]{:S(2)}) collective-permute-start(bf16[256,512]{1,0:T(8,128)(2,1)S(1)} %get-tuple-element.44.refs_0_), channel_id=1, source_target_pairs={{0,8},{4,12},{8,0},{12,4},{16,24},{20,28},{24,16},{28,20},{1,9},{5... | collective-permute-start | bytes 786440 | tf_op jit(solution)/shard_map/ppermute | solution.py:517
  52.2 9.3 %collective-permute-start.12 = (bf16[144,512]{1,0:T(8,128)(2,1)S(1)}, bf16[144,512]{1,0:T(8,128)(2,1)S(1)}, u32[]{:S(2)}, u32[]{:S(2)}) collective-permute-start(bf16[144,512]{1,0:T(8,128)(2,1)S(1)} %add_sent.3.keep_ref), channel_id=1, source_target_pairs={{0,2},{1,3},{2,0},{3,1},{4,6},{5,7},{6,4},{7,5},{8,10},{9,11},{10,... | collective-permute-start | bytes 442376 | tf_op jit(solution)/shard_map/ppermute | solution.py:517
  64.1 3.0 %collective-permute-start.13 = (bf16[256,2048]{1,0:T(8,128)(2,1)S(1)}, bf16[256,2048]{1,0:T(8,128)(2,1)S(1)}, u32[]{:S(2)}, u32[]{:S(2)}) collective-permute-start(bf16[256,2048]{1,0:T(8,128)(2,1)S(1)} %side_by_side.1.mine_ref), channel_id=1, source_target_pairs={{0,4},{4,0},{8,12},{12,8},{16,20},{20,16},{24,28},{28,24},{1,5},{5... | collective-permute-start | bytes 3145736 | tf_op jit(solution)/shard_map/ppermute | solution.py:517
  64.1 8.9 %collective-permute-start.15 = (bf16[144,512]{1,0:T(8,128)(2,1)S(1)}, bf16[144,512]{1,0:T(8,128)(2,1)S(1)}, u32[]{:S(2)}, u32[]{:S(2)}) collective-permute-start(bf16[144,512]{1,0:T(8,128)(2,1)S(1)} %add_sent.4.keep_ref), channel_id=1, source_target_pairs={{0,1},{1,0},{2,3},{3,2},{4,5},{5,4},{6,7},{7,6},{8,9},{9,8},{10,11... | collective-permute-start | bytes 442376 | tf_op jit(solution)/shard_map/ppermute | solution.py:517
  68.6 21.4 %collective-permute-start.22 = (bf16[256,512]{1,0:T(8,128)(2,1)S(1)}, bf16[256,512]{1,0:T(8,128)(2,1)S(1)}, u32[]{:S(2)}, u32[]{:S(2)}) collective-permute-start(bf16[256,512]{1,0:T(8,128)(2,1)S(1)} %get-tuple-element.51), channel_id=1, source_target_pairs={{0,2},{1,3},{2,0},{3,1},{4,6},{5,7},{6,4},{7,5},{8,10},{9,11},{10,... | collective-permute-start | bytes 786440 | tf_op jit(solution)/shard_map/ppermute | solution.py:517
  71.7 18.4 %collective-permute-start.23 = (bf16[256,512]{1,0:T(8,128)(2,1)S(1)}, bf16[256,512]{1,0:T(8,128)(2,1)S(1)}, u32[]{:S(2)}, u32[]{:S(2)}) collective-permute-start(bf16[256,512]{1,0:T(8,128)(2,1)S(1)} %get-tuple-element.52), channel_id=1, source_target_pairs={{0,3},{1,2},{2,1},{3,0},{4,7},{5,6},{6,5},{7,4},{8,11},{9,10},{10,... | collective-permute-start | bytes 786440 | tf_op jit(solution)/shard_map/ppermute | solution.py:517
  73.1 5.1 %collective-permute-start.16 = (f32[48,512]{1,0:T(8,128)S(1)}, f32[48,512]{1,0:T(8,128)S(1)}, u32[]{:S(2)}, u32[]{:S(2)}) collective-permute-start(f32[48,512]{1,0:T(8,128)S(1)} %get-tuple-element.55), channel_id=1, source_target_pairs={{0,8},{4,12},{8,0},{12,4},{16,24},{20,28},{24,16},{28,20},{1,9},{5... | collective-permute-start | bytes 294920 | tf_op jit(solution)/shard_map/ppermute | solution.py:517
  74.3 6.6 %collective-permute-start.17 = (f32[48,512]{1,0:T(8,128)S(1)}, f32[48,512]{1,0:T(8,128)S(1)}, u32[]{:S(2)}, u32[]{:S(2)}) collective-permute-start(f32[48,512]{1,0:T(8,128)S(1)} %get-tuple-element.56), channel_id=1, source_target_pairs={{0,16},{4,20},{8,24},{12,28},{16,0},{20,4},{24,8},{28,12},{1,17},{... | collective-permute-start | bytes 294920 | tf_op jit(solution)/shard_map/ppermute | solution.py:517
  75.1 5.8 %collective-permute-start.18 = (f32[48,512]{1,0:T(8,128)S(1)}, f32[48,512]{1,0:T(8,128)S(1)}, u32[]{:S(2)}, u32[]{:S(2)}) collective-permute-start(f32[48,512]{1,0:T(8,128)S(1)} %get-tuple-element.57), channel_id=1, source_target_pairs={{0,24},{4,28},{8,16},{12,20},{16,8},{20,12},{24,0},{28,4},{1,25},{... | collective-permute-start | bytes 294920 | tf_op jit(solution)/shard_map/ppermute | solution.py:517
  81.5 5.2 %collective-permute-start.21 = (f32[32,512]{1,0:T(8,128)S(1)}, f32[32,512]{1,0:T(8,128)S(1)}, u32[]{:S(2)}, u32[]{:S(2)}) collective-permute-start(f32[32,512]{1,0:T(8,128)S(1)} %get-tuple-element.58.refs_0_), channel_id=1, source_target_pairs={{0,24},{4,28},{8,16},{12,20},{16,8},{20,12},{24,0},{28,4},{1,25},{... | collective-permute-start | bytes 196616 | tf_op jit(solution)/shard_map/ppermute | solution.py:517
  83.1 4.3 %collective-permute-start.20 = (f32[32,512]{1,0:T(8,128)S(1)}, f32[32,512]{1,0:T(8,128)S(1)}, u32[]{:S(2)}, u32[]{:S(2)}) collective-permute-start(f32[32,512]{1,0:T(8,128)S(1)} %get-tuple-element.58.refs_0_), channel_id=1, source_target_pairs={{0,16},{4,20},{8,24},{12,28},{16,0},{20,4},{24,8},{28,12},{1,17},{... | collective-permute-start | bytes 196616 | tf_op jit(solution)/shard_map/ppermute | solution.py:517
  84.1 4.3 %collective-permute-start.19 = (f32[32,512]{1,0:T(8,128)S(1)}, f32[32,512]{1,0:T(8,128)S(1)}, u32[]{:S(2)}, u32[]{:S(2)}) collective-permute-start(f32[32,512]{1,0:T(8,128)S(1)} %get-tuple-element.58.refs_0_), channel_id=1, source_target_pairs={{0,8},{4,12},{8,0},{12,4},{16,24},{20,28},{24,16},{28,20},{1,9},{5... | collective-permute-start | bytes 196616 | tf_op jit(solution)/shard_map/ppermute | solution.py:517
  86.6 8.5 %collective-permute-start.14 = (bf16[256,512]{1,0:T(8,128)(2,1)S(1)}, bf16[256,512]{1,0:T(8,128)(2,1)S(1)}, u32[]{:S(2)}, u32[]{:S(2)}) collective-permute-start(bf16[256,512]{1,0:T(8,128)(2,1)S(1)} %get-tuple-element.49), channel_id=1, source_target_pairs={{0,1},{1,0},{2,3},{3,2},{4,5},{5,4},{6,7},{7,6},{8,9},{9,8},{10,11... | collective-permute-start | bytes 786440 | tf_op jit(solution)/shard_map/ppermute | solution.py:517
  90.0 6.1 %collective-permute-start.24 = (f32[128,512]{1,0:T(8,128)S(1)}, f32[128,512]{1,0:T(8,128)S(1)}, u32[]{:S(2)}, u32[]{:S(2)}) collective-permute-start(f32[128,512]{1,0:T(8,128)S(1)} %join.1.mine_ref), channel_id=1, source_target_pairs={{0,4},{4,0},{8,12},{12,8},{16,20},{20,16},{24,28},{28,24},{1,5},{5... | collective-permute-start | bytes 786440 | tf_op jit(solution)/shard_map/ppermute | solution.py:517

commit v6 on v5

--- a/solution.py
+++ b/solution.py
@@ -462,12 +462,13 @@
     )(*pieces)
 
 
-def weight_grads(mine, siblings, n_row):
+def finish(mine, siblings, d_pre, w_self, own, arrived, n_row):
     chips = n_row // 2
     share = mine.shape[0] // chips
-    width = mine.shape[1] // 2
-
-    def kernel(mine_ref, siblings_ref, self_ref, neigh_ref):
+    nodes, width = d_pre.shape
+
+    def kernel(mine_ref, siblings_ref, d_pre_ref, ws_ref, own_ref, *refs):
+        self_ref, neigh_ref, out_ref = refs[-3:]
         chip = lax.axis_index("row") // 2
         core = lax.axis_index("row") % 2
         for k, ref in enumerate((mine_ref, siblings_ref)):
@@ -476,40 +477,23 @@
                 low = j * share
                 self_ref[pl.ds(at, share), :] = ref[low : low + share, 0:width]
                 neigh_ref[pl.ds(at, share), :] = ref[low : low + share, width:]
-
-    return pl.pallas_call(
-        kernel,
-        out_shape=[sds((width, width), F32)] * 2,
-        in_specs=[vmem()] * 2,
-        out_specs=[vmem()] * 2,
-        compiler_params=params(8),
-        cost_estimate=cost(1),
-        name="weight_grads",
-    )(mine, siblings)
-
-
-def finish(d_pre, w_self, own, arrived):
-    nodes, width = d_pre.shape
-
-    def kernel(d_pre_ref, ws_ref, own_ref, *refs):
-        out_ref = refs[-1]
         direct = lax.dot_general(
             d_pre_ref[...], ws_ref[...], (((1,), (1,)), ((), ())), preferred_element_type=F32
         )
         acc = own_ref[...]
-        for ref in refs[:-1]:
+        for ref in refs[:-3]:
             acc = acc + ref[...].astype(F32)
         out_ref[...] = (direct + jnp.transpose(acc)).astype(BF16)
 
     return pl.pallas_call(
         kernel,
-        out_shape=sds((nodes, width), BF16),
-        in_specs=[vmem()] * (3 + len(arrived)),
-        out_specs=vmem(),
-        compiler_params=params(8),
+        out_shape=[sds((width, width), F32)] * 2 + [sds((nodes, width), BF16)],
+        in_specs=[vmem()] * (5 + len(arrived)),
+        out_specs=[vmem()] * 3,
+        compiler_params=params(12),
         cost_estimate=cost(1),
         name="finish",
-    )(d_pre, w_self, own, *arrived)
+    )(mine, siblings, d_pre, w_self, own, *arrived)
 
 
 def swap(x, axis, mask):
@@ -588,8 +572,9 @@
     piece, grad_bias = share_total([cuts[0]] + arrivals)
     shares = join([piece] + [swap(piece, "row", 2 * j) for j in range(1, chips)])
     shares, far_back = lax.optimization_barrier((shares, far_back))
-    grad_self, grad_neigh = weight_grads(shares, swap(shares, "row", 1), n_row)
-    grad_x = finish(d_pre, w_self, own, [*near_back, *far_back])
+    siblings = swap(shares, "row", 1)
+    back = [*near_back, *far_back]
+    grad_self, grad_neigh, grad_x = finish(shares, siblings, d_pre, w_self, own, back, n_row)
     return (hidden, grad_x, grad_self, grad_neigh, grad_bias.reshape(width))
 
 

time: 97.3 us -> 96.6 us (level)
  transfers between devices with their start and end apart: 25 -> 25, of which waited for: 15 -> 15; matrix products, arithmetic and copies ran while one was open for 1% -> 1% of each run, Pallas kernels for 26% -> 25%
where the time goes in v6:
time: 96.6 us; the launch traced here: 96.3 us
  waiting for transfers between devices  41.4 us (43%)
  Pallas kernels  27.9 us (29%)
  starting transfers between devices  25.3 us (26%)
    ppermute x25, waiting for transfers between devices, swap(): return lax.ppermute(x, axis, [(i, i ^ mask) for i in range(size)])  41.4 us
    ppermute x25, starting transfers between devices, swap(): return lax.ppermute(x, axis, [(i, i ^ mask) for i in range(size)])  25.3 us
    pallas_call x1, Pallas kernels, densify(): pl.pallas_call(kernel, out_shape=pltpu.VMEM(((rows + 1) * tile, cols * ti...  11.5 us
    pallas_call x1, Pallas kernels, forward_early(): pl.pallas_call(kernel, out_shape=sds((n_row, nodes, width), F32), grid=(n...  4.61 us
    pallas_call x2, Pallas kernels, backward_late(): pl.pallas_call(kernel, out_shape=outs, grid=(len(columns),), in_specs=[sp...  2.9 us
    pallas_call x1, Pallas kernels, backward_early(): pl.pallas_call(kernel, out_shape=sds((n_col, wide, nodes), F32), grid=(n_...  2.88 us
    pallas_call x4, Pallas kernels, forward_late(): pl.pallas_call(kernel, out_shape=sds((count, nodes, width), dtype), grid=...  2.4 us
  transfers between devices with their start and end apart: 25, of which 15 were waited for; matrix products, arithmetic and copies ran while one was open for 1% of the time, Pallas kernels for 25%

profile of v6, /device:TPU:0, one launch (start us, length us, event | category | flops | bytes accessed | tf_op | source)
XLA Modules:
  0.0 96.3 jit_solution(1138512182426981309)
XLA Ops:
  0.6 5.1 %collective-permute-start.1 = (bf16[512,256]{1,0:T(8,128)(2,1)}, bf16[512,256]{1,0:T(8,128)(2,1)S(1)}, u32[]{:S(2)}, u32[]{:S(2)}) collective-permute-start(bf16[512,256]{1,0:T(8,128)(2,1)} %feat_ref.1), channel_id=1, source_target_pairs={{0,3},{1,2},{2,1},{3,0},{4,7},{5,6},{6,5},{7,4},{8,11},{9,10},{10,... | collective-permute-start | bytes 786440 | tf_op jit(solution)/shard_map/ppermute | solution.py:501
  5.7 0.0 collective-permute-start
  5.7 0.6 collective-permute-start.2
  6.4 0.7 fusion.6
  7.1 0.0 copy-start
  7.1 11.5 %densify.1.dense_ref = bf16[4224,2048]{1,0:T(8,128)(2,1)S(1)} custom-call(s32[384]{0:T(512)S(1)} %get-tuple-element.67.down_ref, s32[384]{0:T(512)S(1)} %get-tuple-element.68.right_ref, bf16[384,128,128]{2,1,0:T(8,128)(2,1)} %values_ref.1), custom_call_target="tpu_custom_call" | custom-call | bytes 37000000 | tf_op jit(solution)/shard_map/densify/pallas_call | solution.py:139
  18.6 0.0 collective-permute-done.1.refs_2_
  18.6 0.4 collective-permute-done.refs_1_
  19.0 4.6 %forward_early.1.early_ref = f32[8,512,256]{2,1,0:T(8,128)S(1)} custom-call(bf16[4224,2048]{1,0:T(8,128)(2,1)S(1)} %densify.1.dense_ref, bf16[512,256]{1,0:T(8,128)(2,1)S(1)} %copy-done, bf16[512,256]{1,0:T(8,128)(2,1)S(1)} %collective-permute-done.refs_1_, bf16[512,256]{1,0:T(8,128)(2,1)S(1)} %collective-permute-done.1.refs_2_), custom_call_target="tpu_custom_call" | custom-call | bytes 18500000 | tf_op jit(solution)/shard_map/forward_early/pallas_call | solution.py:174
  23.6 4.6 %collective-permute-done.2.piece_ref = bf16[512,256]{1,0:T(8,128)(2,1)S(1)} collective-permute-done((bf16[512,256]{1,0:T(8,128)(2,1)}, bf16[512,256]{1,0:T(8,128)(2,1)S(1)}, u32[]{:S(2)}, u32[]{:S(2)}) %collective-permute-start.2) | collective-permute-done | bytes 262176 | tf_op jit(solution)/shard_map/ppermute | solution.py:501
  28.3 0.9 forward_late.7
  29.2 0.1 collective-permute-start.4
  29.3 0.3 forward_late.5
  29.6 0.6 collective-permute-start.3
  30.1 0.9 forward_late.6.keep_ref
  31.0 0.5 collective-permute-done.4.got_ref
  31.5 0.1 add_parts.1
  31.7 1.6 %collective-permute-start.5 = (bf16[512,256]{1,0:T(8,128)(2,1)S(1)}, bf16[512,256]{1,0:T(8,128)(2,1)S(1)}, u32[]{:S(2)}, u32[]{:S(2)}) collective-permute-start(bf16[512,256]{1,0:T(8,128)(2,1)S(1)} %get-tuple-element.36), channel_id=1, source_target_pairs={{0,8},{4,12},{8,0},{12,4},{16,24},{20,28},{24,16},{28,20},{1,9},{5... | collective-permute-start | bytes 786440 | tf_op jit(solution)/shard_map/ppermute | solution.py:501
  33.2 1.5 %collective-permute-start.6 = (bf16[512,256]{1,0:T(8,128)(2,1)S(1)}, bf16[512,256]{1,0:T(8,128)(2,1)S(1)}, u32[]{:S(2)}, u32[]{:S(2)}) collective-permute-start(bf16[512,256]{1,0:T(8,128)(2,1)S(1)} %get-tuple-element.37), channel_id=1, source_target_pairs={{0,16},{4,20},{8,24},{12,28},{16,0},{20,4},{24,8},{28,12},{1,17},{... | collective-permute-start | bytes 786440 | tf_op jit(solution)/shard_map/ppermute | solution.py:501
  34.8 0.0 copy-start.5
  34.8 0.5 collective-permute-start.7
  35.3 0.3 forward_late.4.refs_6_
  35.6 0.0 collective-permute-done.3.refs_7_
  35.6 5.3 %collective-permute-done.5.refs_8_ = bf16[512,256]{1,0:T(8,128)(2,1)S(1)} collective-permute-done((bf16[512,256]{1,0:T(8,128)(2,1)S(1)}, bf16[512,256]{1,0:T(8,128)(2,1)S(1)}, u32[]{:S(2)}, u32[]{:S(2)}) %collective-permute-start.5) | collective-permute-done | bytes 262176 | tf_op jit(solution)/shard_map/ppermute | solution.py:501
  40.9 6.0 %collective-permute-done.6.refs_9_ = bf16[512,256]{1,0:T(8,128)(2,1)S(1)} collective-permute-done((bf16[512,256]{1,0:T(8,128)(2,1)S(1)}, bf16[512,256]{1,0:T(8,128)(2,1)S(1)}, u32[]{:S(2)}, u32[]{:S(2)}) %collective-permute-start.6) | collective-permute-done | bytes 262176 | tf_op jit(solution)/shard_map/ppermute | solution.py:501
  46.9 0.0 collective-permute-done.7.refs_10_
  47.0 1.2 %middle.1 = (bf16[512,256]{1,0:T(8,128)(2,1)}, bf16[512,256]{1,0:T(8,128)(2,1)S(1)}, bf16[512,256]{1,0:T(8,128)(2,1)S(1)}, bf16[256,512]{1,0:T(8,128)(2,1)S(1)}) custom-call(bf16[512,256]{1,0:T(8,128)(2,1)S(1)} %copy-done, s32[1,512]{1,0:T(1,128)S(1)} %bitcast.3, bf16[512,256]{1,0:T(8,128)(2,1)S(1)} %copy-done.2, bf16[256,256]{1,0:T(8,128)(2,1)S(1)} %copy-done.1, ...), custom_call_target="tpu_custom_call" | custom-call | bytes 5550000 | tf_op jit(solution)/shard_map/middle/pallas_call | solution.py:259
  48.2 0.4 local_grads.1
  48.6 0.1 collective-permute-start.11
  48.6 1.5 %collective-permute-start.10 = (bf16[256,512]{1,0:T(8,128)(2,1)S(1)}, bf16[256,512]{1,0:T(8,128)(2,1)S(1)}, u32[]{:S(2)}, u32[]{:S(2)}) collective-permute-start(bf16[256,512]{1,0:T(8,128)(2,1)S(1)} %get-tuple-element.46.refs_0_), channel_id=1, source_target_pairs={{0,24},{4,28},{8,16},{12,20},{16,8},{20,12},{24,0},{28,4},{1,25},{... | collective-permute-start | bytes 786440 | tf_op jit(solution)/shard_map/ppermute | solution.py:501
  50.2 1.2 %collective-permute-start.9 = (bf16[256,512]{1,0:T(8,128)(2,1)S(1)}, bf16[256,512]{1,0:T(8,128)(2,1)S(1)}, u32[]{:S(2)}, u32[]{:S(2)}) collective-permute-start(bf16[256,512]{1,0:T(8,128)(2,1)S(1)} %get-tuple-element.46.refs_0_), channel_id=1, source_target_pairs={{0,16},{4,20},{8,24},{12,28},{16,0},{20,4},{24,8},{28,12},{1,17},{... | collective-permute-start | bytes 786440 | tf_op jit(solution)/shard_map/ppermute | solution.py:501
  51.4 0.8 collective-permute-start.8
  52.2 0.0 collective-permute-done.11.got_ref
  52.2 0.1 collective-permute-start.12
  52.3 9.2 %collective-permute-done.12.got_ref = bf16[144,512]{1,0:T(8,128)(2,1)S(1)} collective-permute-done((bf16[144,512]{1,0:T(8,128)(2,1)S(1)}, bf16[144,512]{1,0:T(8,128)(2,1)S(1)}, u32[]{:S(2)}, u32[]{:S(2)}) %collective-permute-start.12) | collective-permute-done | bytes 147488 | tf_op jit(solution)/shard_map/ppermute | solution.py:501
  61.6 0.0 collective-permute-done.10.refs_3_
  61.6 2.3 %collective-permute-done.9.refs_2_ = bf16[256,512]{1,0:T(8,128)(2,1)S(1)} collective-permute-done((bf16[256,512]{1,0:T(8,128)(2,1)S(1)}, bf16[256,512]{1,0:T(8,128)(2,1)S(1)}, u32[]{:S(2)}, u32[]{:S(2)}) %collective-permute-start.9) | collective-permute-done | bytes 262176 | tf_op jit(solution)/shard_map/ppermute | solution.py:501
  63.9 0.1 collective-permute-done.8.refs_1_
  64.0 0.1 side_by_side.1.mine_ref
  64.1 0.1 collective-permute-start.14
  64.1 0.1 collective-permute-start.13
  64.2 2.9 %backward_early.1.early_ref = f32[4,256,512]{2,1,0:T(8,128)S(1)} custom-call(bf16[4224,2048]{1,0:T(8,128)(2,1)S(1)} %densify.1.dense_ref, bf16[256,2048]{1,0:T(8,128)(2,1)S(1)} %side_by_side.1.mine_ref), custom_call_target="tpu_custom_call" | custom-call | bytes 9250000 | tf_op jit(solution)/shard_map/backward_early/pallas_call | solution.py:375
  67.1 1.5 %backward_late.2 = (bf16[256,512]{1,0:T(8,128)(2,1)S(1)}, bf16[256,512]{1,0:T(8,128)(2,1)S(1)}) custom-call(bf16[4224,2048]{1,0:T(8,128)(2,1)S(1)} %densify.1.dense_ref, f32[4,256,512]{2,1,0:T(8,128)S(1)} %backward_early.1.early_ref, bf16[256,2048]{1,0:T(8,128)(2,1)S(1)} %collective-permute-done.14.siblings_ref), custom_call_target="tpu_custom_call" | custom-call | bytes 5550000 | tf_op jit(solution)/shard_map/backward_late/pallas_call | solution.py:407
  68.6 3.1 %collective-permute-start.21 = (bf16[256,512]{1,0:T(8,128)(2,1)S(1)}, bf16[256,512]{1,0:T(8,128)(2,1)S(1)}, u32[]{:S(2)}, u32[]{:S(2)}) collective-permute-start(bf16[256,512]{1,0:T(8,128)(2,1)S(1)} %get-tuple-element.50), channel_id=1, source_target_pairs={{0,2},{1,3},{2,0},{3,1},{4,6},{5,7},{6,4},{7,5},{8,10},{9,11},{10,... | collective-permute-start | bytes 786440 | tf_op jit(solution)/shard_map/ppermute | solution.py:501
  71.7 1.3 %collective-permute-start.22 = (bf16[256,512]{1,0:T(8,128)(2,1)S(1)}, bf16[256,512]{1,0:T(8,128)(2,1)S(1)}, u32[]{:S(2)}, u32[]{:S(2)}) collective-permute-start(bf16[256,512]{1,0:T(8,128)(2,1)S(1)} %get-tuple-element.51), channel_id=1, source_target_pairs={{0,3},{1,2},{2,1},{3,0},{4,7},{5,6},{6,5},{7,4},{8,11},{9,10},{10,... | collective-permute-start | bytes 786440 | tf_op jit(solution)/shard_map/ppermute | solution.py:501
  73.0 0.0 collective-permute-done.13.got_ref
  73.1 1.2 %collective-permute-start.15 = (f32[48,512]{1,0:T(8,128)S(1)}, f32[48,512]{1,0:T(8,128)S(1)}, u32[]{:S(2)}, u32[]{:S(2)}) collective-permute-start(f32[48,512]{1,0:T(8,128)S(1)} %get-tuple-element.54), channel_id=1, source_target_pairs={{0,8},{4,12},{8,0},{12,4},{16,24},{20,28},{24,16},{28,20},{1,9},{5... | collective-permute-start | bytes 294920 | tf_op jit(solution)/shard_map/ppermute | solution.py:501
  74.3 0.8 collective-permute-start.16
  75.1 1.5 %collective-permute-start.17 = (f32[48,512]{1,0:T(8,128)S(1)}, f32[48,512]{1,0:T(8,128)S(1)}, u32[]{:S(2)}, u32[]{:S(2)}) collective-permute-start(f32[48,512]{1,0:T(8,128)S(1)} %get-tuple-element.56), channel_id=1, source_target_pairs={{0,24},{4,28},{8,16},{12,20},{16,8},{20,12},{24,0},{28,4},{1,25},{... | collective-permute-start | bytes 294920 | tf_op jit(solution)/shard_map/ppermute | solution.py:501
  76.6 1.6 %collective-permute-done.15.refs_1_ = f32[48,512]{1,0:T(8,128)S(1)} collective-permute-done((f32[48,512]{1,0:T(8,128)S(1)}, f32[48,512]{1,0:T(8,128)S(1)}, u32[]{:S(2)}, u32[]{:S(2)}) %collective-permute-start.15) | collective-permute-done | bytes 98336 | tf_op jit(solution)/shard_map/ppermute | solution.py:501
  78.2 2.7 %collective-permute-done.16.refs_2_ = f32[48,512]{1,0:T(8,128)S(1)} collective-permute-done((f32[48,512]{1,0:T(8,128)S(1)}, f32[48,512]{1,0:T(8,128)S(1)}, u32[]{:S(2)}, u32[]{:S(2)}) %collective-permute-start.16) | collective-permute-done | bytes 98336 | tf_op jit(solution)/shard_map/ppermute | solution.py:501
  80.9 0.0 collective-permute-done.17.refs_3_
  80.9 0.6 share_total.1
  81.5 1.6 %collective-permute-start.20 = (f32[32,512]{1,0:T(8,128)S(1)}, f32[32,512]{1,0:T(8,128)S(1)}, u32[]{:S(2)}, u32[]{:S(2)}) collective-permute-start(f32[32,512]{1,0:T(8,128)S(1)} %get-tuple-element.57.refs_0_), channel_id=1, source_target_pairs={{0,24},{4,28},{8,16},{12,20},{16,8},{20,12},{24,0},{28,4},{1,25},{... | collective-permute-start | bytes 196616 | tf_op jit(solution)/shard_map/ppermute | solution.py:501
  83.1 1.1 %collective-permute-start.19 = (f32[32,512]{1,0:T(8,128)S(1)}, f32[32,512]{1,0:T(8,128)S(1)}, u32[]{:S(2)}, u32[]{:S(2)}) collective-permute-start(f32[32,512]{1,0:T(8,128)S(1)} %get-tuple-element.57.refs_0_), channel_id=1, source_target_pairs={{0,16},{4,20},{8,24},{12,28},{16,0},{20,4},{24,8},{28,12},{1,17},{... | collective-permute-start | bytes 196616 | tf_op jit(solution)/shard_map/ppermute | solution.py:501
  84.1 0.8 collective-permute-start.18
  85.0 1.4 %backward_late.3 = (f32[256,512]{1,0:T(8,128)S(1)}, bf16[256,512]{1,0:T(8,128)(2,1)S(1)}) custom-call(bf16[4224,2048]{1,0:T(8,128)(2,1)S(1)} %densify.1.dense_ref, f32[4,256,512]{2,1,0:T(8,128)S(1)} %backward_early.1.early_ref, bf16[256,2048]{1,0:T(8,128)(2,1)S(1)} %collective-permute-done.14.siblings_ref), custom_call_target="tpu_custom_call" | custom-call | bytes 5550000 | tf_op jit(solution)/shard_map/backward_late/pallas_call | solution.py:407
  86.4 0.2 collective-permute-done.20.refs_3_
  86.6 0.7 collective-permute-done.19.refs_2_
  87.4 1.1 %collective-permute-done.18.refs_1_ = f32[32,512]{1,0:T(8,128)S(1)} collective-permute-done((f32[32,512]{1,0:T(8,128)S(1)}, f32[32,512]{1,0:T(8,128)S(1)}, u32[]{:S(2)}, u32[]{:S(2)}) %collective-permute-start.18) | collective-permute-done | bytes 65568 | tf_op jit(solution)/shard_map/ppermute | solution.py:501
  88.4 1.6 %collective-permute-done.21.refs_1_ = bf16[256,512]{1,0:T(8,128)(2,1)S(1)} collective-permute-done((bf16[256,512]{1,0:T(8,128)(2,1)S(1)}, bf16[256,512]{1,0:T(8,128)(2,1)S(1)}, u32[]{:S(2)}, u32[]{:S(2)}) %collective-permute-start.21) | collective-permute-done | bytes 262176 | tf_op jit(solution)/shard_map/ppermute | solution.py:501
  90.0 5.1 %collective-permute-done.24.refs_0_ = bf16[256,512]{1,0:T(8,128)(2,1)S(1)} collective-permute-done((bf16[256,512]{1,0:T(8,128)(2,1)S(1)}, bf16[256,512]{1,0:T(8,128)(2,1)S(1)}, u32[]{:S(2)}, u32[]{:S(2)}) %collective-permute-start.24) | collective-permute-done | bytes 262176 | tf_op jit(solution)/shard_map/ppermute | solution.py:501
  95.2 0.0 collective-permute-done.23.siblings_ref
  95.2 1.1 %finish.1 = (f32[256,256]{1,0:T(8,128)}, f32[256,256]{1,0:T(8,128)}, bf16[512,256]{1,0:T(8,128)(2,1)}) custom-call(f32[128,512]{1,0:T(8,128)S(1)} %join.1.mine_ref, f32[128,512]{1,0:T(8,128)S(1)} %collective-permute-done.23.siblings_ref, bf16[512,256]{1,0:T(8,128)(2,1)S(1)} %get-tuple-element.42.d_pre_ref, bf16[256,256]{1,0:T(8,128)(2,1)S(1)} %copy-done.1, ...), custom_call_target="tpu_custom_call" | custom-call | bytes 3700000 | tf_op jit(solution)/shard_map/finish/pallas_call | solution.py:488
  (19 shorter events, 0.2 us)
Async XLA Ops:
  0.6 18.0 %collective-permute-start.1 = (bf16[512,256]{1,0:T(8,128)(2,1)}, bf16[512,256]{1,0:T(8,128)(2,1)S(1)}, u32[]{:S(2)}, u32[]{:S(2)}) collective-permute-start(bf16[512,256]{1,0:T(8,128)(2,1)} %feat_ref.1), channel_id=1, source_target_pairs={{0,3},{1,2},{2,1},{3,0},{4,7},{5,6},{6,5},{7,4},{8,11},{9,10},{10,... | collective-permute-start | bytes 786440 | tf_op jit(solution)/shard_map/ppermute | solution.py:501
  5.7 13.3 %collective-permute-start = (bf16[512,256]{1,0:T(8,128)(2,1)}, bf16[512,256]{1,0:T(8,128)(2,1)S(1)}, u32[]{:S(2)}, u32[]{:S(2)}) collective-permute-start(bf16[512,256]{1,0:T(8,128)(2,1)} %feat_ref.1), channel_id=1, source_target_pairs={{0,1},{1,0},{2,3},{3,2},{4,5},{5,4},{6,7},{7,6},{8,9},{9,8},{10,11... | collective-permute-start | bytes 786440 | tf_op jit(solution)/shard_map/ppermute | solution.py:501
  5.7 22.5 %collective-permute-start.2 = (bf16[512,256]{1,0:T(8,128)(2,1)}, bf16[512,256]{1,0:T(8,128)(2,1)S(1)}, u32[]{:S(2)}, u32[]{:S(2)}) collective-permute-start(bf16[512,256]{1,0:T(8,128)(2,1)} %feat_ref.1), channel_id=1, source_target_pairs={{0,2},{1,3},{2,0},{3,1},{4,6},{5,7},{6,4},{7,5},{8,10},{9,11},{10,... | collective-permute-start | bytes 786440 | tf_op jit(solution)/shard_map/ppermute | solution.py:501
  7.1 11.9 %copy-start = (bf16[512,256]{1,0:T(8,128)(2,1)S(1)}, bf16[512,256]{1,0:T(8,128)(2,1)}, u32[]{:S(2)}) copy-start(bf16[512,256]{1,0:T(8,128)(2,1)} %feat_ref.1) | copy-start | bytes 786436
  29.2 2.4 %collective-permute-start.4 = (bf16[3,512,256]{2,1,0:T(8,128)(2,1)S(1)}, bf16[3,512,256]{2,1,0:T(8,128)(2,1)S(1)}, u32[]{:S(2)}, u32[]{:S(2)}) collective-permute-start(bf16[3,512,256]{2,1,0:T(8,128)(2,1)S(1)} %forward_late.7), channel_id=1, source_target_pairs={{0,4},{4,0},{8,12},{12,8},{16,20},{20,16},{24,28},{28,24},{1,5},{5... | collective-permute-start | bytes 2359304 | tf_op jit(solution)/shard_map/ppermute | solution.py:501
  29.6 6.0 %collective-permute-start.3 = (bf16[1,512,256]{2,1,0:T(8,128)(2,1)S(1)}, bf16[1,512,256]{2,1,0:T(8,128)(2,1)S(1)}, u32[]{:S(2)}, u32[]{:S(2)}) collective-permute-start(bf16[1,512,256]{2,1,0:T(8,128)(2,1)S(1)} %forward_late.5), channel_id=1, source_target_pairs={{0,4},{4,0},{8,12},{12,8},{16,20},{20,16},{24,28},{28,24},{1,5},{5... | collective-permute-start | bytes 786440 | tf_op jit(solution)/shard_map/ppermute | solution.py:501
  31.7 9.2 %collective-permute-start.5 = (bf16[512,256]{1,0:T(8,128)(2,1)S(1)}, bf16[512,256]{1,0:T(8,128)(2,1)S(1)}, u32[]{:S(2)}, u32[]{:S(2)}) collective-permute-start(bf16[512,256]{1,0:T(8,128)(2,1)S(1)} %get-tuple-element.36), channel_id=1, source_target_pairs={{0,8},{4,12},{8,0},{12,4},{16,24},{20,28},{24,16},{28,20},{1,9},{5... | collective-permute-start | bytes 786440 | tf_op jit(solution)/shard_map/ppermute | solution.py:501
  33.2 13.7 %collective-permute-start.6 = (bf16[512,256]{1,0:T(8,128)(2,1)S(1)}, bf16[512,256]{1,0:T(8,128)(2,1)S(1)}, u32[]{:S(2)}, u32[]{:S(2)}) collective-permute-start(bf16[512,256]{1,0:T(8,128)(2,1)S(1)} %get-tuple-element.37), channel_id=1, source_target_pairs={{0,16},{4,20},{8,24},{12,28},{16,0},{20,4},{24,8},{28,12},{1,17},{... | collective-permute-start | bytes 786440 | tf_op jit(solution)/shard_map/ppermute | solution.py:501
  34.8 12.2 %copy-start.1 = (bf16[256,256]{1,0:T(8,128)(2,1)S(1)}, bf16[256,256]{1,0:T(8,128)(2,1)}, u32[]{:S(2)}) copy-start(bf16[256,256]{1,0:T(8,128)(2,1)} %ws_ref.1) | copy-start | bytes 393220
  34.8 12.2 %copy-start.2 = (bf16[512,256]{1,0:T(8,128)(2,1)S(1)}, bf16[512,256]{1,0:T(8,128)(2,1)}, u32[]{:S(2)}) copy-start(bf16[512,256]{1,0:T(8,128)(2,1)} %refs_2_.1) | copy-start | bytes 786436
  34.8 12.2 %copy-start.3 = (bf16[256,256]{1,0:T(8,128)(2,1)S(1)}, bf16[256,256]{1,0:T(8,128)(2,1)}, u32[]{:S(2)}) copy-start(bf16[256,256]{1,0:T(8,128)(2,1)} %refs_4_.1) | copy-start | bytes 393220
  34.8 12.2 %copy-start.4 = (s32[512]{0:T(512)S(1)}, s32[512]{0:T(512)}, u32[]{:S(2)}) copy-start(s32[512]{0:T(512)} %param.10) | copy-start | bytes 6148
  34.8 12.2 %copy-start.5 = (f32[256]{0:T(256)S(1)}, f32[256]{0:T(256)}, u32[]{:S(2)}) copy-start(f32[256]{0:T(256)} %param.17) | copy-start | bytes 3076
  34.8 12.1 %collective-permute-start.7 = (bf16[512,256]{1,0:T(8,128)(2,1)S(1)}, bf16[512,256]{1,0:T(8,128)(2,1)S(1)}, u32[]{:S(2)}, u32[]{:S(2)}) collective-permute-start(bf16[512,256]{1,0:T(8,128)(2,1)S(1)} %get-tuple-element.38), channel_id=1, source_target_pairs={{0,24},{4,28},{8,16},{12,20},{16,8},{20,12},{24,0},{28,4},{1,25},{... | collective-permute-start | bytes 786440 | tf_op jit(solution)/shard_map/ppermute | solution.py:501
  48.6 3.6 %collective-permute-start.11 = (bf16[144,512]{1,0:T(8,128)(2,1)S(1)}, bf16[144,512]{1,0:T(8,128)(2,1)S(1)}, u32[]{:S(2)}, u32[]{:S(2)}) collective-permute-start(bf16[144,512]{1,0:T(8,128)(2,1)S(1)} %get-tuple-element.44), channel_id=1, source_target_pairs={{0,4},{4,0},{8,12},{12,8},{16,20},{20,16},{24,28},{28,24},{1,5},{5... | collective-permute-start | bytes 442376 | tf_op jit(solution)/shard_map/ppermute | solution.py:501
  48.6 12.9 %collective-permute-start.10 = (bf16[256,512]{1,0:T(8,128)(2,1)S(1)}, bf16[256,512]{1,0:T(8,128)(2,1)S(1)}, u32[]{:S(2)}, u32[]{:S(2)}) collective-permute-start(bf16[256,512]{1,0:T(8,128)(2,1)S(1)} %get-tuple-element.46.refs_0_), channel_id=1, source_target_pairs={{0,24},{4,28},{8,16},{12,20},{16,8},{20,12},{24,0},{28,4},{1,25},{... | collective-permute-start | bytes 786440 | tf_op jit(solution)/shard_map/ppermute | solution.py:501
  50.2 13.7 %collective-permute-start.9 = (bf16[256,512]{1,0:T(8,128)(2,1)S(1)}, bf16[256,512]{1,0:T(8,128)(2,1)S(1)}, u32[]{:S(2)}, u32[]{:S(2)}) collective-permute-start(bf16[256,512]{1,0:T(8,128)(2,1)S(1)} %get-tuple-element.46.refs_0_), channel_id=1, source_target_pairs={{0,16},{4,20},{8,24},{12,28},{16,0},{20,4},{24,8},{28,12},{1,17},{... | collective-permute-start | bytes 786440 | tf_op jit(solution)/shard_map/ppermute | solution.py:501
  51.4 12.6 %collective-permute-start.8 = (bf16[256,512]{1,0:T(8,128)(2,1)S(1)}, bf16[256,512]{1,0:T(8,128)(2,1)S(1)}, u32[]{:S(2)}, u32[]{:S(2)}) collective-permute-start(bf16[256,512]{1,0:T(8,128)(2,1)S(1)} %get-tuple-element.46.refs_0_), channel_id=1, source_target_pairs={{0,8},{4,12},{8,0},{12,4},{16,24},{20,28},{24,16},{28,20},{1,9},{5... | collective-permute-start | bytes 786440 | tf_op jit(solution)/shard_map/ppermute | solution.py:501
  52.2 9.3 %collective-permute-start.12 = (bf16[144,512]{1,0:T(8,128)(2,1)S(1)}, bf16[144,512]{1,0:T(8,128)(2,1)S(1)}, u32[]{:S(2)}, u32[]{:S(2)}) collective-permute-start(bf16[144,512]{1,0:T(8,128)(2,1)S(1)} %add_sent.3.keep_ref), channel_id=1, source_target_pairs={{0,2},{1,3},{2,0},{3,1},{4,6},{5,7},{6,4},{7,5},{8,10},{9,11},{10,... | collective-permute-start | bytes 442376 | tf_op jit(solution)/shard_map/ppermute | solution.py:501
  64.1 3.0 %collective-permute-start.14 = (bf16[256,2048]{1,0:T(8,128)(2,1)S(1)}, bf16[256,2048]{1,0:T(8,128)(2,1)S(1)}, u32[]{:S(2)}, u32[]{:S(2)}) collective-permute-start(bf16[256,2048]{1,0:T(8,128)(2,1)S(1)} %side_by_side.1.mine_ref), channel_id=1, source_target_pairs={{0,4},{4,0},{8,12},{12,8},{16,20},{20,16},{24,28},{28,24},{1,5},{5... | collective-permute-start | bytes 3145736 | tf_op jit(solution)/shard_map/ppermute | solution.py:501
  64.1 8.9 %collective-permute-start.13 = (bf16[144,512]{1,0:T(8,128)(2,1)S(1)}, bf16[144,512]{1,0:T(8,128)(2,1)S(1)}, u32[]{:S(2)}, u32[]{:S(2)}) collective-permute-start(bf16[144,512]{1,0:T(8,128)(2,1)S(1)} %add_sent.4.keep_ref), channel_id=1, source_target_pairs={{0,1},{1,0},{2,3},{3,2},{4,5},{5,4},{6,7},{7,6},{8,9},{9,8},{10,11... | collective-permute-start | bytes 442376 | tf_op jit(solution)/shard_map/ppermute | solution.py:501
  68.6 21.4 %collective-permute-start.21 = (bf16[256,512]{1,0:T(8,128)(2,1)S(1)}, bf16[256,512]{1,0:T(8,128)(2,1)S(1)}, u32[]{:S(2)}, u32[]{:S(2)}) collective-permute-start(bf16[256,512]{1,0:T(8,128)(2,1)S(1)} %get-tuple-element.50), channel_id=1, source_target_pairs={{0,2},{1,3},{2,0},{3,1},{4,6},{5,7},{6,4},{7,5},{8,10},{9,11},{10,... | collective-permute-start | bytes 786440 | tf_op jit(solution)/shard_map/ppermute | solution.py:501
  71.7 18.4 %collective-permute-start.22 = (bf16[256,512]{1,0:T(8,128)(2,1)S(1)}, bf16[256,512]{1,0:T(8,128)(2,1)S(1)}, u32[]{:S(2)}, u32[]{:S(2)}) collective-permute-start(bf16[256,512]{1,0:T(8,128)(2,1)S(1)} %get-tuple-element.51), channel_id=1, source_target_pairs={{0,3},{1,2},{2,1},{3,0},{4,7},{5,6},{6,5},{7,4},{8,11},{9,10},{10,... | collective-permute-start | bytes 786440 | tf_op jit(solution)/shard_map/ppermute | solution.py:501
  73.1 5.1 %collective-permute-start.15 = (f32[48,512]{1,0:T(8,128)S(1)}, f32[48,512]{1,0:T(8,128)S(1)}, u32[]{:S(2)}, u32[]{:S(2)}) collective-permute-start(f32[48,512]{1,0:T(8,128)S(1)} %get-tuple-element.54), channel_id=1, source_target_pairs={{0,8},{4,12},{8,0},{12,4},{16,24},{20,28},{24,16},{28,20},{1,9},{5... | collective-permute-start | bytes 294920 | tf_op jit(solution)/shard_map/ppermute | solution.py:501
  74.3 6.6 %collective-permute-start.16 = (f32[48,512]{1,0:T(8,128)S(1)}, f32[48,512]{1,0:T(8,128)S(1)}, u32[]{:S(2)}, u32[]{:S(2)}) collective-permute-start(f32[48,512]{1,0:T(8,128)S(1)} %get-tuple-element.55), channel_id=1, source_target_pairs={{0,16},{4,20},{8,24},{12,28},{16,0},{20,4},{24,8},{28,12},{1,17},{... | collective-permute-start | bytes 294920 | tf_op jit(solution)/shard_map/ppermute | solution.py:501
  75.1 5.8 %collective-permute-start.17 = (f32[48,512]{1,0:T(8,128)S(1)}, f32[48,512]{1,0:T(8,128)S(1)}, u32[]{:S(2)}, u32[]{:S(2)}) collective-permute-start(f32[48,512]{1,0:T(8,128)S(1)} %get-tuple-element.56), channel_id=1, source_target_pairs={{0,24},{4,28},{8,16},{12,20},{16,8},{20,12},{24,0},{28,4},{1,25},{... | collective-permute-start | bytes 294920 | tf_op jit(solution)/shard_map/ppermute | solution.py:501
  81.5 5.2 %collective-permute-start.20 = (f32[32,512]{1,0:T(8,128)S(1)}, f32[32,512]{1,0:T(8,128)S(1)}, u32[]{:S(2)}, u32[]{:S(2)}) collective-permute-start(f32[32,512]{1,0:T(8,128)S(1)} %get-tuple-element.57.refs_0_), channel_id=1, source_target_pairs={{0,24},{4,28},{8,16},{12,20},{16,8},{20,12},{24,0},{28,4},{1,25},{... | collective-permute-start | bytes 196616 | tf_op jit(solution)/shard_map/ppermute | solution.py:501
  83.1 4.3 %collective-permute-start.19 = (f32[32,512]{1,0:T(8,128)S(1)}, f32[32,512]{1,0:T(8,128)S(1)}, u32[]{:S(2)}, u32[]{:S(2)}) collective-permute-start(f32[32,512]{1,0:T(8,128)S(1)} %get-tuple-element.57.refs_0_), channel_id=1, source_target_pairs={{0,16},{4,20},{8,24},{12,28},{16,0},{20,4},{24,8},{28,12},{1,17},{... | collective-permute-start | bytes 196616 | tf_op jit(solution)/shard_map/ppermute | solution.py:501
  84.1 4.3 %collective-permute-start.18 = (f32[32,512]{1,0:T(8,128)S(1)}, f32[32,512]{1,0:T(8,128)S(1)}, u32[]{:S(2)}, u32[]{:S(2)}) collective-permute-start(f32[32,512]{1,0:T(8,128)S(1)} %get-tuple-element.57.refs_0_), channel_id=1, source_target_pairs={{0,8},{4,12},{8,0},{12,4},{16,24},{20,28},{24,16},{28,20},{1,9},{5... | collective-permute-start | bytes 196616 | tf_op jit(solution)/shard_map/ppermute | solution.py:501
  86.6 8.5 %collective-permute-start.24 = (bf16[256,512]{1,0:T(8,128)(2,1)S(1)}, bf16[256,512]{1,0:T(8,128)(2,1)S(1)}, u32[]{:S(2)}, u32[]{:S(2)}) collective-permute-start(bf16[256,512]{1,0:T(8,128)(2,1)S(1)} %get-tuple-element.60), channel_id=1, source_target_pairs={{0,1},{1,0},{2,3},{3,2},{4,5},{5,4},{6,7},{7,6},{8,9},{9,8},{10,11... | collective-permute-start | bytes 786440 | tf_op jit(solution)/shard_map/ppermute | solution.py:501
  90.0 5.1 %collective-permute-start.23 = (f32[128,512]{1,0:T(8,128)S(1)}, f32[128,512]{1,0:T(8,128)S(1)}, u32[]{:S(2)}, u32[]{:S(2)}) collective-permute-start(f32[128,512]{1,0:T(8,128)S(1)} %join.1.mine_ref), channel_id=1, source_target_pairs={{0,4},{4,0},{8,12},{12,8},{16,20},{20,16},{24,28},{28,24},{1,5},{5... | collective-permute-start | bytes 786440 | tf_op jit(solution)/shard_map/ppermute | solution.py:501

commit v7 on v6

--- a/solution.py
+++ b/solution.py
@@ -569,6 +569,7 @@
     got_last, _ = lax.optimization_barrier((got_last, far))
     cuts = chip_parts(add_sent(total, got_last, F32), n_row)
     arrivals = [swap(cuts[j], "row", 2 * j) for j in range(1, chips)]
+    arrivals, _ = lax.optimization_barrier((arrivals, near))
     piece, grad_bias = share_total([cuts[0]] + arrivals)
     shares = join([piece] + [swap(piece, "row", 2 * j) for j in range(1, chips)])
     shares, far_back = lax.optimization_barrier((shares, far_back))

time: 96.6 us -> 96.6 us (level)
  no operation moved by 1% of the time
where the time goes in v7:
time: 96.6 us; the launch traced here: 96.3 us
  waiting for transfers between devices  41.3 us (43%)
  Pallas kernels  28 us (29%)
  starting transfers between devices  25.3 us (26%)
    ppermute x25, waiting for transfers between devices, swap(): return lax.ppermute(x, axis, [(i, i ^ mask) for i in range(size)])  41.3 us
    ppermute x25, starting transfers between devices, swap(): return lax.ppermute(x, axis, [(i, i ^ mask) for i in range(size)])  25.3 us
    pallas_call x1, Pallas kernels, densify(): pl.pallas_call(kernel, out_shape=pltpu.VMEM(((rows + 1) * tile, cols * ti...  11.6 us
    pallas_call x1, Pallas kernels, forward_early(): pl.pallas_call(kernel, out_shape=sds((n_row, nodes, width), F32), grid=(n...  4.61 us
    pallas_call x2, Pallas kernels, backward_late(): pl.pallas_call(kernel, out_shape=outs, grid=(len(columns),), in_specs=[sp...  2.9 us
    pallas_call x1, Pallas kernels, backward_early(): pl.pallas_call(kernel, out_shape=sds((n_col, wide, nodes), F32), grid=(n_...  2.88 us
    pallas_call x4, Pallas kernels, forward_late(): pl.pallas_call(kernel, out_shape=sds((count, nodes, width), dtype), grid=...  2.4 us
  transfers between devices with their start and end apart: 25, of which 15 were waited for; matrix products, arithmetic and copies ran while one was open for 1% of the time, Pallas kernels for 25%

profile of v7, /device:TPU:0, one launch (start us, length us, event | category | flops | bytes accessed | tf_op | source)
XLA Modules:
  0.0 96.3 jit_solution(170453071518419484)
XLA Ops:
  0.6 5.1 %collective-permute-start.1 = (bf16[512,256]{1,0:T(8,128)(2,1)}, bf16[512,256]{1,0:T(8,128)(2,1)S(1)}, u32[]{:S(2)}, u32[]{:S(2)}) collective-permute-start(bf16[512,256]{1,0:T(8,128)(2,1)} %feat_ref.1), channel_id=1, source_target_pairs={{0,3},{1,2},{2,1},{3,0},{4,7},{5,6},{6,5},{7,4},{8,11},{9,10},{10,... | collective-permute-start | bytes 786440 | tf_op jit(solution)/shard_map/ppermute | solution.py:501
  5.7 0.0 collective-permute-start
  5.7 0.6 collective-permute-start.2
  6.4 0.7 fusion.6
  7.1 0.0 copy-start
  7.1 11.6 %densify.1.dense_ref = bf16[4224,2048]{1,0:T(8,128)(2,1)S(1)} custom-call(s32[384]{0:T(512)S(1)} %get-tuple-element.73.down_ref, s32[384]{0:T(512)S(1)} %get-tuple-element.74.right_ref, bf16[384,128,128]{2,1,0:T(8,128)(2,1)} %values_ref.1), custom_call_target="tpu_custom_call" | custom-call | bytes 37000000 | tf_op jit(solution)/shard_map/densify/pallas_call | solution.py:139
  18.7 0.0 collective-permute-done.1.refs_2_
  18.7 0.3 collective-permute-done.refs_1_
  19.0 4.6 %forward_early.1.early_ref = f32[8,512,256]{2,1,0:T(8,128)S(1)} custom-call(bf16[4224,2048]{1,0:T(8,128)(2,1)S(1)} %densify.1.dense_ref, bf16[512,256]{1,0:T(8,128)(2,1)S(1)} %copy-done, bf16[512,256]{1,0:T(8,128)(2,1)S(1)} %collective-permute-done.refs_1_, bf16[512,256]{1,0:T(8,128)(2,1)S(1)} %collective-permute-done.1.refs_2_), custom_call_target="tpu_custom_call" | custom-call | bytes 18500000 | tf_op jit(solution)/shard_map/forward_early/pallas_call | solution.py:174
  23.6 4.6 %collective-permute-done.2.piece_ref = bf16[512,256]{1,0:T(8,128)(2,1)S(1)} collective-permute-done((bf16[512,256]{1,0:T(8,128)(2,1)}, bf16[512,256]{1,0:T(8,128)(2,1)S(1)}, u32[]{:S(2)}, u32[]{:S(2)}) %collective-permute-start.2) | collective-permute-done | bytes 262176 | tf_op jit(solution)/shard_map/ppermute | solution.py:501
  28.3 0.9 forward_late.7
  29.2 0.1 collective-permute-start.4
  29.3 0.3 forward_late.5
  29.6 0.6 collective-permute-start.3
  30.1 0.9 forward_late.6.keep_ref
  31.0 0.5 collective-permute-done.4.got_ref
  31.5 0.1 add_parts.1
  31.7 1.6 %collective-permute-start.5 = (bf16[512,256]{1,0:T(8,128)(2,1)S(1)}, bf16[512,256]{1,0:T(8,128)(2,1)S(1)}, u32[]{:S(2)}, u32[]{:S(2)}) collective-permute-start(bf16[512,256]{1,0:T(8,128)(2,1)S(1)} %get-tuple-element.39), channel_id=1, source_target_pairs={{0,8},{4,12},{8,0},{12,4},{16,24},{20,28},{24,16},{28,20},{1,9},{5... | collective-permute-start | bytes 786440 | tf_op jit(solution)/shard_map/ppermute | solution.py:501
  33.2 1.5 %collective-permute-start.6 = (bf16[512,256]{1,0:T(8,128)(2,1)S(1)}, bf16[512,256]{1,0:T(8,128)(2,1)S(1)}, u32[]{:S(2)}, u32[]{:S(2)}) collective-permute-start(bf16[512,256]{1,0:T(8,128)(2,1)S(1)} %get-tuple-element.40), channel_id=1, source_target_pairs={{0,16},{4,20},{8,24},{12,28},{16,0},{20,4},{24,8},{28,12},{1,17},{... | collective-permute-start | bytes 786440 | tf_op jit(solution)/shard_map/ppermute | solution.py:501
  34.8 0.0 copy-start.5
  34.8 0.5 collective-permute-start.7
  35.3 0.3 forward_late.4.refs_6_
  35.6 0.0 collective-permute-done.3.refs_7_
  35.6 5.3 %collective-permute-done.5.refs_8_ = bf16[512,256]{1,0:T(8,128)(2,1)S(1)} collective-permute-done((bf16[512,256]{1,0:T(8,128)(2,1)S(1)}, bf16[512,256]{1,0:T(8,128)(2,1)S(1)}, u32[]{:S(2)}, u32[]{:S(2)}) %collective-permute-start.5) | collective-permute-done | bytes 262176 | tf_op jit(solution)/shard_map/ppermute | solution.py:501
  40.9 6.0 %collective-permute-done.6.refs_9_ = bf16[512,256]{1,0:T(8,128)(2,1)S(1)} collective-permute-done((bf16[512,256]{1,0:T(8,128)(2,1)S(1)}, bf16[512,256]{1,0:T(8,128)(2,1)S(1)}, u32[]{:S(2)}, u32[]{:S(2)}) %collective-permute-start.6) | collective-permute-done | bytes 262176 | tf_op jit(solution)/shard_map/ppermute | solution.py:501
  46.9 0.0 collective-permute-done.7.refs_10_
  47.0 1.2 %middle.1 = (bf16[512,256]{1,0:T(8,128)(2,1)}, bf16[512,256]{1,0:T(8,128)(2,1)S(1)}, bf16[512,256]{1,0:T(8,128)(2,1)S(1)}, bf16[256,512]{1,0:T(8,128)(2,1)S(1)}) custom-call(bf16[512,256]{1,0:T(8,128)(2,1)S(1)} %copy-done, s32[1,512]{1,0:T(1,128)S(1)} %bitcast.3, bf16[512,256]{1,0:T(8,128)(2,1)S(1)} %copy-done.2, bf16[256,256]{1,0:T(8,128)(2,1)S(1)} %copy-done.1, ...), custom_call_target="tpu_custom_call" | custom-call | bytes 5550000 | tf_op jit(solution)/shard_map/middle/pallas_call | solution.py:259
  48.2 0.4 local_grads.1
  48.6 0.1 collective-permute-start.11
  48.6 1.5 %collective-permute-start.10 = (bf16[256,512]{1,0:T(8,128)(2,1)S(1)}, bf16[256,512]{1,0:T(8,128)(2,1)S(1)}, u32[]{:S(2)}, u32[]{:S(2)}) collective-permute-start(bf16[256,512]{1,0:T(8,128)(2,1)S(1)} %get-tuple-element.49.refs_0_), channel_id=1, source_target_pairs={{0,24},{4,28},{8,16},{12,20},{16,8},{20,12},{24,0},{28,4},{1,25},{... | collective-permute-start | bytes 786440 | tf_op jit(solution)/shard_map/ppermute | solution.py:501
  50.2 1.2 %collective-permute-start.9 = (bf16[256,512]{1,0:T(8,128)(2,1)S(1)}, bf16[256,512]{1,0:T(8,128)(2,1)S(1)}, u32[]{:S(2)}, u32[]{:S(2)}) collective-permute-start(bf16[256,512]{1,0:T(8,128)(2,1)S(1)} %get-tuple-element.49.refs_0_), channel_id=1, source_target_pairs={{0,16},{4,20},{8,24},{12,28},{16,0},{20,4},{24,8},{28,12},{1,17},{... | collective-permute-start | bytes 786440 | tf_op jit(solution)/shard_map/ppermute | solution.py:501
  51.4 0.8 collective-permute-start.8
  52.2 0.0 collective-permute-done.11.got_ref
  52.2 0.1 collective-permute-start.12
  52.3 9.2 %collective-permute-done.12.got_ref = bf16[144,512]{1,0:T(8,128)(2,1)S(1)} collective-permute-done((bf16[144,512]{1,0:T(8,128)(2,1)S(1)}, bf16[144,512]{1,0:T(8,128)(2,1)S(1)}, u32[]{:S(2)}, u32[]{:S(2)}) %collective-permute-start.12) | collective-permute-done | bytes 147488 | tf_op jit(solution)/shard_map/ppermute | solution.py:501
  61.6 0.0 collective-permute-done.10.refs_3_
  61.6 2.3 %collective-permute-done.9.refs_2_ = bf16[256,512]{1,0:T(8,128)(2,1)S(1)} collective-permute-done((bf16[256,512]{1,0:T(8,128)(2,1)S(1)}, bf16[256,512]{1,0:T(8,128)(2,1)S(1)}, u32[]{:S(2)}, u32[]{:S(2)}) %collective-permute-start.9) | collective-permute-done | bytes 262176 | tf_op jit(solution)/shard_map/ppermute | solution.py:501
  63.9 0.1 collective-permute-done.8.refs_1_
  64.0 0.1 side_by_side.1.mine_ref
  64.1 0.1 collective-permute-start.14
  64.1 0.1 collective-permute-start.13
  64.2 2.9 %backward_early.1.early_ref = f32[4,256,512]{2,1,0:T(8,128)S(1)} custom-call(bf16[4224,2048]{1,0:T(8,128)(2,1)S(1)} %densify.1.dense_ref, bf16[256,2048]{1,0:T(8,128)(2,1)S(1)} %side_by_side.1.mine_ref), custom_call_target="tpu_custom_call" | custom-call | bytes 9250000 | tf_op jit(solution)/shard_map/backward_early/pallas_call | solution.py:375
  67.1 1.5 %backward_late.2 = (bf16[256,512]{1,0:T(8,128)(2,1)S(1)}, bf16[256,512]{1,0:T(8,128)(2,1)S(1)}) custom-call(bf16[4224,2048]{1,0:T(8,128)(2,1)S(1)} %densify.1.dense_ref, f32[4,256,512]{2,1,0:T(8,128)S(1)} %backward_early.1.early_ref, bf16[256,2048]{1,0:T(8,128)(2,1)S(1)} %collective-permute-done.14.siblings_ref), custom_call_target="tpu_custom_call" | custom-call | bytes 5550000 | tf_op jit(solution)/shard_map/backward_late/pallas_call | solution.py:407
  68.6 3.1 %collective-permute-start.21 = (bf16[256,512]{1,0:T(8,128)(2,1)S(1)}, bf16[256,512]{1,0:T(8,128)(2,1)S(1)}, u32[]{:S(2)}, u32[]{:S(2)}) collective-permute-start(bf16[256,512]{1,0:T(8,128)(2,1)S(1)} %get-tuple-element.53), channel_id=1, source_target_pairs={{0,2},{1,3},{2,0},{3,1},{4,6},{5,7},{6,4},{7,5},{8,10},{9,11},{10,... | collective-permute-start | bytes 786440 | tf_op jit(solution)/shard_map/ppermute | solution.py:501
  71.7 1.3 %collective-permute-start.22 = (bf16[256,512]{1,0:T(8,128)(2,1)S(1)}, bf16[256,512]{1,0:T(8,128)(2,1)S(1)}, u32[]{:S(2)}, u32[]{:S(2)}) collective-permute-start(bf16[256,512]{1,0:T(8,128)(2,1)S(1)} %get-tuple-element.54), channel_id=1, source_target_pairs={{0,3},{1,2},{2,1},{3,0},{4,7},{5,6},{6,5},{7,4},{8,11},{9,10},{10,... | collective-permute-start | bytes 786440 | tf_op jit(solution)/shard_map/ppermute | solution.py:501
  73.0 0.0 collective-permute-done.13.got_ref
  73.1 1.2 %collective-permute-start.15 = (f32[48,512]{1,0:T(8,128)S(1)}, f32[48,512]{1,0:T(8,128)S(1)}, u32[]{:S(2)}, u32[]{:S(2)}) collective-permute-start(f32[48,512]{1,0:T(8,128)S(1)} %get-tuple-element.57), channel_id=1, source_target_pairs={{0,8},{4,12},{8,0},{12,4},{16,24},{20,28},{24,16},{28,20},{1,9},{5... | collective-permute-start | bytes 294920 | tf_op jit(solution)/shard_map/ppermute | solution.py:501
  74.3 0.8 collective-permute-start.16
  75.1 1.5 %collective-permute-start.17 = (f32[48,512]{1,0:T(8,128)S(1)}, f32[48,512]{1,0:T(8,128)S(1)}, u32[]{:S(2)}, u32[]{:S(2)}) collective-permute-start(f32[48,512]{1,0:T(8,128)S(1)} %get-tuple-element.59), channel_id=1, source_target_pairs={{0,24},{4,28},{8,16},{12,20},{16,8},{20,12},{24,0},{28,4},{1,25},{... | collective-permute-start | bytes 294920 | tf_op jit(solution)/shard_map/ppermute | solution.py:501
  76.6 1.4 %backward_late.3 = (f32[256,512]{1,0:T(8,128)S(1)}, bf16[256,512]{1,0:T(8,128)(2,1)S(1)}) custom-call(bf16[4224,2048]{1,0:T(8,128)(2,1)S(1)} %densify.1.dense_ref, f32[4,256,512]{2,1,0:T(8,128)S(1)} %backward_early.1.early_ref, bf16[256,2048]{1,0:T(8,128)(2,1)S(1)} %collective-permute-done.14.siblings_ref), custom_call_target="tpu_custom_call" | custom-call | bytes 5550000 | tf_op jit(solution)/shard_map/backward_late/pallas_call | solution.py:407
  78.1 0.1 collective-permute-done.15.refs_1_
  78.2 2.7 %collective-permute-done.16.refs_2_ = f32[48,512]{1,0:T(8,128)S(1)} collective-permute-done((f32[48,512]{1,0:T(8,128)S(1)}, f32[48,512]{1,0:T(8,128)S(1)}, u32[]{:S(2)}, u32[]{:S(2)}) %collective-permute-start.16) | collective-permute-done | bytes 98336 | tf_op jit(solution)/shard_map/ppermute | solution.py:501
  80.9 0.0 collective-permute-done.17.refs_3_
  80.9 0.6 share_total.1
  81.5 1.6 %collective-permute-start.20 = (f32[32,512]{1,0:T(8,128)S(1)}, f32[32,512]{1,0:T(8,128)S(1)}, u32[]{:S(2)}, u32[]{:S(2)}) collective-permute-start(f32[32,512]{1,0:T(8,128)S(1)} %get-tuple-element.64.refs_0_), channel_id=1, source_target_pairs={{0,24},{4,28},{8,16},{12,20},{16,8},{20,12},{24,0},{28,4},{1,25},{... | collective-permute-start | bytes 196616 | tf_op jit(solution)/shard_map/ppermute | solution.py:501
  83.1 1.1 %collective-permute-start.19 = (f32[32,512]{1,0:T(8,128)S(1)}, f32[32,512]{1,0:T(8,128)S(1)}, u32[]{:S(2)}, u32[]{:S(2)}) collective-permute-start(f32[32,512]{1,0:T(8,128)S(1)} %get-tuple-element.64.refs_0_), channel_id=1, source_target_pairs={{0,16},{4,20},{8,24},{12,28},{16,0},{20,4},{24,8},{28,12},{1,17},{... | collective-permute-start | bytes 196616 | tf_op jit(solution)/shard_map/ppermute | solution.py:501
  84.1 0.8 collective-permute-start.18
  85.0 1.7 %collective-permute-done.20.refs_3_ = f32[32,512]{1,0:T(8,128)S(1)} collective-permute-done((f32[32,512]{1,0:T(8,128)S(1)}, f32[32,512]{1,0:T(8,128)S(1)}, u32[]{:S(2)}, u32[]{:S(2)}) %collective-permute-start.20) | collective-permute-done | bytes 65568 | tf_op jit(solution)/shard_map/ppermute | solution.py:501
  86.6 0.7 collective-permute-done.19.refs_2_
  87.4 1.1 %collective-permute-done.18.refs_1_ = f32[32,512]{1,0:T(8,128)S(1)} collective-permute-done((f32[32,512]{1,0:T(8,128)S(1)}, f32[32,512]{1,0:T(8,128)S(1)}, u32[]{:S(2)}, u32[]{:S(2)}) %collective-permute-start.18) | collective-permute-done | bytes 65568 | tf_op jit(solution)/shard_map/ppermute | solution.py:501
  88.4 1.6 %collective-permute-done.21.refs_1_ = bf16[256,512]{1,0:T(8,128)(2,1)S(1)} collective-permute-done((bf16[256,512]{1,0:T(8,128)(2,1)S(1)}, bf16[256,512]{1,0:T(8,128)(2,1)S(1)}, u32[]{:S(2)}, u32[]{:S(2)}) %collective-permute-start.21) | collective-permute-done | bytes 262176 | tf_op jit(solution)/shard_map/ppermute | solution.py:501
  90.0 5.1 %collective-permute-done.24.refs_0_ = bf16[256,512]{1,0:T(8,128)(2,1)S(1)} collective-permute-done((bf16[256,512]{1,0:T(8,128)(2,1)S(1)}, bf16[256,512]{1,0:T(8,128)(2,1)S(1)}, u32[]{:S(2)}, u32[]{:S(2)}) %collective-permute-start.24) | collective-permute-done | bytes 262176 | tf_op jit(solution)/shard_map/ppermute | solution.py:501
  95.2 0.0 collective-permute-done.23.siblings_ref
  95.2 1.1 %finish.1 = (f32[256,256]{1,0:T(8,128)}, f32[256,256]{1,0:T(8,128)}, bf16[512,256]{1,0:T(8,128)(2,1)}) custom-call(f32[128,512]{1,0:T(8,128)S(1)} %join.1.mine_ref, f32[128,512]{1,0:T(8,128)S(1)} %collective-permute-done.23.siblings_ref, bf16[512,256]{1,0:T(8,128)(2,1)S(1)} %get-tuple-element.45.d_pre_ref, bf16[256,256]{1,0:T(8,128)(2,1)S(1)} %copy-done.1, ...), custom_call_target="tpu_custom_call" | custom-call | bytes 3700000 | tf_op jit(solution)/shard_map/finish/pallas_call | solution.py:488
  (19 shorter events, 0.2 us)
Async XLA Ops:
  0.6 18.1 %collective-permute-start.1 = (bf16[512,256]{1,0:T(8,128)(2,1)}, bf16[512,256]{1,0:T(8,128)(2,1)S(1)}, u32[]{:S(2)}, u32[]{:S(2)}) collective-permute-start(bf16[512,256]{1,0:T(8,128)(2,1)} %feat_ref.1), channel_id=1, source_target_pairs={{0,3},{1,2},{2,1},{3,0},{4,7},{5,6},{6,5},{7,4},{8,11},{9,10},{10,... | collective-permute-start | bytes 786440 | tf_op jit(solution)/shard_map/ppermute | solution.py:501
  5.7 13.3 %collective-permute-start = (bf16[512,256]{1,0:T(8,128)(2,1)}, bf16[512,256]{1,0:T(8,128)(2,1)S(1)}, u32[]{:S(2)}, u32[]{:S(2)}) collective-permute-start(bf16[512,256]{1,0:T(8,128)(2,1)} %feat_ref.1), channel_id=1, source_target_pairs={{0,1},{1,0},{2,3},{3,2},{4,5},{5,4},{6,7},{7,6},{8,9},{9,8},{10,11... | collective-permute-start | bytes 786440 | tf_op jit(solution)/shard_map/ppermute | solution.py:501
  5.7 22.5 %collective-permute-start.2 = (bf16[512,256]{1,0:T(8,128)(2,1)}, bf16[512,256]{1,0:T(8,128)(2,1)S(1)}, u32[]{:S(2)}, u32[]{:S(2)}) collective-permute-start(bf16[512,256]{1,0:T(8,128)(2,1)} %feat_ref.1), channel_id=1, source_target_pairs={{0,2},{1,3},{2,0},{3,1},{4,6},{5,7},{6,4},{7,5},{8,10},{9,11},{10,... | collective-permute-start | bytes 786440 | tf_op jit(solution)/shard_map/ppermute | solution.py:501
  7.1 11.9 %copy-start = (bf16[512,256]{1,0:T(8,128)(2,1)S(1)}, bf16[512,256]{1,0:T(8,128)(2,1)}, u32[]{:S(2)}) copy-start(bf16[512,256]{1,0:T(8,128)(2,1)} %feat_ref.1) | copy-start | bytes 786436
  29.2 2.4 %collective-permute-start.4 = (bf16[3,512,256]{2,1,0:T(8,128)(2,1)S(1)}, bf16[3,512,256]{2,1,0:T(8,128)(2,1)S(1)}, u32[]{:S(2)}, u32[]{:S(2)}) collective-permute-start(bf16[3,512,256]{2,1,0:T(8,128)(2,1)S(1)} %forward_late.7), channel_id=1, source_target_pairs={{0,4},{4,0},{8,12},{12,8},{16,20},{20,16},{24,28},{28,24},{1,5},{5... | collective-permute-start | bytes 2359304 | tf_op jit(solution)/shard_map/ppermute | solution.py:501
  29.6 6.0 %collective-permute-start.3 = (bf16[1,512,256]{2,1,0:T(8,128)(2,1)S(1)}, bf16[1,512,256]{2,1,0:T(8,128)(2,1)S(1)}, u32[]{:S(2)}, u32[]{:S(2)}) collective-permute-start(bf16[1,512,256]{2,1,0:T(8,128)(2,1)S(1)} %forward_late.5), channel_id=1, source_target_pairs={{0,4},{4,0},{8,12},{12,8},{16,20},{20,16},{24,28},{28,24},{1,5},{5... | collective-permute-start | bytes 786440 | tf_op jit(solution)/shard_map/ppermute | solution.py:501
  31.7 9.2 %collective-permute-start.5 = (bf16[512,256]{1,0:T(8,128)(2,1)S(1)}, bf16[512,256]{1,0:T(8,128)(2,1)S(1)}, u32[]{:S(2)}, u32[]{:S(2)}) collective-permute-start(bf16[512,256]{1,0:T(8,128)(2,1)S(1)} %get-tuple-element.39), channel_id=1, source_target_pairs={{0,8},{4,12},{8,0},{12,4},{16,24},{20,28},{24,16},{28,20},{1,9},{5... | collective-permute-start | bytes 786440 | tf_op jit(solution)/shard_map/ppermute | solution.py:501
  33.2 13.7 %collective-permute-start.6 = (bf16[512,256]{1,0:T(8,128)(2,1)S(1)}, bf16[512,256]{1,0:T(8,128)(2,1)S(1)}, u32[]{:S(2)}, u32[]{:S(2)}) collective-permute-start(bf16[512,256]{1,0:T(8,128)(2,1)S(1)} %get-tuple-element.40), channel_id=1, source_target_pairs={{0,16},{4,20},{8,24},{12,28},{16,0},{20,4},{24,8},{28,12},{1,17},{... | collective-permute-start | bytes 786440 | tf_op jit(solution)/shard_map/ppermute | solution.py:501
  34.8 12.2 %copy-start.1 = (bf16[256,256]{1,0:T(8,128)(2,1)S(1)}, bf16[256,256]{1,0:T(8,128)(2,1)}, u32[]{:S(2)}) copy-start(bf16[256,256]{1,0:T(8,128)(2,1)} %ws_ref.1) | copy-start | bytes 393220
  34.8 12.2 %copy-start.2 = (bf16[512,256]{1,0:T(8,128)(2,1)S(1)}, bf16[512,256]{1,0:T(8,128)(2,1)}, u32[]{:S(2)}) copy-start(bf16[512,256]{1,0:T(8,128)(2,1)} %refs_2_.1) | copy-start | bytes 786436
  34.8 12.2 %copy-start.3 = (bf16[256,256]{1,0:T(8,128)(2,1)S(1)}, bf16[256,256]{1,0:T(8,128)(2,1)}, u32[]{:S(2)}) copy-start(bf16[256,256]{1,0:T(8,128)(2,1)} %refs_4_.1) | copy-start | bytes 393220
  34.8 12.2 %copy-start.4 = (s32[512]{0:T(512)S(1)}, s32[512]{0:T(512)}, u32[]{:S(2)}) copy-start(s32[512]{0:T(512)} %param.10) | copy-start | bytes 6148
  34.8 12.2 %copy-start.5 = (f32[256]{0:T(256)S(1)}, f32[256]{0:T(256)}, u32[]{:S(2)}) copy-start(f32[256]{0:T(256)} %param.17) | copy-start | bytes 3076
  34.8 12.1 %collective-permute-start.7 = (bf16[512,256]{1,0:T(8,128)(2,1)S(1)}, bf16[512,256]{1,0:T(8,128)(2,1)S(1)}, u32[]{:S(2)}, u32[]{:S(2)}) collective-permute-start(bf16[512,256]{1,0:T(8,128)(2,1)S(1)} %get-tuple-element.41), channel_id=1, source_target_pairs={{0,24},{4,28},{8,16},{12,20},{16,8},{20,12},{24,0},{28,4},{1,25},{... | collective-permute-start | bytes 786440 | tf_op jit(solution)/shard_map/ppermute | solution.py:501
  48.6 3.6 %collective-permute-start.11 = (bf16[144,512]{1,0:T(8,128)(2,1)S(1)}, bf16[144,512]{1,0:T(8,128)(2,1)S(1)}, u32[]{:S(2)}, u32[]{:S(2)}) collective-permute-start(bf16[144,512]{1,0:T(8,128)(2,1)S(1)} %get-tuple-element.47), channel_id=1, source_target_pairs={{0,4},{4,0},{8,12},{12,8},{16,20},{20,16},{24,28},{28,24},{1,5},{5... | collective-permute-start | bytes 442376 | tf_op jit(solution)/shard_map/ppermute | solution.py:501
  48.6 12.9 %collective-permute-start.10 = (bf16[256,512]{1,0:T(8,128)(2,1)S(1)}, bf16[256,512]{1,0:T(8,128)(2,1)S(1)}, u32[]{:S(2)}, u32[]{:S(2)}) collective-permute-start(bf16[256,512]{1,0:T(8,128)(2,1)S(1)} %get-tuple-element.49.refs_0_), channel_id=1, source_target_pairs={{0,24},{4,28},{8,16},{12,20},{16,8},{20,12},{24,0},{28,4},{1,25},{... | collective-permute-start | bytes 786440 | tf_op jit(solution)/shard_map/ppermute | solution.py:501
  50.2 13.7 %collective-permute-start.9 = (bf16[256,512]{1,0:T(8,128)(2,1)S(1)}, bf16[256,512]{1,0:T(8,128)(2,1)S(1)}, u32[]{:S(2)}, u32[]{:S(2)}) collective-permute-start(bf16[256,512]{1,0:T(8,128)(2,1)S(1)} %get-tuple-element.49.refs_0_), channel_id=1, source_target_pairs={{0,16},{4,20},{8,24},{12,28},{16,0},{20,4},{24,8},{28,12},{1,17},{... | collective-permute-start | bytes 786440 | tf_op jit(solution)/shard_map/ppermute | solution.py:501
  51.4 12.6 %collective-permute-start.8 = (bf16[256,512]{1,0:T(8,128)(2,1)S(1)}, bf16[256,512]{1,0:T(8,128)(2,1)S(1)}, u32[]{:S(2)}, u32[]{:S(2)}) collective-permute-start(bf16[256,512]{1,0:T(8,128)(2,1)S(1)} %get-tuple-element.49.refs_0_), channel_id=1, source_target_pairs={{0,8},{4,12},{8,0},{12,4},{16,24},{20,28},{24,16},{28,20},{1,9},{5... | collective-permute-start | bytes 786440 | tf_op jit(solution)/shard_map/ppermute | solution.py:501
  52.2 9.3 %collective-permute-start.12 = (bf16[144,512]{1,0:T(8,128)(2,1)S(1)}, bf16[144,512]{1,0:T(8,128)(2,1)S(1)}, u32[]{:S(2)}, u32[]{:S(2)}) collective-permute-start(bf16[144,512]{1,0:T(8,128)(2,1)S(1)} %add_sent.3.keep_ref), channel_id=1, source_target_pairs={{0,2},{1,3},{2,0},{3,1},{4,6},{5,7},{6,4},{7,5},{8,10},{9,11},{10,... | collective-permute-start | bytes 442376 | tf_op jit(solution)/shard_map/ppermute | solution.py:501
  64.1 3.0 %collective-permute-start.14 = (bf16[256,2048]{1,0:T(8,128)(2,1)S(1)}, bf16[256,2048]{1,0:T(8,128)(2,1)S(1)}, u32[]{:S(2)}, u32[]{:S(2)}) collective-permute-start(bf16[256,2048]{1,0:T(8,128)(2,1)S(1)} %side_by_side.1.mine_ref), channel_id=1, source_target_pairs={{0,4},{4,0},{8,12},{12,8},{16,20},{20,16},{24,28},{28,24},{1,5},{5... | collective-permute-start | bytes 3145736 | tf_op jit(solution)/shard_map/ppermute | solution.py:501
  64.1 8.9 %collective-permute-start.13 = (bf16[144,512]{1,0:T(8,128)(2,1)S(1)}, bf16[144,512]{1,0:T(8,128)(2,1)S(1)}, u32[]{:S(2)}, u32[]{:S(2)}) collective-permute-start(bf16[144,512]{1,0:T(8,128)(2,1)S(1)} %add_sent.4.keep_ref), channel_id=1, source_target_pairs={{0,1},{1,0},{2,3},{3,2},{4,5},{5,4},{6,7},{7,6},{8,9},{9,8},{10,11... | collective-permute-start | bytes 442376 | tf_op jit(solution)/shard_map/ppermute | solution.py:501
  68.6 21.4 %collective-permute-start.21 = (bf16[256,512]{1,0:T(8,128)(2,1)S(1)}, bf16[256,512]{1,0:T(8,128)(2,1)S(1)}, u32[]{:S(2)}, u32[]{:S(2)}) collective-permute-start(bf16[256,512]{1,0:T(8,128)(2,1)S(1)} %get-tuple-element.53), channel_id=1, source_target_pairs={{0,2},{1,3},{2,0},{3,1},{4,6},{5,7},{6,4},{7,5},{8,10},{9,11},{10,... | collective-permute-start | bytes 786440 | tf_op jit(solution)/shard_map/ppermute | solution.py:501
  71.7 18.4 %collective-permute-start.22 = (bf16[256,512]{1,0:T(8,128)(2,1)S(1)}, bf16[256,512]{1,0:T(8,128)(2,1)S(1)}, u32[]{:S(2)}, u32[]{:S(2)}) collective-permute-start(bf16[256,512]{1,0:T(8,128)(2,1)S(1)} %get-tuple-element.54), channel_id=1, source_target_pairs={{0,3},{1,2},{2,1},{3,0},{4,7},{5,6},{6,5},{7,4},{8,11},{9,10},{10,... | collective-permute-start | bytes 786440 | tf_op jit(solution)/shard_map/ppermute | solution.py:501
  73.1 5.1 %collective-permute-start.15 = (f32[48,512]{1,0:T(8,128)S(1)}, f32[48,512]{1,0:T(8,128)S(1)}, u32[]{:S(2)}, u32[]{:S(2)}) collective-permute-start(f32[48,512]{1,0:T(8,128)S(1)} %get-tuple-element.57), channel_id=1, source_target_pairs={{0,8},{4,12},{8,0},{12,4},{16,24},{20,28},{24,16},{28,20},{1,9},{5... | collective-permute-start | bytes 294920 | tf_op jit(solution)/shard_map/ppermute | solution.py:501
  74.3 6.6 %collective-permute-start.16 = (f32[48,512]{1,0:T(8,128)S(1)}, f32[48,512]{1,0:T(8,128)S(1)}, u32[]{:S(2)}, u32[]{:S(2)}) collective-permute-start(f32[48,512]{1,0:T(8,128)S(1)} %get-tuple-element.58), channel_id=1, source_target_pairs={{0,16},{4,20},{8,24},{12,28},{16,0},{20,4},{24,8},{28,12},{1,17},{... | collective-permute-start | bytes 294920 | tf_op jit(solution)/shard_map/ppermute | solution.py:501
  75.1 5.8 %collective-permute-start.17 = (f32[48,512]{1,0:T(8,128)S(1)}, f32[48,512]{1,0:T(8,128)S(1)}, u32[]{:S(2)}, u32[]{:S(2)}) collective-permute-start(f32[48,512]{1,0:T(8,128)S(1)} %get-tuple-element.59), channel_id=1, source_target_pairs={{0,24},{4,28},{8,16},{12,20},{16,8},{20,12},{24,0},{28,4},{1,25},{... | collective-permute-start | bytes 294920 | tf_op jit(solution)/shard_map/ppermute | solution.py:501
  81.5 5.2 %collective-permute-start.20 = (f32[32,512]{1,0:T(8,128)S(1)}, f32[32,512]{1,0:T(8,128)S(1)}, u32[]{:S(2)}, u32[]{:S(2)}) collective-permute-start(f32[32,512]{1,0:T(8,128)S(1)} %get-tuple-element.64.refs_0_), channel_id=1, source_target_pairs={{0,24},{4,28},{8,16},{12,20},{16,8},{20,12},{24,0},{28,4},{1,25},{... | collective-permute-start | bytes 196616 | tf_op jit(solution)/shard_map/ppermute | solution.py:501
  83.1 4.3 %collective-permute-start.19 = (f32[32,512]{1,0:T(8,128)S(1)}, f32[32,512]{1,0:T(8,128)S(1)}, u32[]{:S(2)}, u32[]{:S(2)}) collective-permute-start(f32[32,512]{1,0:T(8,128)S(1)} %get-tuple-element.64.refs_0_), channel_id=1, source_target_pairs={{0,16},{4,20},{8,24},{12,28},{16,0},{20,4},{24,8},{28,12},{1,17},{... | collective-permute-start | bytes 196616 | tf_op jit(solution)/shard_map/ppermute | solution.py:501
  84.1 4.3 %collective-permute-start.18 = (f32[32,512]{1,0:T(8,128)S(1)}, f32[32,512]{1,0:T(8,128)S(1)}, u32[]{:S(2)}, u32[]{:S(2)}) collective-permute-start(f32[32,512]{1,0:T(8,128)S(1)} %get-tuple-element.64.refs_0_), channel_id=1, source_target_pairs={{0,8},{4,12},{8,0},{12,4},{16,24},{20,28},{24,16},{28,20},{1,9},{5... | collective-permute-start | bytes 196616 | tf_op jit(solution)/shard_map/ppermute | solution.py:501
  86.6 8.5 %collective-permute-start.24 = (bf16[256,512]{1,0:T(8,128)(2,1)S(1)}, bf16[256,512]{1,0:T(8,128)(2,1)S(1)}, u32[]{:S(2)}, u32[]{:S(2)}) collective-permute-start(bf16[256,512]{1,0:T(8,128)(2,1)S(1)} %get-tuple-element.60), channel_id=1, source_target_pairs={{0,1},{1,0},{2,3},{3,2},{4,5},{5,4},{6,7},{7,6},{8,9},{9,8},{10,11... | collective-permute-start | bytes 786440 | tf_op jit(solution)/shard_map/ppermute | solution.py:501
  90.0 5.1 %collective-permute-start.23 = (f32[128,512]{1,0:T(8,128)S(1)}, f32[128,512]{1,0:T(8,128)S(1)}, u32[]{:S(2)}, u32[]{:S(2)}) collective-permute-start(f32[128,512]{1,0:T(8,128)S(1)} %join.1.mine_ref), channel_id=1, source_target_pairs={{0,4},{4,0},{8,12},{12,8},{16,20},{20,16},{24,28},{28,24},{1,5},{5... | collective-permute-start | bytes 786440 | tf_op jit(solution)/shard_map/ppermute | solution.py:501
